TPU v7x, 32 devices: a whole 2x2x4 slice. The times are simulated.
32 devices in a mesh: gx: 4 (over z), gy: 2 (over x), gz: 4 (over y, core).
Axes of the slice: x: 2, y: 2, z: 4, core: 2. Of those that a mesh axis runs over, the one named last changes fastest.
Arguments:
- inputs: bfloat16 [1, 32, 16, 8, 512], P(None, None, 'gx', 'gy', 'gz'), may hold values from -40 to 40
- noise: bfloat16 [1, 32, 16, 8, 512], P(None, None, 'gx', 'gy', 'gz'), may hold values from -6 to 6
- w_first: bfloat16 [32, 864], replicated, may hold values from -0.21875 to 0.21875
- w_second: bfloat16 [32, 864], replicated, may hold values from -0.21875 to 0.21875
Outputs:
- prediction: bfloat16 [1, 32, 16, 8, 512], P(None, None, 'gx', 'gy', 'gz')
- fisher_first: float32 [32, 864], replicated
- fisher_second: float32 [32, 864], replicated
All inputs are finite; a program needn't handle non-finite values.
Results may differ from a plain program's by a relative error of at most 0.0049.
Values may be sent and summed in bfloat16 or wider, within the bound.
No kernel may reach another device: no remote copies, remote signals or barrier semaphores. Data moves between devices by JAX's collectives and lax.ppermute only.
A program may use at most 128 MiB of HBM per device.

v0:
```python
import math

import jax
import jax.numpy as jnp
from jax import lax
from jax.sharding import PartitionSpec as P


def padded_2(x, sides, width):
    for axis, dim in sides:
        size, length = (lax.axis_size(axis), x.shape[dim])
        up = [(i, (i + 1) % size) for i in range(size - 1)]
        down = [(j, i) for i, j in up]
        last = lax.slice_in_dim(x, length - width, length, axis=dim)
        initial = lax.slice_in_dim(x, 0, width, axis=dim)
        before = lax.ppermute(last, axis, up)
        after = lax.ppermute(initial, axis, down)
        x = jnp.concatenate([before, x, after], axis=dim)
    return x


def stack_taps(padded, extent, flipped):
    size_x, size_y, size_z = extent
    pieces = []
    for shift_x in range(3):
        for shift_y in range(3):
            for shift_z in range(3):
                if flipped:
                    anchor = (2 - shift_x, 2 - shift_y, 2 - shift_z)
                else:
                    anchor = (shift_x, shift_y, shift_z)
                pieces.append(
                    padded[
                        :,
                        anchor[0] : anchor[0] + size_x,
                        anchor[1] : anchor[1] + size_y,
                        anchor[2] : anchor[2] + size_z,
                    ]
                )
    stacked = jnp.stack(pieces, axis=0)
    return stacked.reshape(27 * padded.shape[0], size_x * size_y * size_z)


def silu_slope(pre_act):
    sigmoid_value = jax.nn.sigmoid(pre_act)
    return sigmoid_value * (1.0 + pre_act * (1.0 - sigmoid_value))


def weight_grad(left_side, patches):
    return lax.dot_general(
        left_side, patches, (((1,), (1,)), ((), ())), preferred_element_type=jnp.float32
    )


def local(inputs, noise, w_first, w_second):
    samples, channels, size_x, size_y, size_z = inputs.shape
    extent = (size_x, size_y, size_z)
    cell_count = size_x * size_y * size_z
    devices = lax.axis_size("gx") * lax.axis_size("gy") * lax.axis_size("gz")
    norm_factor = 1.0 / math.sqrt(cell_count * devices)
    w_back = (
        w_second.reshape(channels, 27, channels).transpose(2, 1, 0).reshape(channels, 27 * channels)
    )
    noise_wide = padded_2(noise, (("gx", 2), ("gy", 3), ("gz", 4)), 1)
    input_wide = padded_2(inputs, (("gx", 2), ("gy", 3), ("gz", 4)), 1)
    sample = 0
    patches = stack_taps(input_wide[sample], extent, False)
    pre_act = jnp.dot(w_first, patches, preferred_element_type=jnp.float32)
    hidden = jax.nn.silu(pre_act).astype(jnp.bfloat16).reshape(channels, size_x, size_y, size_z)
    hidden_pads = [padded_2(hidden, (("gx", 1), ("gy", 2), ("gz", 3)), 1)]
    pre_all = [pre_act]
    input_patches = [patches]
    sample = 0
    hidden_patches = stack_taps(hidden_pads[sample], extent, False)
    output_value = jnp.dot(w_second, hidden_patches, preferred_element_type=jnp.float32)
    predictions = [output_value.astype(jnp.bfloat16).reshape(channels, size_x, size_y, size_z)]
    noise_flat = noise[sample].reshape(channels, cell_count)
    second_grads = [weight_grad(noise_flat, hidden_patches)]
    back_grad = jnp.dot(
        w_back, stack_taps(noise_wide[sample], extent, True), preferred_element_type=jnp.float32
    )
    pre_grad = (back_grad * silu_slope(pre_all[sample])).astype(jnp.bfloat16)
    first_grads = [weight_grad(pre_grad, input_patches[sample])]
    prediction = jnp.stack(predictions, axis=0)
    first_all = jnp.stack(first_grads, axis=0)
    second_all = jnp.stack(second_grads, axis=0)
    first_sum, second_sum = lax.psum((first_all, second_all), ("gx", "gy", "gz"))
    fisher_first = jnp.mean(jnp.square(first_sum * norm_factor), axis=0)
    fisher_second = jnp.mean(jnp.square(second_sum * norm_factor), axis=0)
    return (prediction, fisher_first, fisher_second)


def solution(mesh):
    in_specs = (P(None, None, "gx", "gy", "gz"), P(None, None, "gx", "gy", "gz"), P(), P())
    out_specs = (P(None, None, "gx", "gy", "gz"), P(), P())
    return jax.shard_map(local, mesh=mesh, in_specs=in_specs, out_specs=out_specs, check_vma=False)
```

profile of v0, /device:TPU:0, one launch (start us, length us, event | category | flops | bytes accessed | tf_op | source)
XLA Modules:
  0.0 292.6 jit_solution(9628496558548862126)
XLA Ops:
  8.0 4.9 %collective-permute-start.12 = (bf16[1,32,1,4,128]{4,3,2,1,0:T(4,128)(2,1)S(1)}, bf16[1,32,1,4,128]{4,3,2,1,0:T(4,128)(2,1)S(1)}, u32[]{:S(2)}, u32[]{:S(2)}) collective-permute-start(bf16[1,32,1,4,128]{4,3,2,1,0:T(4,128)(2,1)S(1)} %get-tuple-element.20), channel_id=1, source_target_pairs={{0,8},{8,16},{16,24},{1,9},{9,17},{17,25},{2,10},{10,18},{18,26},{... | collective-permute-start | bytes 98312 | tf_op jit(solution)/shard_map/ppermute | solution.py:16
  13.0 1.3 collective-permute-start.13
  15.1 4.5 %collective-permute-start = (bf16[1,32,1,4,128]{4,3,2,1,0:T(4,128)(2,1)S(1)}, bf16[1,32,1,4,128]{4,3,2,1,0:T(4,128)(2,1)S(1)}, u32[]{:S(2)}, u32[]{:S(2)}) collective-permute-start(bf16[1,32,1,4,128]{4,3,2,1,0:T(4,128)(2,1)S(1)} %get-tuple-element.24), channel_id=1, source_target_pairs={{0,8},{8,16},{16,24},{1,9},{9,17},{17,25},{2,10},{10,18},{18,26},{... | collective-permute-start | bytes 98312 | tf_op jit(solution)/shard_map/ppermute | solution.py:16
  19.6 1.3 collective-permute-start.1
  20.9 1.0 reshape_squeeze.3
  21.9 1.0 reshape.30
  23.8 1.0 constant_dynamic-update-slice_fusion.61
  24.9 3.4 %collective-permute-start.14 = (bf16[1,32,6,1,128]{4,3,2,1,0:T(2,128)(2,1)S(1)}, bf16[1,32,6,1,128]{4,3,2,1,0:T(2,128)(2,1)S(1)}, u32[]{:S(2)}, u32[]{:S(2)}) collective-permute-start(bf16[1,32,6,1,128]{4,3,2,1,0:T(2,128)(2,1)S(1)} %get-tuple-element.13), channel_id=1, source_target_pairs={{0,4},{1,5},{2,6},{3,7},{8,12},{9,13},{10,14},{11,15},{16,20},{17,... | collective-permute-start | bytes 147464 | tf_op jit(solution)/shard_map/ppermute | solution.py:16
  28.4 1.3 collective-permute-start.15
  29.7 1.0 constant_dynamic-update-slice_fusion.1
  30.8 4.6 %collective-permute-start.2 = (bf16[1,32,6,1,128]{4,3,2,1,0:T(2,128)(2,1)S(1)}, bf16[1,32,6,1,128]{4,3,2,1,0:T(2,128)(2,1)S(1)}, u32[]{:S(2)}, u32[]{:S(2)}) collective-permute-start(bf16[1,32,6,1,128]{4,3,2,1,0:T(2,128)(2,1)S(1)} %get-tuple-element.17), channel_id=1, source_target_pairs={{0,4},{1,5},{2,6},{3,7},{8,12},{9,13},{10,14},{11,15},{16,20},{17,... | collective-permute-start | bytes 147464 | tf_op jit(solution)/shard_map/ppermute | solution.py:16
  35.4 1.3 collective-permute-start.3
  37.3 1.3 collective-permute-start.16
  38.6 1.3 collective-permute-start.17
  39.9 2.0 collective-permute-done.3
  42.5 2.8 collective-permute-start.4
  45.3 1.5 collective-permute-start.5
  46.8 1.2 maximum_bitcast_fusion.1
  52.2 1.7 copy-done.1
  53.9 1.2 maximum_bitcast_fusion
  58.2 0.8 constant_dynamic-update-slice_fusion.25
  59.0 0.9 constant_dynamic-update-slice_fusion.24
  60.6 0.9 constant_dynamic-update-slice_fusion.22
  66.2 0.9 constant_dynamic-update-slice_fusion.15
  68.6 0.9 constant_dynamic-update-slice_fusion.12
  72.4 0.8 constant_dynamic-update-slice_fusion.7
  73.3 0.8 constant_dynamic-update-slice_fusion.6
  75.7 0.9 constant_dynamic-update-slice_fusion.3
  76.6 7.0 %reshape.26 = bf16[864,2048]{1,0:T(8,128)(2,1)} reshape(bf16[27,32,4,4,128]{4,3,2,1,0:T(4,128)(2,1)} %constant_dynamic-update-slice_fusion.3) | data formatting | bytes 7077888 | tf_op jit(solution)/shard_map/reshape | solution.py:41
  83.5 2.7 multiply_convert_fusion
  86.4 4.8 %collective-permute-start.6 = (bf16[32,1,4,128]{3,2,1,0:T(4,128)(2,1)S(1)}, bf16[32,1,4,128]{3,2,1,0:T(4,128)(2,1)S(1)}, u32[]{:S(2)}, u32[]{:S(2)}) collective-permute-start(bf16[32,1,4,128]{3,2,1,0:T(4,128)(2,1)S(1)} %get-tuple-element.22), channel_id=1, source_target_pairs={{0,8},{8,16},{16,24},{1,9},{9,17},{17,25},{2,10},{10,18},{18,26},{... | collective-permute-start | bytes 98312 | tf_op jit(solution)/shard_map/ppermute | solution.py:16
  92.0 1.3 collective-permute-start.7
  93.4 4.4 %collective-permute-done.7 = bf16[32,1,4,128]{3,2,1,0:T(4,128)(2,1)S(1)} collective-permute-done((bf16[32,1,4,128]{3,2,1,0:T(4,128)(2,1)S(1)}, bf16[32,1,4,128]{3,2,1,0:T(4,128)(2,1)S(1)}, u32[]{:S(2)}, u32[]{:S(2)}) %collective-permute-start.7) | collective-permute-done | bytes 32800 | tf_op jit(solution)/shard_map/ppermute | solution.py:17
  97.9 4.6 %collective-permute-start.8 = (bf16[32,6,1,128]{3,2,1,0:T(2,128)(2,1)S(1)}, bf16[32,6,1,128]{3,2,1,0:T(2,128)(2,1)S(1)}, u32[]{:S(2)}, u32[]{:S(2)}) collective-permute-start(bf16[32,6,1,128]{3,2,1,0:T(2,128)(2,1)S(1)} %get-tuple-element.15), channel_id=1, source_target_pairs={{0,4},{1,5},{2,6},{3,7},{8,12},{9,13},{10,14},{11,15},{16,20},{17,... | collective-permute-start | bytes 147464 | tf_op jit(solution)/shard_map/ppermute | solution.py:16
  102.5 1.3 collective-permute-start.9
  104.5 7.0 %reshape.29 = bf16[864,2048]{1,0:T(8,128)(2,1)} reshape(bf16[27,32,4,4,128]{4,3,2,1,0:T(4,128)(2,1)} %constant_dynamic-update-slice_fusion.63) | data formatting | bytes 7077888 | tf_op jit(solution)/shard_map/reshape | solution.py:41
  112.0 3.4 %collective-permute-start.10 = (bf16[32,6,6,1]{3,2,1,0:T(8,128)(2,1)S(1)}, bf16[32,6,6,1]{3,2,1,0:T(8,128)(2,1)S(1)}, u32[]{:S(2)}, u32[]{:S(2)}) collective-permute-start(bf16[32,6,6,1]{3,2,1,0:T(8,128)(2,1)S(1)} %get-tuple-element.10), channel_id=1, source_target_pairs={{0,1},{1,2},{2,3},{4,5},{5,6},{6,7},{8,9},{9,10},{10,11},{12,13},{... | collective-permute-start | bytes 6920 | tf_op jit(solution)/shard_map/ppermute | solution.py:16
  115.4 1.3 collective-permute-start.11
  116.7 5.4 %fusion.4 = f32[1,32,864]{2,1,0:T(8,128)} fusion(bf16[864,2048]{1,0:T(8,128)(2,1)} %reshape.26, bf16[32,864]{1,0:T(8,128)(2,1)S(1)} %reshape.31, bf16[864,2048]{1,0:T(8,128)(2,1)} %reshape.29, f32[32,2048]{1,0:T(8,128)S(1)} %get-tuple-element.26), kind=kOutput, calls=%fused_computation.7 | convolution fusion | flops 227082240 | bytes 7505920 | tf_op jit(solution)/shard_map/dot_general | solution.py:50
  122.2 1.6 pad_maximum_fusion
  129.9 0.9 constant_dynamic-update-slice_fusion.51
  134.5 0.9 constant_dynamic-update-slice_fusion.45
  136.9 0.9 constant_dynamic-update-slice_fusion.42
  144.7 7.0 %reshape.28 = bf16[864,2048]{1,0:T(8,128)(2,1)} reshape(bf16[27,32,4,4,128]{4,3,2,1,0:T(4,128)(2,1)} %constant_dynamic-update-slice_fusion.33) | data formatting | bytes 7077888 | tf_op jit(solution)/shard_map/reshape | solution.py:41
  151.6 3.8 %convolution_bitcast_fusion.2 = f32[1,32,864]{2,1,0:T(8,128)} fusion(bf16[864,2048]{1,0:T(8,128)(2,1)} %reshape.28, bf16[32,2048]{1,0:T(8,128)(2,1)S(1)} %reshape_squeeze.3), kind=kOutput, calls=%fused_computation.8 | convolution fusion | flops 113246208 | bytes 3780608 | tf_op jit(solution)/shard_map/dot_general | solution.py:50
  155.5 2.7 fusion.2
  159.0 125.1 %all-reduce.3.cloned.1.call-done = (f32[1,32,864]{2,1,0:T(8,128)}, f32[1,32,864]{2,1,0:T(8,128)}) async-done(((f32[1,32,864]{2,1,0:T(8,128)}, f32[1,32,864]{2,1,0:T(8,128)}), (f32[1,32,864]{2,1,0:T(8,128)}, f32[1,32,864]{2,1,0:T(8,128)})) %all-reduce.3.cloned.1.call-update) | async-done | bytes 221200 | tf_op jit(solution)/shard_map/psum | solution.py:87
  284.1 1.7 multiply_bitcast_fusion
  (117 shorter events, 44.0 us)
Async XLA Ops:
  7.2 76.4 %copy-start = (bf16[32,864]{1,0:T(8,128)(2,1)S(1)}, bf16[32,864]{1,0:T(8,128)(2,1)}, u32[]{:S(2)}) copy-start(bf16[32,864]{1,0:T(8,128)(2,1)} %param.6) | copy-start | bytes 165892
  7.2 276.9 %all-reduce.3.cloned.1.call-start = ((), (), s32[]{:S(2)}) async-start(), calls=%async_computation | async-start | bytes 458752 | tf_op jit(solution)/shard_map/psum | solution.py:87
  8.0 15.7 %collective-permute-start.12 = (bf16[1,32,1,4,128]{4,3,2,1,0:T(4,128)(2,1)S(1)}, bf16[1,32,1,4,128]{4,3,2,1,0:T(4,128)(2,1)S(1)}, u32[]{:S(2)}, u32[]{:S(2)}) collective-permute-start(bf16[1,32,1,4,128]{4,3,2,1,0:T(4,128)(2,1)S(1)} %get-tuple-element.20), channel_id=1, source_target_pairs={{0,8},{8,16},{16,24},{1,9},{9,17},{17,25},{2,10},{10,18},{18,26},{... | collective-permute-start | bytes 98312 | tf_op jit(solution)/shard_map/ppermute | solution.py:16
  13.0 11.8 %collective-permute-start.13 = (bf16[1,32,1,4,128]{4,3,2,1,0:T(4,128)(2,1)S(1)}, bf16[1,32,1,4,128]{4,3,2,1,0:T(4,128)(2,1)S(1)}, u32[]{:S(2)}, u32[]{:S(2)}) collective-permute-start(bf16[1,32,1,4,128]{4,3,2,1,0:T(4,128)(2,1)S(1)} %get-tuple-element.19), channel_id=1, source_target_pairs={{8,0},{16,8},{24,16},{9,1},{17,9},{25,17},{10,2},{18,10},{26,18},{... | collective-permute-start | bytes 98312 | tf_op jit(solution)/shard_map/ppermute | solution.py:17
  15.1 14.6 %collective-permute-start = (bf16[1,32,1,4,128]{4,3,2,1,0:T(4,128)(2,1)S(1)}, bf16[1,32,1,4,128]{4,3,2,1,0:T(4,128)(2,1)S(1)}, u32[]{:S(2)}, u32[]{:S(2)}) collective-permute-start(bf16[1,32,1,4,128]{4,3,2,1,0:T(4,128)(2,1)S(1)} %get-tuple-element.24), channel_id=1, source_target_pairs={{0,8},{8,16},{16,24},{1,9},{9,17},{17,25},{2,10},{10,18},{18,26},{... | collective-permute-start | bytes 98312 | tf_op jit(solution)/shard_map/ppermute | solution.py:16
  19.6 11.0 %collective-permute-start.1 = (bf16[1,32,1,4,128]{4,3,2,1,0:T(4,128)(2,1)S(1)}, bf16[1,32,1,4,128]{4,3,2,1,0:T(4,128)(2,1)S(1)}, u32[]{:S(2)}, u32[]{:S(2)}) collective-permute-start(bf16[1,32,1,4,128]{4,3,2,1,0:T(4,128)(2,1)S(1)} %get-tuple-element.23), channel_id=1, source_target_pairs={{8,0},{16,8},{24,16},{9,1},{17,9},{25,17},{10,2},{18,10},{26,18},{... | collective-permute-start | bytes 98312 | tf_op jit(solution)/shard_map/ppermute | solution.py:17
  24.9 11.8 %collective-permute-start.14 = (bf16[1,32,6,1,128]{4,3,2,1,0:T(2,128)(2,1)S(1)}, bf16[1,32,6,1,128]{4,3,2,1,0:T(2,128)(2,1)S(1)}, u32[]{:S(2)}, u32[]{:S(2)}) collective-permute-start(bf16[1,32,6,1,128]{4,3,2,1,0:T(2,128)(2,1)S(1)} %get-tuple-element.13), channel_id=1, source_target_pairs={{0,4},{1,5},{2,6},{3,7},{8,12},{9,13},{10,14},{11,15},{16,20},{17,... | collective-permute-start | bytes 147464 | tf_op jit(solution)/shard_map/ppermute | solution.py:16
  28.4 8.4 %collective-permute-start.15 = (bf16[1,32,6,1,128]{4,3,2,1,0:T(2,128)(2,1)S(1)}, bf16[1,32,6,1,128]{4,3,2,1,0:T(2,128)(2,1)S(1)}, u32[]{:S(2)}, u32[]{:S(2)}) collective-permute-start(bf16[1,32,6,1,128]{4,3,2,1,0:T(2,128)(2,1)S(1)} %get-tuple-element.14), channel_id=1, source_target_pairs={{4,0},{5,1},{6,2},{7,3},{12,8},{13,9},{14,10},{15,11},{20,16},{21,... | collective-permute-start | bytes 147464 | tf_op jit(solution)/shard_map/ppermute | solution.py:17
  30.8 9.1 %collective-permute-start.2 = (bf16[1,32,6,1,128]{4,3,2,1,0:T(2,128)(2,1)S(1)}, bf16[1,32,6,1,128]{4,3,2,1,0:T(2,128)(2,1)S(1)}, u32[]{:S(2)}, u32[]{:S(2)}) collective-permute-start(bf16[1,32,6,1,128]{4,3,2,1,0:T(2,128)(2,1)S(1)} %get-tuple-element.17), channel_id=1, source_target_pairs={{0,4},{1,5},{2,6},{3,7},{8,12},{9,13},{10,14},{11,15},{16,20},{17,... | collective-permute-start | bytes 147464 | tf_op jit(solution)/shard_map/ppermute | solution.py:16
  35.4 6.5 %collective-permute-start.3 = (bf16[1,32,6,1,128]{4,3,2,1,0:T(2,128)(2,1)S(1)}, bf16[1,32,6,1,128]{4,3,2,1,0:T(2,128)(2,1)S(1)}, u32[]{:S(2)}, u32[]{:S(2)}) collective-permute-start(bf16[1,32,6,1,128]{4,3,2,1,0:T(2,128)(2,1)S(1)} %get-tuple-element.18), channel_id=1, source_target_pairs={{4,0},{5,1},{6,2},{7,3},{12,8},{13,9},{14,10},{15,11},{20,16},{21,... | collective-permute-start | bytes 147464 | tf_op jit(solution)/shard_map/ppermute | solution.py:17
  37.3 9.5 %collective-permute-start.16 = (bf16[1,32,6,6,1]{4,3,2,1,0:T(8,128)(2,1)S(1)}, bf16[1,32,6,6,1]{4,3,2,1,0:T(8,128)(2,1)S(1)}, u32[]{:S(2)}, u32[]{:S(2)}) collective-permute-start(bf16[1,32,6,6,1]{4,3,2,1,0:T(8,128)(2,1)S(1)} %get-tuple-element.5), channel_id=1, source_target_pairs={{0,1},{1,2},{2,3},{4,5},{5,6},{6,7},{8,9},{9,10},{10,11},{12,13},{... | collective-permute-start | bytes 6920 | tf_op jit(solution)/shard_map/ppermute | solution.py:16
  38.6 8.2 %collective-permute-start.17 = (bf16[1,32,6,6,1]{4,3,2,1,0:T(8,128)(2,1)S(1)}, bf16[1,32,6,6,1]{4,3,2,1,0:T(8,128)(2,1)S(1)}, u32[]{:S(2)}, u32[]{:S(2)}) collective-permute-start(bf16[1,32,6,6,1]{4,3,2,1,0:T(8,128)(2,1)S(1)} %get-tuple-element.6), channel_id=1, source_target_pairs={{1,0},{2,1},{3,2},{5,4},{6,5},{7,6},{9,8},{10,9},{11,10},{13,12},{... | collective-permute-start | bytes 6920 | tf_op jit(solution)/shard_map/ppermute | solution.py:17
  42.5 9.7 %collective-permute-start.4 = (bf16[1,32,6,6,1]{4,3,2,1,0:T(8,128)(2,1)S(1)}, bf16[1,32,6,6,1]{4,3,2,1,0:T(8,128)(2,1)S(1)}, u32[]{:S(2)}, u32[]{:S(2)}) collective-permute-start(bf16[1,32,6,6,1]{4,3,2,1,0:T(8,128)(2,1)S(1)} %get-tuple-element.11), channel_id=1, source_target_pairs={{0,1},{1,2},{2,3},{4,5},{5,6},{6,7},{8,9},{9,10},{10,11},{12,13},{... | collective-permute-start | bytes 6920 | tf_op jit(solution)/shard_map/ppermute | solution.py:16
  45.3 8.7 %collective-permute-start.5 = (bf16[1,32,6,6,1]{4,3,2,1,0:T(8,128)(2,1)S(1)}, bf16[1,32,6,6,1]{4,3,2,1,0:T(8,128)(2,1)S(1)}, u32[]{:S(2)}, u32[]{:S(2)}) collective-permute-start(bf16[1,32,6,6,1]{4,3,2,1,0:T(8,128)(2,1)S(1)} %get-tuple-element.12), channel_id=1, source_target_pairs={{1,0},{2,1},{3,2},{5,4},{6,5},{7,6},{9,8},{10,9},{11,10},{13,12},{... | collective-permute-start | bytes 6920 | tf_op jit(solution)/shard_map/ppermute | solution.py:17
  52.2 1.7 copy-start.1
  86.4 6.9 %collective-permute-start.6 = (bf16[32,1,4,128]{3,2,1,0:T(4,128)(2,1)S(1)}, bf16[32,1,4,128]{3,2,1,0:T(4,128)(2,1)S(1)}, u32[]{:S(2)}, u32[]{:S(2)}) collective-permute-start(bf16[32,1,4,128]{3,2,1,0:T(4,128)(2,1)S(1)} %get-tuple-element.22), channel_id=1, source_target_pairs={{0,8},{8,16},{16,24},{1,9},{9,17},{17,25},{2,10},{10,18},{18,26},{... | collective-permute-start | bytes 98312 | tf_op jit(solution)/shard_map/ppermute | solution.py:16
  92.0 5.8 %collective-permute-start.7 = (bf16[32,1,4,128]{3,2,1,0:T(4,128)(2,1)S(1)}, bf16[32,1,4,128]{3,2,1,0:T(4,128)(2,1)S(1)}, u32[]{:S(2)}, u32[]{:S(2)}) collective-permute-start(bf16[32,1,4,128]{3,2,1,0:T(4,128)(2,1)S(1)} %get-tuple-element.21), channel_id=1, source_target_pairs={{8,0},{16,8},{24,16},{9,1},{17,9},{25,17},{10,2},{18,10},{26,18},{... | collective-permute-start | bytes 98312 | tf_op jit(solution)/shard_map/ppermute | solution.py:17
  97.9 13.5 %collective-permute-start.8 = (bf16[32,6,1,128]{3,2,1,0:T(2,128)(2,1)S(1)}, bf16[32,6,1,128]{3,2,1,0:T(2,128)(2,1)S(1)}, u32[]{:S(2)}, u32[]{:S(2)}) collective-permute-start(bf16[32,6,1,128]{3,2,1,0:T(2,128)(2,1)S(1)} %get-tuple-element.15), channel_id=1, source_target_pairs={{0,4},{1,5},{2,6},{3,7},{8,12},{9,13},{10,14},{11,15},{16,20},{17,... | collective-permute-start | bytes 147464 | tf_op jit(solution)/shard_map/ppermute | solution.py:16
  102.5 9.0 %collective-permute-start.9 = (bf16[32,6,1,128]{3,2,1,0:T(2,128)(2,1)S(1)}, bf16[32,6,1,128]{3,2,1,0:T(2,128)(2,1)S(1)}, u32[]{:S(2)}, u32[]{:S(2)}) collective-permute-start(bf16[32,6,1,128]{3,2,1,0:T(2,128)(2,1)S(1)} %get-tuple-element.16), channel_id=1, source_target_pairs={{4,0},{5,1},{6,2},{7,3},{12,8},{13,9},{14,10},{15,11},{20,16},{21,... | collective-permute-start | bytes 147464 | tf_op jit(solution)/shard_map/ppermute | solution.py:17
  112.0 10.2 %collective-permute-start.10 = (bf16[32,6,6,1]{3,2,1,0:T(8,128)(2,1)S(1)}, bf16[32,6,6,1]{3,2,1,0:T(8,128)(2,1)S(1)}, u32[]{:S(2)}, u32[]{:S(2)}) collective-permute-start(bf16[32,6,6,1]{3,2,1,0:T(8,128)(2,1)S(1)} %get-tuple-element.10), channel_id=1, source_target_pairs={{0,1},{1,2},{2,3},{4,5},{5,6},{6,7},{8,9},{9,10},{10,11},{12,13},{... | collective-permute-start | bytes 6920 | tf_op jit(solution)/shard_map/ppermute | solution.py:16
  115.4 6.8 %collective-permute-start.11 = (bf16[32,6,6,1]{3,2,1,0:T(8,128)(2,1)S(1)}, bf16[32,6,6,1]{3,2,1,0:T(8,128)(2,1)S(1)}, u32[]{:S(2)}, u32[]{:S(2)}) collective-permute-start(bf16[32,6,6,1]{3,2,1,0:T(8,128)(2,1)S(1)} %get-tuple-element.9), channel_id=1, source_target_pairs={{1,0},{2,1},{3,2},{5,4},{6,5},{7,6},{9,8},{10,9},{11,10},{13,12},{... | collective-permute-start | bytes 6920 | tf_op jit(solution)/shard_map/ppermute | solution.py:17
  151.6 3.9 %copy-start.2 = (bf16[32,864]{1,0:T(8,128)(2,1)S(1)}, bf16[32,864]{1,0:T(8,128)(2,1)}, u32[]{:S(2)}) copy-start(bf16[32,864]{1,0:T(8,128)(2,1)} %param.7) | copy-start | bytes 165892
Sparse Core Ops, SparseCore 0:
  155.6 128.4 all-reduce.2
where the time goes:
time: 294 us; the launch traced here: 293 us
  waiting for transfers between devices  132 us (45%)
  local copies, waits for them, and re-layouts  72.7 us (25%)
  starting transfers between devices  46.1 us (16%)
  matrix products  14.7 us (5%)
  between operations  14.6 us (5%)
  other arithmetic  12.9 us (4%)
    psum x1, waiting for transfers between devices, local(): lax.psum((first_all, second_all), ('gx', 'gy', 'gz'))  125 us
    unnamed x82, local copies, waits for them, and re-layouts  43 us
    ppermute x9, starting transfers between devices, padded_2(): before = lax.ppermute(last, axis, up)  34.2 us
    reshape x3, local copies, waits for them, and re-layouts, stack_taps(): return stacked.reshape(27 * padded.shape[0], size_x * size_y * size_z)  20.9 us
    ppermute x9, starting transfers between devices, padded_2(): after = lax.ppermute(initial, axis, down)  11.8 us
    dot_general x2, matrix products, weight_grad(): lax.dot_general(left_side, patches, (((1,), (1,)), ((), ())), preferred_e...  9.22 us
    ppermute x9, waiting for transfers between devices, padded_2(): after = lax.ppermute(initial, axis, down)  6.44 us
    unnamed x8, other arithmetic  6.24 us
  transfers between devices with their start and end apart: 19, of which 3 were waited for; matrix products, arithmetic and copies ran while one was open for 10% of the time, Pallas kernels for 0%

commit v1 on v0

v1 whole, which is shorter than its diff:
```python
import functools
import math

import jax
import jax.numpy as jnp
from jax import lax
from jax.experimental import pallas as pl
from jax.experimental.pallas import tpu as pltpu
from jax.sharding import PartitionSpec as P

F32 = jnp.float32
BF16 = jnp.bfloat16
C = 32


def call(body, out_shapes, scratch=(), flops=1_000_000, moved=1_000_000, vmem=24, **more):
    return pl.pallas_call(
        body,
        **more,
        out_shape=out_shapes,
        scratch_shapes=list(scratch),
        compiler_params=pltpu.CompilerParams(vmem_limit_bytes=vmem * 1024 * 1024),
        cost_estimate=pl.CostEstimate(flops=flops, bytes_accessed=moved, transcendentals=0),
    )


def struct(shape, dtype):
    return jax.ShapeDtypeStruct(shape, dtype)


def even_index(axis):
    return lax.rem(lax.axis_index(axis), 2) == 0


def partner(index, side, size):
    other = index ^ 1 if side == 0 else ((index + 1) ^ 1) - 1
    return other if 0 <= other < size else None


def swap(x, moves):
    axes = tuple(axis for axis, _ in moves)
    sizes = [lax.axis_size(axis) for axis in axes]
    pairs = []
    for source in range(math.prod(sizes)):
        rest, target, factor = source, 0, 1
        for (_, side), size in zip(moves[::-1], sizes[::-1]):
            other = partner(rest % size, side, size)
            if other is None:
                target = None
                break
            target += other * factor
            rest //= size
            factor *= size
        if target is not None:
            pairs.append((source, target))
    return lax.ppermute(x, axes, pairs) if pairs else None


def exchange(face_a, face_b, axis):
    got = [swap(face_a, [(axis, 0)]), swap(face_b, [(axis, 1)])]
    return [g for g in got if g is not None]


def choose(flag, a, b):
    if a is None and b is None:
        return None
    a = jnp.zeros_like(b) if a is None else a
    b = jnp.zeros_like(a) if b is None else b
    return jnp.where(flag, a, b)


def pack_faces(y_sides, in_ref, noise_ref, field_ref, wide_noise_ref, *faces):
    size_x = in_ref.shape[0]
    lanes = in_ref.shape[1]
    for x in range(size_x):
        field_ref[x] = in_ref[x].T
        wide_noise_ref[x] = noise_ref[x].T
    even_x, even_y = even_index("gx"), even_index("gy")
    face_x = faces[:2]
    face_y = faces[2 : 2 + y_sides]
    corner = faces[2 + y_sides :]

    for side in range(2):
        high = even_x if side == 0 else jnp.logical_not(even_x)
        face_x[side][0] = jnp.where(high, field_ref[size_x - 2], field_ref[0])
        face_x[side][1] = jnp.where(high, field_ref[size_x - 1], field_ref[1])
        face_x[side][2] = jnp.where(high, wide_noise_ref[size_x - 1], wide_noise_ref[0])

    for k in range(y_sides):
        high = even_y if k == 0 else jnp.logical_not(even_y)
        two = lambda p: jnp.where(high, p[:, lanes - 2 * C :], p[:, : 2 * C])
        one = lambda p: jnp.where(high, p[:, lanes - C :], p[:, :C])
        for j in range(0, size_x, 2):
            face_y[k][j // 2] = jnp.concatenate([two(field_ref[j]), two(field_ref[j + 1])], axis=1)
        for j in range(0, size_x, 4):
            face_y[k][size_x // 2 + j // 4] = jnp.concatenate([one(wide_noise_ref[j + i]) for i in range(4)], axis=1)
        for side in range(2):
            ref = corner[2 * k + side]
            ref[:128] = jnp.concatenate([two(face_x[side][0]), two(face_x[side][1])], axis=1)
            strip = one(face_x[side][2])
            ref[128:] = jnp.concatenate([strip[i * 32 : (i + 1) * 32] for i in range(4)], axis=1)


class Pieces:
    def __init__(self, y_sides, field, noise, face_x, face_y, corner):
        self.field, self.noise = field, noise
        self.size_x, self.size_z = field.shape[0], field.shape[1]
        even_x, even_y = even_index("gx"), even_index("gy")
        self.flag_x = {"below": even_x, "above": jnp.logical_not(even_x)}
        self.flag_y = {"below": even_y, "above": jnp.logical_not(even_y)}
        self.face_x = list(face_x)
        self.face_y = list(face_y) + [None] * (2 - y_sides)
        self.corner = [list(corner[2 * k : 2 * k + 2]) for k in range(y_sides)] + [[None, None]] * (2 - y_sides)

    def from_x(self, where, index, rows):
        return choose(self.flag_x[where], self.face_x[1][index, rows], self.face_x[0][index, rows])

    def from_y(self, where, read):
        a = [None if ref is None else read(ref) for ref in self.face_y]
        return choose(self.flag_y[where], a[1], a[0])

    def from_corner(self, where_x, where_y, read):
        a = []
        for pair in self.corner:
            if pair[0] is None:
                a.append(None)
            else:
                a.append(choose(self.flag_x[where_x], read(pair[1]), read(pair[0])))
        return choose(self.flag_y[where_y], a[1], a[0])

    def side_of(self, x, width):
        if x < width:
            return "below", x
        if x >= self.size_x + width:
            return "above", x - self.size_x - width
        return "own", x - width

    def field_plane(self, x, z0, z1):
        rows = slice(z0, z1)
        where, i = self.side_of(x, 2)
        if where == "own":
            middle = self.field[i, rows]
            read = lambda ref: ref[i // 2, rows, (i % 2) * 2 * C : (i % 2 + 1) * 2 * C]
            low, high = self.from_y("below", read), self.from_y("above", read)
        else:
            middle = self.from_x(where, i, rows)
            read = lambda ref: ref[rows, i * 2 * C : (i + 1) * 2 * C]
            low, high = self.from_corner(where, "below", read), self.from_corner(where, "above", read)
        return jnp.concatenate([low, middle, high], axis=1)

    def noise_plane(self, x, z0, z1):
        rows = slice(z0, z1)
        where, i = self.side_of(x, 1)
        if where == "own":
            middle = self.noise[i, rows]
            read = lambda ref: ref[self.size_x // 2 + i // 4, rows, (i % 4) * C : (i % 4 + 1) * C]
            low, high = self.from_y("below", read), self.from_y("above", read)
        else:
            middle = self.from_x(where, 2, rows)

            def read(ref):
                parts = []
                for b in range(4):
                    first, last = max(z0, b * 32), min(z1, (b + 1) * 32)
                    if first < last:
                        parts.append(ref[128 + first - b * 32 : 128 + last - b * 32, b * C : (b + 1) * C])
                return jnp.concatenate(parts, axis=0) if len(parts) > 1 else parts[0]

            low, high = self.from_corner(where, "below", read), self.from_corner(where, "above", read)
        return jnp.concatenate([low, middle, high, jnp.zeros((z1 - z0, 2 * C), BF16)], axis=1)


def take_pieces(y_sides, refs):
    n = 4 + 3 * y_sides
    return Pieces(y_sides, refs[0], refs[1], refs[2:4], refs[4 : 4 + y_sides], refs[4 + y_sides : n]), refs[n:]


def pack_z(y_sides, *refs):
    pieces, (low_out, high_out, face_a, face_b) = take_pieces(y_sides, refs)
    n_field, n_noise, size_z = pieces.size_x + 4, pieces.size_x + 2, pieces.size_z

    def gather(tile, first, noise_row):
        planes = [pieces.field_plane(x, tile, tile + 16).astype(F32) for x in range(n_field)]
        rows = [plane[first + k - tile : first + k - tile + 1] for k in range(2) for plane in planes]
        for x in range(n_noise):
            rows.append(pieces.noise_plane(x, tile, tile + 16).astype(F32)[noise_row - tile : noise_row - tile + 1])
        while len(rows) % 16:
            rows.append(jnp.zeros_like(rows[0]))
        return jnp.concatenate(rows, axis=0).astype(BF16)

    low = gather(0, 0, 0)
    high = gather(size_z - 16, size_z - 2, size_z - 1)
    low_out[...] = low
    high_out[...] = high
    even = even_index("gz")
    face_a[...] = jnp.where(even, high, low)
    face_b[...] = jnp.where(even, low, high)


def stack(ref, dz, first, count):
    return ref[dz, first : first + count].reshape(count * ref.shape[2], 256)


def taps(ref, count):
    return jnp.concatenate([stack(ref, dz, dx, count) for dx in range(3) for dz in range(3)], axis=1)


def widen(y_sides, *refs):
    pieces, (a1_ref, xs_ref, ns_ref, pre_ref) = take_pieces(y_sides, refs)
    size_z = pieces.size_z
    for ref, read in ((xs_ref, pieces.field_plane), (ns_ref, pieces.noise_plane)):
        for x in range(ref.shape[1]):
            plane = read(x, 0, size_z)
            ref[1, x] = plane
            ref[0, x] = shifted(plane, 0.0, True)
            ref[2, x] = shifted(plane, 0.0, False)
    n_noise = pre_ref.shape[0]
    total = jnp.dot(taps(xs_ref, n_noise), a1_ref[...], preferred_element_type=F32)
    pre_ref[...] = total.reshape(n_noise, size_z, 256)


def band(ref, row, taps, shift, lo, hi):
    moved = pltpu.roll(taps, shift % 128, 1) if shift % 128 else taps
    lane = lax.broadcasted_iota(jnp.int32, moved.shape, 1)
    for half in range(ref.shape[1] // 128):
        first = max(shift, lo) - 128 * half
        last = min(shift + 3 * C, hi) - 128 * half
        if last <= 0 or first >= 128:
            value = jnp.zeros_like(moved)
        else:
            value = jnp.where((lane >= first) & (lane < last), moved, 0.0)
        ref[row : row + C, half * 128 : (half + 1) * 128] = value.astype(BF16)


def spread_weights(both_ref, a1_ref, ab_ref, second_out):
    def columns(rows):
        wide = both_ref[rows].astype(F32)
        return jnp.concatenate([wide, jnp.zeros((C, 896 - wide.shape[1]), F32)], axis=1)

    def transposed(wide):
        return jnp.concatenate([wide[:, t * 128 : (t + 1) * 128].T for t in range(7)], axis=0)

    first = transposed(columns(slice(0, C)))
    second_rows = columns(slice(C, 2 * C))
    second = transposed(second_rows)
    fill = jnp.zeros((C, C), F32)
    for dx in range(3):
        for dz in range(3):
            t = 3 * dx + dz
            picks = [9 * dx + 3 * dy + dz for dy in range(3)]
            one = jnp.concatenate([first[k * C : (k + 1) * C, :] for k in picks[::-1]] + [fill], axis=1)
            two = jnp.concatenate([second[k * C : (k + 1) * C, :] for k in picks[::-1]] + [fill], axis=1)
            second_out[t] = two
            picks = [9 * (2 - dx) + 3 * dy + 2 - dz for dy in range(3)]
            back = jnp.concatenate([second_rows[:, k * C : (k + 1) * C] for k in picks] + [fill], axis=1)
            for yi in range(8):
                band(a1_ref, t * 256 + yi * C, one, (yi - 2) * C, 0, 6 * C)
            for yi in range(8):
                if yi < 6:
                    band(ab_ref, t * 256 + yi * C, back, (yi - 1) * C, C, 5 * C)
                else:
                    ab_ref[t * 256 + yi * C : t * 256 + (yi + 1) * C, :] = jnp.zeros((C, 256), BF16)


def shifted(plane, row, down):
    wide = plane.astype(F32)
    rows = wide.shape[0]
    index = lax.broadcasted_iota(jnp.int32, wide.shape, 0)
    if down:
        moved, place = pltpu.roll(wide, 1, 0), 0
    else:
        moved, place = pltpu.roll(wide, rows - 1, 0), rows - 1
    return jnp.where(index == place, row, moved).astype(BF16)


def silu_parts(value):
    s = 0.5 + 0.5 * jnp.tanh(0.5 * value)
    return value * s, s


def patch(ref, dz, x, row, last):
    rows = ref.shape[2]
    at = slice(rows - 16, rows) if last else slice(0, 16)
    tile = ref[dz, x, at, :].astype(F32)
    index = lax.broadcasted_iota(jnp.int32, tile.shape, 0)
    ref[dz, x, at, :] = jnp.where(index == (15 if last else 0), row, tile).astype(BF16)


def activate(n_recv, *refs):
    pre_ref, wide_field_ref, wide_noise_ref, low_ref, high_ref, a1_ref = refs[:6]
    recv = refs[6 : 6 + n_recv]
    hid_ref, slope_ref, xs_ref, ns_ref = refs[6 + n_recv :]
    n_field, size_z = xs_ref.shape[1], xs_ref.shape[2]
    n_noise = ns_ref.shape[1]
    size_x = n_noise - 2
    even = even_index("gz")
    recv_b = recv[1][...] if n_recv > 1 else None
    below_rows = choose(even, recv_b, recv[0][...]).astype(F32)
    above_rows = choose(even, recv[0][...], recv_b).astype(F32)
    own_low = low_ref[...].astype(F32)
    own_high = high_ref[...].astype(F32)

    gx, gy, gz = lax.axis_index("gx"), lax.axis_index("gy"), lax.axis_index("gz")
    first_x, last_x = gx == 0, gx == lax.axis_size("gx") - 1
    first_y, last_y = gy == 0, gy == lax.axis_size("gy") - 1
    first_z, last_z = gz == 0, gz == lax.axis_size("gz") - 1

    before = jnp.concatenate([below_rows[:n_field], own_high[n_field : 2 * n_field]], axis=0).astype(BF16)
    halo = jnp.concatenate([below_rows[n_field : 2 * n_field], above_rows[:n_field]], axis=0).astype(BF16)
    after = jnp.concatenate([own_low[:n_field], above_rows[n_field : 2 * n_field]], axis=0).astype(BF16)
    rows = 2 * n_field
    edge_total, row_total = None, None
    for dx in range(3):
        weight = lambda dz: a1_ref[(3 * dx + dz) * 256 : (3 * dx + dz + 1) * 256]
        first = jnp.dot(jnp.concatenate([before, halo], axis=0), weight(0), preferred_element_type=F32)
        middle = jnp.dot(halo, weight(1), preferred_element_type=F32)
        last = jnp.dot(jnp.concatenate([after, halo], axis=0), weight(2), preferred_element_type=F32)
        edge = first[:rows] + middle + last[:rows]
        row = jnp.concatenate([first[rows : rows + n_field], last[rows + n_field :]], axis=0)
        if dx:
            edge = pltpu.roll(edge, rows - dx, 0)
            row = pltpu.roll(row, rows - dx, 0)
        edge_total = edge if edge_total is None else edge_total + edge
        row_total = row if row_total is None else row_total + row

    lane = lax.broadcasted_iota(jnp.int32, (1, 256), 1)
    drop_y = ((lane < C) & first_y) | ((lane >= 5 * C) & last_y)
    edge_hidden = silu_parts(edge_total)[0]
    row = lax.broadcasted_iota(jnp.int32, edge_hidden.shape, 0)
    drop = drop_y | ((row < n_field) & first_z) | ((row >= n_field) & last_z)
    x_row = jnp.where(row < n_field, row, row - n_field)
    drop = drop | ((x_row == 0) & first_x) | ((x_row == n_noise - 1) & last_x)
    edge_hidden = jnp.where(drop, 0.0, edge_hidden).astype(BF16).astype(F32)

    index = lax.broadcasted_iota(jnp.int32, (size_z, 256), 0)
    for x in range(n_noise):
        value = pre_ref[x]
        value = value + jnp.where(index == 0, row_total[x : x + 1], 0.0)
        value = value + jnp.where(index == size_z - 1, row_total[n_field + x : n_field + x + 1], 0.0)
        hidden, s = silu_parts(value)
        gone = drop_y
        if x == 0:
            gone = gone | first_x
        if x == n_noise - 1:
            gone = gone | last_x
        hidden = jnp.where(gone, 0.0, hidden).astype(BF16)
        hid_ref[1, x] = hidden
        hid_ref[0, x] = shifted(hidden, edge_hidden[x : x + 1], True)
        hid_ref[2, x] = shifted(hidden, edge_hidden[n_field + x : n_field + x + 1], False)
        if 1 <= x <= size_x:
            slope_ref[x - 1] = s * (1.0 + value * (1.0 - s))

    xs_ref[...] = wide_field_ref[...]
    ns_ref[...] = wide_noise_ref[...]
    for x in range(n_field):
        patch(xs_ref, 0, x, below_rows[n_field + x : n_field + x + 1], False)
        patch(xs_ref, 2, x, above_rows[x : x + 1], True)
    base = 2 * n_field
    for x in range(n_noise):
        patch(ns_ref, 0, x, below_rows[base + x : base + x + 1], False)
        patch(ns_ref, 2, x, above_rows[base + x : base + x + 1], True)


def backward(ns_ref, slope_ref, ab_ref, out_ref, acc_ref):
    size_x, size_z = slope_ref.shape[:2]
    total = jnp.dot(taps(ns_ref, size_x), ab_ref[...], preferred_element_type=F32)
    acc_ref[...] = total.reshape(size_x, size_z, 256)
    for x in range(size_x):
        value = (acc_ref[x] * slope_ref[x]).astype(BF16)
        rows = jnp.concatenate([value[:, :128].T, value[:, 128:].T], axis=0)
        out_ref[:, x * size_z : (x + 1) * size_z] = rows[C : 5 * C, :]


def collect(left, ref, size_x, skip, offset):
    tiles = [jnp.zeros((C, 128), F32) for _ in range(7)]
    lanes = lax.broadcasted_iota(jnp.int32, (C, 128), 1)
    for dx in range(3):
        for dz in range(3):
            block = jnp.dot(left, stack(ref, dz, dx + skip, size_x), preferred_element_type=F32)
            total = None
            for y in range(4):
                part = block[y * C : (y + 1) * C, :]
                shift = (256 - (y + offset) * C) % 256
                part = pltpu.roll(part, shift, 1) if shift else part
                total = part if total is None else total + part
            total = total[:, :128]
            for dy in range(3):
                tap = 9 * dx + 3 * dy + dz
                shift = ((tap - dy) * C) % 128
                moved = pltpu.roll(total, shift, 1) if shift else total
                at = (tap % 4) * C
                tiles[tap // 4] = jnp.where((lanes >= at) & (lanes < at + C), moved, tiles[tap // 4])
    return jnp.concatenate(tiles, axis=1)


def weight_grad(give, xs_ref, hid_ref, pre_grad_ref, rows_ref, out_ref):
    size_x = rows_ref.shape[0]
    even = even_index("gz")

    @pl.when(even if give else jnp.logical_not(even))
    def _():
        noise_rows = jnp.concatenate([rows_ref[x] for x in range(size_x)], axis=1)
        out_ref[...] = collect(noise_rows, hid_ref, size_x, 0, 0)

    @pl.when(jnp.logical_not(even) if give else even)
    def _():
        out_ref[...] = collect(pre_grad_ref[...], xs_ref, size_x, 1, 1)


def predict(hid_ref, second_ref, out_ref, acc_ref, a2_ref):
    size_x, size_z = out_ref.shape[0], out_ref.shape[2]
    for t in range(9):
        for yi in range(8):
            band(a2_ref, t * 256 + yi * C, second_ref[t], (yi - 2) * C, 0, 4 * C)
    total = jnp.dot(taps(hid_ref, size_x), a2_ref[...], preferred_element_type=F32)
    acc_ref[...] = total.reshape(size_x, size_z, 128)
    for x in range(size_x):
        out_ref[x] = acc_ref[x].astype(BF16).T


def finish(norm, mine_ref, other_ref, first_ref, second_ref):
    even = even_index("gz")
    mine = mine_ref[...]
    other = other_ref[...]
    first = jnp.where(even, mine, other) * norm
    second = jnp.where(even, other, mine) * norm
    first_ref[...] = (first * first)[:, : 27 * C]
    second_ref[...] = (second * second)[:, : 27 * C]


def first_sum(keep_ref, taken_ref, send_ref):
    send_ref[...] = (keep_ref[...] + taken_ref[...]).astype(BF16)


def round_sum(own_ref, *refs):
    got, out_ref = refs[:-1], refs[-1]
    total = own_ref[...].astype(F32) + got[0][...].astype(F32)
    if len(got) == 3:
        total = total + (got[1][...].astype(F32) + got[2][...].astype(F32))
    out_ref[...] = total.astype(out_ref.dtype)


def butterfly(x, axis, bit):
    size = lax.axis_size(axis)
    return lax.ppermute(x, axis, [(i, i ^ bit) for i in range(size)])


AXES = ("gx", "gy", "gz")


def masked_swap(x, flip_even, flip_odd):
    sizes = [lax.axis_size(axis) for axis in AXES]
    pairs = []
    for gx in range(sizes[0]):
        for gy in range(sizes[1]):
            for gz in range(sizes[2]):
                at = [gx, gy, gz]
                to = list(at)
                for axis, bit in flip_odd if gz % 2 else flip_even:
                    to[AXES.index(axis)] ^= bit
                source, target = [(p[0] * sizes[1] + p[1]) * sizes[2] + p[2] for p in (at, to)]
                pairs.append((source, target))
    return lax.ppermute(x, AXES, pairs)


def local(inputs, noise, w_first, w_second):
    _, channels, size_x, size_y, size_z = inputs.shape
    cells = size_x * size_y * size_z
    devices = lax.axis_size("gx") * lax.axis_size("gy") * lax.axis_size("gz")
    norm = 1.0 / math.sqrt(cells * devices)
    lanes = size_y * channels

    def rows(x):
        return x[0].transpose(1, 2, 0, 3).reshape(size_x, lanes, size_z)

    in_rows, noise_rows = rows(inputs), rows(noise)
    plane = (size_z, lanes)
    y_sides = 2 if lax.axis_size("gy") > 2 else 1
    y_planes = size_x // 2 + size_x // 4
    field, wide_noise, *faces = call(
        functools.partial(pack_faces, y_sides),
        [struct((size_x,) + plane, BF16)] * 2
        + [struct((3,) + plane, BF16)] * 2
        + [struct((y_planes,) + plane, BF16)] * y_sides
        + [struct((160, 128), BF16)] * (2 * y_sides),
    )(in_rows, noise_rows)
    moves = [[("gx", side)] for side in range(2)]
    moves += [[("gy", side)] for side in range(y_sides)]
    moves += [[("gx", side), ("gy", k)] for k in range(y_sides) for side in range(2)]
    order = sorted(range(len(moves)), key=lambda k: (moves[k][0] == ("gx", 1), len(moves[k]), moves[k]))
    sent = {k: swap(faces[k], moves[k]) for k in order}
    got = [sent[k] for k in range(len(moves))]

    a1, ab, second = call(
        spread_weights,
        [struct((9 * 256, 256), BF16), struct((9 * 256, 256), BF16), struct((9, C, 128), F32)],
        moved=4_000_000,
    )(jnp.concatenate([w_first, w_second], axis=0))
    *got, a1, ab, second = lax.optimization_barrier((*got, a1, ab, second))

    n_field, n_noise = size_x + 4, size_x + 2
    z_rows = -(-(2 * n_field + n_noise) // 16) * 16
    low, high, face_a, face_b = call(
        functools.partial(pack_z, y_sides), [struct((z_rows, 256), BF16)] * 4
    )(field, wide_noise, *got)
    z_got = exchange(face_a, face_b, "gz")
    pre_shape = (n_noise, size_z, 256)
    xs, ns, pre = call(
        functools.partial(widen, y_sides),
        [struct((3, n_field, size_z, 256), BF16), struct((3,) + pre_shape, BF16), struct(pre_shape, F32)],
        flops=1_000_000_000,
    )(field, wide_noise, *got, a1)
    *z_got, xs, ns, pre = lax.optimization_barrier((*z_got, xs, ns, pre))

    slope_shape = (size_x, size_z, 256)
    hidden, slope, xs, ns = call(
        functools.partial(activate, len(z_got)),
        [struct((3,) + pre_shape, BF16), struct(slope_shape, F32), struct(xs.shape, BF16), struct(ns.shape, BF16)],
    )(pre, xs, ns, low, high, a1, *z_got)
    pre_grad = call(
        backward,
        struct((lanes, size_x * size_z), BF16),
        scratch=[pltpu.VMEM(slope_shape, F32)],
        flops=1_000_000_000,
    )(ns, slope, ab)

    half = struct((C, 896), F32)
    rounded = struct((C, 896), BF16)
    parts = (xs, hidden, pre_grad, noise_rows)
    give = call(functools.partial(weight_grad, True), half, flops=1_000_000_000)(*parts)
    taken = butterfly(give, "gz", 1)
    keep = call(functools.partial(weight_grad, False), half, flops=1_000_000_000)(*parts)
    send = call(first_sum, rounded)(keep, taken)

    prediction_rows = call(
        predict,
        struct((size_x, lanes, size_z), BF16),
        scratch=[pltpu.VMEM((size_x, size_z, lanes), F32), pltpu.VMEM((9 * 256, 128), BF16)],
        flops=500_000_000,
    )(hidden, second)
    prediction = prediction_rows.reshape(size_x, size_y, channels, size_z).transpose(2, 0, 1, 3)[None]

    steps = []
    for axis, start in (("gx", 1), ("gz", 2), ("gy", 1)):
        bit = start
        while bit < lax.axis_size(axis):
            steps.append((axis, bit))
            bit *= 2
    rounds = [steps[k : k + 2] for k in range(0, len(steps), 2)]
    turn = len(rounds) // 2 if len(steps) % 2 == 0 else 0
    for k, even in enumerate(rounds):
        odd = rounds[(k + turn) % len(rounds)]
        flips = [(even[:1], odd[:1])]
        if len(even) == 2:
            flips += [(even[1:], odd[1:]), (even, odd)]
        got = [masked_swap(send, *flip) for flip in flips]
        if k == 0:
            *got, prediction = lax.optimization_barrier((*got, prediction))
        send = call(round_sum, half if k == len(rounds) - 1 else rounded)(send, *got)
    mine = send
    other = butterfly(mine, "gz", 1)
    fisher_first, fisher_second = call(
        functools.partial(finish, norm), [struct((C, 27 * C), F32)] * 2
    )(mine, other)
    return prediction, fisher_first, fisher_second


def solution(mesh):
    in_specs = (P(None, None, "gx", "gy", "gz"), P(None, None, "gx", "gy", "gz"), P(), P())
    out_specs = (P(None, None, "gx", "gy", "gz"), P(), P())
    return jax.shard_map(local, mesh=mesh, in_specs=in_specs, out_specs=out_specs, check_vma=False)
```

time: 294 us -> 43.6 us (0.15)
  waiting for transfers between devices: 132 us -> 7.55 us
  local copies, waits for them, and re-layouts: 72.7 us -> 2.61 us
  starting transfers between devices: 46.1 us -> 23.8 us
  matrix products: 14.7 us -> 0 us
  between operations: 14.6 us -> 0.8 us
  other arithmetic: 12.9 us -> 0.86 us
  Pallas kernels: 0 us -> 7.69 us
    psum x1 -> x0, waiting for transfers between devices: 125 us -> none  [local(): lax.psum((first_all, second_all), ('gx', 'gy', 'gz'))]
    unnamed x82 -> x0, local copies, waits for them, and re-layouts: 43 us -> none
    ppermute x18 -> x15, starting transfers between devices: 46 us -> 23.8 us  [the longest x7 12 us: swap(): return lax.ppermute(x, axes, pairs) if pairs else None]
    reshape x6 -> x1, local copies, waits for them, and re-layouts: 22.3 us -> 0.72 us  [local(): prediction_rows.reshape(size_x, size_y, channels, size_z)]
    dot_general x4 -> x0, matrix products: 14.7 us -> none  [the longest x2 9.22 us: weight_grad(): lax.dot_general(left_side, patches, (((1,), (1,)), ((), ())), preferred_e...]
    pallas_call x0 -> x13, Pallas kernels: none -> 7.69 us  [the longest x1 1.19 us: local(): call(functools.partial(widen, y_sides), [struct((3, n_field, size_z, 256)...]
    unnamed x8 -> x0, other arithmetic: 6.24 us -> none
    another operation x6 -> x0, local copies, waits for them, and re-layouts: 4.21 us -> none  [the longest x4 2.48 us: stack_taps(): stacked = jnp.stack(pieces, axis=0)]
  transfers between devices with their start and end apart: 19 -> 15, of which waited for: 3 -> 8; matrix products, arithmetic and copies ran while one was open for 10% -> 4% of each run, Pallas kernels for 0% -> 9%
where the time goes in v1:
time: 43.6 us; the launch traced here: 43.3 us
  starting transfers between devices  23.8 us (55%)
  Pallas kernels  7.69 us (18%)
  waiting for transfers between devices  7.55 us (17%)
  local copies, waits for them, and re-layouts  2.61 us (6%)
  other arithmetic  0.86 us (2%)
  between operations  0.8 us (2%)
    ppermute x7, starting transfers between devices, swap(): return lax.ppermute(x, axes, pairs) if pairs else None  12 us
    ppermute x6, starting transfers between devices, masked_swap(): return lax.ppermute(x, AXES, pairs)  8.01 us
    ppermute x6, waiting for transfers between devices, masked_swap(): return lax.ppermute(x, AXES, pairs)  4.74 us
    ppermute x2, starting transfers between devices, butterfly(): return lax.ppermute(x, axis, [(i, i ^ bit) for i in range(size)])  3.76 us
    transpose x2, local copies, waits for them, and re-layouts, rows(): return x[0].transpose(1, 2, 0, 3).reshape(size_x, lanes, size_z)  1.88 us
    ppermute x2, waiting for transfers between devices, butterfly(): return lax.ppermute(x, axis, [(i, i ^ bit) for i in range(size)])  1.64 us
    pallas_call x1, Pallas kernels, local(): call(functools.partial(widen, y_sides), [struct((3, n_field, size_z, 256)...  1.19 us
    ppermute x7, waiting for transfers between devices, swap(): return lax.ppermute(x, axes, pairs) if pairs else None  1.18 us
  transfers between devices with their start and end apart: 15, of which 8 were waited for; matrix products, arithmetic and copies ran while one was open for 4% of the time, Pallas kernels for 9%

profile of v1, /device:TPU:0, one launch (start us, length us, event | category | flops | bytes accessed | tf_op | source)
XLA Modules:
  0.0 43.3 jit_solution(15596780845720260131)
XLA Ops:
  0.6 0.9 %copy.7 = bf16[4,4,32,128]{3,2,1,0:T(8,128)(2,1)S(1)} copy(bf16[4,4,32,128]{3,1,0,2:T(4,128)(2,1)} %bitcast.19) | data formatting | bytes 262144 | tf_op jit(solution)/shard_map/transpose | solution.py:474
  1.6 0.9 %copy.8 = bf16[4,4,32,128]{3,2,1,0:T(8,128)(2,1)S(1)} copy(bf16[4,4,32,128]{3,1,0,2:T(4,128)(2,1)} %bitcast.20) | data formatting | bytes 262144 | tf_op jit(solution)/shard_map/transpose | solution.py:474
  2.5 0.6 %shard_map.67 = (bf16[4,128,128]{2,1,0:T(8,128)(2,1)S(1)}, bf16[4,128,128]{2,1,0:T(8,128)(2,1)S(1)}, bf16[3,128,128]{2,1,0:T(8,128)(2,1)S(1)}, bf16[3,128,128]{2...) custom-call(bf16[4,128,128]{2,1,0:T(8,128)(2,1)S(1)} %bitcast.17, ...), custom_call_target="tpu_custom_call" | custom-call | flops 1000000 | bytes 1000000 | tf_op jit(solution)/shard_map/pallas_call | solution.py:480
  3.1 4.0 %collective-permute-start.3 = (bf16[160,128]{1,0:T(8,128)(2,1)S(1)}, bf16[160,128]{1,0:T(8,128)(2,1)S(1)}, u32[]{:S(2)}, u32[]{:S(2)}) collective-permute-start(bf16[160,128]{1,0:T(8,128)(2,1)S(1)} %get-tuple-element.48), channel_id=1, source_target_pairs={{0,12},{4,8},{8,4},{12,0},{16,28},{20,24},{24,20},{28,16},{1,13},{... | collective-permute-start | bytes 122888 | tf_op jit(solution)/shard_map/ppermute | solution.py:56
  7.1 0.7 %collective-permute-start.4 = (bf16[160,128]{1,0:T(8,128)(2,1)S(1)}, bf16[160,128]{1,0:T(8,128)(2,1)S(1)}, u32[]{:S(2)}, u32[]{:S(2)}) collective-permute-start(bf16[160,128]{1,0:T(8,128)(2,1)S(1)} %get-tuple-element.49), channel_id=1, source_target_pairs={{8,20},{12,16},{16,12},{20,8},{9,21},{13,17},{17,13},{21,9},{10,22... | collective-permute-start | bytes 122888 | tf_op jit(solution)/shard_map/ppermute | solution.py:56
  7.8 4.4 %collective-permute-start = (bf16[3,128,128]{2,1,0:T(8,128)(2,1)S(1)}, bf16[3,128,128]{2,1,0:T(8,128)(2,1)S(1)}, u32[]{:S(2)}, u32[]{:S(2)}) collective-permute-start(bf16[3,128,128]{2,1,0:T(8,128)(2,1)S(1)} %get-tuple-element.45), channel_id=1, source_target_pairs={{0,8},{8,0},{16,24},{24,16},{1,9},{9,1},{17,25},{25,17},{2,10},{10... | collective-permute-start | bytes 294920 | tf_op jit(solution)/shard_map/ppermute | solution.py:56
  12.2 0.7 %collective-permute-start.1 = (bf16[3,128,128]{2,1,0:T(8,128)(2,1)S(1)}, bf16[3,128,128]{2,1,0:T(8,128)(2,1)S(1)}, u32[]{:S(2)}, u32[]{:S(2)}) collective-permute-start(bf16[3,128,128]{2,1,0:T(8,128)(2,1)S(1)} %get-tuple-element.46), channel_id=1, source_target_pairs={{8,16},{16,8},{9,17},{17,9},{10,18},{18,10},{11,19},{19,11},{12,20... | collective-permute-start | bytes 294920 | tf_op jit(solution)/shard_map/ppermute | solution.py:56
  12.9 1.6 %collective-permute-start.2 = (bf16[3,128,128]{2,1,0:T(8,128)(2,1)S(1)}, bf16[3,128,128]{2,1,0:T(8,128)(2,1)S(1)}, u32[]{:S(2)}, u32[]{:S(2)}) collective-permute-start(bf16[3,128,128]{2,1,0:T(8,128)(2,1)S(1)} %get-tuple-element.47), channel_id=1, source_target_pairs={{0,4},{4,0},{1,5},{5,1},{2,6},{6,2},{3,7},{7,3},{8,12},{12,8},{9,1... | collective-permute-start | bytes 294920 | tf_op jit(solution)/shard_map/ppermute | solution.py:56
  14.5 0.9 %pad_maximum_fusion.both_ref = bf16[64,864]{1,0:T(8,128)(2,1)S(1)} fusion(bf16[32,864]{1,0:T(8,128)(2,1)} %param.7, bf16[32,864]{1,0:T(8,128)(2,1)} %param.6), kind=kLoop, calls=%fused_computation.1 | loop fusion | flops 221184 | bytes 221184 | tf_op jit(solution)/shard_map/concatenate | solution.py:498
  15.3 1.0 %shard_map.68 = (bf16[2304,256]{1,0:T(8,128)(2,1)S(1)}, bf16[2304,256]{1,0:T(8,128)(2,1)S(1)}, f32[9,32,128]{2,1,0:T(8,128)S(1)}) custom-call(bf16[64,864]{1,0:T(8,128)(2,1)S(1)} %pad_maximum_fusion.both_ref), custom_call_target="tpu_custom_call" | custom-call | flops 1000000 | bytes 4000000 | tf_op jit(solution)/shard_map/pallas_call | solution.py:494
  16.4 0.0 collective-permute-done.3.refs_5_
  16.4 0.0 collective-permute-done.4.refs_6_
  16.4 0.0 collective-permute-done.refs_2_
  16.4 0.0 collective-permute-done.1.refs_3_
  16.4 1.2 %collective-permute-done.2.refs_4_ = bf16[3,128,128]{2,1,0:T(8,128)(2,1)S(1)} collective-permute-done((bf16[3,128,128]{2,1,0:T(8,128)(2,1)S(1)}, bf16[3,128,128]{2,1,0:T(8,128)(2,1)S(1)}, u32[]{:S(2)}, u32[]{:S(2)}) %collective-permute-start.2) | collective-permute-done | bytes 98336 | tf_op jit(solution)/shard_map/ppermute | solution.py:56
  17.6 0.1 shard_map.69
  17.7 0.1 collective-permute-start.5
  17.8 0.7 %collective-permute-start.6 = (bf16[32,256]{1,0:T(8,128)(2,1)S(1)}, bf16[32,256]{1,0:T(8,128)(2,1)S(1)}, u32[]{:S(2)}, u32[]{:S(2)}) collective-permute-start(bf16[32,256]{1,0:T(8,128)(2,1)S(1)} %get-tuple-element.59), channel_id=1, source_target_pairs={{1,2},{2,1},{5,6},{6,5},{9,10},{10,9},{13,14},{14,13},{17,18},{18,... | collective-permute-start | bytes 49160 | tf_op jit(solution)/shard_map/ppermute | solution.py:56
  18.5 1.2 %shard_map.70 = (bf16[3,8,128,256]{3,2,1,0:T(8,128)(2,1)S(1)}, bf16[3,6,128,256]{3,2,1,0:T(8,128)(2,1)S(1)}, f32[6,128,256]{2,1,0:T(8,128)S(1)}) custom-call(bf16[4,128,128]{2,1,0:T(8,128)(2,1)S(1)} %get-tuple-element.43.refs_0_, bf16[4,128,128]{2,1,0:T(8,128)(2,1)S(1)} %get-tuple-element.44.refs_1_, bf16[3,128,128]{2,1,0:T(8,128)(2,1)S(1)} %collective-permute-done.refs_2_, ...), custom_call_target="tpu_custom_call" | custom-call | flops 1000000000 | bytes 1000000 | tf_op jit(solution)/shard_map/pallas_call | solution.py:508
  19.7 0.0 collective-permute-done.5.refs_6_
  19.7 0.0 collective-permute-done.6.refs_7_
  19.7 0.8 %shard_map.71 = (bf16[3,6,128,256]{3,2,1,0:T(8,128)(2,1)S(1)}, f32[4,128,256]{2,1,0:T(8,128)S(1)}, bf16[3,8,128,256]{3,2,1,0:T(8,128)(2,1)S(1)}, bf16[3,6,128,256]{3,2,1,0:T(8,128)(2,1)S(1)}) custom-call(f32[6,128,256]{2,1,0:T(8,128)S(1)} %get-tuple-element.64.refs_0_, bf16[3,8,128,256]{3,2,1,0:T(8,128)(2,1)S(1)} %get-tuple-element.65.refs_1_, ...), custom_call_target="tpu_custom_call" | custom-call | flops 1000000 | bytes 1000000 | tf_op jit(solution)/shard_map/pallas_call | solution.py:516
  20.5 0.8 %shard_map.72.pre_grad_ref = bf16[128,512]{1,0:T(8,128)(2,1)S(1)} custom-call(bf16[3,6,128,256]{3,2,1,0:T(8,128)(2,1)S(1)} %get-tuple-element.73.ns_ref, f32[4,128,256]{2,1,0:T(8,128)S(1)} %get-tuple-element.74.slope_ref, bf16[2304,256]{1,0:T(8,128)(2,1)S(1)} %get-tuple-element.75.ab_ref), custom_call_target="tpu_custom_call" | custom-call | flops 1000000000 | bytes 1000000 | tf_op jit(solution)/shard_map/pallas_call | solution.py:520
  21.4 0.7 %shard_map.74 = f32[32,896]{1,0:T(8,128)S(1)} custom-call(bf16[3,8,128,256]{3,2,1,0:T(8,128)(2,1)S(1)} %get-tuple-element.71.xs_ref, bf16[3,6,128,256]{3,2,1,0:T(8,128)(2,1)S(1)} %get-tuple-element.72.hid_ref, bf16[128,512]{1,0:T(8,128)(2,1)S(1)} %shard_map.72.pre_grad_ref, bf16[4,128,128]{2,1,0:T(8,128)(2,1)S(1)} %bitcast.15), custom_call_target="tpu_custom_call" | custom-call | flops 1000000000 | bytes 1000000 | tf_op jit(solution)/shard_map/pallas_call | solution.py:530
  22.1 3.7 %collective-permute-start.7 = (f32[32,896]{1,0:T(8,128)S(1)}, f32[32,896]{1,0:T(8,128)S(1)}, u32[]{:S(2)}, u32[]{:S(2)}) collective-permute-start(f32[32,896]{1,0:T(8,128)S(1)} %shard_map.74), channel_id=1, source_target_pairs={{0,1},{1,0},{2,3},{3,2},{4,5},{5,4},{6,7},{7,6},{8,9},{9,8},{10,11... | collective-permute-start | bytes 344072 | tf_op jit(solution)/shard_map/ppermute | solution.py:445
  25.8 0.6 %shard_map.73.keep_ref = f32[32,896]{1,0:T(8,128)S(1)} custom-call(bf16[3,8,128,256]{3,2,1,0:T(8,128)(2,1)S(1)} %get-tuple-element.71.xs_ref, bf16[3,6,128,256]{3,2,1,0:T(8,128)(2,1)S(1)} %get-tuple-element.72.hid_ref, bf16[128,512]{1,0:T(8,128)(2,1)S(1)} %shard_map.72.pre_grad_ref, bf16[4,128,128]{2,1,0:T(8,128)(2,1)S(1)} %bitcast.16), custom_call_target="tpu_custom_call" | custom-call | flops 1000000000 | bytes 1000000 | tf_op jit(solution)/shard_map/pallas_call | solution.py:532
  26.4 0.3 collective-permute-done.7.taken_ref
  26.8 1.0 %collective-permute-start.10 = (bf16[32,896]{1,0:T(8,128)(2,1)S(1)}, bf16[32,896]{1,0:T(8,128)(2,1)S(1)}, u32[]{:S(2)}, u32[]{:S(2)}) collective-permute-start(bf16[32,896]{1,0:T(8,128)(2,1)S(1)} %shard_map.75.own_ref), channel_id=1, source_target_pairs={{0,24},{1,7},{2,26},{3,5},{4,28},{5,3},{6,30},{7,1},{8,16},{9,15},... | collective-permute-start | bytes 172040 | tf_op jit(solution)/shard_map/ppermute | solution.py:463
  27.8 1.9 %collective-permute-start.9 = (bf16[32,896]{1,0:T(8,128)(2,1)S(1)}, bf16[32,896]{1,0:T(8,128)(2,1)S(1)}, u32[]{:S(2)}, u32[]{:S(2)}) collective-permute-start(bf16[32,896]{1,0:T(8,128)(2,1)S(1)} %shard_map.75.own_ref), channel_id=1, source_target_pairs={{0,16},{1,5},{2,18},{3,7},{4,20},{5,1},{6,22},{7,3},{8,24},{9,13},... | collective-permute-start | bytes 172040 | tf_op jit(solution)/shard_map/ppermute | solution.py:463
  29.6 1.6 %collective-permute-start.8 = (bf16[32,896]{1,0:T(8,128)(2,1)S(1)}, bf16[32,896]{1,0:T(8,128)(2,1)S(1)}, u32[]{:S(2)}, u32[]{:S(2)}) collective-permute-start(bf16[32,896]{1,0:T(8,128)(2,1)S(1)} %shard_map.75.own_ref), channel_id=1, source_target_pairs={{0,8},{1,3},{2,10},{3,1},{4,12},{5,7},{6,14},{7,5},{8,0},{9,11},{1... | collective-permute-start | bytes 172040 | tf_op jit(solution)/shard_map/ppermute | solution.py:463
  31.2 0.9 %shard_map.76 = bf16[4,128,128]{2,1,0:T(8,128)(2,1)S(1)} custom-call(bf16[3,6,128,256]{3,2,1,0:T(8,128)(2,1)S(1)} %get-tuple-element.72.hid_ref, f32[9,32,128]{2,1,0:T(8,128)S(1)} %get-tuple-element.76.second_ref), custom_call_target="tpu_custom_call" | custom-call | flops 500000000 | bytes 1000000 | tf_op jit(solution)/shard_map/pallas_call | solution.py:535
  32.1 0.7 %copy.11 = bf16[4,4,32,128]{3,1,0,2:T(4,128)(2,1)} copy(bf16[4,4,32,128]{3,2,1,0:T(8,128)(2,1)S(1)} %bitcast.18) | data formatting | bytes 262144 | tf_op jit(solution)/shard_map/reshape | solution.py:541
  32.9 0.0 collective-permute-done.10.refs_2_
  32.9 0.6 %collective-permute-done.9.refs_1_ = bf16[32,896]{1,0:T(8,128)(2,1)S(1)} collective-permute-done((bf16[32,896]{1,0:T(8,128)(2,1)S(1)}, bf16[32,896]{1,0:T(8,128)(2,1)S(1)}, u32[]{:S(2)}, u32[]{:S(2)}) %collective-permute-start.9) | collective-permute-done | bytes 57376 | tf_op jit(solution)/shard_map/ppermute | solution.py:463
  33.4 0.6 %collective-permute-done.8.refs_0_ = bf16[32,896]{1,0:T(8,128)(2,1)S(1)} collective-permute-done((bf16[32,896]{1,0:T(8,128)(2,1)S(1)}, bf16[32,896]{1,0:T(8,128)(2,1)S(1)}, u32[]{:S(2)}, u32[]{:S(2)}) %collective-permute-start.8) | collective-permute-done | bytes 57376 | tf_op jit(solution)/shard_map/ppermute | solution.py:463
  34.1 2.2 %collective-permute-start.13 = (bf16[32,896]{1,0:T(8,128)(2,1)S(1)}, bf16[32,896]{1,0:T(8,128)(2,1)S(1)}, u32[]{:S(2)}, u32[]{:S(2)}) collective-permute-start(bf16[32,896]{1,0:T(8,128)(2,1)S(1)} %shard_map.77.own_ref), channel_id=1, source_target_pairs={{0,6},{1,25},{2,4},{3,27},{4,2},{5,29},{6,0},{7,31},{8,14},{9,17},... | collective-permute-start | bytes 172040 | tf_op jit(solution)/shard_map/ppermute | solution.py:463
  36.3 0.8 %collective-permute-start.12 = (bf16[32,896]{1,0:T(8,128)(2,1)S(1)}, bf16[32,896]{1,0:T(8,128)(2,1)S(1)}, u32[]{:S(2)}, u32[]{:S(2)}) collective-permute-start(bf16[32,896]{1,0:T(8,128)(2,1)S(1)} %shard_map.77.own_ref), channel_id=1, source_target_pairs={{0,4},{1,17},{2,6},{3,19},{4,0},{5,21},{6,2},{7,23},{8,12},{9,25},... | collective-permute-start | bytes 172040 | tf_op jit(solution)/shard_map/ppermute | solution.py:463
  37.0 0.6 %collective-permute-start.11 = (bf16[32,896]{1,0:T(8,128)(2,1)S(1)}, bf16[32,896]{1,0:T(8,128)(2,1)S(1)}, u32[]{:S(2)}, u32[]{:S(2)}) collective-permute-start(bf16[32,896]{1,0:T(8,128)(2,1)S(1)} %shard_map.77.own_ref), channel_id=1, source_target_pairs={{0,2},{1,9},{2,0},{3,11},{4,6},{5,13},{6,4},{7,15},{8,10},{9,1},{1... | collective-permute-start | bytes 172040 | tf_op jit(solution)/shard_map/ppermute | solution.py:463
  37.6 1.6 %collective-permute-done.13.refs_2_ = bf16[32,896]{1,0:T(8,128)(2,1)S(1)} collective-permute-done((bf16[32,896]{1,0:T(8,128)(2,1)S(1)}, bf16[32,896]{1,0:T(8,128)(2,1)S(1)}, u32[]{:S(2)}, u32[]{:S(2)}) %collective-permute-start.13) | collective-permute-done | bytes 57376 | tf_op jit(solution)/shard_map/ppermute | solution.py:463
  39.2 1.2 %collective-permute-done.12.refs_1_ = bf16[32,896]{1,0:T(8,128)(2,1)S(1)} collective-permute-done((bf16[32,896]{1,0:T(8,128)(2,1)S(1)}, bf16[32,896]{1,0:T(8,128)(2,1)S(1)}, u32[]{:S(2)}, u32[]{:S(2)}) %collective-permute-start.12) | collective-permute-done | bytes 57376 | tf_op jit(solution)/shard_map/ppermute | solution.py:463
  40.4 0.8 %collective-permute-done.11.refs_0_ = bf16[32,896]{1,0:T(8,128)(2,1)S(1)} collective-permute-done((bf16[32,896]{1,0:T(8,128)(2,1)S(1)}, bf16[32,896]{1,0:T(8,128)(2,1)S(1)}, u32[]{:S(2)}, u32[]{:S(2)}) %collective-permute-start.11) | collective-permute-done | bytes 57376 | tf_op jit(solution)/shard_map/ppermute | solution.py:463
  41.2 0.1 collective-permute-start.14
  41.3 1.3 %collective-permute-done.14.other_ref = f32[32,896]{1,0:T(8,128)S(1)} collective-permute-done((f32[32,896]{1,0:T(8,128)S(1)}, f32[32,896]{1,0:T(8,128)S(1)}, u32[]{:S(2)}, u32[]{:S(2)}) %collective-permute-start.14) | collective-permute-done | bytes 114720 | tf_op jit(solution)/shard_map/ppermute | solution.py:445
  42.6 0.7 %shard_map.79 = (f32[32,864]{1,0:T(8,128)}, f32[32,864]{1,0:T(8,128)}) custom-call(f32[32,896]{1,0:T(8,128)S(1)} %shard_map.78.mine_ref, f32[32,896]{1,0:T(8,128)S(1)} %collective-permute-done.14.other_ref), custom_call_target="tpu_custom_call" | custom-call | flops 1000000 | bytes 1000000 | tf_op jit(solution)/shard_map/pallas_call | solution.py:562
  (3 shorter events, 0.1 us)
Async XLA Ops:
  3.1 13.3 %collective-permute-start.3 = (bf16[160,128]{1,0:T(8,128)(2,1)S(1)}, bf16[160,128]{1,0:T(8,128)(2,1)S(1)}, u32[]{:S(2)}, u32[]{:S(2)}) collective-permute-start(bf16[160,128]{1,0:T(8,128)(2,1)S(1)} %get-tuple-element.48), channel_id=1, source_target_pairs={{0,12},{4,8},{8,4},{12,0},{16,28},{20,24},{24,20},{28,16},{1,13},{... | collective-permute-start | bytes 122888 | tf_op jit(solution)/shard_map/ppermute | solution.py:56
  7.1 9.2 %collective-permute-start.4 = (bf16[160,128]{1,0:T(8,128)(2,1)S(1)}, bf16[160,128]{1,0:T(8,128)(2,1)S(1)}, u32[]{:S(2)}, u32[]{:S(2)}) collective-permute-start(bf16[160,128]{1,0:T(8,128)(2,1)S(1)} %get-tuple-element.49), channel_id=1, source_target_pairs={{8,20},{12,16},{16,12},{20,8},{9,21},{13,17},{17,13},{21,9},{10,22... | collective-permute-start | bytes 122888 | tf_op jit(solution)/shard_map/ppermute | solution.py:56
  7.8 8.6 %collective-permute-start = (bf16[3,128,128]{2,1,0:T(8,128)(2,1)S(1)}, bf16[3,128,128]{2,1,0:T(8,128)(2,1)S(1)}, u32[]{:S(2)}, u32[]{:S(2)}) collective-permute-start(bf16[3,128,128]{2,1,0:T(8,128)(2,1)S(1)} %get-tuple-element.45), channel_id=1, source_target_pairs={{0,8},{8,0},{16,24},{24,16},{1,9},{9,1},{17,25},{25,17},{2,10},{10... | collective-permute-start | bytes 294920 | tf_op jit(solution)/shard_map/ppermute | solution.py:56
  12.2 4.2 %collective-permute-start.1 = (bf16[3,128,128]{2,1,0:T(8,128)(2,1)S(1)}, bf16[3,128,128]{2,1,0:T(8,128)(2,1)S(1)}, u32[]{:S(2)}, u32[]{:S(2)}) collective-permute-start(bf16[3,128,128]{2,1,0:T(8,128)(2,1)S(1)} %get-tuple-element.46), channel_id=1, source_target_pairs={{8,16},{16,8},{9,17},{17,9},{10,18},{18,10},{11,19},{19,11},{12,20... | collective-permute-start | bytes 294920 | tf_op jit(solution)/shard_map/ppermute | solution.py:56
  12.9 4.7 %collective-permute-start.2 = (bf16[3,128,128]{2,1,0:T(8,128)(2,1)S(1)}, bf16[3,128,128]{2,1,0:T(8,128)(2,1)S(1)}, u32[]{:S(2)}, u32[]{:S(2)}) collective-permute-start(bf16[3,128,128]{2,1,0:T(8,128)(2,1)S(1)} %get-tuple-element.47), channel_id=1, source_target_pairs={{0,4},{4,0},{1,5},{5,1},{2,6},{6,2},{3,7},{7,3},{8,12},{12,8},{9,1... | collective-permute-start | bytes 294920 | tf_op jit(solution)/shard_map/ppermute | solution.py:56
  17.7 1.9 %collective-permute-start.5 = (bf16[32,256]{1,0:T(8,128)(2,1)S(1)}, bf16[32,256]{1,0:T(8,128)(2,1)S(1)}, u32[]{:S(2)}, u32[]{:S(2)}) collective-permute-start(bf16[32,256]{1,0:T(8,128)(2,1)S(1)} %get-tuple-element.58), channel_id=1, source_target_pairs={{0,1},{1,0},{2,3},{3,2},{4,5},{5,4},{6,7},{7,6},{8,9},{9,8},{10,11... | collective-permute-start | bytes 49160 | tf_op jit(solution)/shard_map/ppermute | solution.py:56
  17.8 1.9 %collective-permute-start.6 = (bf16[32,256]{1,0:T(8,128)(2,1)S(1)}, bf16[32,256]{1,0:T(8,128)(2,1)S(1)}, u32[]{:S(2)}, u32[]{:S(2)}) collective-permute-start(bf16[32,256]{1,0:T(8,128)(2,1)S(1)} %get-tuple-element.59), channel_id=1, source_target_pairs={{1,2},{2,1},{5,6},{6,5},{9,10},{10,9},{13,14},{14,13},{17,18},{18,... | collective-permute-start | bytes 49160 | tf_op jit(solution)/shard_map/ppermute | solution.py:56
  22.1 4.7 %collective-permute-start.7 = (f32[32,896]{1,0:T(8,128)S(1)}, f32[32,896]{1,0:T(8,128)S(1)}, u32[]{:S(2)}, u32[]{:S(2)}) collective-permute-start(f32[32,896]{1,0:T(8,128)S(1)} %shard_map.74), channel_id=1, source_target_pairs={{0,1},{1,0},{2,3},{3,2},{4,5},{5,4},{6,7},{7,6},{8,9},{9,8},{10,11... | collective-permute-start | bytes 344072 | tf_op jit(solution)/shard_map/ppermute | solution.py:445
  26.8 6.1 %collective-permute-start.10 = (bf16[32,896]{1,0:T(8,128)(2,1)S(1)}, bf16[32,896]{1,0:T(8,128)(2,1)S(1)}, u32[]{:S(2)}, u32[]{:S(2)}) collective-permute-start(bf16[32,896]{1,0:T(8,128)(2,1)S(1)} %shard_map.75.own_ref), channel_id=1, source_target_pairs={{0,24},{1,7},{2,26},{3,5},{4,28},{5,3},{6,30},{7,1},{8,16},{9,15},... | collective-permute-start | bytes 172040 | tf_op jit(solution)/shard_map/ppermute | solution.py:463
  27.8 5.7 %collective-permute-start.9 = (bf16[32,896]{1,0:T(8,128)(2,1)S(1)}, bf16[32,896]{1,0:T(8,128)(2,1)S(1)}, u32[]{:S(2)}, u32[]{:S(2)}) collective-permute-start(bf16[32,896]{1,0:T(8,128)(2,1)S(1)} %shard_map.75.own_ref), channel_id=1, source_target_pairs={{0,16},{1,5},{2,18},{3,7},{4,20},{5,1},{6,22},{7,3},{8,24},{9,13},... | collective-permute-start | bytes 172040 | tf_op jit(solution)/shard_map/ppermute | solution.py:463
  29.6 4.4 %collective-permute-start.8 = (bf16[32,896]{1,0:T(8,128)(2,1)S(1)}, bf16[32,896]{1,0:T(8,128)(2,1)S(1)}, u32[]{:S(2)}, u32[]{:S(2)}) collective-permute-start(bf16[32,896]{1,0:T(8,128)(2,1)S(1)} %shard_map.75.own_ref), channel_id=1, source_target_pairs={{0,8},{1,3},{2,10},{3,1},{4,12},{5,7},{6,14},{7,5},{8,0},{9,11},{1... | collective-permute-start | bytes 172040 | tf_op jit(solution)/shard_map/ppermute | solution.py:463
  34.1 5.1 %collective-permute-start.13 = (bf16[32,896]{1,0:T(8,128)(2,1)S(1)}, bf16[32,896]{1,0:T(8,128)(2,1)S(1)}, u32[]{:S(2)}, u32[]{:S(2)}) collective-permute-start(bf16[32,896]{1,0:T(8,128)(2,1)S(1)} %shard_map.77.own_ref), channel_id=1, source_target_pairs={{0,6},{1,25},{2,4},{3,27},{4,2},{5,29},{6,0},{7,31},{8,14},{9,17},... | collective-permute-start | bytes 172040 | tf_op jit(solution)/shard_map/ppermute | solution.py:463
  36.3 4.2 %collective-permute-start.12 = (bf16[32,896]{1,0:T(8,128)(2,1)S(1)}, bf16[32,896]{1,0:T(8,128)(2,1)S(1)}, u32[]{:S(2)}, u32[]{:S(2)}) collective-permute-start(bf16[32,896]{1,0:T(8,128)(2,1)S(1)} %shard_map.77.own_ref), channel_id=1, source_target_pairs={{0,4},{1,17},{2,6},{3,19},{4,0},{5,21},{6,2},{7,23},{8,12},{9,25},... | collective-permute-start | bytes 172040 | tf_op jit(solution)/shard_map/ppermute | solution.py:463
  37.0 4.2 %collective-permute-start.11 = (bf16[32,896]{1,0:T(8,128)(2,1)S(1)}, bf16[32,896]{1,0:T(8,128)(2,1)S(1)}, u32[]{:S(2)}, u32[]{:S(2)}) collective-permute-start(bf16[32,896]{1,0:T(8,128)(2,1)S(1)} %shard_map.77.own_ref), channel_id=1, source_target_pairs={{0,2},{1,9},{2,0},{3,11},{4,6},{5,13},{6,4},{7,15},{8,10},{9,1},{1... | collective-permute-start | bytes 172040 | tf_op jit(solution)/shard_map/ppermute | solution.py:463
  41.2 1.4 %collective-permute-start.14 = (f32[32,896]{1,0:T(8,128)S(1)}, f32[32,896]{1,0:T(8,128)S(1)}, u32[]{:S(2)}, u32[]{:S(2)}) collective-permute-start(f32[32,896]{1,0:T(8,128)S(1)} %shard_map.78.mine_ref), channel_id=1, source_target_pairs={{0,1},{1,0},{2,3},{3,2},{4,5},{5,4},{6,7},{7,6},{8,9},{9,8},{10,11... | collective-permute-start | bytes 344072 | tf_op jit(solution)/shard_map/ppermute | solution.py:445

commit v2 on v1

--- a/solution.py
+++ b/solution.py
@@ -38,27 +38,24 @@
 
 
 def swap(x, moves):
-    axes = tuple(axis for axis, _ in moves)
+    axes = ("gx", "gy")
     sizes = [lax.axis_size(axis) for axis in axes]
-    pairs = []
-    for source in range(math.prod(sizes)):
-        rest, target, factor = source, 0, 1
-        for (_, side), size in zip(moves[::-1], sizes[::-1]):
-            other = partner(rest % size, side, size)
-            if other is None:
-                target = None
-                break
-            target += other * factor
-            rest //= size
-            factor *= size
-        if target is not None:
-            pairs.append((source, target))
-    return lax.ppermute(x, axes, pairs) if pairs else None
-
-
-def exchange(face_a, face_b, axis):
-    got = [swap(face_a, [(axis, 0)]), swap(face_b, [(axis, 1)])]
-    return [g for g in got if g is not None]
+    side = dict(moves)
+    places = [(i, j) for i in range(sizes[0]) for j in range(sizes[1])]
+    target = {}
+    for place in places:
+        to = [partner(i, side[axis], size) if axis in side else i for i, axis, size in zip(place, axes, sizes)]
+        if None not in to:
+            target[place] = tuple(to)
+    if not target:
+        return None
+    alone = [place for place in places if place not in target]
+    for fill in (lambda i, j: (i, j ^ 1), lambda i, j: (i ^ 1, j), lambda i, j: (i, j)):
+        if all(fill(*place) in alone for place in alone):
+            target.update({place: fill(*place) for place in alone})
+            break
+    number = lambda place: place[0] * sizes[1] + place[1]
+    return lax.ppermute(x, axes, [(number(place), number(target[place])) for place in places])
 
 
 def choose(flag, a, b):
@@ -108,16 +105,21 @@
         even_x, even_y = even_index("gx"), even_index("gy")
         self.flag_x = {"below": even_x, "above": jnp.logical_not(even_x)}
         self.flag_y = {"below": even_y, "above": jnp.logical_not(even_y)}
+        ends = lambda axis: (lax.axis_index(axis) == 0, lax.axis_index(axis) == lax.axis_size(axis) - 1)
+        self.outside_x = dict(zip(("below", "above"), ends("gx")))
+        self.outside_y = dict(zip(("below", "above"), ends("gy")))
         self.face_x = list(face_x)
         self.face_y = list(face_y) + [None] * (2 - y_sides)
         self.corner = [list(corner[2 * k : 2 * k + 2]) for k in range(y_sides)] + [[None, None]] * (2 - y_sides)
 
     def from_x(self, where, index, rows):
-        return choose(self.flag_x[where], self.face_x[1][index, rows], self.face_x[0][index, rows])
+        value = choose(self.flag_x[where], self.face_x[1][index, rows], self.face_x[0][index, rows])
+        return jnp.where(self.outside_x[where], jnp.zeros_like(value), value)
 
     def from_y(self, where, read):
         a = [None if ref is None else read(ref) for ref in self.face_y]
-        return choose(self.flag_y[where], a[1], a[0])
+        value = choose(self.flag_y[where], a[1], a[0])
+        return jnp.where(self.outside_y[where], jnp.zeros_like(value), value)
 
     def from_corner(self, where_x, where_y, read):
         a = []
@@ -126,7 +128,9 @@
                 a.append(None)
             else:
                 a.append(choose(self.flag_x[where_x], read(pair[1]), read(pair[0])))
-        return choose(self.flag_y[where_y], a[1], a[0])
+        value = choose(self.flag_y[where_y], a[1], a[0])
+        outside = self.outside_x[where_x] | self.outside_y[where_y]
+        return jnp.where(outside, jnp.zeros_like(value), value)
 
     def side_of(self, x, width):
         if x < width:
@@ -176,7 +180,7 @@
 
 
 def pack_z(y_sides, *refs):
-    pieces, (low_out, high_out, face_a, face_b) = take_pieces(y_sides, refs)
+    pieces, (low_out, high_out, middle_out) = take_pieces(y_sides, refs)
     n_field, n_noise, size_z = pieces.size_x + 4, pieces.size_x + 2, pieces.size_z
 
     def gather(tile, first, noise_row):
@@ -192,9 +196,12 @@
     high = gather(size_z - 16, size_z - 2, size_z - 1)
     low_out[...] = low
     high_out[...] = high
-    even = even_index("gz")
-    face_a[...] = jnp.where(even, high, low)
-    face_b[...] = jnp.where(even, low, high)
+    middle_out[...] = jnp.where(lax.axis_index("gz") == 1, high, low)
+
+
+def pack_pair(low_ref, high_ref, passed_ref, out_ref):
+    out_ref[0] = jnp.where(even_index("gz"), high_ref[...], low_ref[...])
+    out_ref[1] = passed_ref[...]
 
 
 def stack(ref, dz, first, count):
@@ -286,17 +293,17 @@
     ref[dz, x, at, :] = jnp.where(index == (15 if last else 0), row, tile).astype(BF16)
 
 
-def activate(n_recv, *refs):
-    pre_ref, wide_field_ref, wide_noise_ref, low_ref, high_ref, a1_ref = refs[:6]
-    recv = refs[6 : 6 + n_recv]
-    hid_ref, slope_ref, xs_ref, ns_ref = refs[6 + n_recv :]
+def activate(
+    pre_ref, wide_field_ref, wide_noise_ref, low_ref, high_ref, a1_ref, recv_ref, hid_ref, slope_ref, xs_ref, ns_ref
+):
     n_field, size_z = xs_ref.shape[1], xs_ref.shape[2]
     n_noise = ns_ref.shape[1]
     size_x = n_noise - 2
     even = even_index("gz")
-    recv_b = recv[1][...] if n_recv > 1 else None
-    below_rows = choose(even, recv_b, recv[0][...]).astype(F32)
-    above_rows = choose(even, recv[0][...], recv_b).astype(F32)
+    near, far = recv_ref[0].astype(F32), recv_ref[1].astype(F32)
+    index = lax.axis_index("gz")
+    below_rows = jnp.where(even, jnp.where(index == 2, far, 0.0), near)
+    above_rows = jnp.where(even, near, jnp.where(index == 1, far, 0.0))
     own_low = low_ref[...].astype(F32)
     own_high = high_ref[...].astype(F32)
 
@@ -332,11 +339,11 @@
     drop = drop | ((x_row == 0) & first_x) | ((x_row == n_noise - 1) & last_x)
     edge_hidden = jnp.where(drop, 0.0, edge_hidden).astype(BF16).astype(F32)
 
-    index = lax.broadcasted_iota(jnp.int32, (size_z, 256), 0)
+    row = lax.broadcasted_iota(jnp.int32, (size_z, 256), 0)
     for x in range(n_noise):
         value = pre_ref[x]
-        value = value + jnp.where(index == 0, row_total[x : x + 1], 0.0)
-        value = value + jnp.where(index == size_z - 1, row_total[n_field + x : n_field + x + 1], 0.0)
+        value = value + jnp.where(row == 0, row_total[x : x + 1], 0.0)
+        value = value + jnp.where(row == size_z - 1, row_total[n_field + x : n_field + x + 1], 0.0)
         hidden, s = silu_parts(value)
         gone = drop_y
         if x == 0:
@@ -440,7 +447,7 @@
     out_ref[...] = total.astype(out_ref.dtype)
 
 
-def butterfly(x, axis, bit):
+def flip(x, axis, bit):
     size = lax.axis_size(axis)
     return lax.ppermute(x, axis, [(i, i ^ bit) for i in range(size)])
 
@@ -487,36 +494,38 @@
     moves = [[("gx", side)] for side in range(2)]
     moves += [[("gy", side)] for side in range(y_sides)]
     moves += [[("gx", side), ("gy", k)] for k in range(y_sides) for side in range(2)]
-    order = sorted(range(len(moves)), key=lambda k: (moves[k][0] == ("gx", 1), len(moves[k]), moves[k]))
-    sent = {k: swap(faces[k], moves[k]) for k in order}
-    got = [sent[k] for k in range(len(moves))]
+    both = jnp.concatenate([w_first, w_second], axis=0)
+    near = 2 + y_sides
+    *faces[near:], both = lax.optimization_barrier((*faces[near:], both))
+    got = [swap(face, move) for face, move in zip(faces, moves)]
 
     a1, ab, second = call(
         spread_weights,
         [struct((9 * 256, 256), BF16), struct((9 * 256, 256), BF16), struct((9, C, 128), F32)],
         moved=4_000_000,
-    )(jnp.concatenate([w_first, w_second], axis=0))
+    )(both)
     *got, a1, ab, second = lax.optimization_barrier((*got, a1, ab, second))
 
     n_field, n_noise = size_x + 4, size_x + 2
     z_rows = -(-(2 * n_field + n_noise) // 16) * 16
-    low, high, face_a, face_b = call(
-        functools.partial(pack_z, y_sides), [struct((z_rows, 256), BF16)] * 4
+    low, high, middle = call(
+        functools.partial(pack_z, y_sides), [struct((z_rows, 256), BF16)] * 3
     )(field, wide_noise, *got)
-    z_got = exchange(face_a, face_b, "gz")
+    passed = flip(middle, "gz", 2)
     pre_shape = (n_noise, size_z, 256)
     xs, ns, pre = call(
         functools.partial(widen, y_sides),
         [struct((3, n_field, size_z, 256), BF16), struct((3,) + pre_shape, BF16), struct(pre_shape, F32)],
         flops=1_000_000_000,
     )(field, wide_noise, *got, a1)
-    *z_got, xs, ns, pre = lax.optimization_barrier((*z_got, xs, ns, pre))
+    passed, xs, ns, pre = lax.optimization_barrier((passed, xs, ns, pre))
+    z_got = flip(call(pack_pair, struct((2, z_rows, 256), BF16))(low, high, passed), "gz", 1)
 
     slope_shape = (size_x, size_z, 256)
     hidden, slope, xs, ns = call(
-        functools.partial(activate, len(z_got)),
+        activate,
         [struct((3,) + pre_shape, BF16), struct(slope_shape, F32), struct(xs.shape, BF16), struct(ns.shape, BF16)],
-    )(pre, xs, ns, low, high, a1, *z_got)
+    )(pre, xs, ns, low, high, a1, z_got)
     pre_grad = call(
         backward,
         struct((lanes, size_x * size_z), BF16),
@@ -528,7 +537,7 @@
     rounded = struct((C, 896), BF16)
     parts = (xs, hidden, pre_grad, noise_rows)
     give = call(functools.partial(weight_grad, True), half, flops=1_000_000_000)(*parts)
-    taken = butterfly(give, "gz", 1)
+    taken = flip(give, "gz", 1)
     keep = call(functools.partial(weight_grad, False), half, flops=1_000_000_000)(*parts)
     send = call(first_sum, rounded)(keep, taken)
 
@@ -553,12 +562,12 @@
         flips = [(even[:1], odd[:1])]
         if len(even) == 2:
             flips += [(even[1:], odd[1:]), (even, odd)]
-        got = [masked_swap(send, *flip) for flip in flips]
+        got = [masked_swap(send, *pair) for pair in flips]
         if k == 0:
             *got, prediction = lax.optimization_barrier((*got, prediction))
         send = call(round_sum, half if k == len(rounds) - 1 else rounded)(send, *got)
     mine = send
-    other = butterfly(mine, "gz", 1)
+    other = flip(mine, "gz", 1)
     fisher_first, fisher_second = call(
         functools.partial(finish, norm), [struct((C, 27 * C), F32)] * 2
     )(mine, other)

time: 43.6 us -> 41.6 us (0.954)
  starting transfers between devices: 23.8 us -> 19.1 us
  waiting for transfers between devices: 7.55 us -> 10.4 us
    ppermute x9, starting transfers between devices: 15.8 us -> 11.1 us  [the longest x5 9.26 us: swap(): lax.ppermute(x, axes, [(number(place), number(target[place])) for place i...]
    ppermute x9, waiting for transfers between devices: 2.82 us -> 5.54 us  [the longest x4 4.08 us: flip(): return lax.ppermute(x, axis, [(i, i ^ bit) for i in range(size)])]
    pallas_call x2 -> x3, Pallas kernels: 0.98 us -> 0.98 us  [the longest x1 0.82 us: local(): call(activate, [struct((3,) + pre_shape, BF16), struct(slope_shape, F32),...]
  transfers between devices with their start and end apart: 15 -> 15, of which waited for: 8 -> 10; matrix products, arithmetic and copies ran while one was open for 4% -> 4% of each run, Pallas kernels for 9% -> 9%
where the time goes in v2:
time: 41.6 us; the launch traced here: 41.4 us
  starting transfers between devices  19.1 us (46%)
  waiting for transfers between devices  10.4 us (25%)
  Pallas kernels  7.69 us (18%)
  local copies, waits for them, and re-layouts  2.61 us (6%)
  other arithmetic  0.86 us (2%)
  between operations  0.75 us (2%)
    ppermute x5, starting transfers between devices, swap(): lax.ppermute(x, axes, [(number(place), number(target[place])) for place i...  9.26 us
    ppermute x6, starting transfers between devices, masked_swap(): return lax.ppermute(x, AXES, pairs)  8.01 us
    ppermute x6, waiting for transfers between devices, masked_swap(): return lax.ppermute(x, AXES, pairs)  4.83 us
    ppermute x4, waiting for transfers between devices, flip(): return lax.ppermute(x, axis, [(i, i ^ bit) for i in range(size)])  4.08 us
    transpose x2, local copies, waits for them, and re-layouts, rows(): return x[0].transpose(1, 2, 0, 3).reshape(size_x, lanes, size_z)  1.88 us
    ppermute x4, starting transfers between devices, flip(): return lax.ppermute(x, axis, [(i, i ^ bit) for i in range(size)])  1.86 us
    ppermute x5, waiting for transfers between devices, swap(): lax.ppermute(x, axes, [(number(place), number(target[place])) for place i...  1.45 us
    pallas_call x1, Pallas kernels, local(): call(functools.partial(widen, y_sides), [struct((3, n_field, size_z, 256)...  1.18 us
  transfers between devices with their start and end apart: 15, of which 10 were waited for; matrix products, arithmetic and copies ran while one was open for 4% of the time, Pallas kernels for 9%

profile of v2, /device:TPU:0, one launch (start us, length us, event | category | flops | bytes accessed | tf_op | source)
XLA Modules:
  0.0 41.4 jit_solution(15630554905523359785)
XLA Ops:
  0.6 0.9 %copy.7 = bf16[4,4,32,128]{3,2,1,0:T(8,128)(2,1)S(1)} copy(bf16[4,4,32,128]{3,1,0,2:T(4,128)(2,1)} %bitcast.19) | data formatting | bytes 262144 | tf_op jit(solution)/shard_map/transpose | solution.py:481
  1.6 0.9 %copy.8 = bf16[4,4,32,128]{3,2,1,0:T(8,128)(2,1)S(1)} copy(bf16[4,4,32,128]{3,1,0,2:T(4,128)(2,1)} %bitcast.20) | data formatting | bytes 262144 | tf_op jit(solution)/shard_map/transpose | solution.py:481
  2.5 0.6 %shard_map.67 = (bf16[4,128,128]{2,1,0:T(8,128)(2,1)S(1)}, bf16[4,128,128]{2,1,0:T(8,128)(2,1)S(1)}, bf16[3,128,128]{2,1,0:T(8,128)(2,1)S(1)}, bf16[3,128,128]{2...) custom-call(bf16[4,128,128]{2,1,0:T(8,128)(2,1)S(1)} %bitcast.17, ...), custom_call_target="tpu_custom_call" | custom-call | flops 1000000 | bytes 1000000 | tf_op jit(solution)/shard_map/pallas_call | solution.py:487
  3.1 3.1 %collective-permute-start = (bf16[3,128,128]{2,1,0:T(8,128)(2,1)S(1)}, bf16[3,128,128]{2,1,0:T(8,128)(2,1)S(1)}, u32[]{:S(2)}, u32[]{:S(2)}) collective-permute-start(bf16[3,128,128]{2,1,0:T(8,128)(2,1)S(1)} %get-tuple-element.46), channel_id=1, source_target_pairs={{0,8},{4,12},{8,0},{12,4},{16,24},{20,28},{24,16},{28,20},{1,9},{5... | collective-permute-start | bytes 294920 | tf_op jit(solution)/shard_map/ppermute | solution.py:58
  6.2 1.5 %collective-permute-start.1 = (bf16[3,128,128]{2,1,0:T(8,128)(2,1)S(1)}, bf16[3,128,128]{2,1,0:T(8,128)(2,1)S(1)}, u32[]{:S(2)}, u32[]{:S(2)}) collective-permute-start(bf16[3,128,128]{2,1,0:T(8,128)(2,1)S(1)} %get-tuple-element.47), channel_id=1, source_target_pairs={{0,4},{4,0},{8,16},{12,20},{16,8},{20,12},{24,28},{28,24},{1,5},{5... | collective-permute-start | bytes 294920 | tf_op jit(solution)/shard_map/ppermute | solution.py:58
  7.7 0.5 %collective-permute-start.2 = (bf16[3,128,128]{2,1,0:T(8,128)(2,1)S(1)}, bf16[3,128,128]{2,1,0:T(8,128)(2,1)S(1)}, u32[]{:S(2)}, u32[]{:S(2)}) collective-permute-start(bf16[3,128,128]{2,1,0:T(8,128)(2,1)S(1)} %get-tuple-element.48), channel_id=1, source_target_pairs={{0,4},{4,0},{8,12},{12,8},{16,20},{20,16},{24,28},{28,24},{1,5},{5... | collective-permute-start | bytes 294920 | tf_op jit(solution)/shard_map/ppermute | solution.py:58
  8.2 0.9 %pad_maximum_fusion.both_ref = bf16[64,864]{1,0:T(8,128)(2,1)S(1)} fusion(bf16[32,864]{1,0:T(8,128)(2,1)} %param.7, bf16[32,864]{1,0:T(8,128)(2,1)} %param.6), kind=kLoop, calls=%fused_computation.1 | loop fusion | flops 221184 | bytes 221184 | tf_op jit(solution)/shard_map/concatenate | solution.py:497
  9.1 2.7 %collective-permute-start.3 = (bf16[160,128]{1,0:T(8,128)(2,1)S(1)}, bf16[160,128]{1,0:T(8,128)(2,1)S(1)}, u32[]{:S(2)}, u32[]{:S(2)}) collective-permute-start(bf16[160,128]{1,0:T(8,128)(2,1)S(1)} %get-tuple-element.51), channel_id=1, source_target_pairs={{0,12},{4,8},{8,4},{12,0},{16,28},{20,24},{24,20},{28,16},{1,13},{... | collective-permute-start | bytes 122888 | tf_op jit(solution)/shard_map/ppermute | solution.py:58
  11.8 1.5 %collective-permute-start.4 = (bf16[160,128]{1,0:T(8,128)(2,1)S(1)}, bf16[160,128]{1,0:T(8,128)(2,1)S(1)}, u32[]{:S(2)}, u32[]{:S(2)}) collective-permute-start(bf16[160,128]{1,0:T(8,128)(2,1)S(1)} %get-tuple-element.52), channel_id=1, source_target_pairs={{0,4},{4,0},{8,20},{12,16},{16,12},{20,8},{24,28},{28,24},{1,5},{5... | collective-permute-start | bytes 122888 | tf_op jit(solution)/shard_map/ppermute | solution.py:58
  13.3 1.0 %shard_map.68 = (bf16[2304,256]{1,0:T(8,128)(2,1)S(1)}, bf16[2304,256]{1,0:T(8,128)(2,1)S(1)}, f32[9,32,128]{2,1,0:T(8,128)S(1)}) custom-call(bf16[64,864]{1,0:T(8,128)(2,1)S(1)} %pad_maximum_fusion.both_ref), custom_call_target="tpu_custom_call" | custom-call | flops 1000000 | bytes 4000000 | tf_op jit(solution)/shard_map/pallas_call | solution.py:502
  14.3 0.0 collective-permute-done.3.refs_5_
  14.3 1.4 %collective-permute-done.4.refs_6_ = bf16[160,128]{1,0:T(8,128)(2,1)S(1)} collective-permute-done((bf16[160,128]{1,0:T(8,128)(2,1)S(1)}, bf16[160,128]{1,0:T(8,128)(2,1)S(1)}, u32[]{:S(2)}, u32[]{:S(2)}) %collective-permute-start.4) | collective-permute-done | bytes 40992 | tf_op jit(solution)/shard_map/ppermute | solution.py:58
  15.8 0.0 collective-permute-done.refs_2_
  15.8 0.0 collective-permute-done.1.refs_3_
  15.8 0.0 collective-permute-done.2.refs_4_
  15.8 0.2 shard_map.69
  15.9 1.6 %collective-permute-start.5 = (bf16[32,256]{1,0:T(8,128)(2,1)S(1)}, bf16[32,256]{1,0:T(8,128)(2,1)S(1)}, u32[]{:S(2)}, u32[]{:S(2)}) collective-permute-start(bf16[32,256]{1,0:T(8,128)(2,1)S(1)} %get-tuple-element.62), channel_id=1, source_target_pairs={{0,2},{1,3},{2,0},{3,1},{4,6},{5,7},{6,4},{7,5},{8,10},{9,11},{10,... | collective-permute-start | bytes 49160 | tf_op jit(solution)/shard_map/ppermute | solution.py:452
  17.5 1.2 %shard_map.70 = (bf16[3,8,128,256]{3,2,1,0:T(8,128)(2,1)S(1)}, bf16[3,6,128,256]{3,2,1,0:T(8,128)(2,1)S(1)}, f32[6,128,256]{2,1,0:T(8,128)S(1)}) custom-call(bf16[4,128,128]{2,1,0:T(8,128)(2,1)S(1)} %get-tuple-element.44.refs_0_, bf16[4,128,128]{2,1,0:T(8,128)(2,1)S(1)} %get-tuple-element.45.refs_1_, bf16[3,128,128]{2,1,0:T(8,128)(2,1)S(1)} %collective-permute-done.refs_2_, ...), custom_call_target="tpu_custom_call" | custom-call | flops 1000000000 | bytes 1000000 | tf_op jit(solution)/shard_map/pallas_call | solution.py:516
  18.7 1.0 %collective-permute-done.5.passed_ref = bf16[32,256]{1,0:T(8,128)(2,1)S(1)} collective-permute-done((bf16[32,256]{1,0:T(8,128)(2,1)S(1)}, bf16[32,256]{1,0:T(8,128)(2,1)S(1)}, u32[]{:S(2)}, u32[]{:S(2)}) %collective-permute-start.5) | collective-permute-done | bytes 16416 | tf_op jit(solution)/shard_map/ppermute | solution.py:452
  19.7 0.0 collective-permute-start.6
  19.8 1.2 %collective-permute-done.6.recv_ref = bf16[2,32,256]{2,1,0:T(8,128)(2,1)S(1)} collective-permute-done((bf16[2,32,256]{2,1,0:T(8,128)(2,1)S(1)}, bf16[2,32,256]{2,1,0:T(8,128)(2,1)S(1)}, u32[]{:S(2)}, u32[]{:S(2)}) %collective-permute-start.6) | collective-permute-done | bytes 32800 | tf_op jit(solution)/shard_map/ppermute | solution.py:452
  21.0 0.8 %shard_map.72 = (bf16[3,6,128,256]{3,2,1,0:T(8,128)(2,1)S(1)}, f32[4,128,256]{2,1,0:T(8,128)S(1)}, bf16[3,8,128,256]{3,2,1,0:T(8,128)(2,1)S(1)}, bf16[3,6,128,256]{3,2,1,0:T(8,128)(2,1)S(1)}) custom-call(f32[6,128,256]{2,1,0:T(8,128)S(1)} %get-tuple-element.67.pre_ref, bf16[3,8,128,256]{3,2,1,0:T(8,128)(2,1)S(1)} %get-tuple-element.68.wide_field_ref, ...), custom_call_target="tpu_custom_call" | custom-call | flops 1000000 | bytes 1000000 | tf_op jit(solution)/shard_map/pallas_call | solution.py:525
  21.8 0.8 %shard_map.73.pre_grad_ref = bf16[128,512]{1,0:T(8,128)(2,1)S(1)} custom-call(bf16[3,6,128,256]{3,2,1,0:T(8,128)(2,1)S(1)} %get-tuple-element.75.ns_ref, f32[4,128,256]{2,1,0:T(8,128)S(1)} %get-tuple-element.76.slope_ref, bf16[2304,256]{1,0:T(8,128)(2,1)S(1)} %get-tuple-element.77.ab_ref), custom_call_target="tpu_custom_call" | custom-call | flops 1000000000 | bytes 1000000 | tf_op jit(solution)/shard_map/pallas_call | solution.py:529
  22.6 0.7 %shard_map.75 = f32[32,896]{1,0:T(8,128)S(1)} custom-call(bf16[3,8,128,256]{3,2,1,0:T(8,128)(2,1)S(1)} %get-tuple-element.73.xs_ref, bf16[3,6,128,256]{3,2,1,0:T(8,128)(2,1)S(1)} %get-tuple-element.74.hid_ref, bf16[128,512]{1,0:T(8,128)(2,1)S(1)} %shard_map.73.pre_grad_ref, bf16[4,128,128]{2,1,0:T(8,128)(2,1)S(1)} %bitcast.15), custom_call_target="tpu_custom_call" | custom-call | flops 1000000000 | bytes 1000000 | tf_op jit(solution)/shard_map/pallas_call | solution.py:539
  23.3 0.2 collective-permute-start.7
  23.5 0.6 %shard_map.74.keep_ref = f32[32,896]{1,0:T(8,128)S(1)} custom-call(bf16[3,8,128,256]{3,2,1,0:T(8,128)(2,1)S(1)} %get-tuple-element.73.xs_ref, bf16[3,6,128,256]{3,2,1,0:T(8,128)(2,1)S(1)} %get-tuple-element.74.hid_ref, bf16[128,512]{1,0:T(8,128)(2,1)S(1)} %shard_map.73.pre_grad_ref, bf16[4,128,128]{2,1,0:T(8,128)(2,1)S(1)} %bitcast.16), custom_call_target="tpu_custom_call" | custom-call | flops 1000000000 | bytes 1000000 | tf_op jit(solution)/shard_map/pallas_call | solution.py:541
  24.2 0.5 %collective-permute-done.7.taken_ref = f32[32,896]{1,0:T(8,128)S(1)} collective-permute-done((f32[32,896]{1,0:T(8,128)S(1)}, f32[32,896]{1,0:T(8,128)S(1)}, u32[]{:S(2)}, u32[]{:S(2)}) %collective-permute-start.7) | collective-permute-done | bytes 114720 | tf_op jit(solution)/shard_map/ppermute | solution.py:452
  24.7 1.3 %collective-permute-start.10 = (bf16[32,896]{1,0:T(8,128)(2,1)S(1)}, bf16[32,896]{1,0:T(8,128)(2,1)S(1)}, u32[]{:S(2)}, u32[]{:S(2)}) collective-permute-start(bf16[32,896]{1,0:T(8,128)(2,1)S(1)} %shard_map.76.own_ref), channel_id=1, source_target_pairs={{0,24},{1,7},{2,26},{3,5},{4,28},{5,3},{6,30},{7,1},{8,16},{9,15},... | collective-permute-start | bytes 172040 | tf_op jit(solution)/shard_map/ppermute | solution.py:470
  26.0 1.6 %collective-permute-start.9 = (bf16[32,896]{1,0:T(8,128)(2,1)S(1)}, bf16[32,896]{1,0:T(8,128)(2,1)S(1)}, u32[]{:S(2)}, u32[]{:S(2)}) collective-permute-start(bf16[32,896]{1,0:T(8,128)(2,1)S(1)} %shard_map.76.own_ref), channel_id=1, source_target_pairs={{0,16},{1,5},{2,18},{3,7},{4,20},{5,1},{6,22},{7,3},{8,24},{9,13},... | collective-permute-start | bytes 172040 | tf_op jit(solution)/shard_map/ppermute | solution.py:470
  27.6 1.6 %collective-permute-start.8 = (bf16[32,896]{1,0:T(8,128)(2,1)S(1)}, bf16[32,896]{1,0:T(8,128)(2,1)S(1)}, u32[]{:S(2)}, u32[]{:S(2)}) collective-permute-start(bf16[32,896]{1,0:T(8,128)(2,1)S(1)} %shard_map.76.own_ref), channel_id=1, source_target_pairs={{0,8},{1,3},{2,10},{3,1},{4,12},{5,7},{6,14},{7,5},{8,0},{9,11},{1... | collective-permute-start | bytes 172040 | tf_op jit(solution)/shard_map/ppermute | solution.py:470
  29.2 0.9 %shard_map.77 = bf16[4,128,128]{2,1,0:T(8,128)(2,1)S(1)} custom-call(bf16[3,6,128,256]{3,2,1,0:T(8,128)(2,1)S(1)} %get-tuple-element.74.hid_ref, f32[9,32,128]{2,1,0:T(8,128)S(1)} %get-tuple-element.78.second_ref), custom_call_target="tpu_custom_call" | custom-call | flops 500000000 | bytes 1000000 | tf_op jit(solution)/shard_map/pallas_call | solution.py:544
  30.1 0.7 %copy.11 = bf16[4,4,32,128]{3,1,0,2:T(4,128)(2,1)} copy(bf16[4,4,32,128]{3,2,1,0:T(8,128)(2,1)S(1)} %bitcast.18) | data formatting | bytes 262144 | tf_op jit(solution)/shard_map/reshape | solution.py:550
  30.8 0.0 collective-permute-done.10.refs_2_
  30.8 0.6 %collective-permute-done.9.refs_1_ = bf16[32,896]{1,0:T(8,128)(2,1)S(1)} collective-permute-done((bf16[32,896]{1,0:T(8,128)(2,1)S(1)}, bf16[32,896]{1,0:T(8,128)(2,1)S(1)}, u32[]{:S(2)}, u32[]{:S(2)}) %collective-permute-start.9) | collective-permute-done | bytes 57376 | tf_op jit(solution)/shard_map/ppermute | solution.py:470
  31.4 0.6 %collective-permute-done.8.refs_0_ = bf16[32,896]{1,0:T(8,128)(2,1)S(1)} collective-permute-done((bf16[32,896]{1,0:T(8,128)(2,1)S(1)}, bf16[32,896]{1,0:T(8,128)(2,1)S(1)}, u32[]{:S(2)}, u32[]{:S(2)}) %collective-permute-start.8) | collective-permute-done | bytes 57376 | tf_op jit(solution)/shard_map/ppermute | solution.py:470
  32.0 2.5 %collective-permute-start.13 = (bf16[32,896]{1,0:T(8,128)(2,1)S(1)}, bf16[32,896]{1,0:T(8,128)(2,1)S(1)}, u32[]{:S(2)}, u32[]{:S(2)}) collective-permute-start(bf16[32,896]{1,0:T(8,128)(2,1)S(1)} %shard_map.78.own_ref), channel_id=1, source_target_pairs={{0,6},{1,25},{2,4},{3,27},{4,2},{5,29},{6,0},{7,31},{8,14},{9,17},... | collective-permute-start | bytes 172040 | tf_op jit(solution)/shard_map/ppermute | solution.py:470
  34.6 0.5 %collective-permute-start.12 = (bf16[32,896]{1,0:T(8,128)(2,1)S(1)}, bf16[32,896]{1,0:T(8,128)(2,1)S(1)}, u32[]{:S(2)}, u32[]{:S(2)}) collective-permute-start(bf16[32,896]{1,0:T(8,128)(2,1)S(1)} %shard_map.78.own_ref), channel_id=1, source_target_pairs={{0,4},{1,17},{2,6},{3,19},{4,0},{5,21},{6,2},{7,23},{8,12},{9,25},... | collective-permute-start | bytes 172040 | tf_op jit(solution)/shard_map/ppermute | solution.py:470
  35.1 0.5 %collective-permute-start.11 = (bf16[32,896]{1,0:T(8,128)(2,1)S(1)}, bf16[32,896]{1,0:T(8,128)(2,1)S(1)}, u32[]{:S(2)}, u32[]{:S(2)}) collective-permute-start(bf16[32,896]{1,0:T(8,128)(2,1)S(1)} %shard_map.78.own_ref), channel_id=1, source_target_pairs={{0,2},{1,9},{2,0},{3,11},{4,6},{5,13},{6,4},{7,15},{8,10},{9,1},{1... | collective-permute-start | bytes 172040 | tf_op jit(solution)/shard_map/ppermute | solution.py:470
  35.6 1.6 %collective-permute-done.13.refs_2_ = bf16[32,896]{1,0:T(8,128)(2,1)S(1)} collective-permute-done((bf16[32,896]{1,0:T(8,128)(2,1)S(1)}, bf16[32,896]{1,0:T(8,128)(2,1)S(1)}, u32[]{:S(2)}, u32[]{:S(2)}) %collective-permute-start.13) | collective-permute-done | bytes 57376 | tf_op jit(solution)/shard_map/ppermute | solution.py:470
  37.2 1.6 %collective-permute-done.12.refs_1_ = bf16[32,896]{1,0:T(8,128)(2,1)S(1)} collective-permute-done((bf16[32,896]{1,0:T(8,128)(2,1)S(1)}, bf16[32,896]{1,0:T(8,128)(2,1)S(1)}, u32[]{:S(2)}, u32[]{:S(2)}) %collective-permute-start.12) | collective-permute-done | bytes 57376 | tf_op jit(solution)/shard_map/ppermute | solution.py:470
  38.7 0.5 %collective-permute-done.11.refs_0_ = bf16[32,896]{1,0:T(8,128)(2,1)S(1)} collective-permute-done((bf16[32,896]{1,0:T(8,128)(2,1)S(1)}, bf16[32,896]{1,0:T(8,128)(2,1)S(1)}, u32[]{:S(2)}, u32[]{:S(2)}) %collective-permute-start.11) | collective-permute-done | bytes 57376 | tf_op jit(solution)/shard_map/ppermute | solution.py:470
  39.3 0.1 collective-permute-start.14
  39.4 1.3 %collective-permute-done.14.other_ref = f32[32,896]{1,0:T(8,128)S(1)} collective-permute-done((f32[32,896]{1,0:T(8,128)S(1)}, f32[32,896]{1,0:T(8,128)S(1)}, u32[]{:S(2)}, u32[]{:S(2)}) %collective-permute-start.14) | collective-permute-done | bytes 114720 | tf_op jit(solution)/shard_map/ppermute | solution.py:452
  40.7 0.7 %shard_map.80 = (f32[32,864]{1,0:T(8,128)}, f32[32,864]{1,0:T(8,128)}) custom-call(f32[32,896]{1,0:T(8,128)S(1)} %shard_map.79.mine_ref, f32[32,896]{1,0:T(8,128)S(1)} %collective-permute-done.14.other_ref), custom_call_target="tpu_custom_call" | custom-call | flops 1000000 | bytes 1000000 | tf_op jit(solution)/shard_map/pallas_call | solution.py:571
  (4 shorter events, 0.1 us)
Async XLA Ops:
  3.1 12.6 %collective-permute-start = (bf16[3,128,128]{2,1,0:T(8,128)(2,1)S(1)}, bf16[3,128,128]{2,1,0:T(8,128)(2,1)S(1)}, u32[]{:S(2)}, u32[]{:S(2)}) collective-permute-start(bf16[3,128,128]{2,1,0:T(8,128)(2,1)S(1)} %get-tuple-element.46), channel_id=1, source_target_pairs={{0,8},{4,12},{8,0},{12,4},{16,24},{20,28},{24,16},{28,20},{1,9},{5... | collective-permute-start | bytes 294920 | tf_op jit(solution)/shard_map/ppermute | solution.py:58
  6.2 9.6 %collective-permute-start.1 = (bf16[3,128,128]{2,1,0:T(8,128)(2,1)S(1)}, bf16[3,128,128]{2,1,0:T(8,128)(2,1)S(1)}, u32[]{:S(2)}, u32[]{:S(2)}) collective-permute-start(bf16[3,128,128]{2,1,0:T(8,128)(2,1)S(1)} %get-tuple-element.47), channel_id=1, source_target_pairs={{0,4},{4,0},{8,16},{12,20},{16,8},{20,12},{24,28},{28,24},{1,5},{5... | collective-permute-start | bytes 294920 | tf_op jit(solution)/shard_map/ppermute | solution.py:58
  7.7 8.1 %collective-permute-start.2 = (bf16[3,128,128]{2,1,0:T(8,128)(2,1)S(1)}, bf16[3,128,128]{2,1,0:T(8,128)(2,1)S(1)}, u32[]{:S(2)}, u32[]{:S(2)}) collective-permute-start(bf16[3,128,128]{2,1,0:T(8,128)(2,1)S(1)} %get-tuple-element.48), channel_id=1, source_target_pairs={{0,4},{4,0},{8,12},{12,8},{16,20},{20,16},{24,28},{28,24},{1,5},{5... | collective-permute-start | bytes 294920 | tf_op jit(solution)/shard_map/ppermute | solution.py:58
  9.1 5.2 %collective-permute-start.3 = (bf16[160,128]{1,0:T(8,128)(2,1)S(1)}, bf16[160,128]{1,0:T(8,128)(2,1)S(1)}, u32[]{:S(2)}, u32[]{:S(2)}) collective-permute-start(bf16[160,128]{1,0:T(8,128)(2,1)S(1)} %get-tuple-element.51), channel_id=1, source_target_pairs={{0,12},{4,8},{8,4},{12,0},{16,28},{20,24},{24,20},{28,16},{1,13},{... | collective-permute-start | bytes 122888 | tf_op jit(solution)/shard_map/ppermute | solution.py:58
  11.8 4.0 %collective-permute-start.4 = (bf16[160,128]{1,0:T(8,128)(2,1)S(1)}, bf16[160,128]{1,0:T(8,128)(2,1)S(1)}, u32[]{:S(2)}, u32[]{:S(2)}) collective-permute-start(bf16[160,128]{1,0:T(8,128)(2,1)S(1)} %get-tuple-element.52), channel_id=1, source_target_pairs={{0,4},{4,0},{8,20},{12,16},{16,12},{20,8},{24,28},{28,24},{1,5},{5... | collective-permute-start | bytes 122888 | tf_op jit(solution)/shard_map/ppermute | solution.py:58
  15.9 3.8 %collective-permute-start.5 = (bf16[32,256]{1,0:T(8,128)(2,1)S(1)}, bf16[32,256]{1,0:T(8,128)(2,1)S(1)}, u32[]{:S(2)}, u32[]{:S(2)}) collective-permute-start(bf16[32,256]{1,0:T(8,128)(2,1)S(1)} %get-tuple-element.62), channel_id=1, source_target_pairs={{0,2},{1,3},{2,0},{3,1},{4,6},{5,7},{6,4},{7,5},{8,10},{9,11},{10,... | collective-permute-start | bytes 49160 | tf_op jit(solution)/shard_map/ppermute | solution.py:452
  19.7 1.2 %collective-permute-start.6 = (bf16[2,32,256]{2,1,0:T(8,128)(2,1)S(1)}, bf16[2,32,256]{2,1,0:T(8,128)(2,1)S(1)}, u32[]{:S(2)}, u32[]{:S(2)}) collective-permute-start(bf16[2,32,256]{2,1,0:T(8,128)(2,1)S(1)} %shard_map.71), channel_id=1, source_target_pairs={{0,1},{1,0},{2,3},{3,2},{4,5},{5,4},{6,7},{7,6},{8,9},{9,8},{10,11... | collective-permute-start | bytes 98312 | tf_op jit(solution)/shard_map/ppermute | solution.py:452
  23.3 1.4 %collective-permute-start.7 = (f32[32,896]{1,0:T(8,128)S(1)}, f32[32,896]{1,0:T(8,128)S(1)}, u32[]{:S(2)}, u32[]{:S(2)}) collective-permute-start(f32[32,896]{1,0:T(8,128)S(1)} %shard_map.75), channel_id=1, source_target_pairs={{0,1},{1,0},{2,3},{3,2},{4,5},{5,4},{6,7},{7,6},{8,9},{9,8},{10,11... | collective-permute-start | bytes 344072 | tf_op jit(solution)/shard_map/ppermute | solution.py:452
  24.7 6.1 %collective-permute-start.10 = (bf16[32,896]{1,0:T(8,128)(2,1)S(1)}, bf16[32,896]{1,0:T(8,128)(2,1)S(1)}, u32[]{:S(2)}, u32[]{:S(2)}) collective-permute-start(bf16[32,896]{1,0:T(8,128)(2,1)S(1)} %shard_map.76.own_ref), channel_id=1, source_target_pairs={{0,24},{1,7},{2,26},{3,5},{4,28},{5,3},{6,30},{7,1},{8,16},{9,15},... | collective-permute-start | bytes 172040 | tf_op jit(solution)/shard_map/ppermute | solution.py:470
  26.0 5.4 %collective-permute-start.9 = (bf16[32,896]{1,0:T(8,128)(2,1)S(1)}, bf16[32,896]{1,0:T(8,128)(2,1)S(1)}, u32[]{:S(2)}, u32[]{:S(2)}) collective-permute-start(bf16[32,896]{1,0:T(8,128)(2,1)S(1)} %shard_map.76.own_ref), channel_id=1, source_target_pairs={{0,16},{1,5},{2,18},{3,7},{4,20},{5,1},{6,22},{7,3},{8,24},{9,13},... | collective-permute-start | bytes 172040 | tf_op jit(solution)/shard_map/ppermute | solution.py:470
  27.6 4.4 %collective-permute-start.8 = (bf16[32,896]{1,0:T(8,128)(2,1)S(1)}, bf16[32,896]{1,0:T(8,128)(2,1)S(1)}, u32[]{:S(2)}, u32[]{:S(2)}) collective-permute-start(bf16[32,896]{1,0:T(8,128)(2,1)S(1)} %shard_map.76.own_ref), channel_id=1, source_target_pairs={{0,8},{1,3},{2,10},{3,1},{4,12},{5,7},{6,14},{7,5},{8,0},{9,11},{1... | collective-permute-start | bytes 172040 | tf_op jit(solution)/shard_map/ppermute | solution.py:470
  32.0 5.1 %collective-permute-start.13 = (bf16[32,896]{1,0:T(8,128)(2,1)S(1)}, bf16[32,896]{1,0:T(8,128)(2,1)S(1)}, u32[]{:S(2)}, u32[]{:S(2)}) collective-permute-start(bf16[32,896]{1,0:T(8,128)(2,1)S(1)} %shard_map.78.own_ref), channel_id=1, source_target_pairs={{0,6},{1,25},{2,4},{3,27},{4,2},{5,29},{6,0},{7,31},{8,14},{9,17},... | collective-permute-start | bytes 172040 | tf_op jit(solution)/shard_map/ppermute | solution.py:470
  34.6 4.2 %collective-permute-start.12 = (bf16[32,896]{1,0:T(8,128)(2,1)S(1)}, bf16[32,896]{1,0:T(8,128)(2,1)S(1)}, u32[]{:S(2)}, u32[]{:S(2)}) collective-permute-start(bf16[32,896]{1,0:T(8,128)(2,1)S(1)} %shard_map.78.own_ref), channel_id=1, source_target_pairs={{0,4},{1,17},{2,6},{3,19},{4,0},{5,21},{6,2},{7,23},{8,12},{9,25},... | collective-permute-start | bytes 172040 | tf_op jit(solution)/shard_map/ppermute | solution.py:470
  35.1 4.2 %collective-permute-start.11 = (bf16[32,896]{1,0:T(8,128)(2,1)S(1)}, bf16[32,896]{1,0:T(8,128)(2,1)S(1)}, u32[]{:S(2)}, u32[]{:S(2)}) collective-permute-start(bf16[32,896]{1,0:T(8,128)(2,1)S(1)} %shard_map.78.own_ref), channel_id=1, source_target_pairs={{0,2},{1,9},{2,0},{3,11},{4,6},{5,13},{6,4},{7,15},{8,10},{9,1},{1... | collective-permute-start | bytes 172040 | tf_op jit(solution)/shard_map/ppermute | solution.py:470
  39.3 1.4 %collective-permute-start.14 = (f32[32,896]{1,0:T(8,128)S(1)}, f32[32,896]{1,0:T(8,128)S(1)}, u32[]{:S(2)}, u32[]{:S(2)}) collective-permute-start(f32[32,896]{1,0:T(8,128)S(1)} %shard_map.79.mine_ref), channel_id=1, source_target_pairs={{0,1},{1,0},{2,3},{3,2},{4,5},{5,4},{6,7},{7,6},{8,9},{9,8},{10,11... | collective-permute-start | bytes 344072 | tf_op jit(solution)/shard_map/ppermute | solution.py:452

commit v3 on v2

--- a/solution.py
+++ b/solution.py
@@ -37,25 +37,43 @@
     return other if 0 <= other < size else None
 
 
+AXES = ("gx", "gy", "gz")
+
+
+def all_places():
+    sizes = [lax.axis_size(axis) for axis in AXES]
+    return [(i, j, k) for i in range(sizes[0]) for j in range(sizes[1]) for k in range(sizes[2])]
+
+
+def permute(x, target):
+    sizes = [lax.axis_size(axis) for axis in AXES]
+    number = lambda place: (place[0] * sizes[1] + place[1]) * sizes[2] + place[2]
+    return lax.ppermute(x, AXES, [(number(place), number(to)) for place, to in target.items()])
+
+
 def swap(x, moves):
-    axes = ("gx", "gy")
-    sizes = [lax.axis_size(axis) for axis in axes]
+    sizes = [lax.axis_size(axis) for axis in AXES]
     side = dict(moves)
-    places = [(i, j) for i in range(sizes[0]) for j in range(sizes[1])]
+    places = all_places()
     target = {}
     for place in places:
-        to = [partner(i, side[axis], size) if axis in side else i for i, axis, size in zip(place, axes, sizes)]
+        to = [partner(i, side[axis], size) if axis in side else i for i, axis, size in zip(place, AXES, sizes)]
         if None not in to:
             target[place] = tuple(to)
     if not target:
         return None
     alone = [place for place in places if place not in target]
-    for fill in (lambda i, j: (i, j ^ 1), lambda i, j: (i ^ 1, j), lambda i, j: (i, j)):
+    fills = (
+        lambda i, j, k: (i, j, k ^ 2),
+        lambda i, j, k: (i, j ^ 1, k),
+        lambda i, j, k: (i ^ 1, j, k),
+        lambda i, j, k: (i, j, k),
+    )
+    for fill in fills:
         if all(fill(*place) in alone for place in alone):
             target.update({place: fill(*place) for place in alone})
             break
-    number = lambda place: place[0] * sizes[1] + place[1]
-    return lax.ppermute(x, axes, [(number(place), number(target[place])) for place in places])
+    return permute(x, target)
 
 
 def choose(flag, a, b):
@@ -66,35 +84,46 @@
     return jnp.where(flag, a, b)
 
 
-def pack_faces(y_sides, in_ref, noise_ref, field_ref, wide_noise_ref, *faces):
-    size_x = in_ref.shape[0]
-    lanes = in_ref.shape[1]
+def pack_faces(y_sides, raw_ref, noise_rows_ref, field_ref, wide_noise_ref, *face_y):
+    size_x, size_z = raw_ref.shape[2], raw_ref.shape[4]
+    lanes = raw_ref.shape[1] * raw_ref.shape[3]
     for x in range(size_x):
-        field_ref[x] = in_ref[x].T
-        wide_noise_ref[x] = noise_ref[x].T
+        for a, ref in enumerate((field_ref, wide_noise_ref)):
+            rows = jnp.transpose(raw_ref[a, :, x].astype(F32), (1, 0, 2)).reshape(lanes, size_z).astype(BF16)
+            if a:
+                noise_rows_ref[x] = rows
+            ref[x] = rows.T
+    even_y = even_index("gy")
+    for k in range(y_sides):
+        two, one = cut_y(even_y if k == 0 else jnp.logical_not(even_y))
+        for j in range(0, size_x, 2):
+            face_y[k][j // 2] = jnp.concatenate([two(field_ref[j]), two(field_ref[j + 1])], axis=1)
+        for j in range(0, size_x, 4):
+            face_y[k][size_x // 2 + j // 4] = jnp.concatenate([one(wide_noise_ref[j + i]) for i in range(4)], axis=1)
+
+
+def cut_y(high):
+    two = lambda p: jnp.where(high, p[:, p.shape[1] - 2 * C :], p[:, : 2 * C])
+    one = lambda p: jnp.where(high, p[:, p.shape[1] - C :], p[:, :C])
+    return two, one
+
+
+def pack_corners(y_sides, field_ref, wide_noise_ref, token_ref, *faces):
+    token_ref[...] = jnp.zeros_like(token_ref)
     even_x, even_y = even_index("gx"), even_index("gy")
-    face_x = faces[:2]
-    face_y = faces[2 : 2 + y_sides]
-    corner = faces[2 + y_sides :]
-
+    size_x = field_ref.shape[0]
+    face_x, corners = faces[:2], faces[2:]
     for side in range(2):
         high = even_x if side == 0 else jnp.logical_not(even_x)
         face_x[side][0] = jnp.where(high, field_ref[size_x - 2], field_ref[0])
         face_x[side][1] = jnp.where(high, field_ref[size_x - 1], field_ref[1])
         face_x[side][2] = jnp.where(high, wide_noise_ref[size_x - 1], wide_noise_ref[0])
-
     for k in range(y_sides):
-        high = even_y if k == 0 else jnp.logical_not(even_y)
-        two = lambda p: jnp.where(high, p[:, lanes - 2 * C :], p[:, : 2 * C])
-        one = lambda p: jnp.where(high, p[:, lanes - C :], p[:, :C])
-        for j in range(0, size_x, 2):
-            face_y[k][j // 2] = jnp.concatenate([two(field_ref[j]), two(field_ref[j + 1])], axis=1)
-        for j in range(0, size_x, 4):
-            face_y[k][size_x // 2 + j // 4] = jnp.concatenate([one(wide_noise_ref[j + i]) for i in range(4)], axis=1)
-        for side in range(2):
-            ref = corner[2 * k + side]
-            ref[:128] = jnp.concatenate([two(face_x[side][0]), two(face_x[side][1])], axis=1)
-            strip = one(face_x[side][2])
+        two, one = cut_y(even_y if k == 0 else jnp.logical_not(even_y))
+        for side, face in enumerate(face_x):
+            ref = corners[2 * k + side]
+            ref[:128] = jnp.concatenate([two(face[0]), two(face[1])], axis=1)
+            strip = one(face[2])
             ref[128:] = jnp.concatenate([strip[i * 32 : (i + 1) * 32] for i in range(4)], axis=1)
 
 
@@ -180,7 +209,7 @@
 
 
 def pack_z(y_sides, *refs):
-    pieces, (low_out, high_out, middle_out) = take_pieces(y_sides, refs)
+    pieces, (low_out, high_out, face_a, face_b) = take_pieces(y_sides, refs)
     n_field, n_noise, size_z = pieces.size_x + 4, pieces.size_x + 2, pieces.size_z
 
     def gather(tile, first, noise_row):
@@ -196,15 +225,14 @@
     high = gather(size_z - 16, size_z - 2, size_z - 1)
     low_out[...] = low
     high_out[...] = high
-    middle_out[...] = jnp.where(lax.axis_index("gz") == 1, high, low)
-
-
-def pack_pair(low_ref, high_ref, passed_ref, out_ref):
-    out_ref[0] = jnp.where(even_index("gz"), high_ref[...], low_ref[...])
-    out_ref[1] = passed_ref[...]
+    even = even_index("gz")
+    face_a[...] = jnp.where(even, high, low)
+    face_b[...] = jnp.where(even, low, high)
 
 
 def stack(ref, dz, first, count):
+    if isinstance(ref, Edged):
+        return ref.stack(dz, first, count)
     return ref[dz, first : first + count].reshape(count * ref.shape[2], 256)
 
 
@@ -239,7 +267,7 @@
         ref[row : row + C, half * 128 : (half + 1) * 128] = value.astype(BF16)
 
 
-def spread_weights(both_ref, a1_ref, ab_ref, second_out):
+def spread_weights(both_ref, _, a1_ref, ab_ref, second_out):
     def columns(rows):
         wide = both_ref[rows].astype(F32)
         return jnp.concatenate([wide, jnp.zeros((C, 896 - wide.shape[1]), F32)], axis=1)
@@ -285,25 +313,37 @@
     return value * s, s
 
 
-def patch(ref, dz, x, row, last):
+def edge_tile(ref, dz, x, row):
     rows = ref.shape[2]
-    at = slice(rows - 16, rows) if last else slice(0, 16)
+    at = slice(rows - 16, rows) if dz else slice(0, 16)
     tile = ref[dz, x, at, :].astype(F32)
     index = lax.broadcasted_iota(jnp.int32, tile.shape, 0)
-    ref[dz, x, at, :] = jnp.where(index == (15 if last else 0), row, tile).astype(BF16)
+    return jnp.where(index == (15 if dz else 0), row, tile).astype(BF16)
+
+
+class Edged:
+    def __init__(self, ref, edge_ref):
+        self.ref, self.edge_ref = ref, edge_ref
+
+    def stack(self, dz, first, count):
+        parts = []
+        for x in range(first, first + count):
+            if dz == 0:
+                parts += [self.edge_ref[0, x], self.ref[0, x, 16:]]
+            elif dz == 1:
+                parts += [self.ref[1, x]]
+            else:
+                parts += [self.ref[2, x, : self.ref.shape[2] - 16], self.edge_ref[1, x]]
+        return jnp.concatenate(parts, axis=0)
 
 
 def activate(
-    pre_ref, wide_field_ref, wide_noise_ref, low_ref, high_ref, a1_ref, recv_ref, hid_ref, slope_ref, xs_ref, ns_ref
+    pre_ref, wide_field_ref, wide_noise_ref, low_ref, high_ref, a1_ref, side_0, side_1, hid_ref, slope_ref, xs_edge, ns_edge
 ):
-    n_field, size_z = xs_ref.shape[1], xs_ref.shape[2]
-    n_noise = ns_ref.shape[1]
+    n_field, size_z = wide_field_ref.shape[1], wide_field_ref.shape[2]
+    n_noise = wide_noise_ref.shape[1]
     size_x = n_noise - 2
     even = even_index("gz")
-    near, far = recv_ref[0].astype(F32), recv_ref[1].astype(F32)
-    index = lax.axis_index("gz")
-    below_rows = jnp.where(even, jnp.where(index == 2, far, 0.0), near)
-    above_rows = jnp.where(even, near, jnp.where(index == 1, far, 0.0))
     own_low = low_ref[...].astype(F32)
     own_high = high_ref[...].astype(F32)
 
@@ -311,6 +351,9 @@
     first_x, last_x = gx == 0, gx == lax.axis_size("gx") - 1
     first_y, last_y = gy == 0, gy == lax.axis_size("gy") - 1
     first_z, last_z = gz == 0, gz == lax.axis_size("gz") - 1
+
+    below_rows = jnp.where(first_z, 0.0, jnp.where(even, side_1[...], side_0[...]).astype(F32))
+    above_rows = jnp.where(last_z, 0.0, jnp.where(even, side_0[...], side_1[...]).astype(F32))
 
     before = jnp.concatenate([below_rows[:n_field], own_high[n_field : 2 * n_field]], axis=0).astype(BF16)
     halo = jnp.concatenate([below_rows[n_field : 2 * n_field], above_rows[:n_field]], axis=0).astype(BF16)
@@ -357,20 +400,18 @@
         if 1 <= x <= size_x:
             slope_ref[x - 1] = s * (1.0 + value * (1.0 - s))
 
-    xs_ref[...] = wide_field_ref[...]
-    ns_ref[...] = wide_noise_ref[...]
     for x in range(n_field):
-        patch(xs_ref, 0, x, below_rows[n_field + x : n_field + x + 1], False)
-        patch(xs_ref, 2, x, above_rows[x : x + 1], True)
+        xs_edge[0, x] = edge_tile(wide_field_ref, 0, x, below_rows[n_field + x : n_field + x + 1])
+        xs_edge[1, x] = edge_tile(wide_field_ref, 2, x, above_rows[x : x + 1])
     base = 2 * n_field
     for x in range(n_noise):
-        patch(ns_ref, 0, x, below_rows[base + x : base + x + 1], False)
-        patch(ns_ref, 2, x, above_rows[base + x : base + x + 1], True)
-
-
-def backward(ns_ref, slope_ref, ab_ref, out_ref, acc_ref):
+        ns_edge[0, x] = edge_tile(wide_noise_ref, 0, x, below_rows[base + x : base + x + 1])
+        ns_edge[1, x] = edge_tile(wide_noise_ref, 2, x, above_rows[base + x : base + x + 1])
+
+
+def backward(ns_ref, ns_edge, slope_ref, ab_ref, out_ref, acc_ref):
     size_x, size_z = slope_ref.shape[:2]
-    total = jnp.dot(taps(ns_ref, size_x), ab_ref[...], preferred_element_type=F32)
+    total = jnp.dot(taps(Edged(ns_ref, ns_edge), size_x), ab_ref[...], preferred_element_type=F32)
     acc_ref[...] = total.reshape(size_x, size_z, 256)
     for x in range(size_x):
         value = (acc_ref[x] * slope_ref[x]).astype(BF16)
@@ -400,7 +441,7 @@
     return jnp.concatenate(tiles, axis=1)
 
 
-def weight_grad(give, xs_ref, hid_ref, pre_grad_ref, rows_ref, out_ref):
+def weight_grad(give, xs_ref, xs_edge, hid_ref, pre_grad_ref, rows_ref, out_ref):
     size_x = rows_ref.shape[0]
     even = even_index("gz")
 
@@ -411,7 +452,7 @@
 
     @pl.when(jnp.logical_not(even) if give else even)
     def _():
-        out_ref[...] = collect(pre_grad_ref[...], xs_ref, size_x, 1, 1)
+        out_ref[...] = collect(pre_grad_ref[...], Edged(xs_ref, xs_edge), size_x, 1, 1)
 
 
 def predict(hid_ref, second_ref, out_ref, acc_ref, a2_ref):
@@ -452,22 +493,14 @@
     return lax.ppermute(x, axis, [(i, i ^ bit) for i in range(size)])
 
 
-AXES = ("gx", "gy", "gz")
-
-
 def masked_swap(x, flip_even, flip_odd):
-    sizes = [lax.axis_size(axis) for axis in AXES]
-    pairs = []
-    for gx in range(sizes[0]):
-        for gy in range(sizes[1]):
-            for gz in range(sizes[2]):
-                at = [gx, gy, gz]
-                to = list(at)
-                for axis, bit in flip_odd if gz % 2 else flip_even:
-                    to[AXES.index(axis)] ^= bit
-                source, target = [(p[0] * sizes[1] + p[1]) * sizes[2] + p[2] for p in (at, to)]
-                pairs.append((source, target))
-    return lax.ppermute(x, AXES, pairs)
+    target = {}
+    for place in all_places():
+        to = list(place)
+        for axis, bit in flip_odd if place[2] % 2 else flip_even:
+            to[AXES.index(axis)] ^= bit
+        target[place] = tuple(to)
+    return permute(x, target)
 
 
 def local(inputs, noise, w_first, w_second):
@@ -477,65 +510,70 @@
     norm = 1.0 / math.sqrt(cells * devices)
     lanes = size_y * channels
 
-    def rows(x):
-        return x[0].transpose(1, 2, 0, 3).reshape(size_x, lanes, size_z)
-
-    in_rows, noise_rows = rows(inputs), rows(noise)
     plane = (size_z, lanes)
     y_sides = 2 if lax.axis_size("gy") > 2 else 1
     y_planes = size_x // 2 + size_x // 4
-    field, wide_noise, *faces = call(
+    noise_rows, field, wide_noise, *face_y = call(
         functools.partial(pack_faces, y_sides),
-        [struct((size_x,) + plane, BF16)] * 2
+        [struct((size_x, lanes, size_z), BF16)]
+        + [struct((size_x,) + plane, BF16)] * 2
+        + [struct((y_planes,) + plane, BF16)] * y_sides,
+    )(jnp.concatenate([inputs, noise], axis=0))
+    token, *faces = call(
+        functools.partial(pack_corners, y_sides),
+        [struct((8, 128), F32)]
         + [struct((3,) + plane, BF16)] * 2
-        + [struct((y_planes,) + plane, BF16)] * y_sides
         + [struct((160, 128), BF16)] * (2 * y_sides),
-    )(in_rows, noise_rows)
+    )(field, wide_noise)
+    faces[2:2] = face_y
     moves = [[("gx", side)] for side in range(2)]
     moves += [[("gy", side)] for side in range(y_sides)]
     moves += [[("gx", side), ("gy", k)] for k in range(y_sides) for side in range(2)]
-    both = jnp.concatenate([w_first, w_second], axis=0)
-    near = 2 + y_sides
-    *faces[near:], both = lax.optimization_barrier((*faces[near:], both))
     got = [swap(face, move) for face, move in zip(faces, moves)]
 
     a1, ab, second = call(
         spread_weights,
         [struct((9 * 256, 256), BF16), struct((9 * 256, 256), BF16), struct((9, C, 128), F32)],
         moved=4_000_000,
-    )(both)
-    *got, a1, ab, second = lax.optimization_barrier((*got, a1, ab, second))
+    )(jnp.concatenate([w_first, w_second], axis=0), token)
+    order = [1, 0] + list(range(2, 2 + y_sides)) + list(range(2 + y_sides, len(moves)))[::-1]
+    *sent, a1, ab, second = lax.optimization_barrier((*[got[k] for k in order], a1, ab, second))
+    got = [sent[order.index(k)] for k in range(len(moves))]
 
     n_field, n_noise = size_x + 4, size_x + 2
     z_rows = -(-(2 * n_field + n_noise) // 16) * 16
-    low, high, middle = call(
-        functools.partial(pack_z, y_sides), [struct((z_rows, 256), BF16)] * 3
+    low, high, face_a, face_b = call(
+        functools.partial(pack_z, y_sides), [struct((z_rows, 256), BF16)] * 4
     )(field, wide_noise, *got)
-    passed = flip(middle, "gz", 2)
+    z_got = [swap(face, [("gz", side)]) for side, face in enumerate((face_a, face_b))]
     pre_shape = (n_noise, size_z, 256)
     xs, ns, pre = call(
         functools.partial(widen, y_sides),
         [struct((3, n_field, size_z, 256), BF16), struct((3,) + pre_shape, BF16), struct(pre_shape, F32)],
         flops=1_000_000_000,
     )(field, wide_noise, *got, a1)
-    passed, xs, ns, pre = lax.optimization_barrier((passed, xs, ns, pre))
-    z_got = flip(call(pack_pair, struct((2, z_rows, 256), BF16))(low, high, passed), "gz", 1)
+    *z_got, xs, ns, pre = lax.optimization_barrier((*z_got, xs, ns, pre))
 
     slope_shape = (size_x, size_z, 256)
-    hidden, slope, xs, ns = call(
+    hidden, slope, xs_edge, ns_edge = call(
         activate,
-        [struct((3,) + pre_shape, BF16), struct(slope_shape, F32), struct(xs.shape, BF16), struct(ns.shape, BF16)],
-    )(pre, xs, ns, low, high, a1, z_got)
+        [
+            struct((3,) + pre_shape, BF16),
+            struct(slope_shape, F32),
+            struct((2, n_field, 16, 256), BF16),
+            struct((2, n_noise, 16, 256), BF16),
+        ],
+    )(pre, xs, ns, low, high, a1, *z_got)
     pre_grad = call(
         backward,
         struct((lanes, size_x * size_z), BF16),
         scratch=[pltpu.VMEM(slope_shape, F32)],
         flops=1_000_000_000,
-    )(ns, slope, ab)
+    )(ns, ns_edge, slope, ab)
 
     half = struct((C, 896), F32)
     rounded = struct((C, 896), BF16)
-    parts = (xs, hidden, pre_grad, noise_rows)
+    parts = (xs, xs_edge, hidden, pre_grad, noise_rows)
     give = call(functools.partial(weight_grad, True), half, flops=1_000_000_000)(*parts)
     taken = flip(give, "gz", 1)
     keep = call(functools.partial(weight_grad, False), half, flops=1_000_000_000)(*parts)

time: 41.6 us -> 38.8 us (0.933)
  local copies, waits for them, and re-layouts: 2.61 us -> 0.72 us
  other arithmetic: 0.86 us -> 2.02 us
  waiting for transfers between devices: 10.4 us -> 9.27 us
  starting transfers between devices: 19.1 us -> 18.2 us
    ppermute x4 -> x2, waiting for transfers between devices: 4.08 us -> 1.89 us  [flip(): return lax.ppermute(x, axis, [(i, i ^ bit) for i in range(size)])]
    transpose x2 -> x0, local copies, waits for them, and re-layouts: 1.88 us -> none  [rows(): return x[0].transpose(1, 2, 0, 3).reshape(size_x, lanes, size_z)]
    ppermute x4 -> x2, starting transfers between devices: 1.86 us -> 0.24 us  [flip(): return lax.ppermute(x, axis, [(i, i ^ bit) for i in range(size)])]
    concatenate x1 -> x2, other arithmetic: 0.86 us -> 2.02 us  [the longest x1 1.16 us: local(): jnp.concatenate([inputs, noise], axis=0)]
    ppermute x11 -> x13, waiting for transfers between devices: 6.29 us -> 7.38 us  [permute(): lax.ppermute(x, AXES, [(number(place), number(to)) for place, to in targe...]
    ppermute x11 -> x13, starting transfers between devices: 17.3 us -> 18 us  [permute(): lax.ppermute(x, AXES, [(number(place), number(to)) for place, to in targe...]
  transfers between devices with their start and end apart: 15 -> 15, of which waited for: 10 -> 8; matrix products, arithmetic and copies ran while one was open for 4% -> 4% of each run, Pallas kernels for 9% -> 10%
where the time goes in v3:
time: 38.8 us; the launch traced here: 38.7 us
  starting transfers between devices  18.2 us (47%)
  waiting for transfers between devices  9.27 us (24%)
  Pallas kernels  7.67 us (20%)
  other arithmetic  2.02 us (5%)
  between operations  0.77 us (2%)
  local copies, waits for them, and re-layouts  0.72 us (2%)
    ppermute x13, starting transfers between devices, permute(): lax.ppermute(x, AXES, [(number(place), number(to)) for place, to in targe...  18 us
    ppermute x13, waiting for transfers between devices, permute(): lax.ppermute(x, AXES, [(number(place), number(to)) for place, to in targe...  7.38 us
    ppermute x2, waiting for transfers between devices, flip(): return lax.ppermute(x, axis, [(i, i ^ bit) for i in range(size)])  1.89 us
    pallas_call x1, Pallas kernels, local(): call(functools.partial(widen, y_sides), [struct((3, n_field, size_z, 256)...  1.19 us
    concatenate x1, other arithmetic, local(): jnp.concatenate([inputs, noise], axis=0)  1.16 us
    pallas_call x1, Pallas kernels, local(): call(spread_weights, [struct((9 * 256, 256), BF16), struct((9 * 256, 256)...  1.05 us
    pallas_call x1, Pallas kernels, local(): call(predict, struct((size_x, lanes, size_z), BF16), scratch=[pltpu.VMEM(...  0.93 us
    concatenate x1, other arithmetic, local(): jnp.concatenate([w_first, w_second], axis=0)  0.86 us
  transfers between devices with their start and end apart: 15, of which 8 were waited for; matrix products, arithmetic and copies ran while one was open for 4% of the time, Pallas kernels for 10%

profile of v3, /device:TPU:0, one launch (start us, length us, event | category | flops | bytes accessed | tf_op | source)
XLA Modules:
  0.0 38.7 jit_solution(17056505023271939229)
XLA Ops:
  0.6 1.2 %pad_maximum_fusion.raw_ref = bf16[2,32,4,4,128]{4,3,2,1,0:T(4,128)(2,1)S(1)} fusion(bf16[1,32,4,4,128]{4,3,2,1,0:T(4,128)(2,1)} %param.5, bf16[1,32,4,4,128]{4,3,2,1,0:T(4,128)(2,1)} %param.4), kind=kLoop, calls=%fused_computation | loop fusion | flops 131072 | bytes 524288 | tf_op jit(solution)/shard_map/concatenate | solution.py:521
  1.8 0.5 %shard_map.67 = (bf16[4,128,128]{2,1,0:T(8,128)(2,1)S(1)}, bf16[4,128,128]{2,1,0:T(8,128)(2,1)S(1)}, bf16[4,128,128]{2,1,0:T(8,128)(2,1)S(1)}, bf16[3,128,128]{2,1,0:T(8,128)(2,1)S(1)}) custom-call(bf16[2,32,4,4,128]{4,3,2,1,0:T(4,128)(2,1)S(1)} %pad_maximum_fusion.raw_ref), custom_call_target="tpu_custom_call" | custom-call | flops 1000000 | bytes 1000000 | tf_op jit(solution)/shard_map/pallas_call | solution.py:516
  2.3 3.0 %collective-permute-start.2 = (bf16[3,128,128]{2,1,0:T(8,128)(2,1)S(1)}, bf16[3,128,128]{2,1,0:T(8,128)(2,1)S(1)}, u32[]{:S(2)}, u32[]{:S(2)}) collective-permute-start(bf16[3,128,128]{2,1,0:T(8,128)(2,1)S(1)} %get-tuple-element.49), channel_id=1, source_target_pairs={{0,4},{1,5},{2,6},{3,7},{4,0},{5,1},{6,2},{7,3},{8,12},{9,13},{10,... | collective-permute-start | bytes 294920 | tf_op jit(solution)/shard_map/ppermute | solution.py:51
  5.3 0.2 shard_map.68
  5.5 1.6 %collective-permute-start.3 = (bf16[160,128]{1,0:T(8,128)(2,1)S(1)}, bf16[160,128]{1,0:T(8,128)(2,1)S(1)}, u32[]{:S(2)}, u32[]{:S(2)}) collective-permute-start(bf16[160,128]{1,0:T(8,128)(2,1)S(1)} %get-tuple-element.50), channel_id=1, source_target_pairs={{8,20},{9,21},{10,22},{11,23},{12,16},{13,17},{14,18},{15,19},{16,... | collective-permute-start | bytes 122888 | tf_op jit(solution)/shard_map/ppermute | solution.py:51
  7.1 2.5 %collective-permute-start.4 = (bf16[160,128]{1,0:T(8,128)(2,1)S(1)}, bf16[160,128]{1,0:T(8,128)(2,1)S(1)}, u32[]{:S(2)}, u32[]{:S(2)}) collective-permute-start(bf16[160,128]{1,0:T(8,128)(2,1)S(1)} %get-tuple-element.51), channel_id=1, source_target_pairs={{0,12},{1,13},{2,14},{3,15},{4,8},{5,9},{6,10},{7,11},{8,4},{9,5},... | collective-permute-start | bytes 122888 | tf_op jit(solution)/shard_map/ppermute | solution.py:51
  9.6 1.5 %collective-permute-start = (bf16[3,128,128]{2,1,0:T(8,128)(2,1)S(1)}, bf16[3,128,128]{2,1,0:T(8,128)(2,1)S(1)}, u32[]{:S(2)}, u32[]{:S(2)}) collective-permute-start(bf16[3,128,128]{2,1,0:T(8,128)(2,1)S(1)} %get-tuple-element.47), channel_id=1, source_target_pairs={{8,16},{9,17},{10,18},{11,19},{12,20},{13,21},{14,22},{15,23},{16,... | collective-permute-start | bytes 294920 | tf_op jit(solution)/shard_map/ppermute | solution.py:51
  11.2 0.6 %collective-permute-start.1 = (bf16[3,128,128]{2,1,0:T(8,128)(2,1)S(1)}, bf16[3,128,128]{2,1,0:T(8,128)(2,1)S(1)}, u32[]{:S(2)}, u32[]{:S(2)}) collective-permute-start(bf16[3,128,128]{2,1,0:T(8,128)(2,1)S(1)} %get-tuple-element.48), channel_id=1, source_target_pairs={{0,8},{1,9},{2,10},{3,11},{4,12},{5,13},{6,14},{7,15},{8,0},{9,1},... | collective-permute-start | bytes 294920 | tf_op jit(solution)/shard_map/ppermute | solution.py:51
  11.8 0.9 %pad_maximum_fusion.1.both_ref = bf16[64,864]{1,0:T(8,128)(2,1)S(1)} fusion(bf16[32,864]{1,0:T(8,128)(2,1)} %param.7, bf16[32,864]{1,0:T(8,128)(2,1)} %param.6), kind=kLoop, calls=%fused_computation.2 | loop fusion | flops 221184 | bytes 221184 | tf_op jit(solution)/shard_map/concatenate | solution.py:538
  12.7 1.0 %shard_map.69 = (bf16[2304,256]{1,0:T(8,128)(2,1)S(1)}, bf16[2304,256]{1,0:T(8,128)(2,1)S(1)}, f32[9,32,128]{2,1,0:T(8,128)S(1)}) custom-call(bf16[64,864]{1,0:T(8,128)(2,1)S(1)} %pad_maximum_fusion.1.both_ref, f32[8,128]{1,0:T(8,128)S(1)} %get-tuple-element.52._), custom_call_target="tpu_custom_call" | custom-call | flops 1000000 | bytes 4000000 | tf_op jit(solution)/shard_map/pallas_call | solution.py:534
  13.7 0.0 collective-permute-done.3.refs_6_
  13.7 0.0 collective-permute-done.4.refs_5_
  13.7 0.0 collective-permute-done.2.refs_4_
  13.8 0.5 %collective-permute-done.refs_3_ = bf16[3,128,128]{2,1,0:T(8,128)(2,1)S(1)} collective-permute-done((bf16[3,128,128]{2,1,0:T(8,128)(2,1)S(1)}, bf16[3,128,128]{2,1,0:T(8,128)(2,1)S(1)}, u32[]{:S(2)}, u32[]{:S(2)}) %collective-permute-start) | collective-permute-done | bytes 98336 | tf_op jit(solution)/shard_map/ppermute | solution.py:51
  14.3 1.5 %collective-permute-done.1.refs_2_ = bf16[3,128,128]{2,1,0:T(8,128)(2,1)S(1)} collective-permute-done((bf16[3,128,128]{2,1,0:T(8,128)(2,1)S(1)}, bf16[3,128,128]{2,1,0:T(8,128)(2,1)S(1)}, u32[]{:S(2)}, u32[]{:S(2)}) %collective-permute-start.1) | collective-permute-done | bytes 98336 | tf_op jit(solution)/shard_map/ppermute | solution.py:51
  15.8 0.2 shard_map.70
  15.9 0.1 collective-permute-start.5
  16.0 0.6 %collective-permute-start.6 = (bf16[32,256]{1,0:T(8,128)(2,1)S(1)}, bf16[32,256]{1,0:T(8,128)(2,1)S(1)}, u32[]{:S(2)}, u32[]{:S(2)}) collective-permute-start(bf16[32,256]{1,0:T(8,128)(2,1)S(1)} %get-tuple-element.62), channel_id=1, source_target_pairs={{1,2},{2,1},{5,6},{6,5},{9,10},{10,9},{13,14},{14,13},{17,18},{18,... | collective-permute-start | bytes 49160 | tf_op jit(solution)/shard_map/ppermute | solution.py:51
  16.6 1.2 %shard_map.71 = (bf16[3,8,128,256]{3,2,1,0:T(8,128)(2,1)S(1)}, bf16[3,6,128,256]{3,2,1,0:T(8,128)(2,1)S(1)}, f32[6,128,256]{2,1,0:T(8,128)S(1)}) custom-call(bf16[4,128,128]{2,1,0:T(8,128)(2,1)S(1)} %get-tuple-element.45.field_ref.refs_0_, bf16[4,128,128]{2,1,0:T(8,128)(2,1)S(1)} %get-tuple-element.46.wide_noise_ref.refs_1_, ...), custom_call_target="tpu_custom_call" | custom-call | flops 1000000000 | bytes 1000000 | tf_op jit(solution)/shard_map/pallas_call | solution.py:550
  17.8 0.0 collective-permute-done.5.side_0
  17.8 2.0 %collective-permute-done.6.side_1 = bf16[32,256]{1,0:T(8,128)(2,1)S(1)} collective-permute-done((bf16[32,256]{1,0:T(8,128)(2,1)S(1)}, bf16[32,256]{1,0:T(8,128)(2,1)S(1)}, u32[]{:S(2)}, u32[]{:S(2)}) %collective-permute-start.6) | collective-permute-done | bytes 16416 | tf_op jit(solution)/shard_map/ppermute | solution.py:51
  19.8 0.7 %shard_map.72 = (bf16[3,6,128,256]{3,2,1,0:T(8,128)(2,1)S(1)}, f32[4,128,256]{2,1,0:T(8,128)S(1)}, bf16[2,8,16,256]{3,2,1,0:T(8,128)(2,1)S(1)}, bf16[2,6,16,256]{3,2,1,0:T(8,128)(2,1)S(1)}) custom-call(f32[6,128,256]{2,1,0:T(8,128)S(1)} %get-tuple-element.68.pre_ref, bf16[3,8,128,256]{3,2,1,0:T(8,128)(2,1)S(1)} %get-tuple-element.67.wide_field_ref.xs_ref, ...), custom_call_target="tpu_custom_call" | custom-call | flops 1000000 | bytes 1000000 | tf_op jit(solution)/shard_map/pallas_call | solution.py:558
  20.5 0.8 %shard_map.73.pre_grad_ref = bf16[128,512]{1,0:T(8,128)(2,1)S(1)} custom-call(bf16[3,6,128,256]{3,2,1,0:T(8,128)(2,1)S(1)} %get-tuple-element.69.wide_noise_ref.ns_ref, bf16[2,6,16,256]{3,2,1,0:T(8,128)(2,1)S(1)} %get-tuple-element.76.ns_edge, f32[4,128,256]{2,1,0:T(8,128)S(1)} %get-tuple-element.77.slope_ref, bf16[2304,256]{1,0:T(8,128)(2,1)S(1)} %get-tuple-element.78.ab_ref), custom_call_target="tpu_custom_call" | custom-call | flops 1000000000 | bytes 1000000 | tf_op jit(solution)/shard_map/pallas_call | solution.py:567
  21.4 0.7 %shard_map.75 = f32[32,896]{1,0:T(8,128)S(1)} custom-call(bf16[3,8,128,256]{3,2,1,0:T(8,128)(2,1)S(1)} %get-tuple-element.67.wide_field_ref.xs_ref, bf16[2,8,16,256]{3,2,1,0:T(8,128)(2,1)S(1)} %get-tuple-element.74.xs_edge, bf16[3,6,128,256]{3,2,1,0:T(8,128)(2,1)S(1)} %get-tuple-element.75.hid_ref, bf16[128,512]{1,0:T(8,128)(2,1)S(1)} %shard_map.73.pre_grad_ref, ...), custom_call_target="tpu_custom_call" | custom-call | flops 1000000000 | bytes 1000000 | tf_op jit(solution)/shard_map/pallas_call | solution.py:577
  22.1 0.2 collective-permute-start.7
  22.2 0.6 %shard_map.74.keep_ref = f32[32,896]{1,0:T(8,128)S(1)} custom-call(bf16[3,8,128,256]{3,2,1,0:T(8,128)(2,1)S(1)} %get-tuple-element.67.wide_field_ref.xs_ref, bf16[2,8,16,256]{3,2,1,0:T(8,128)(2,1)S(1)} %get-tuple-element.74.xs_edge, bf16[3,6,128,256]{3,2,1,0:T(8,128)(2,1)S(1)} %get-tuple-element.75.hid_ref, bf16[128,512]{1,0:T(8,128)(2,1)S(1)} %shard_map.73.pre_grad_ref, ...), custom_call_target="tpu_custom_call" | custom-call | flops 1000000000 | bytes 1000000 | tf_op jit(solution)/shard_map/pallas_call | solution.py:579
  22.9 0.6 %collective-permute-done.7.taken_ref = f32[32,896]{1,0:T(8,128)S(1)} collective-permute-done((f32[32,896]{1,0:T(8,128)S(1)}, f32[32,896]{1,0:T(8,128)S(1)}, u32[]{:S(2)}, u32[]{:S(2)}) %collective-permute-start.7) | collective-permute-done | bytes 114720 | tf_op jit(solution)/shard_map/ppermute | solution.py:493
  23.5 1.4 %collective-permute-start.10 = (bf16[32,896]{1,0:T(8,128)(2,1)S(1)}, bf16[32,896]{1,0:T(8,128)(2,1)S(1)}, u32[]{:S(2)}, u32[]{:S(2)}) collective-permute-start(bf16[32,896]{1,0:T(8,128)(2,1)S(1)} %shard_map.76.own_ref), channel_id=1, source_target_pairs={{0,24},{1,7},{2,26},{3,5},{4,28},{5,3},{6,30},{7,1},{8,16},{9,15},... | collective-permute-start | bytes 172040 | tf_op jit(solution)/shard_map/ppermute | solution.py:51
  24.9 0.8 %collective-permute-start.9 = (bf16[32,896]{1,0:T(8,128)(2,1)S(1)}, bf16[32,896]{1,0:T(8,128)(2,1)S(1)}, u32[]{:S(2)}, u32[]{:S(2)}) collective-permute-start(bf16[32,896]{1,0:T(8,128)(2,1)S(1)} %shard_map.76.own_ref), channel_id=1, source_target_pairs={{0,16},{1,5},{2,18},{3,7},{4,20},{5,1},{6,22},{7,3},{8,24},{9,13},... | collective-permute-start | bytes 172040 | tf_op jit(solution)/shard_map/ppermute | solution.py:51
  25.6 2.3 %collective-permute-start.8 = (bf16[32,896]{1,0:T(8,128)(2,1)S(1)}, bf16[32,896]{1,0:T(8,128)(2,1)S(1)}, u32[]{:S(2)}, u32[]{:S(2)}) collective-permute-start(bf16[32,896]{1,0:T(8,128)(2,1)S(1)} %shard_map.76.own_ref), channel_id=1, source_target_pairs={{0,8},{1,3},{2,10},{3,1},{4,12},{5,7},{6,14},{7,5},{8,0},{9,11},{1... | collective-permute-start | bytes 172040 | tf_op jit(solution)/shard_map/ppermute | solution.py:51
  27.9 0.9 %shard_map.77 = bf16[4,128,128]{2,1,0:T(8,128)(2,1)S(1)} custom-call(bf16[3,6,128,256]{3,2,1,0:T(8,128)(2,1)S(1)} %get-tuple-element.75.hid_ref, f32[9,32,128]{2,1,0:T(8,128)S(1)} %get-tuple-element.80.second_ref), custom_call_target="tpu_custom_call" | custom-call | flops 500000000 | bytes 1000000 | tf_op jit(solution)/shard_map/pallas_call | solution.py:582
  28.9 0.7 %copy.9 = bf16[4,4,32,128]{3,1,0,2:T(4,128)(2,1)} copy(bf16[4,4,32,128]{3,2,1,0:T(8,128)(2,1)S(1)} %bitcast.6) | data formatting | bytes 262144 | tf_op jit(solution)/shard_map/reshape | solution.py:588
  29.6 0.0 collective-permute-done.10.refs_2_
  29.6 1.2 %collective-permute-done.9.refs_1_ = bf16[32,896]{1,0:T(8,128)(2,1)S(1)} collective-permute-done((bf16[32,896]{1,0:T(8,128)(2,1)S(1)}, bf16[32,896]{1,0:T(8,128)(2,1)S(1)}, u32[]{:S(2)}, u32[]{:S(2)}) %collective-permute-start.9) | collective-permute-done | bytes 57376 | tf_op jit(solution)/shard_map/ppermute | solution.py:51
  30.7 0.0 collective-permute-done.8.refs_0_
  30.8 0.5 %collective-permute-start.13 = (bf16[32,896]{1,0:T(8,128)(2,1)S(1)}, bf16[32,896]{1,0:T(8,128)(2,1)S(1)}, u32[]{:S(2)}, u32[]{:S(2)}) collective-permute-start(bf16[32,896]{1,0:T(8,128)(2,1)S(1)} %shard_map.78.own_ref), channel_id=1, source_target_pairs={{0,6},{1,25},{2,4},{3,27},{4,2},{5,29},{6,0},{7,31},{8,14},{9,17},... | collective-permute-start | bytes 172040 | tf_op jit(solution)/shard_map/ppermute | solution.py:51
  31.3 0.9 %collective-permute-start.12 = (bf16[32,896]{1,0:T(8,128)(2,1)S(1)}, bf16[32,896]{1,0:T(8,128)(2,1)S(1)}, u32[]{:S(2)}, u32[]{:S(2)}) collective-permute-start(bf16[32,896]{1,0:T(8,128)(2,1)S(1)} %shard_map.78.own_ref), channel_id=1, source_target_pairs={{0,4},{1,17},{2,6},{3,19},{4,0},{5,21},{6,2},{7,23},{8,12},{9,25},... | collective-permute-start | bytes 172040 | tf_op jit(solution)/shard_map/ppermute | solution.py:51
  32.2 2.1 %collective-permute-start.11 = (bf16[32,896]{1,0:T(8,128)(2,1)S(1)}, bf16[32,896]{1,0:T(8,128)(2,1)S(1)}, u32[]{:S(2)}, u32[]{:S(2)}) collective-permute-start(bf16[32,896]{1,0:T(8,128)(2,1)S(1)} %shard_map.78.own_ref), channel_id=1, source_target_pairs={{0,2},{1,9},{2,0},{3,11},{4,6},{5,13},{6,4},{7,15},{8,10},{9,1},{1... | collective-permute-start | bytes 172040 | tf_op jit(solution)/shard_map/ppermute | solution.py:51
  34.3 1.6 %collective-permute-done.13.refs_2_ = bf16[32,896]{1,0:T(8,128)(2,1)S(1)} collective-permute-done((bf16[32,896]{1,0:T(8,128)(2,1)S(1)}, bf16[32,896]{1,0:T(8,128)(2,1)S(1)}, u32[]{:S(2)}, u32[]{:S(2)}) %collective-permute-start.13) | collective-permute-done | bytes 57376 | tf_op jit(solution)/shard_map/ppermute | solution.py:51
  35.9 0.0 collective-permute-done.12.refs_1_
  35.9 0.6 %collective-permute-done.11.refs_0_ = bf16[32,896]{1,0:T(8,128)(2,1)S(1)} collective-permute-done((bf16[32,896]{1,0:T(8,128)(2,1)S(1)}, bf16[32,896]{1,0:T(8,128)(2,1)S(1)}, u32[]{:S(2)}, u32[]{:S(2)}) %collective-permute-start.11) | collective-permute-done | bytes 57376 | tf_op jit(solution)/shard_map/ppermute | solution.py:51
  36.6 0.1 collective-permute-start.14
  36.6 1.3 %collective-permute-done.14.other_ref = f32[32,896]{1,0:T(8,128)S(1)} collective-permute-done((f32[32,896]{1,0:T(8,128)S(1)}, f32[32,896]{1,0:T(8,128)S(1)}, u32[]{:S(2)}, u32[]{:S(2)}) %collective-permute-start.14) | collective-permute-done | bytes 114720 | tf_op jit(solution)/shard_map/ppermute | solution.py:493
  38.0 0.7 %shard_map.80 = (f32[32,864]{1,0:T(8,128)}, f32[32,864]{1,0:T(8,128)}) custom-call(f32[32,896]{1,0:T(8,128)S(1)} %shard_map.79.mine_ref, f32[32,896]{1,0:T(8,128)S(1)} %collective-permute-done.14.other_ref), custom_call_target="tpu_custom_call" | custom-call | flops 1000000 | bytes 1000000 | tf_op jit(solution)/shard_map/pallas_call | solution.py:609
  (3 shorter events, 0.1 us)
Async XLA Ops:
  2.3 11.5 %collective-permute-start.2 = (bf16[3,128,128]{2,1,0:T(8,128)(2,1)S(1)}, bf16[3,128,128]{2,1,0:T(8,128)(2,1)S(1)}, u32[]{:S(2)}, u32[]{:S(2)}) collective-permute-start(bf16[3,128,128]{2,1,0:T(8,128)(2,1)S(1)} %get-tuple-element.49), channel_id=1, source_target_pairs={{0,4},{1,5},{2,6},{3,7},{4,0},{5,1},{6,2},{7,3},{8,12},{9,13},{10,... | collective-permute-start | bytes 294920 | tf_op jit(solution)/shard_map/ppermute | solution.py:51
  5.5 8.2 %collective-permute-start.3 = (bf16[160,128]{1,0:T(8,128)(2,1)S(1)}, bf16[160,128]{1,0:T(8,128)(2,1)S(1)}, u32[]{:S(2)}, u32[]{:S(2)}) collective-permute-start(bf16[160,128]{1,0:T(8,128)(2,1)S(1)} %get-tuple-element.50), channel_id=1, source_target_pairs={{8,20},{9,21},{10,22},{11,23},{12,16},{13,17},{14,18},{15,19},{16,... | collective-permute-start | bytes 122888 | tf_op jit(solution)/shard_map/ppermute | solution.py:51
  7.1 6.6 %collective-permute-start.4 = (bf16[160,128]{1,0:T(8,128)(2,1)S(1)}, bf16[160,128]{1,0:T(8,128)(2,1)S(1)}, u32[]{:S(2)}, u32[]{:S(2)}) collective-permute-start(bf16[160,128]{1,0:T(8,128)(2,1)S(1)} %get-tuple-element.51), channel_id=1, source_target_pairs={{0,12},{1,13},{2,14},{3,15},{4,8},{5,9},{6,10},{7,11},{8,4},{9,5},... | collective-permute-start | bytes 122888 | tf_op jit(solution)/shard_map/ppermute | solution.py:51
  9.6 4.6 %collective-permute-start = (bf16[3,128,128]{2,1,0:T(8,128)(2,1)S(1)}, bf16[3,128,128]{2,1,0:T(8,128)(2,1)S(1)}, u32[]{:S(2)}, u32[]{:S(2)}) collective-permute-start(bf16[3,128,128]{2,1,0:T(8,128)(2,1)S(1)} %get-tuple-element.47), channel_id=1, source_target_pairs={{8,16},{9,17},{10,18},{11,19},{12,20},{13,21},{14,22},{15,23},{16,... | collective-permute-start | bytes 294920 | tf_op jit(solution)/shard_map/ppermute | solution.py:51
  11.2 4.6 %collective-permute-start.1 = (bf16[3,128,128]{2,1,0:T(8,128)(2,1)S(1)}, bf16[3,128,128]{2,1,0:T(8,128)(2,1)S(1)}, u32[]{:S(2)}, u32[]{:S(2)}) collective-permute-start(bf16[3,128,128]{2,1,0:T(8,128)(2,1)S(1)} %get-tuple-element.48), channel_id=1, source_target_pairs={{0,8},{1,9},{2,10},{3,11},{4,12},{5,13},{6,14},{7,15},{8,0},{9,1},... | collective-permute-start | bytes 294920 | tf_op jit(solution)/shard_map/ppermute | solution.py:51
  15.9 1.9 %collective-permute-start.5 = (bf16[32,256]{1,0:T(8,128)(2,1)S(1)}, bf16[32,256]{1,0:T(8,128)(2,1)S(1)}, u32[]{:S(2)}, u32[]{:S(2)}) collective-permute-start(bf16[32,256]{1,0:T(8,128)(2,1)S(1)} %get-tuple-element.61), channel_id=1, source_target_pairs={{0,1},{1,0},{2,3},{3,2},{4,5},{5,4},{6,7},{7,6},{8,9},{9,8},{10,11... | collective-permute-start | bytes 49160 | tf_op jit(solution)/shard_map/ppermute | solution.py:51
  16.0 3.8 %collective-permute-start.6 = (bf16[32,256]{1,0:T(8,128)(2,1)S(1)}, bf16[32,256]{1,0:T(8,128)(2,1)S(1)}, u32[]{:S(2)}, u32[]{:S(2)}) collective-permute-start(bf16[32,256]{1,0:T(8,128)(2,1)S(1)} %get-tuple-element.62), channel_id=1, source_target_pairs={{1,2},{2,1},{5,6},{6,5},{9,10},{10,9},{13,14},{14,13},{17,18},{18,... | collective-permute-start | bytes 49160 | tf_op jit(solution)/shard_map/ppermute | solution.py:51
  22.1 1.4 %collective-permute-start.7 = (f32[32,896]{1,0:T(8,128)S(1)}, f32[32,896]{1,0:T(8,128)S(1)}, u32[]{:S(2)}, u32[]{:S(2)}) collective-permute-start(f32[32,896]{1,0:T(8,128)S(1)} %shard_map.75), channel_id=1, source_target_pairs={{0,1},{1,0},{2,3},{3,2},{4,5},{5,4},{6,7},{7,6},{8,9},{9,8},{10,11... | collective-permute-start | bytes 344072 | tf_op jit(solution)/shard_map/ppermute | solution.py:493
  23.5 6.1 %collective-permute-start.10 = (bf16[32,896]{1,0:T(8,128)(2,1)S(1)}, bf16[32,896]{1,0:T(8,128)(2,1)S(1)}, u32[]{:S(2)}, u32[]{:S(2)}) collective-permute-start(bf16[32,896]{1,0:T(8,128)(2,1)S(1)} %shard_map.76.own_ref), channel_id=1, source_target_pairs={{0,24},{1,7},{2,26},{3,5},{4,28},{5,3},{6,30},{7,1},{8,16},{9,15},... | collective-permute-start | bytes 172040 | tf_op jit(solution)/shard_map/ppermute | solution.py:51
  24.9 5.9 %collective-permute-start.9 = (bf16[32,896]{1,0:T(8,128)(2,1)S(1)}, bf16[32,896]{1,0:T(8,128)(2,1)S(1)}, u32[]{:S(2)}, u32[]{:S(2)}) collective-permute-start(bf16[32,896]{1,0:T(8,128)(2,1)S(1)} %shard_map.76.own_ref), channel_id=1, source_target_pairs={{0,16},{1,5},{2,18},{3,7},{4,20},{5,1},{6,22},{7,3},{8,24},{9,13},... | collective-permute-start | bytes 172040 | tf_op jit(solution)/shard_map/ppermute | solution.py:51
  25.6 5.1 %collective-permute-start.8 = (bf16[32,896]{1,0:T(8,128)(2,1)S(1)}, bf16[32,896]{1,0:T(8,128)(2,1)S(1)}, u32[]{:S(2)}, u32[]{:S(2)}) collective-permute-start(bf16[32,896]{1,0:T(8,128)(2,1)S(1)} %shard_map.76.own_ref), channel_id=1, source_target_pairs={{0,8},{1,3},{2,10},{3,1},{4,12},{5,7},{6,14},{7,5},{8,0},{9,11},{1... | collective-permute-start | bytes 172040 | tf_op jit(solution)/shard_map/ppermute | solution.py:51
  30.8 5.1 %collective-permute-start.13 = (bf16[32,896]{1,0:T(8,128)(2,1)S(1)}, bf16[32,896]{1,0:T(8,128)(2,1)S(1)}, u32[]{:S(2)}, u32[]{:S(2)}) collective-permute-start(bf16[32,896]{1,0:T(8,128)(2,1)S(1)} %shard_map.78.own_ref), channel_id=1, source_target_pairs={{0,6},{1,25},{2,4},{3,27},{4,2},{5,29},{6,0},{7,31},{8,14},{9,17},... | collective-permute-start | bytes 172040 | tf_op jit(solution)/shard_map/ppermute | solution.py:51
  31.3 4.6 %collective-permute-start.12 = (bf16[32,896]{1,0:T(8,128)(2,1)S(1)}, bf16[32,896]{1,0:T(8,128)(2,1)S(1)}, u32[]{:S(2)}, u32[]{:S(2)}) collective-permute-start(bf16[32,896]{1,0:T(8,128)(2,1)S(1)} %shard_map.78.own_ref), channel_id=1, source_target_pairs={{0,4},{1,17},{2,6},{3,19},{4,0},{5,21},{6,2},{7,23},{8,12},{9,25},... | collective-permute-start | bytes 172040 | tf_op jit(solution)/shard_map/ppermute | solution.py:51
  32.2 4.3 %collective-permute-start.11 = (bf16[32,896]{1,0:T(8,128)(2,1)S(1)}, bf16[32,896]{1,0:T(8,128)(2,1)S(1)}, u32[]{:S(2)}, u32[]{:S(2)}) collective-permute-start(bf16[32,896]{1,0:T(8,128)(2,1)S(1)} %shard_map.78.own_ref), channel_id=1, source_target_pairs={{0,2},{1,9},{2,0},{3,11},{4,6},{5,13},{6,4},{7,15},{8,10},{9,1},{1... | collective-permute-start | bytes 172040 | tf_op jit(solution)/shard_map/ppermute | solution.py:51
  36.6 1.4 %collective-permute-start.14 = (f32[32,896]{1,0:T(8,128)S(1)}, f32[32,896]{1,0:T(8,128)S(1)}, u32[]{:S(2)}, u32[]{:S(2)}) collective-permute-start(f32[32,896]{1,0:T(8,128)S(1)} %shard_map.79.mine_ref), channel_id=1, source_target_pairs={{0,1},{1,0},{2,3},{3,2},{4,5},{5,4},{6,7},{7,6},{8,9},{9,8},{10,11... | collective-permute-start | bytes 344072 | tf_op jit(solution)/shard_map/ppermute | solution.py:493

commit v4 on v3

--- a/solution.py
+++ b/solution.py
@@ -588,7 +588,7 @@
     prediction = prediction_rows.reshape(size_x, size_y, channels, size_z).transpose(2, 0, 1, 3)[None]
 
     steps = []
-    for axis, start in (("gx", 1), ("gz", 2), ("gy", 1)):
+    for axis, start in (("gz", 2), ("gy", 1), ("gx", 1)):
         bit = start
         while bit < lax.axis_size(axis):
             steps.append((axis, bit))

time: 38.8 us -> 38.8 us (level)
  no operation moved by 1% of the time
where the time goes in v4:
time: 38.8 us; the launch traced here: 38.7 us
  starting transfers between devices  18.2 us (47%)
  waiting for transfers between devices  9.27 us (24%)
  Pallas kernels  7.67 us (20%)
  other arithmetic  2.02 us (5%)
  between operations  0.78 us (2%)
  local copies, waits for them, and re-layouts  0.72 us (2%)
    ppermute x13, starting transfers between devices, permute(): lax.ppermute(x, AXES, [(number(place), number(to)) for place, to in targe...  18 us
    ppermute x13, waiting for transfers between devices, permute(): lax.ppermute(x, AXES, [(number(place), number(to)) for place, to in targe...  7.38 us
    ppermute x2, waiting for transfers between devices, flip(): return lax.ppermute(x, axis, [(i, i ^ bit) for i in range(size)])  1.89 us
    pallas_call x1, Pallas kernels, local(): call(functools.partial(widen, y_sides), [struct((3, n_field, size_z, 256)...  1.19 us
    concatenate x1, other arithmetic, local(): jnp.concatenate([inputs, noise], axis=0)  1.16 us
    pallas_call x1, Pallas kernels, local(): call(spread_weights, [struct((9 * 256, 256), BF16), struct((9 * 256, 256)...  1.05 us
    pallas_call x1, Pallas kernels, local(): call(predict, struct((size_x, lanes, size_z), BF16), scratch=[pltpu.VMEM(...  0.93 us
    concatenate x1, other arithmetic, local(): jnp.concatenate([w_first, w_second], axis=0)  0.86 us
  transfers between devices with their start and end apart: 15, of which 8 were waited for; matrix products, arithmetic and copies ran while one was open for 4% of the time, Pallas kernels for 10%

profile of v4, /device:TPU:0, one launch (start us, length us, event | category | flops | bytes accessed | tf_op | source)
XLA Modules:
  0.0 38.7 jit_solution(15233956217970026358)
XLA Ops:
  0.6 1.2 %pad_maximum_fusion.raw_ref = bf16[2,32,4,4,128]{4,3,2,1,0:T(4,128)(2,1)S(1)} fusion(bf16[1,32,4,4,128]{4,3,2,1,0:T(4,128)(2,1)} %param.5, bf16[1,32,4,4,128]{4,3,2,1,0:T(4,128)(2,1)} %param.4), kind=kLoop, calls=%fused_computation | loop fusion | flops 131072 | bytes 524288 | tf_op jit(solution)/shard_map/concatenate | solution.py:521
  1.8 0.5 %shard_map.67 = (bf16[4,128,128]{2,1,0:T(8,128)(2,1)S(1)}, bf16[4,128,128]{2,1,0:T(8,128)(2,1)S(1)}, bf16[4,128,128]{2,1,0:T(8,128)(2,1)S(1)}, bf16[3,128,128]{2,1,0:T(8,128)(2,1)S(1)}) custom-call(bf16[2,32,4,4,128]{4,3,2,1,0:T(4,128)(2,1)S(1)} %pad_maximum_fusion.raw_ref), custom_call_target="tpu_custom_call" | custom-call | flops 1000000 | bytes 1000000 | tf_op jit(solution)/shard_map/pallas_call | solution.py:516
  2.3 3.0 %collective-permute-start.2 = (bf16[3,128,128]{2,1,0:T(8,128)(2,1)S(1)}, bf16[3,128,128]{2,1,0:T(8,128)(2,1)S(1)}, u32[]{:S(2)}, u32[]{:S(2)}) collective-permute-start(bf16[3,128,128]{2,1,0:T(8,128)(2,1)S(1)} %get-tuple-element.49), channel_id=1, source_target_pairs={{0,4},{1,5},{2,6},{3,7},{4,0},{5,1},{6,2},{7,3},{8,12},{9,13},{10,... | collective-permute-start | bytes 294920 | tf_op jit(solution)/shard_map/ppermute | solution.py:51
  5.3 0.2 shard_map.68
  5.5 1.6 %collective-permute-start.3 = (bf16[160,128]{1,0:T(8,128)(2,1)S(1)}, bf16[160,128]{1,0:T(8,128)(2,1)S(1)}, u32[]{:S(2)}, u32[]{:S(2)}) collective-permute-start(bf16[160,128]{1,0:T(8,128)(2,1)S(1)} %get-tuple-element.50), channel_id=1, source_target_pairs={{8,20},{9,21},{10,22},{11,23},{12,16},{13,17},{14,18},{15,19},{16,... | collective-permute-start | bytes 122888 | tf_op jit(solution)/shard_map/ppermute | solution.py:51
  7.1 2.5 %collective-permute-start.4 = (bf16[160,128]{1,0:T(8,128)(2,1)S(1)}, bf16[160,128]{1,0:T(8,128)(2,1)S(1)}, u32[]{:S(2)}, u32[]{:S(2)}) collective-permute-start(bf16[160,128]{1,0:T(8,128)(2,1)S(1)} %get-tuple-element.51), channel_id=1, source_target_pairs={{0,12},{1,13},{2,14},{3,15},{4,8},{5,9},{6,10},{7,11},{8,4},{9,5},... | collective-permute-start | bytes 122888 | tf_op jit(solution)/shard_map/ppermute | solution.py:51
  9.6 1.5 %collective-permute-start = (bf16[3,128,128]{2,1,0:T(8,128)(2,1)S(1)}, bf16[3,128,128]{2,1,0:T(8,128)(2,1)S(1)}, u32[]{:S(2)}, u32[]{:S(2)}) collective-permute-start(bf16[3,128,128]{2,1,0:T(8,128)(2,1)S(1)} %get-tuple-element.47), channel_id=1, source_target_pairs={{8,16},{9,17},{10,18},{11,19},{12,20},{13,21},{14,22},{15,23},{16,... | collective-permute-start | bytes 294920 | tf_op jit(solution)/shard_map/ppermute | solution.py:51
  11.2 0.6 %collective-permute-start.1 = (bf16[3,128,128]{2,1,0:T(8,128)(2,1)S(1)}, bf16[3,128,128]{2,1,0:T(8,128)(2,1)S(1)}, u32[]{:S(2)}, u32[]{:S(2)}) collective-permute-start(bf16[3,128,128]{2,1,0:T(8,128)(2,1)S(1)} %get-tuple-element.48), channel_id=1, source_target_pairs={{0,8},{1,9},{2,10},{3,11},{4,12},{5,13},{6,14},{7,15},{8,0},{9,1},... | collective-permute-start | bytes 294920 | tf_op jit(solution)/shard_map/ppermute | solution.py:51
  11.8 0.9 %pad_maximum_fusion.1.both_ref = bf16[64,864]{1,0:T(8,128)(2,1)S(1)} fusion(bf16[32,864]{1,0:T(8,128)(2,1)} %param.7, bf16[32,864]{1,0:T(8,128)(2,1)} %param.6), kind=kLoop, calls=%fused_computation.2 | loop fusion | flops 221184 | bytes 221184 | tf_op jit(solution)/shard_map/concatenate | solution.py:538
  12.7 1.0 %shard_map.69 = (bf16[2304,256]{1,0:T(8,128)(2,1)S(1)}, bf16[2304,256]{1,0:T(8,128)(2,1)S(1)}, f32[9,32,128]{2,1,0:T(8,128)S(1)}) custom-call(bf16[64,864]{1,0:T(8,128)(2,1)S(1)} %pad_maximum_fusion.1.both_ref, f32[8,128]{1,0:T(8,128)S(1)} %get-tuple-element.52._), custom_call_target="tpu_custom_call" | custom-call | flops 1000000 | bytes 4000000 | tf_op jit(solution)/shard_map/pallas_call | solution.py:534
  13.7 0.0 collective-permute-done.3.refs_6_
  13.7 0.0 collective-permute-done.4.refs_5_
  13.7 0.0 collective-permute-done.2.refs_4_
  13.8 0.5 %collective-permute-done.refs_3_ = bf16[3,128,128]{2,1,0:T(8,128)(2,1)S(1)} collective-permute-done((bf16[3,128,128]{2,1,0:T(8,128)(2,1)S(1)}, bf16[3,128,128]{2,1,0:T(8,128)(2,1)S(1)}, u32[]{:S(2)}, u32[]{:S(2)}) %collective-permute-start) | collective-permute-done | bytes 98336 | tf_op jit(solution)/shard_map/ppermute | solution.py:51
  14.3 1.5 %collective-permute-done.1.refs_2_ = bf16[3,128,128]{2,1,0:T(8,128)(2,1)S(1)} collective-permute-done((bf16[3,128,128]{2,1,0:T(8,128)(2,1)S(1)}, bf16[3,128,128]{2,1,0:T(8,128)(2,1)S(1)}, u32[]{:S(2)}, u32[]{:S(2)}) %collective-permute-start.1) | collective-permute-done | bytes 98336 | tf_op jit(solution)/shard_map/ppermute | solution.py:51
  15.8 0.2 shard_map.70
  15.9 0.1 collective-permute-start.5
  16.0 0.6 %collective-permute-start.6 = (bf16[32,256]{1,0:T(8,128)(2,1)S(1)}, bf16[32,256]{1,0:T(8,128)(2,1)S(1)}, u32[]{:S(2)}, u32[]{:S(2)}) collective-permute-start(bf16[32,256]{1,0:T(8,128)(2,1)S(1)} %get-tuple-element.62), channel_id=1, source_target_pairs={{1,2},{2,1},{5,6},{6,5},{9,10},{10,9},{13,14},{14,13},{17,18},{18,... | collective-permute-start | bytes 49160 | tf_op jit(solution)/shard_map/ppermute | solution.py:51
  16.6 1.2 %shard_map.71 = (bf16[3,8,128,256]{3,2,1,0:T(8,128)(2,1)S(1)}, bf16[3,6,128,256]{3,2,1,0:T(8,128)(2,1)S(1)}, f32[6,128,256]{2,1,0:T(8,128)S(1)}) custom-call(bf16[4,128,128]{2,1,0:T(8,128)(2,1)S(1)} %get-tuple-element.45.field_ref.refs_0_, bf16[4,128,128]{2,1,0:T(8,128)(2,1)S(1)} %get-tuple-element.46.wide_noise_ref.refs_1_, ...), custom_call_target="tpu_custom_call" | custom-call | flops 1000000000 | bytes 1000000 | tf_op jit(solution)/shard_map/pallas_call | solution.py:550
  17.8 0.0 collective-permute-done.5.side_0
  17.8 2.0 %collective-permute-done.6.side_1 = bf16[32,256]{1,0:T(8,128)(2,1)S(1)} collective-permute-done((bf16[32,256]{1,0:T(8,128)(2,1)S(1)}, bf16[32,256]{1,0:T(8,128)(2,1)S(1)}, u32[]{:S(2)}, u32[]{:S(2)}) %collective-permute-start.6) | collective-permute-done | bytes 16416 | tf_op jit(solution)/shard_map/ppermute | solution.py:51
  19.8 0.7 %shard_map.72 = (bf16[3,6,128,256]{3,2,1,0:T(8,128)(2,1)S(1)}, f32[4,128,256]{2,1,0:T(8,128)S(1)}, bf16[2,8,16,256]{3,2,1,0:T(8,128)(2,1)S(1)}, bf16[2,6,16,256]{3,2,1,0:T(8,128)(2,1)S(1)}) custom-call(f32[6,128,256]{2,1,0:T(8,128)S(1)} %get-tuple-element.68.pre_ref, bf16[3,8,128,256]{3,2,1,0:T(8,128)(2,1)S(1)} %get-tuple-element.67.wide_field_ref.xs_ref, ...), custom_call_target="tpu_custom_call" | custom-call | flops 1000000 | bytes 1000000 | tf_op jit(solution)/shard_map/pallas_call | solution.py:558
  20.5 0.8 %shard_map.73.pre_grad_ref = bf16[128,512]{1,0:T(8,128)(2,1)S(1)} custom-call(bf16[3,6,128,256]{3,2,1,0:T(8,128)(2,1)S(1)} %get-tuple-element.69.wide_noise_ref.ns_ref, bf16[2,6,16,256]{3,2,1,0:T(8,128)(2,1)S(1)} %get-tuple-element.76.ns_edge, f32[4,128,256]{2,1,0:T(8,128)S(1)} %get-tuple-element.77.slope_ref, bf16[2304,256]{1,0:T(8,128)(2,1)S(1)} %get-tuple-element.78.ab_ref), custom_call_target="tpu_custom_call" | custom-call | flops 1000000000 | bytes 1000000 | tf_op jit(solution)/shard_map/pallas_call | solution.py:567
  21.4 0.7 %shard_map.75 = f32[32,896]{1,0:T(8,128)S(1)} custom-call(bf16[3,8,128,256]{3,2,1,0:T(8,128)(2,1)S(1)} %get-tuple-element.67.wide_field_ref.xs_ref, bf16[2,8,16,256]{3,2,1,0:T(8,128)(2,1)S(1)} %get-tuple-element.74.xs_edge, bf16[3,6,128,256]{3,2,1,0:T(8,128)(2,1)S(1)} %get-tuple-element.75.hid_ref, bf16[128,512]{1,0:T(8,128)(2,1)S(1)} %shard_map.73.pre_grad_ref, ...), custom_call_target="tpu_custom_call" | custom-call | flops 1000000000 | bytes 1000000 | tf_op jit(solution)/shard_map/pallas_call | solution.py:577
  22.1 0.2 collective-permute-start.7
  22.2 0.6 %shard_map.74.keep_ref = f32[32,896]{1,0:T(8,128)S(1)} custom-call(bf16[3,8,128,256]{3,2,1,0:T(8,128)(2,1)S(1)} %get-tuple-element.67.wide_field_ref.xs_ref, bf16[2,8,16,256]{3,2,1,0:T(8,128)(2,1)S(1)} %get-tuple-element.74.xs_edge, bf16[3,6,128,256]{3,2,1,0:T(8,128)(2,1)S(1)} %get-tuple-element.75.hid_ref, bf16[128,512]{1,0:T(8,128)(2,1)S(1)} %shard_map.73.pre_grad_ref, ...), custom_call_target="tpu_custom_call" | custom-call | flops 1000000000 | bytes 1000000 | tf_op jit(solution)/shard_map/pallas_call | solution.py:579
  22.9 0.6 %collective-permute-done.7.taken_ref = f32[32,896]{1,0:T(8,128)S(1)} collective-permute-done((f32[32,896]{1,0:T(8,128)S(1)}, f32[32,896]{1,0:T(8,128)S(1)}, u32[]{:S(2)}, u32[]{:S(2)}) %collective-permute-start.7) | collective-permute-done | bytes 114720 | tf_op jit(solution)/shard_map/ppermute | solution.py:493
  23.5 0.1 collective-permute-start.10
  23.5 1.4 %collective-permute-start.9 = (bf16[32,896]{1,0:T(8,128)(2,1)S(1)}, bf16[32,896]{1,0:T(8,128)(2,1)S(1)}, u32[]{:S(2)}, u32[]{:S(2)}) collective-permute-start(bf16[32,896]{1,0:T(8,128)(2,1)S(1)} %shard_map.76.own_ref), channel_id=1, source_target_pairs={{0,4},{1,17},{2,6},{3,19},{4,0},{5,21},{6,2},{7,23},{8,12},{9,25},... | collective-permute-start | bytes 172040 | tf_op jit(solution)/shard_map/ppermute | solution.py:51
  24.9 2.1 %collective-permute-start.8 = (bf16[32,896]{1,0:T(8,128)(2,1)S(1)}, bf16[32,896]{1,0:T(8,128)(2,1)S(1)}, u32[]{:S(2)}, u32[]{:S(2)}) collective-permute-start(bf16[32,896]{1,0:T(8,128)(2,1)S(1)} %shard_map.76.own_ref), channel_id=1, source_target_pairs={{0,2},{1,9},{2,0},{3,11},{4,6},{5,13},{6,4},{7,15},{8,10},{9,1},{1... | collective-permute-start | bytes 172040 | tf_op jit(solution)/shard_map/ppermute | solution.py:51
  27.0 0.9 %shard_map.77 = bf16[4,128,128]{2,1,0:T(8,128)(2,1)S(1)} custom-call(bf16[3,6,128,256]{3,2,1,0:T(8,128)(2,1)S(1)} %get-tuple-element.75.hid_ref, f32[9,32,128]{2,1,0:T(8,128)S(1)} %get-tuple-element.80.second_ref), custom_call_target="tpu_custom_call" | custom-call | flops 500000000 | bytes 1000000 | tf_op jit(solution)/shard_map/pallas_call | solution.py:582
  28.0 0.7 %copy.9 = bf16[4,4,32,128]{3,1,0,2:T(4,128)(2,1)} copy(bf16[4,4,32,128]{3,2,1,0:T(8,128)(2,1)S(1)} %bitcast.6) | data formatting | bytes 262144 | tf_op jit(solution)/shard_map/reshape | solution.py:588
  28.7 0.0 collective-permute-done.10.refs_2_
  28.7 0.0 collective-permute-done.9.refs_1_
  28.7 0.5 %collective-permute-done.8.refs_0_ = bf16[32,896]{1,0:T(8,128)(2,1)S(1)} collective-permute-done((bf16[32,896]{1,0:T(8,128)(2,1)S(1)}, bf16[32,896]{1,0:T(8,128)(2,1)S(1)}, u32[]{:S(2)}, u32[]{:S(2)}) %collective-permute-start.8) | collective-permute-done | bytes 57376 | tf_op jit(solution)/shard_map/ppermute | solution.py:51
  29.3 1.4 %collective-permute-start.13 = (bf16[32,896]{1,0:T(8,128)(2,1)S(1)}, bf16[32,896]{1,0:T(8,128)(2,1)S(1)}, u32[]{:S(2)}, u32[]{:S(2)}) collective-permute-start(bf16[32,896]{1,0:T(8,128)(2,1)S(1)} %shard_map.78.own_ref), channel_id=1, source_target_pairs={{0,24},{1,7},{2,26},{3,5},{4,28},{5,3},{6,30},{7,1},{8,16},{9,15},... | collective-permute-start | bytes 172040 | tf_op jit(solution)/shard_map/ppermute | solution.py:51
  30.7 0.8 %collective-permute-start.12 = (bf16[32,896]{1,0:T(8,128)(2,1)S(1)}, bf16[32,896]{1,0:T(8,128)(2,1)S(1)}, u32[]{:S(2)}, u32[]{:S(2)}) collective-permute-start(bf16[32,896]{1,0:T(8,128)(2,1)S(1)} %shard_map.78.own_ref), channel_id=1, source_target_pairs={{0,16},{1,5},{2,18},{3,7},{4,20},{5,1},{6,22},{7,3},{8,24},{9,13},... | collective-permute-start | bytes 172040 | tf_op jit(solution)/shard_map/ppermute | solution.py:51
  31.5 2.2 %collective-permute-start.11 = (bf16[32,896]{1,0:T(8,128)(2,1)S(1)}, bf16[32,896]{1,0:T(8,128)(2,1)S(1)}, u32[]{:S(2)}, u32[]{:S(2)}) collective-permute-start(bf16[32,896]{1,0:T(8,128)(2,1)S(1)} %shard_map.78.own_ref), channel_id=1, source_target_pairs={{0,8},{1,3},{2,10},{3,1},{4,12},{5,7},{6,14},{7,5},{8,0},{9,11},{1... | collective-permute-start | bytes 172040 | tf_op jit(solution)/shard_map/ppermute | solution.py:51
  33.7 1.6 %collective-permute-done.13.refs_2_ = bf16[32,896]{1,0:T(8,128)(2,1)S(1)} collective-permute-done((bf16[32,896]{1,0:T(8,128)(2,1)S(1)}, bf16[32,896]{1,0:T(8,128)(2,1)S(1)}, u32[]{:S(2)}, u32[]{:S(2)}) %collective-permute-start.13) | collective-permute-done | bytes 57376 | tf_op jit(solution)/shard_map/ppermute | solution.py:51
  35.3 1.2 %collective-permute-done.12.refs_1_ = bf16[32,896]{1,0:T(8,128)(2,1)S(1)} collective-permute-done((bf16[32,896]{1,0:T(8,128)(2,1)S(1)}, bf16[32,896]{1,0:T(8,128)(2,1)S(1)}, u32[]{:S(2)}, u32[]{:S(2)}) %collective-permute-start.12) | collective-permute-done | bytes 57376 | tf_op jit(solution)/shard_map/ppermute | solution.py:51
  36.5 0.0 collective-permute-done.11.refs_0_
  36.6 0.1 collective-permute-start.14
  36.6 1.3 %collective-permute-done.14.other_ref = f32[32,896]{1,0:T(8,128)S(1)} collective-permute-done((f32[32,896]{1,0:T(8,128)S(1)}, f32[32,896]{1,0:T(8,128)S(1)}, u32[]{:S(2)}, u32[]{:S(2)}) %collective-permute-start.14) | collective-permute-done | bytes 114720 | tf_op jit(solution)/shard_map/ppermute | solution.py:493
  38.0 0.7 %shard_map.80 = (f32[32,864]{1,0:T(8,128)}, f32[32,864]{1,0:T(8,128)}) custom-call(f32[32,896]{1,0:T(8,128)S(1)} %shard_map.79.mine_ref, f32[32,896]{1,0:T(8,128)S(1)} %collective-permute-done.14.other_ref), custom_call_target="tpu_custom_call" | custom-call | flops 1000000 | bytes 1000000 | tf_op jit(solution)/shard_map/pallas_call | solution.py:609
  (3 shorter events, 0.1 us)
Async XLA Ops:
  2.3 11.5 %collective-permute-start.2 = (bf16[3,128,128]{2,1,0:T(8,128)(2,1)S(1)}, bf16[3,128,128]{2,1,0:T(8,128)(2,1)S(1)}, u32[]{:S(2)}, u32[]{:S(2)}) collective-permute-start(bf16[3,128,128]{2,1,0:T(8,128)(2,1)S(1)} %get-tuple-element.49), channel_id=1, source_target_pairs={{0,4},{1,5},{2,6},{3,7},{4,0},{5,1},{6,2},{7,3},{8,12},{9,13},{10,... | collective-permute-start | bytes 294920 | tf_op jit(solution)/shard_map/ppermute | solution.py:51
  5.5 8.2 %collective-permute-start.3 = (bf16[160,128]{1,0:T(8,128)(2,1)S(1)}, bf16[160,128]{1,0:T(8,128)(2,1)S(1)}, u32[]{:S(2)}, u32[]{:S(2)}) collective-permute-start(bf16[160,128]{1,0:T(8,128)(2,1)S(1)} %get-tuple-element.50), channel_id=1, source_target_pairs={{8,20},{9,21},{10,22},{11,23},{12,16},{13,17},{14,18},{15,19},{16,... | collective-permute-start | bytes 122888 | tf_op jit(solution)/shard_map/ppermute | solution.py:51
  7.1 6.6 %collective-permute-start.4 = (bf16[160,128]{1,0:T(8,128)(2,1)S(1)}, bf16[160,128]{1,0:T(8,128)(2,1)S(1)}, u32[]{:S(2)}, u32[]{:S(2)}) collective-permute-start(bf16[160,128]{1,0:T(8,128)(2,1)S(1)} %get-tuple-element.51), channel_id=1, source_target_pairs={{0,12},{1,13},{2,14},{3,15},{4,8},{5,9},{6,10},{7,11},{8,4},{9,5},... | collective-permute-start | bytes 122888 | tf_op jit(solution)/shard_map/ppermute | solution.py:51
  9.6 4.6 %collective-permute-start = (bf16[3,128,128]{2,1,0:T(8,128)(2,1)S(1)}, bf16[3,128,128]{2,1,0:T(8,128)(2,1)S(1)}, u32[]{:S(2)}, u32[]{:S(2)}) collective-permute-start(bf16[3,128,128]{2,1,0:T(8,128)(2,1)S(1)} %get-tuple-element.47), channel_id=1, source_target_pairs={{8,16},{9,17},{10,18},{11,19},{12,20},{13,21},{14,22},{15,23},{16,... | collective-permute-start | bytes 294920 | tf_op jit(solution)/shard_map/ppermute | solution.py:51
  11.2 4.6 %collective-permute-start.1 = (bf16[3,128,128]{2,1,0:T(8,128)(2,1)S(1)}, bf16[3,128,128]{2,1,0:T(8,128)(2,1)S(1)}, u32[]{:S(2)}, u32[]{:S(2)}) collective-permute-start(bf16[3,128,128]{2,1,0:T(8,128)(2,1)S(1)} %get-tuple-element.48), channel_id=1, source_target_pairs={{0,8},{1,9},{2,10},{3,11},{4,12},{5,13},{6,14},{7,15},{8,0},{9,1},... | collective-permute-start | bytes 294920 | tf_op jit(solution)/shard_map/ppermute | solution.py:51
  15.9 1.9 %collective-permute-start.5 = (bf16[32,256]{1,0:T(8,128)(2,1)S(1)}, bf16[32,256]{1,0:T(8,128)(2,1)S(1)}, u32[]{:S(2)}, u32[]{:S(2)}) collective-permute-start(bf16[32,256]{1,0:T(8,128)(2,1)S(1)} %get-tuple-element.61), channel_id=1, source_target_pairs={{0,1},{1,0},{2,3},{3,2},{4,5},{5,4},{6,7},{7,6},{8,9},{9,8},{10,11... | collective-permute-start | bytes 49160 | tf_op jit(solution)/shard_map/ppermute | solution.py:51
  16.0 3.8 %collective-permute-start.6 = (bf16[32,256]{1,0:T(8,128)(2,1)S(1)}, bf16[32,256]{1,0:T(8,128)(2,1)S(1)}, u32[]{:S(2)}, u32[]{:S(2)}) collective-permute-start(bf16[32,256]{1,0:T(8,128)(2,1)S(1)} %get-tuple-element.62), channel_id=1, source_target_pairs={{1,2},{2,1},{5,6},{6,5},{9,10},{10,9},{13,14},{14,13},{17,18},{18,... | collective-permute-start | bytes 49160 | tf_op jit(solution)/shard_map/ppermute | solution.py:51
  22.1 1.4 %collective-permute-start.7 = (f32[32,896]{1,0:T(8,128)S(1)}, f32[32,896]{1,0:T(8,128)S(1)}, u32[]{:S(2)}, u32[]{:S(2)}) collective-permute-start(f32[32,896]{1,0:T(8,128)S(1)} %shard_map.75), channel_id=1, source_target_pairs={{0,1},{1,0},{2,3},{3,2},{4,5},{5,4},{6,7},{7,6},{8,9},{9,8},{10,11... | collective-permute-start | bytes 344072 | tf_op jit(solution)/shard_map/ppermute | solution.py:493
  23.5 5.2 %collective-permute-start.10 = (bf16[32,896]{1,0:T(8,128)(2,1)S(1)}, bf16[32,896]{1,0:T(8,128)(2,1)S(1)}, u32[]{:S(2)}, u32[]{:S(2)}) collective-permute-start(bf16[32,896]{1,0:T(8,128)(2,1)S(1)} %shard_map.76.own_ref), channel_id=1, source_target_pairs={{0,6},{1,25},{2,4},{3,27},{4,2},{5,29},{6,0},{7,31},{8,14},{9,17},... | collective-permute-start | bytes 172040 | tf_op jit(solution)/shard_map/ppermute | solution.py:51
  23.5 5.1 %collective-permute-start.9 = (bf16[32,896]{1,0:T(8,128)(2,1)S(1)}, bf16[32,896]{1,0:T(8,128)(2,1)S(1)}, u32[]{:S(2)}, u32[]{:S(2)}) collective-permute-start(bf16[32,896]{1,0:T(8,128)(2,1)S(1)} %shard_map.76.own_ref), channel_id=1, source_target_pairs={{0,4},{1,17},{2,6},{3,19},{4,0},{5,21},{6,2},{7,23},{8,12},{9,25},... | collective-permute-start | bytes 172040 | tf_op jit(solution)/shard_map/ppermute | solution.py:51
  24.9 4.3 %collective-permute-start.8 = (bf16[32,896]{1,0:T(8,128)(2,1)S(1)}, bf16[32,896]{1,0:T(8,128)(2,1)S(1)}, u32[]{:S(2)}, u32[]{:S(2)}) collective-permute-start(bf16[32,896]{1,0:T(8,128)(2,1)S(1)} %shard_map.76.own_ref), channel_id=1, source_target_pairs={{0,2},{1,9},{2,0},{3,11},{4,6},{5,13},{6,4},{7,15},{8,10},{9,1},{1... | collective-permute-start | bytes 172040 | tf_op jit(solution)/shard_map/ppermute | solution.py:51
  29.3 6.1 %collective-permute-start.13 = (bf16[32,896]{1,0:T(8,128)(2,1)S(1)}, bf16[32,896]{1,0:T(8,128)(2,1)S(1)}, u32[]{:S(2)}, u32[]{:S(2)}) collective-permute-start(bf16[32,896]{1,0:T(8,128)(2,1)S(1)} %shard_map.78.own_ref), channel_id=1, source_target_pairs={{0,24},{1,7},{2,26},{3,5},{4,28},{5,3},{6,30},{7,1},{8,16},{9,15},... | collective-permute-start | bytes 172040 | tf_op jit(solution)/shard_map/ppermute | solution.py:51
  30.7 5.9 %collective-permute-start.12 = (bf16[32,896]{1,0:T(8,128)(2,1)S(1)}, bf16[32,896]{1,0:T(8,128)(2,1)S(1)}, u32[]{:S(2)}, u32[]{:S(2)}) collective-permute-start(bf16[32,896]{1,0:T(8,128)(2,1)S(1)} %shard_map.78.own_ref), channel_id=1, source_target_pairs={{0,16},{1,5},{2,18},{3,7},{4,20},{5,1},{6,22},{7,3},{8,24},{9,13},... | collective-permute-start | bytes 172040 | tf_op jit(solution)/shard_map/ppermute | solution.py:51
  31.5 5.0 %collective-permute-start.11 = (bf16[32,896]{1,0:T(8,128)(2,1)S(1)}, bf16[32,896]{1,0:T(8,128)(2,1)S(1)}, u32[]{:S(2)}, u32[]{:S(2)}) collective-permute-start(bf16[32,896]{1,0:T(8,128)(2,1)S(1)} %shard_map.78.own_ref), channel_id=1, source_target_pairs={{0,8},{1,3},{2,10},{3,1},{4,12},{5,7},{6,14},{7,5},{8,0},{9,11},{1... | collective-permute-start | bytes 172040 | tf_op jit(solution)/shard_map/ppermute | solution.py:51
  36.6 1.4 %collective-permute-start.14 = (f32[32,896]{1,0:T(8,128)S(1)}, f32[32,896]{1,0:T(8,128)S(1)}, u32[]{:S(2)}, u32[]{:S(2)}) collective-permute-start(f32[32,896]{1,0:T(8,128)S(1)} %shard_map.79.mine_ref), channel_id=1, source_target_pairs={{0,1},{1,0},{2,3},{3,2},{4,5},{5,4},{6,7},{7,6},{8,9},{9,8},{10,11... | collective-permute-start | bytes 344072 | tf_op jit(solution)/shard_map/ppermute | solution.py:493

commit v5 on v3

--- a/solution.py
+++ b/solution.py
@@ -84,7 +84,7 @@
     return jnp.where(flag, a, b)
 
 
-def pack_faces(y_sides, raw_ref, noise_rows_ref, field_ref, wide_noise_ref, *face_y):
+def pack_faces(y_sides, raw_ref, noise_rows_ref, field_ref, wide_noise_ref, *faces):
     size_x, size_z = raw_ref.shape[2], raw_ref.shape[4]
     lanes = raw_ref.shape[1] * raw_ref.shape[3]
     for x in range(size_x):
@@ -93,9 +93,16 @@
             if a:
                 noise_rows_ref[x] = rows
             ref[x] = rows.T
-    even_y = even_index("gy")
+    face_x, face_y = faces[:2], faces[2:]
+    even = even_index("gx")
+    for side in range(2):
+        high = even if side == 0 else jnp.logical_not(even)
+        face_x[side][0] = jnp.where(high, field_ref[size_x - 2], field_ref[0])
+        face_x[side][1] = jnp.where(high, field_ref[size_x - 1], field_ref[1])
+        face_x[side][2] = jnp.where(high, wide_noise_ref[size_x - 1], wide_noise_ref[0])
+    even = even_index("gy")
     for k in range(y_sides):
-        two, one = cut_y(even_y if k == 0 else jnp.logical_not(even_y))
+        two, one = cut_y(even if k == 0 else jnp.logical_not(even))
         for j in range(0, size_x, 2):
             face_y[k][j // 2] = jnp.concatenate([two(field_ref[j]), two(field_ref[j + 1])], axis=1)
         for j in range(0, size_x, 4):
@@ -108,23 +115,28 @@
     return two, one
 
 
-def pack_corners(y_sides, field_ref, wide_noise_ref, token_ref, *faces):
-    token_ref[...] = jnp.zeros_like(token_ref)
-    even_x, even_y = even_index("gx"), even_index("gy")
-    size_x = field_ref.shape[0]
-    face_x, corners = faces[:2], faces[2:]
-    for side in range(2):
-        high = even_x if side == 0 else jnp.logical_not(even_x)
-        face_x[side][0] = jnp.where(high, field_ref[size_x - 2], field_ref[0])
-        face_x[side][1] = jnp.where(high, field_ref[size_x - 1], field_ref[1])
-        face_x[side][2] = jnp.where(high, wide_noise_ref[size_x - 1], wide_noise_ref[0])
+def pack_corners(y_sides, face_0, face_1, *refs):
+    corners = refs[y_sides:]
+    even = even_index("gy")
     for k in range(y_sides):
-        two, one = cut_y(even_y if k == 0 else jnp.logical_not(even_y))
-        for side, face in enumerate(face_x):
+        two, one = cut_y(even if k == 0 else jnp.logical_not(even))
+        for side, face in enumerate((face_0, face_1)):
             ref = corners[2 * k + side]
             ref[:128] = jnp.concatenate([two(face[0]), two(face[1])], axis=1)
             strip = one(face[2])
             ref[128:] = jnp.concatenate([strip[i * 32 : (i + 1) * 32] for i in range(4)], axis=1)
+
+
+def sort_faces(y_sides, *refs):
+    x_refs, y_refs, out = refs[:2], list(refs[2 : 2 + y_sides]), refs[2 + y_sides :]
+    y_refs += [None] * (2 - y_sides)
+    for axis, pair, below_ref, above_ref in (("gx", x_refs, *out[:2]), ("gy", y_refs, *out[2:])):
+        even = even_index(axis)
+        index = lax.axis_index(axis)
+        side_0, side_1 = [None if ref is None else ref[...] for ref in pair]
+        below, above = choose(even, side_1, side_0), choose(even, side_0, side_1)
+        below_ref[...] = jnp.where(index == 0, jnp.zeros_like(below), below)
+        above_ref[...] = jnp.where(index == lax.axis_size(axis) - 1, jnp.zeros_like(above), above)
 
 
 class Pieces:
@@ -137,18 +149,15 @@
         ends = lambda axis: (lax.axis_index(axis) == 0, lax.axis_index(axis) == lax.axis_size(axis) - 1)
         self.outside_x = dict(zip(("below", "above"), ends("gx")))
         self.outside_y = dict(zip(("below", "above"), ends("gy")))
-        self.face_x = list(face_x)
-        self.face_y = list(face_y) + [None] * (2 - y_sides)
+        self.face_x = dict(zip(("below", "above"), face_x))
+        self.face_y = dict(zip(("below", "above"), face_y))
         self.corner = [list(corner[2 * k : 2 * k + 2]) for k in range(y_sides)] + [[None, None]] * (2 - y_sides)
 
     def from_x(self, where, index, rows):
-        value = choose(self.flag_x[where], self.face_x[1][index, rows], self.face_x[0][index, rows])
-        return jnp.where(self.outside_x[where], jnp.zeros_like(value), value)
+        return self.face_x[where][index, rows]
 
     def from_y(self, where, read):
-        a = [None if ref is None else read(ref) for ref in self.face_y]
-        value = choose(self.flag_y[where], a[1], a[0])
-        return jnp.where(self.outside_y[where], jnp.zeros_like(value), value)
+        return read(self.face_y[where])
 
     def from_corner(self, where_x, where_y, read):
         a = []
@@ -204,8 +213,8 @@
 
 
 def take_pieces(y_sides, refs):
-    n = 4 + 3 * y_sides
-    return Pieces(y_sides, refs[0], refs[1], refs[2:4], refs[4 : 4 + y_sides], refs[4 + y_sides : n]), refs[n:]
+    n = 6 + 2 * y_sides
+    return Pieces(y_sides, refs[0], refs[1], refs[2:4], refs[4:6], refs[6:n]), refs[n:]
 
 
 def pack_z(y_sides, *refs):
@@ -241,7 +250,7 @@
 
 
 def widen(y_sides, *refs):
-    pieces, (a1_ref, xs_ref, ns_ref, pre_ref) = take_pieces(y_sides, refs)
+    pieces, (a1_ref, ab_ref, xs_ref, pre_ref, back_ref, hid_ref, slope_ref, ns_ref) = take_pieces(y_sides, refs)
     size_z = pieces.size_z
     for ref, read in ((xs_ref, pieces.field_plane), (ns_ref, pieces.noise_plane)):
         for x in range(ref.shape[1]):
@@ -252,6 +261,25 @@
     n_noise = pre_ref.shape[0]
     total = jnp.dot(taps(xs_ref, n_noise), a1_ref[...], preferred_element_type=F32)
     pre_ref[...] = total.reshape(n_noise, size_z, 256)
+    size_x = back_ref.shape[0]
+    total = jnp.dot(taps(ns_ref, size_x), ab_ref[...], preferred_element_type=F32)
+    back_ref[...] = total.reshape(size_x, size_z, 256)
+
+    index = lax.axis_index("gx")
+    for x in range(n_noise):
+        value = pre_ref[x]
+        hidden, s = silu_parts(value)
+        gone = outside_y()
+        if x == 0:
+            gone = gone | (index == 0)
+        if x == n_noise - 1:
+            gone = gone | (index == lax.axis_size("gx") - 1)
+        hidden = jnp.where(gone, 0.0, hidden).astype(BF16)
+        hid_ref[1, x] = hidden
+        hid_ref[0, x] = shifted(hidden, 0.0, True)
+        hid_ref[2, x] = shifted(hidden, 0.0, False)
+        if 1 <= x <= size_x:
+            slope_ref[x - 1] = slope_of(value, s)
 
 
 def band(ref, row, taps, shift, lo, hi):
@@ -267,7 +295,7 @@
         ref[row : row + C, half * 128 : (half + 1) * 128] = value.astype(BF16)
 
 
-def spread_weights(both_ref, _, a1_ref, ab_ref, second_out):
+def spread_weights(both_ref, a1_ref, ab_ref, second_out):
     def columns(rows):
         wide = both_ref[rows].astype(F32)
         return jnp.concatenate([wide, jnp.zeros((C, 896 - wide.shape[1]), F32)], axis=1)
@@ -322,99 +350,115 @@
 
 
 class Edged:
-    def __init__(self, ref, edge_ref):
-        self.ref, self.edge_ref = ref, edge_ref
+    def __init__(self, ref, edge_ref, tiles=((0, None), (None, None), (None, 1))):
+        self.ref, self.edge_ref, self.tiles = ref, edge_ref, tiles
 
     def stack(self, dz, first, count):
         parts = []
+        begin, end = self.tiles[dz]
+        size_z = self.ref.shape[2]
         for x in range(first, first + count):
-            if dz == 0:
-                parts += [self.edge_ref[0, x], self.ref[0, x, 16:]]
-            elif dz == 1:
-                parts += [self.ref[1, x]]
-            else:
-                parts += [self.ref[2, x, : self.ref.shape[2] - 16], self.edge_ref[1, x]]
+            if begin is not None:
+                parts.append(self.edge_ref[begin, x])
+            parts.append(self.ref[dz, x, 0 if begin is None else 16 : size_z if end is None else size_z - 16])
+            if end is not None:
+                parts.append(self.edge_ref[end, x])
         return jnp.concatenate(parts, axis=0)
 
 
-def activate(
-    pre_ref, wide_field_ref, wide_noise_ref, low_ref, high_ref, a1_ref, side_0, side_1, hid_ref, slope_ref, xs_edge, ns_edge
+HIDDEN_TILES = ((0, None), (1, 2), (None, 3))
+
+
+def outside_y():
+    lane = lax.broadcasted_iota(jnp.int32, (1, 256), 1)
+    index = lax.axis_index("gy")
+    return ((lane < C) & (index == 0)) | ((lane >= 5 * C) & (index == lax.axis_size("gy") - 1))
+
+
+def slope_of(value, s):
+    return s * (1.0 + value * (1.0 - s))
+
+
+def mend(
+    pre_ref, hid_ref, wide_field_ref, low_ref, high_ref, a1_ref, ab_ref, side_0, side_1, hid_edge, xs_edge, slope_rows, back_rows
 ):
     n_field, size_z = wide_field_ref.shape[1], wide_field_ref.shape[2]
-    n_noise = wide_noise_ref.shape[1]
-    size_x = n_noise - 2
+    n_noise = pre_ref.shape[0]
     even = even_index("gz")
     own_low = low_ref[...].astype(F32)
     own_high = high_ref[...].astype(F32)
 
-    gx, gy, gz = lax.axis_index("gx"), lax.axis_index("gy"), lax.axis_index("gz")
+    gx, gz = lax.axis_index("gx"), lax.axis_index("gz")
     first_x, last_x = gx == 0, gx == lax.axis_size("gx") - 1
-    first_y, last_y = gy == 0, gy == lax.axis_size("gy") - 1
     first_z, last_z = gz == 0, gz == lax.axis_size("gz") - 1
-
     below_rows = jnp.where(first_z, 0.0, jnp.where(even, side_1[...], side_0[...]).astype(F32))
     above_rows = jnp.where(last_z, 0.0, jnp.where(even, side_0[...], side_1[...]).astype(F32))
 
     before = jnp.concatenate([below_rows[:n_field], own_high[n_field : 2 * n_field]], axis=0).astype(BF16)
     halo = jnp.concatenate([below_rows[n_field : 2 * n_field], above_rows[:n_field]], axis=0).astype(BF16)
     after = jnp.concatenate([own_low[:n_field], above_rows[n_field : 2 * n_field]], axis=0).astype(BF16)
+    base = 2 * n_field
+    noise_halo = jnp.concatenate(
+        [below_rows[base : base + n_field], above_rows[base : base + n_field]], axis=0
+    ).astype(BF16)
     rows = 2 * n_field
-    edge_total, row_total = None, None
+    edge_total, row_total, back_total = None, None, None
     for dx in range(3):
-        weight = lambda dz: a1_ref[(3 * dx + dz) * 256 : (3 * dx + dz + 1) * 256]
-        first = jnp.dot(jnp.concatenate([before, halo], axis=0), weight(0), preferred_element_type=F32)
-        middle = jnp.dot(halo, weight(1), preferred_element_type=F32)
-        last = jnp.dot(jnp.concatenate([after, halo], axis=0), weight(2), preferred_element_type=F32)
+        at = lambda ref, dz: ref[(3 * dx + dz) * 256 : (3 * dx + dz + 1) * 256]
+        first = jnp.dot(jnp.concatenate([before, halo], axis=0), at(a1_ref, 0), preferred_element_type=F32)
+        middle = jnp.dot(halo, at(a1_ref, 1), preferred_element_type=F32)
+        last = jnp.dot(jnp.concatenate([after, halo], axis=0), at(a1_ref, 2), preferred_element_type=F32)
+        back_first = jnp.dot(noise_halo, at(ab_ref, 0), preferred_element_type=F32)
+        back_last = jnp.dot(noise_halo, at(ab_ref, 2), preferred_element_type=F32)
         edge = first[:rows] + middle + last[:rows]
         row = jnp.concatenate([first[rows : rows + n_field], last[rows + n_field :]], axis=0)
+        back = jnp.concatenate([back_first[:n_field], back_last[n_field:]], axis=0)
         if dx:
-            edge = pltpu.roll(edge, rows - dx, 0)
-            row = pltpu.roll(row, rows - dx, 0)
+            edge, row, back = [pltpu.roll(part, rows - dx, 0) for part in (edge, row, back)]
         edge_total = edge if edge_total is None else edge_total + edge
         row_total = row if row_total is None else row_total + row
-
-    lane = lax.broadcasted_iota(jnp.int32, (1, 256), 1)
-    drop_y = ((lane < C) & first_y) | ((lane >= 5 * C) & last_y)
-    edge_hidden = silu_parts(edge_total)[0]
-    row = lax.broadcasted_iota(jnp.int32, edge_hidden.shape, 0)
-    drop = drop_y | ((row < n_field) & first_z) | ((row >= n_field) & last_z)
-    x_row = jnp.where(row < n_field, row, row - n_field)
-    drop = drop | ((x_row == 0) & first_x) | ((x_row == n_noise - 1) & last_x)
-    edge_hidden = jnp.where(drop, 0.0, edge_hidden).astype(BF16).astype(F32)
-
-    row = lax.broadcasted_iota(jnp.int32, (size_z, 256), 0)
+        back_total = back if back_total is None else back_total + back
+    back_rows[...] = back_total
+
+    index = lax.broadcasted_iota(jnp.int32, (rows, 256), 0)
+    x_row = jnp.where(index < n_field, index, index - n_field)
+    drop = outside_y() | ((x_row == 0) & first_x) | ((x_row == n_noise - 1) & last_x)
+    drop_edge = drop | ((index < n_field) & first_z) | ((index >= n_field) & last_z)
+    edge_hidden = jnp.where(drop_edge, 0.0, silu_parts(edge_total)[0]).astype(BF16).astype(F32)
+
+    zeros = [jnp.zeros((1, 256), F32)] * (n_field - n_noise)
+    ends = [pre_ref[x, 0:8][0:1] for x in range(n_noise)] + zeros
+    ends += [pre_ref[x, size_z - 8 :][7:8] for x in range(n_noise)] + zeros
+    value = jnp.concatenate(ends, axis=0) + row_total
+    row_hidden, s = silu_parts(value)
+    row_hidden = jnp.where(drop, 0.0, row_hidden).astype(BF16).astype(F32)
+    slope_rows[...] = slope_of(value, s)
+
+    tile_row = lax.broadcasted_iota(jnp.int32, (16, 256), 0)
     for x in range(n_noise):
-        value = pre_ref[x]
-        value = value + jnp.where(row == 0, row_total[x : x + 1], 0.0)
-        value = value + jnp.where(row == size_z - 1, row_total[n_field + x : n_field + x + 1], 0.0)
-        hidden, s = silu_parts(value)
-        gone = drop_y
-        if x == 0:
-            gone = gone | first_x
-        if x == n_noise - 1:
-            gone = gone | last_x
-        hidden = jnp.where(gone, 0.0, hidden).astype(BF16)
-        hid_ref[1, x] = hidden
-        hid_ref[0, x] = shifted(hidden, edge_hidden[x : x + 1], True)
-        hid_ref[2, x] = shifted(hidden, edge_hidden[n_field + x : n_field + x + 1], False)
-        if 1 <= x <= size_x:
-            slope_ref[x - 1] = s * (1.0 + value * (1.0 - s))
-
+        low, high = row_hidden[x : x + 1], row_hidden[n_field + x : n_field + x + 1]
+        below, above = edge_hidden[x : x + 1], edge_hidden[n_field + x : n_field + x + 1]
+        begin = [hid_ref[dz, x, 0:16].astype(F32) for dz in range(2)]
+        end = [hid_ref[dz, x, size_z - 16 :].astype(F32) for dz in range(1, 3)]
+        hid_edge[0, x] = jnp.where(tile_row == 0, below, jnp.where(tile_row == 1, low, begin[0])).astype(BF16)
+        hid_edge[1, x] = jnp.where(tile_row == 0, low, begin[1]).astype(BF16)
+        hid_edge[2, x] = jnp.where(tile_row == 15, high, end[0]).astype(BF16)
+        hid_edge[3, x] = jnp.where(tile_row == 15, above, jnp.where(tile_row == 14, high, end[1])).astype(BF16)
     for x in range(n_field):
         xs_edge[0, x] = edge_tile(wide_field_ref, 0, x, below_rows[n_field + x : n_field + x + 1])
         xs_edge[1, x] = edge_tile(wide_field_ref, 2, x, above_rows[x : x + 1])
-    base = 2 * n_field
-    for x in range(n_noise):
-        ns_edge[0, x] = edge_tile(wide_noise_ref, 0, x, below_rows[base + x : base + x + 1])
-        ns_edge[1, x] = edge_tile(wide_noise_ref, 2, x, above_rows[base + x : base + x + 1])
-
-
-def backward(ns_ref, ns_edge, slope_ref, ab_ref, out_ref, acc_ref):
+
+
+def backward(back_ref, slope_ref, slope_rows, back_rows, out_ref):
     size_x, size_z = slope_ref.shape[:2]
-    total = jnp.dot(taps(Edged(ns_ref, ns_edge), size_x), ab_ref[...], preferred_element_type=F32)
-    acc_ref[...] = total.reshape(size_x, size_z, 256)
+    half = slope_rows.shape[0] // 2
+    index = lax.broadcasted_iota(jnp.int32, (size_z, 256), 0)
     for x in range(size_x):
-        value = (acc_ref[x] * slope_ref[x]).astype(BF16)
+        back, slope = back_ref[x], slope_ref[x]
+        for row, at in ((0, 0), (size_z - 1, half)):
+            back = jnp.where(index == row, back + back_rows[at + x : at + x + 1], back)
+            slope = jnp.where(index == row, slope_rows[at + x + 1 : at + x + 2], slope)
+        value = (back * slope).astype(BF16)
         rows = jnp.concatenate([value[:, :128].T, value[:, 128:].T], axis=0)
         out_ref[:, x * size_z : (x + 1) * size_z] = rows[C : 5 * C, :]
 
@@ -441,26 +485,26 @@
     return jnp.concatenate(tiles, axis=1)
 
 
-def weight_grad(give, xs_ref, xs_edge, hid_ref, pre_grad_ref, rows_ref, out_ref):
+def weight_grad(give, xs_ref, xs_edge, hid_ref, hid_edge, pre_grad_ref, rows_ref, out_ref):
     size_x = rows_ref.shape[0]
     even = even_index("gz")
 
     @pl.when(even if give else jnp.logical_not(even))
     def _():
         noise_rows = jnp.concatenate([rows_ref[x] for x in range(size_x)], axis=1)
-        out_ref[...] = collect(noise_rows, hid_ref, size_x, 0, 0)
+        out_ref[...] = collect(noise_rows, Edged(hid_ref, hid_edge, HIDDEN_TILES), size_x, 0, 0)
 
     @pl.when(jnp.logical_not(even) if give else even)
     def _():
         out_ref[...] = collect(pre_grad_ref[...], Edged(xs_ref, xs_edge), size_x, 1, 1)
 
 
-def predict(hid_ref, second_ref, out_ref, acc_ref, a2_ref):
+def predict(hid_ref, hid_edge, second_ref, out_ref, acc_ref, a2_ref):
     size_x, size_z = out_ref.shape[0], out_ref.shape[2]
     for t in range(9):
         for yi in range(8):
             band(a2_ref, t * 256 + yi * C, second_ref[t], (yi - 2) * C, 0, 4 * C)
-    total = jnp.dot(taps(hid_ref, size_x), a2_ref[...], preferred_element_type=F32)
+    total = jnp.dot(taps(Edged(hid_ref, hid_edge, HIDDEN_TILES), size_x), a2_ref[...], preferred_element_type=F32)
     acc_ref[...] = total.reshape(size_x, size_z, 128)
     for x in range(size_x):
         out_ref[x] = acc_ref[x].astype(BF16).T
@@ -513,19 +557,18 @@
     plane = (size_z, lanes)
     y_sides = 2 if lax.axis_size("gy") > 2 else 1
     y_planes = size_x // 2 + size_x // 4
-    noise_rows, field, wide_noise, *face_y = call(
+    face = struct((3,) + plane, BF16)
+    y_face = struct((y_planes,) + plane, BF16)
+    n_near = 2 + y_sides
+    noise_rows, field, wide_noise, *faces = call(
         functools.partial(pack_faces, y_sides),
         [struct((size_x, lanes, size_z), BF16)]
         + [struct((size_x,) + plane, BF16)] * 2
-        + [struct((y_planes,) + plane, BF16)] * y_sides,
+        + [face] * 2
+        + [y_face] * y_sides,
     )(jnp.concatenate([inputs, noise], axis=0))
-    token, *faces = call(
-        functools.partial(pack_corners, y_sides),
-        [struct((8, 128), F32)]
-        + [struct((3,) + plane, BF16)] * 2
-        + [struct((160, 128), BF16)] * (2 * y_sides),
-    )(field, wide_noise)
-    faces[2:2] = face_y
+    corners = call(functools.partial(pack_corners, y_sides), [struct((160, 128), BF16)] * (2 * y_sides))(*faces)
+    faces = [*faces, *corners]
     moves = [[("gx", side)] for side in range(2)]
     moves += [[("gy", side)] for side in range(y_sides)]
     moves += [[("gx", side), ("gy", k)] for k in range(y_sides) for side in range(2)]
@@ -535,10 +578,9 @@
         spread_weights,
         [struct((9 * 256, 256), BF16), struct((9 * 256, 256), BF16), struct((9, C, 128), F32)],
         moved=4_000_000,
-    )(jnp.concatenate([w_first, w_second], axis=0), token)
-    order = [1, 0] + list(range(2, 2 + y_sides)) + list(range(2 + y_sides, len(moves)))[::-1]
-    *sent, a1, ab, second = lax.optimization_barrier((*[got[k] for k in order], a1, ab, second))
-    got = [sent[order.index(k)] for k in range(len(moves))]
+    )(jnp.concatenate([w_first, w_second], axis=0))
+    *near, a1, ab, second = lax.optimization_barrier((*got[:n_near], a1, ab, second))
+    got = [*call(functools.partial(sort_faces, y_sides), [face] * 2 + [y_face] * 2)(*near), *got[n_near:]]
 
     n_field, n_noise = size_x + 4, size_x + 2
     z_rows = -(-(2 * n_field + n_noise) // 16) * 16
@@ -547,33 +589,35 @@
     )(field, wide_noise, *got)
     z_got = [swap(face, [("gz", side)]) for side, face in enumerate((face_a, face_b))]
     pre_shape = (n_noise, size_z, 256)
-    xs, ns, pre = call(
+    slope_shape = (size_x, size_z, 256)
+    xs, pre, back, hidden, slope = call(
         functools.partial(widen, y_sides),
-        [struct((3, n_field, size_z, 256), BF16), struct((3,) + pre_shape, BF16), struct(pre_shape, F32)],
-        flops=1_000_000_000,
-    )(field, wide_noise, *got, a1)
-    *z_got, xs, ns, pre = lax.optimization_barrier((*z_got, xs, ns, pre))
-
-    slope_shape = (size_x, size_z, 256)
-    hidden, slope, xs_edge, ns_edge = call(
-        activate,
         [
+            struct((3, n_field, size_z, 256), BF16),
+            struct(pre_shape, F32),
+            struct(slope_shape, F32),
             struct((3,) + pre_shape, BF16),
             struct(slope_shape, F32),
+        ],
+        scratch=[pltpu.VMEM((3,) + pre_shape, BF16)],
+        flops=1_000_000_000,
+    )(field, wide_noise, *got, a1, ab)
+    *z_got, xs, pre, back, hidden, slope = lax.optimization_barrier((*z_got, xs, pre, back, hidden, slope))
+
+    hidden_edge, xs_edge, slope_rows, back_rows = call(
+        mend,
+        [
+            struct((4, n_noise, 16, 256), BF16),
             struct((2, n_field, 16, 256), BF16),
-            struct((2, n_noise, 16, 256), BF16),
+            struct((2 * n_field, 256), F32),
+            struct((2 * n_field, 256), F32),
         ],
-    )(pre, xs, ns, low, high, a1, *z_got)
-    pre_grad = call(
-        backward,
-        struct((lanes, size_x * size_z), BF16),
-        scratch=[pltpu.VMEM(slope_shape, F32)],
-        flops=1_000_000_000,
-    )(ns, ns_edge, slope, ab)
+    )(pre, hidden, xs, low, high, a1, ab, *z_got)
+    pre_grad = call(backward, struct((lanes, size_x * size_z), BF16))(back, slope, slope_rows, back_rows)
 
     half = struct((C, 896), F32)
     rounded = struct((C, 896), BF16)
-    parts = (xs, xs_edge, hidden, pre_grad, noise_rows)
+    parts = (xs, xs_edge, hidden, hidden_edge, pre_grad, noise_rows)
     give = call(functools.partial(weight_grad, True), half, flops=1_000_000_000)(*parts)
     taken = flip(give, "gz", 1)
     keep = call(functools.partial(weight_grad, False), half, flops=1_000_000_000)(*parts)
@@ -584,7 +628,7 @@
         struct((size_x, lanes, size_z), BF16),
         scratch=[pltpu.VMEM((size_x, size_z, lanes), F32), pltpu.VMEM((9 * 256, 128), BF16)],
         flops=500_000_000,
-    )(hidden, second)
+    )(hidden, hidden_edge, second)
     prediction = prediction_rows.reshape(size_x, size_y, channels, size_z).transpose(2, 0, 1, 3)[None]
 
     steps = []

time: 38.8 us -> 37.5 us (0.966)
  waiting for transfers between devices: 9.27 us -> 7.14 us
  starting transfers between devices: 18.2 us -> 19.2 us
    ppermute x13, waiting for transfers between devices: 7.38 us -> 5.26 us  [permute(): lax.ppermute(x, AXES, [(number(place), number(to)) for place, to in targe...]
    ppermute x13, starting transfers between devices: 18 us -> 18.9 us  [permute(): lax.ppermute(x, AXES, [(number(place), number(to)) for place, to in targe...]
    pallas_call x3 -> x4, Pallas kernels: 1.79 us -> 0.86 us  [the longest x1 0.4 us: local(): call(mend, [struct((4, n_noise, 16, 256), BF16), struct((2, n_field, 16,...]
    pallas_call x1, Pallas kernels: 1.19 us -> 1.98 us  [local(): call(functools.partial(widen, y_sides), [struct((3, n_field, size_z, 256)...]
  transfers between devices with their start and end apart: 15 -> 15, of which waited for: 8 -> 9; matrix products, arithmetic and copies ran while one was open for 4% -> 4% of each run, Pallas kernels for 10% -> 13%
where the time goes in v5:
time: 37.5 us; the launch traced here: 37.3 us
  starting transfers between devices  19.2 us (51%)
  Pallas kernels  7.5 us (20%)
  waiting for transfers between devices  7.14 us (19%)
  other arithmetic  2.02 us (5%)
  between operations  0.78 us (2%)
  local copies, waits for them, and re-layouts  0.72 us (2%)
    ppermute x13, starting transfers between devices, permute(): lax.ppermute(x, AXES, [(number(place), number(to)) for place, to in targe...  18.9 us
    ppermute x13, waiting for transfers between devices, permute(): lax.ppermute(x, AXES, [(number(place), number(to)) for place, to in targe...  5.26 us
    pallas_call x1, Pallas kernels, local(): call(functools.partial(widen, y_sides), [struct((3, n_field, size_z, 256)...  1.98 us
    ppermute x2, waiting for transfers between devices, flip(): return lax.ppermute(x, axis, [(i, i ^ bit) for i in range(size)])  1.88 us
    concatenate x1, other arithmetic, local(): jnp.concatenate([inputs, noise], axis=0)  1.16 us
    pallas_call x1, Pallas kernels, local(): call(spread_weights, [struct((9 * 256, 256), BF16), struct((9 * 256, 256)...  1.05 us
    pallas_call x1, Pallas kernels, local(): call(predict, struct((size_x, lanes, size_z), BF16), scratch=[pltpu.VMEM(...  0.92 us
    concatenate x1, other arithmetic, local(): jnp.concatenate([w_first, w_second], axis=0)  0.86 us
  transfers between devices with their start and end apart: 15, of which 9 were waited for; matrix products, arithmetic and copies ran while one was open for 4% of the time, Pallas kernels for 13%

profile of v5, /device:TPU:0, one launch (start us, length us, event | category | flops | bytes accessed | tf_op | source)
XLA Modules:
  0.0 37.3 jit_solution(14955901866309931978)
XLA Ops:
  0.6 1.2 %pad_maximum_fusion.raw_ref = bf16[2,32,4,4,128]{4,3,2,1,0:T(4,128)(2,1)S(1)} fusion(bf16[1,32,4,4,128]{4,3,2,1,0:T(4,128)(2,1)} %param.5, bf16[1,32,4,4,128]{4,3,2,1,0:T(4,128)(2,1)} %param.4), kind=kLoop, calls=%fused_computation | loop fusion | flops 131072 | bytes 524288 | tf_op jit(solution)/shard_map/concatenate | solution.py:569
  1.8 0.5 %shard_map.67 = (bf16[4,128,128]{2,1,0:T(8,128)(2,1)S(1)}, bf16[4,128,128]{2,1,0:T(8,128)(2,1)S(1)}, bf16[4,128,128]{2,1,0:T(8,128)(2,1)S(1)}, bf16[3,128,128]{2...) custom-call(bf16[2,32,4,4,128]{4,3,2,1,0:T(4,128)(2,1)S(1)} %pad_maximum_fusion.raw_ref), custom_call_target="tpu_custom_call" | custom-call | flops 1000000 | bytes 1000000 | tf_op jit(solution)/shard_map/pallas_call | solution.py:563
  2.3 3.1 %collective-permute-start = (bf16[3,128,128]{2,1,0:T(8,128)(2,1)S(1)}, bf16[3,128,128]{2,1,0:T(8,128)(2,1)S(1)}, u32[]{:S(2)}, u32[]{:S(2)}) collective-permute-start(bf16[3,128,128]{2,1,0:T(8,128)(2,1)S(1)} %get-tuple-element.52.face_0), channel_id=1, source_target_pairs={{0,8},{1,9},{2,10},{3,11},{4,12},{5,13},{6,14},{7,15},{8,0},{9,1},... | collective-permute-start | bytes 294920 | tf_op jit(solution)/shard_map/ppermute | solution.py:51
  5.4 1.5 %collective-permute-start.1 = (bf16[3,128,128]{2,1,0:T(8,128)(2,1)S(1)}, bf16[3,128,128]{2,1,0:T(8,128)(2,1)S(1)}, u32[]{:S(2)}, u32[]{:S(2)}) collective-permute-start(bf16[3,128,128]{2,1,0:T(8,128)(2,1)S(1)} %get-tuple-element.53.face_1), channel_id=1, source_target_pairs={{8,16},{9,17},{10,18},{11,19},{12,20},{13,21},{14,22},{15,23},{16,... | collective-permute-start | bytes 294920 | tf_op jit(solution)/shard_map/ppermute | solution.py:51
  6.9 1.5 %collective-permute-start.2 = (bf16[3,128,128]{2,1,0:T(8,128)(2,1)S(1)}, bf16[3,128,128]{2,1,0:T(8,128)(2,1)S(1)}, u32[]{:S(2)}, u32[]{:S(2)}) collective-permute-start(bf16[3,128,128]{2,1,0:T(8,128)(2,1)S(1)} %get-tuple-element.54.refs_0_), channel_id=1, source_target_pairs={{0,4},{1,5},{2,6},{3,7},{4,0},{5,1},{6,2},{7,3},{8,12},{9,13},{10,... | collective-permute-start | bytes 294920 | tf_op jit(solution)/shard_map/ppermute | solution.py:51
  8.4 0.2 shard_map.70
  8.6 1.7 %collective-permute-start.3 = (bf16[160,128]{1,0:T(8,128)(2,1)S(1)}, bf16[160,128]{1,0:T(8,128)(2,1)S(1)}, u32[]{:S(2)}, u32[]{:S(2)}) collective-permute-start(bf16[160,128]{1,0:T(8,128)(2,1)S(1)} %get-tuple-element.65), channel_id=1, source_target_pairs={{0,12},{1,13},{2,14},{3,15},{4,8},{5,9},{6,10},{7,11},{8,4},{9,5},... | collective-permute-start | bytes 122888 | tf_op jit(solution)/shard_map/ppermute | solution.py:51
  10.3 1.5 %collective-permute-start.4 = (bf16[160,128]{1,0:T(8,128)(2,1)S(1)}, bf16[160,128]{1,0:T(8,128)(2,1)S(1)}, u32[]{:S(2)}, u32[]{:S(2)}) collective-permute-start(bf16[160,128]{1,0:T(8,128)(2,1)S(1)} %get-tuple-element.66), channel_id=1, source_target_pairs={{8,20},{9,21},{10,22},{11,23},{12,16},{13,17},{14,18},{15,19},{16,... | collective-permute-start | bytes 122888 | tf_op jit(solution)/shard_map/ppermute | solution.py:51
  11.8 0.9 %pad_maximum_fusion.1.both_ref = bf16[64,864]{1,0:T(8,128)(2,1)S(1)} fusion(bf16[32,864]{1,0:T(8,128)(2,1)} %param.7, bf16[32,864]{1,0:T(8,128)(2,1)} %param.6), kind=kLoop, calls=%fused_computation.2 | loop fusion | flops 221184 | bytes 221184 | tf_op jit(solution)/shard_map/concatenate | solution.py:581
  12.7 1.0 %shard_map.68 = (bf16[2304,256]{1,0:T(8,128)(2,1)S(1)}, bf16[2304,256]{1,0:T(8,128)(2,1)S(1)}, f32[9,32,128]{2,1,0:T(8,128)S(1)}) custom-call(bf16[64,864]{1,0:T(8,128)(2,1)S(1)} %pad_maximum_fusion.1.both_ref), custom_call_target="tpu_custom_call" | custom-call | flops 1000000 | bytes 4000000 | tf_op jit(solution)/shard_map/pallas_call | solution.py:577
  13.7 0.0 collective-permute-done.refs_0_
  13.7 0.0 collective-permute-done.1.refs_1_
  13.7 0.0 collective-permute-done.2.refs_2_
  13.8 0.1 shard_map.69
  13.9 0.0 collective-permute-done.3.refs_6_
  13.9 0.4 %collective-permute-done.4.refs_7_ = bf16[160,128]{1,0:T(8,128)(2,1)S(1)} collective-permute-done((bf16[160,128]{1,0:T(8,128)(2,1)S(1)}, bf16[160,128]{1,0:T(8,128)(2,1)S(1)}, u32[]{:S(2)}, u32[]{:S(2)}) %collective-permute-start.4) | collective-permute-done | bytes 40992 | tf_op jit(solution)/shard_map/ppermute | solution.py:51
  14.3 0.1 shard_map.71
  14.4 0.1 collective-permute-start.5
  14.5 1.6 %collective-permute-start.6 = (bf16[32,256]{1,0:T(8,128)(2,1)S(1)}, bf16[32,256]{1,0:T(8,128)(2,1)S(1)}, u32[]{:S(2)}, u32[]{:S(2)}) collective-permute-start(bf16[32,256]{1,0:T(8,128)(2,1)S(1)} %get-tuple-element.68), channel_id=1, source_target_pairs={{1,2},{2,1},{5,6},{6,5},{9,10},{10,9},{13,14},{14,13},{17,18},{18,... | collective-permute-start | bytes 49160 | tf_op jit(solution)/shard_map/ppermute | solution.py:51
  16.1 2.0 %shard_map.72 = (bf16[3,8,128,256]{3,2,1,0:T(8,128)(2,1)S(1)}, f32[6,128,256]{2,1,0:T(8,128)S(1)}, f32[4,128,256]{2,1,0:T(8,128)S(1)}, bf16[3,6,128,256]{3,2,1,0:T(8,128)(2,1)S(1)}, f32[4,128,256]{2,1,0:T(8,128)S(1)}) custom-call(bf16[4,128,128]{2,1,0:T(8,128)(2,1)S(1)} %get-tuple-element.50.refs_0_, bf16[4,128,128]{2,1,0:T(8,128)(2,1)S(1)} %get-tuple-element.51.refs_1_, ...), custom_call_target="tpu_custom_call" | custom-call | flops 1000000000 | bytes 1000000 | tf_op jit(solution)/shard_map/pallas_call | solution.py:593
  18.1 0.0 collective-permute-done.5.side_0
  18.1 0.2 collective-permute-done.6.side_1
  18.3 0.4 %shard_map.73 = (bf16[4,6,16,256]{3,2,1,0:T(8,128)(2,1)S(1)}, bf16[2,8,16,256]{3,2,1,0:T(8,128)(2,1)S(1)}, f32[16,256]{1,0:T(8,128)S(1)}, f32[16,256]{1,0:T(8,128)S(1)}) custom-call(f32[6,128,256]{2,1,0:T(8,128)S(1)} %get-tuple-element.77.pre_ref, bf16[3,6,128,256]{3,2,1,0:T(8,128)(2,1)S(1)} %get-tuple-element.78.hid_ref, ...), custom_call_target="tpu_custom_call" | custom-call | flops 1000000 | bytes 1000000 | tf_op jit(solution)/shard_map/pallas_call | solution.py:607
  18.7 0.1 shard_map.74.pre_grad_ref
  18.8 0.7 %shard_map.76 = f32[32,896]{1,0:T(8,128)S(1)} custom-call(bf16[3,8,128,256]{3,2,1,0:T(8,128)(2,1)S(1)} %get-tuple-element.76.wide_field_ref.xs_ref, bf16[2,8,16,256]{3,2,1,0:T(8,128)(2,1)S(1)} %get-tuple-element.83.xs_edge, bf16[3,6,128,256]{3,2,1,0:T(8,128)(2,1)S(1)} %get-tuple-element.78.hid_ref, bf16[4,6,16,256]{3,2,1,0:T(8,128)(2,1)S(1)} %get-tuple-element.84.hid_edge, ...), custom_call_target="tpu_custom_call" | custom-call | flops 1000000000 | bytes 1000000 | tf_op jit(solution)/shard_map/pallas_call | solution.py:621
  19.5 0.2 collective-permute-start.7
  19.7 0.6 %shard_map.75.keep_ref = f32[32,896]{1,0:T(8,128)S(1)} custom-call(bf16[3,8,128,256]{3,2,1,0:T(8,128)(2,1)S(1)} %get-tuple-element.76.wide_field_ref.xs_ref, bf16[2,8,16,256]{3,2,1,0:T(8,128)(2,1)S(1)} %get-tuple-element.83.xs_edge, bf16[3,6,128,256]{3,2,1,0:T(8,128)(2,1)S(1)} %get-tuple-element.78.hid_ref, ...), custom_call_target="tpu_custom_call" | custom-call | flops 1000000000 | bytes 1000000 | tf_op jit(solution)/shard_map/pallas_call | solution.py:623
  20.3 0.6 %collective-permute-done.7.taken_ref = f32[32,896]{1,0:T(8,128)S(1)} collective-permute-done((f32[32,896]{1,0:T(8,128)S(1)}, f32[32,896]{1,0:T(8,128)S(1)}, u32[]{:S(2)}, u32[]{:S(2)}) %collective-permute-start.7) | collective-permute-done | bytes 114720 | tf_op jit(solution)/shard_map/ppermute | solution.py:537
  20.9 1.8 %collective-permute-start.10 = (bf16[32,896]{1,0:T(8,128)(2,1)S(1)}, bf16[32,896]{1,0:T(8,128)(2,1)S(1)}, u32[]{:S(2)}, u32[]{:S(2)}) collective-permute-start(bf16[32,896]{1,0:T(8,128)(2,1)S(1)} %shard_map.77.own_ref), channel_id=1, source_target_pairs={{0,24},{1,7},{2,26},{3,5},{4,28},{5,3},{6,30},{7,1},{8,16},{9,15},... | collective-permute-start | bytes 172040 | tf_op jit(solution)/shard_map/ppermute | solution.py:51
  22.8 1.1 %collective-permute-start.9 = (bf16[32,896]{1,0:T(8,128)(2,1)S(1)}, bf16[32,896]{1,0:T(8,128)(2,1)S(1)}, u32[]{:S(2)}, u32[]{:S(2)}) collective-permute-start(bf16[32,896]{1,0:T(8,128)(2,1)S(1)} %shard_map.77.own_ref), channel_id=1, source_target_pairs={{0,16},{1,5},{2,18},{3,7},{4,20},{5,1},{6,22},{7,3},{8,24},{9,13},... | collective-permute-start | bytes 172040 | tf_op jit(solution)/shard_map/ppermute | solution.py:51
  23.8 1.6 %collective-permute-start.8 = (bf16[32,896]{1,0:T(8,128)(2,1)S(1)}, bf16[32,896]{1,0:T(8,128)(2,1)S(1)}, u32[]{:S(2)}, u32[]{:S(2)}) collective-permute-start(bf16[32,896]{1,0:T(8,128)(2,1)S(1)} %shard_map.77.own_ref), channel_id=1, source_target_pairs={{0,8},{1,3},{2,10},{3,1},{4,12},{5,7},{6,14},{7,5},{8,0},{9,11},{1... | collective-permute-start | bytes 172040 | tf_op jit(solution)/shard_map/ppermute | solution.py:51
  25.4 0.9 %shard_map.78 = bf16[4,128,128]{2,1,0:T(8,128)(2,1)S(1)} custom-call(bf16[3,6,128,256]{3,2,1,0:T(8,128)(2,1)S(1)} %get-tuple-element.78.hid_ref, bf16[4,6,16,256]{3,2,1,0:T(8,128)(2,1)S(1)} %get-tuple-element.84.hid_edge, f32[9,32,128]{2,1,0:T(8,128)S(1)} %get-tuple-element.90.second_ref), custom_call_target="tpu_custom_call" | custom-call | flops 500000000 | bytes 1000000 | tf_op jit(solution)/shard_map/pallas_call | solution.py:626
  26.3 0.7 %copy.9 = bf16[4,4,32,128]{3,1,0,2:T(4,128)(2,1)} copy(bf16[4,4,32,128]{3,2,1,0:T(8,128)(2,1)S(1)} %bitcast.6) | data formatting | bytes 262144 | tf_op jit(solution)/shard_map/reshape | solution.py:632
  27.0 0.0 collective-permute-done.10.refs_2_
  27.0 0.9 %collective-permute-done.9.refs_1_ = bf16[32,896]{1,0:T(8,128)(2,1)S(1)} collective-permute-done((bf16[32,896]{1,0:T(8,128)(2,1)S(1)}, bf16[32,896]{1,0:T(8,128)(2,1)S(1)}, u32[]{:S(2)}, u32[]{:S(2)}) %collective-permute-start.9) | collective-permute-done | bytes 57376 | tf_op jit(solution)/shard_map/ppermute | solution.py:51
  27.9 0.6 %collective-permute-done.8.refs_0_ = bf16[32,896]{1,0:T(8,128)(2,1)S(1)} collective-permute-done((bf16[32,896]{1,0:T(8,128)(2,1)S(1)}, bf16[32,896]{1,0:T(8,128)(2,1)S(1)}, u32[]{:S(2)}, u32[]{:S(2)}) %collective-permute-start.8) | collective-permute-done | bytes 57376 | tf_op jit(solution)/shard_map/ppermute | solution.py:51
  28.5 1.7 %collective-permute-start.13 = (bf16[32,896]{1,0:T(8,128)(2,1)S(1)}, bf16[32,896]{1,0:T(8,128)(2,1)S(1)}, u32[]{:S(2)}, u32[]{:S(2)}) collective-permute-start(bf16[32,896]{1,0:T(8,128)(2,1)S(1)} %shard_map.79.own_ref), channel_id=1, source_target_pairs={{0,6},{1,25},{2,4},{3,27},{4,2},{5,29},{6,0},{7,31},{8,14},{9,17},... | collective-permute-start | bytes 172040 | tf_op jit(solution)/shard_map/ppermute | solution.py:51
  30.2 0.9 %collective-permute-start.12 = (bf16[32,896]{1,0:T(8,128)(2,1)S(1)}, bf16[32,896]{1,0:T(8,128)(2,1)S(1)}, u32[]{:S(2)}, u32[]{:S(2)}) collective-permute-start(bf16[32,896]{1,0:T(8,128)(2,1)S(1)} %shard_map.79.own_ref), channel_id=1, source_target_pairs={{0,4},{1,17},{2,6},{3,19},{4,0},{5,21},{6,2},{7,23},{8,12},{9,25},... | collective-permute-start | bytes 172040 | tf_op jit(solution)/shard_map/ppermute | solution.py:51
  31.0 1.0 %collective-permute-start.11 = (bf16[32,896]{1,0:T(8,128)(2,1)S(1)}, bf16[32,896]{1,0:T(8,128)(2,1)S(1)}, u32[]{:S(2)}, u32[]{:S(2)}) collective-permute-start(bf16[32,896]{1,0:T(8,128)(2,1)S(1)} %shard_map.79.own_ref), channel_id=1, source_target_pairs={{0,2},{1,9},{2,0},{3,11},{4,6},{5,13},{6,4},{7,15},{8,10},{9,1},{1... | collective-permute-start | bytes 172040 | tf_op jit(solution)/shard_map/ppermute | solution.py:51
  32.0 1.6 %collective-permute-done.13.refs_2_ = bf16[32,896]{1,0:T(8,128)(2,1)S(1)} collective-permute-done((bf16[32,896]{1,0:T(8,128)(2,1)S(1)}, bf16[32,896]{1,0:T(8,128)(2,1)S(1)}, u32[]{:S(2)}, u32[]{:S(2)}) %collective-permute-start.13) | collective-permute-done | bytes 57376 | tf_op jit(solution)/shard_map/ppermute | solution.py:51
  33.6 0.7 %collective-permute-done.12.refs_1_ = bf16[32,896]{1,0:T(8,128)(2,1)S(1)} collective-permute-done((bf16[32,896]{1,0:T(8,128)(2,1)S(1)}, bf16[32,896]{1,0:T(8,128)(2,1)S(1)}, u32[]{:S(2)}, u32[]{:S(2)}) %collective-permute-start.12) | collective-permute-done | bytes 57376 | tf_op jit(solution)/shard_map/ppermute | solution.py:51
  34.3 0.9 %collective-permute-done.11.refs_0_ = bf16[32,896]{1,0:T(8,128)(2,1)S(1)} collective-permute-done((bf16[32,896]{1,0:T(8,128)(2,1)S(1)}, bf16[32,896]{1,0:T(8,128)(2,1)S(1)}, u32[]{:S(2)}, u32[]{:S(2)}) %collective-permute-start.11) | collective-permute-done | bytes 57376 | tf_op jit(solution)/shard_map/ppermute | solution.py:51
  35.2 0.1 collective-permute-start.14
  35.3 1.3 %collective-permute-done.14.other_ref = f32[32,896]{1,0:T(8,128)S(1)} collective-permute-done((f32[32,896]{1,0:T(8,128)S(1)}, f32[32,896]{1,0:T(8,128)S(1)}, u32[]{:S(2)}, u32[]{:S(2)}) %collective-permute-start.14) | collective-permute-done | bytes 114720 | tf_op jit(solution)/shard_map/ppermute | solution.py:537
  36.6 0.7 %shard_map.81 = (f32[32,864]{1,0:T(8,128)}, f32[32,864]{1,0:T(8,128)}) custom-call(f32[32,896]{1,0:T(8,128)S(1)} %shard_map.80.mine_ref, f32[32,896]{1,0:T(8,128)S(1)} %collective-permute-done.14.other_ref), custom_call_target="tpu_custom_call" | custom-call | flops 1000000 | bytes 1000000 | tf_op jit(solution)/shard_map/pallas_call | solution.py:653
  (3 shorter events, 0.1 us)
Async XLA Ops:
  2.3 11.5 %collective-permute-start = (bf16[3,128,128]{2,1,0:T(8,128)(2,1)S(1)}, bf16[3,128,128]{2,1,0:T(8,128)(2,1)S(1)}, u32[]{:S(2)}, u32[]{:S(2)}) collective-permute-start(bf16[3,128,128]{2,1,0:T(8,128)(2,1)S(1)} %get-tuple-element.52.face_0), channel_id=1, source_target_pairs={{0,8},{1,9},{2,10},{3,11},{4,12},{5,13},{6,14},{7,15},{8,0},{9,1},... | collective-permute-start | bytes 294920 | tf_op jit(solution)/shard_map/ppermute | solution.py:51
  5.4 8.4 %collective-permute-start.1 = (bf16[3,128,128]{2,1,0:T(8,128)(2,1)S(1)}, bf16[3,128,128]{2,1,0:T(8,128)(2,1)S(1)}, u32[]{:S(2)}, u32[]{:S(2)}) collective-permute-start(bf16[3,128,128]{2,1,0:T(8,128)(2,1)S(1)} %get-tuple-element.53.face_1), channel_id=1, source_target_pairs={{8,16},{9,17},{10,18},{11,19},{12,20},{13,21},{14,22},{15,23},{16,... | collective-permute-start | bytes 294920 | tf_op jit(solution)/shard_map/ppermute | solution.py:51
  6.9 6.9 %collective-permute-start.2 = (bf16[3,128,128]{2,1,0:T(8,128)(2,1)S(1)}, bf16[3,128,128]{2,1,0:T(8,128)(2,1)S(1)}, u32[]{:S(2)}, u32[]{:S(2)}) collective-permute-start(bf16[3,128,128]{2,1,0:T(8,128)(2,1)S(1)} %get-tuple-element.54.refs_0_), channel_id=1, source_target_pairs={{0,4},{1,5},{2,6},{3,7},{4,0},{5,1},{6,2},{7,3},{8,12},{9,13},{10,... | collective-permute-start | bytes 294920 | tf_op jit(solution)/shard_map/ppermute | solution.py:51
  8.6 5.3 %collective-permute-start.3 = (bf16[160,128]{1,0:T(8,128)(2,1)S(1)}, bf16[160,128]{1,0:T(8,128)(2,1)S(1)}, u32[]{:S(2)}, u32[]{:S(2)}) collective-permute-start(bf16[160,128]{1,0:T(8,128)(2,1)S(1)} %get-tuple-element.65), channel_id=1, source_target_pairs={{0,12},{1,13},{2,14},{3,15},{4,8},{5,9},{6,10},{7,11},{8,4},{9,5},... | collective-permute-start | bytes 122888 | tf_op jit(solution)/shard_map/ppermute | solution.py:51
  10.3 4.0 %collective-permute-start.4 = (bf16[160,128]{1,0:T(8,128)(2,1)S(1)}, bf16[160,128]{1,0:T(8,128)(2,1)S(1)}, u32[]{:S(2)}, u32[]{:S(2)}) collective-permute-start(bf16[160,128]{1,0:T(8,128)(2,1)S(1)} %get-tuple-element.66), channel_id=1, source_target_pairs={{8,20},{9,21},{10,22},{11,23},{12,16},{13,17},{14,18},{15,19},{16,... | collective-permute-start | bytes 122888 | tf_op jit(solution)/shard_map/ppermute | solution.py:51
  14.4 3.6 %collective-permute-start.5 = (bf16[32,256]{1,0:T(8,128)(2,1)S(1)}, bf16[32,256]{1,0:T(8,128)(2,1)S(1)}, u32[]{:S(2)}, u32[]{:S(2)}) collective-permute-start(bf16[32,256]{1,0:T(8,128)(2,1)S(1)} %get-tuple-element.67), channel_id=1, source_target_pairs={{0,1},{1,0},{2,3},{3,2},{4,5},{5,4},{6,7},{7,6},{8,9},{9,8},{10,11... | collective-permute-start | bytes 49160 | tf_op jit(solution)/shard_map/ppermute | solution.py:51
  14.5 3.8 %collective-permute-start.6 = (bf16[32,256]{1,0:T(8,128)(2,1)S(1)}, bf16[32,256]{1,0:T(8,128)(2,1)S(1)}, u32[]{:S(2)}, u32[]{:S(2)}) collective-permute-start(bf16[32,256]{1,0:T(8,128)(2,1)S(1)} %get-tuple-element.68), channel_id=1, source_target_pairs={{1,2},{2,1},{5,6},{6,5},{9,10},{10,9},{13,14},{14,13},{17,18},{18,... | collective-permute-start | bytes 49160 | tf_op jit(solution)/shard_map/ppermute | solution.py:51
  19.5 1.4 %collective-permute-start.7 = (f32[32,896]{1,0:T(8,128)S(1)}, f32[32,896]{1,0:T(8,128)S(1)}, u32[]{:S(2)}, u32[]{:S(2)}) collective-permute-start(f32[32,896]{1,0:T(8,128)S(1)} %shard_map.76), channel_id=1, source_target_pairs={{0,1},{1,0},{2,3},{3,2},{4,5},{5,4},{6,7},{7,6},{8,9},{9,8},{10,11... | collective-permute-start | bytes 344072 | tf_op jit(solution)/shard_map/ppermute | solution.py:537
  20.9 6.1 %collective-permute-start.10 = (bf16[32,896]{1,0:T(8,128)(2,1)S(1)}, bf16[32,896]{1,0:T(8,128)(2,1)S(1)}, u32[]{:S(2)}, u32[]{:S(2)}) collective-permute-start(bf16[32,896]{1,0:T(8,128)(2,1)S(1)} %shard_map.77.own_ref), channel_id=1, source_target_pairs={{0,24},{1,7},{2,26},{3,5},{4,28},{5,3},{6,30},{7,1},{8,16},{9,15},... | collective-permute-start | bytes 172040 | tf_op jit(solution)/shard_map/ppermute | solution.py:51
  22.8 5.1 %collective-permute-start.9 = (bf16[32,896]{1,0:T(8,128)(2,1)S(1)}, bf16[32,896]{1,0:T(8,128)(2,1)S(1)}, u32[]{:S(2)}, u32[]{:S(2)}) collective-permute-start(bf16[32,896]{1,0:T(8,128)(2,1)S(1)} %shard_map.77.own_ref), channel_id=1, source_target_pairs={{0,16},{1,5},{2,18},{3,7},{4,20},{5,1},{6,22},{7,3},{8,24},{9,13},... | collective-permute-start | bytes 172040 | tf_op jit(solution)/shard_map/ppermute | solution.py:51
  23.8 4.6 %collective-permute-start.8 = (bf16[32,896]{1,0:T(8,128)(2,1)S(1)}, bf16[32,896]{1,0:T(8,128)(2,1)S(1)}, u32[]{:S(2)}, u32[]{:S(2)}) collective-permute-start(bf16[32,896]{1,0:T(8,128)(2,1)S(1)} %shard_map.77.own_ref), channel_id=1, source_target_pairs={{0,8},{1,3},{2,10},{3,1},{4,12},{5,7},{6,14},{7,5},{8,0},{9,11},{1... | collective-permute-start | bytes 172040 | tf_op jit(solution)/shard_map/ppermute | solution.py:51
  28.5 5.1 %collective-permute-start.13 = (bf16[32,896]{1,0:T(8,128)(2,1)S(1)}, bf16[32,896]{1,0:T(8,128)(2,1)S(1)}, u32[]{:S(2)}, u32[]{:S(2)}) collective-permute-start(bf16[32,896]{1,0:T(8,128)(2,1)S(1)} %shard_map.79.own_ref), channel_id=1, source_target_pairs={{0,6},{1,25},{2,4},{3,27},{4,2},{5,29},{6,0},{7,31},{8,14},{9,17},... | collective-permute-start | bytes 172040 | tf_op jit(solution)/shard_map/ppermute | solution.py:51
  30.2 4.2 %collective-permute-start.12 = (bf16[32,896]{1,0:T(8,128)(2,1)S(1)}, bf16[32,896]{1,0:T(8,128)(2,1)S(1)}, u32[]{:S(2)}, u32[]{:S(2)}) collective-permute-start(bf16[32,896]{1,0:T(8,128)(2,1)S(1)} %shard_map.79.own_ref), channel_id=1, source_target_pairs={{0,4},{1,17},{2,6},{3,19},{4,0},{5,21},{6,2},{7,23},{8,12},{9,25},... | collective-permute-start | bytes 172040 | tf_op jit(solution)/shard_map/ppermute | solution.py:51
  31.0 4.2 %collective-permute-start.11 = (bf16[32,896]{1,0:T(8,128)(2,1)S(1)}, bf16[32,896]{1,0:T(8,128)(2,1)S(1)}, u32[]{:S(2)}, u32[]{:S(2)}) collective-permute-start(bf16[32,896]{1,0:T(8,128)(2,1)S(1)} %shard_map.79.own_ref), channel_id=1, source_target_pairs={{0,2},{1,9},{2,0},{3,11},{4,6},{5,13},{6,4},{7,15},{8,10},{9,1},{1... | collective-permute-start | bytes 172040 | tf_op jit(solution)/shard_map/ppermute | solution.py:51
  35.2 1.4 %collective-permute-start.14 = (f32[32,896]{1,0:T(8,128)S(1)}, f32[32,896]{1,0:T(8,128)S(1)}, u32[]{:S(2)}, u32[]{:S(2)}) collective-permute-start(f32[32,896]{1,0:T(8,128)S(1)} %shard_map.80.mine_ref), channel_id=1, source_target_pairs={{0,1},{1,0},{2,3},{3,2},{4,5},{5,4},{6,7},{7,6},{8,9},{9,8},{10,11... | collective-permute-start | bytes 344072 | tf_op jit(solution)/shard_map/ppermute | solution.py:537

commit v6 on v5

--- a/solution.py
+++ b/solution.py
@@ -579,7 +579,8 @@
         [struct((9 * 256, 256), BF16), struct((9 * 256, 256), BF16), struct((9, C, 128), F32)],
         moved=4_000_000,
     )(jnp.concatenate([w_first, w_second], axis=0))
-    *near, a1, ab, second = lax.optimization_barrier((*got[:n_near], a1, ab, second))
+    *near, a1, ab, second = lax.optimization_barrier((*got[2:n_near], *got[:2], a1, ab, second))
+    near = [*near[y_sides:], *near[:y_sides]]
     got = [*call(functools.partial(sort_faces, y_sides), [face] * 2 + [y_face] * 2)(*near), *got[n_near:]]
 
     n_field, n_noise = size_x + 4, size_x + 2

time: 37.5 us -> 37.5 us (level)
  no operation moved by 1% of the time
where the time goes in v6:
time: 37.5 us; the launch traced here: 37.3 us
  starting transfers between devices  19.2 us (51%)
  Pallas kernels  7.5 us (20%)
  waiting for transfers between devices  7.14 us (19%)
  other arithmetic  2.02 us (5%)
  between operations  0.78 us (2%)
  local copies, waits for them, and re-layouts  0.72 us (2%)
    ppermute x13, starting transfers between devices, permute(): lax.ppermute(x, AXES, [(number(place), number(to)) for place, to in targe...  18.9 us
    ppermute x13, waiting for transfers between devices, permute(): lax.ppermute(x, AXES, [(number(place), number(to)) for place, to in targe...  5.26 us
    pallas_call x1, Pallas kernels, local(): call(functools.partial(widen, y_sides), [struct((3, n_field, size_z, 256)...  1.98 us
    ppermute x2, waiting for transfers between devices, flip(): return lax.ppermute(x, axis, [(i, i ^ bit) for i in range(size)])  1.88 us
    concatenate x1, other arithmetic, local(): jnp.concatenate([inputs, noise], axis=0)  1.16 us
    pallas_call x1, Pallas kernels, local(): call(spread_weights, [struct((9 * 256, 256), BF16), struct((9 * 256, 256)...  1.05 us
    pallas_call x1, Pallas kernels, local(): call(predict, struct((size_x, lanes, size_z), BF16), scratch=[pltpu.VMEM(...  0.92 us
    concatenate x1, other arithmetic, local(): jnp.concatenate([w_first, w_second], axis=0)  0.86 us
  transfers between devices with their start and end apart: 15, of which 9 were waited for; matrix products, arithmetic and copies ran while one was open for 4% of the time, Pallas kernels for 13%

profile of v6, /device:TPU:0, one launch (start us, length us, event | category | flops | bytes accessed | tf_op | source)
XLA Modules:
  0.0 37.3 jit_solution(2839083211807002629)
XLA Ops:
  0.6 1.2 %pad_maximum_fusion.raw_ref = bf16[2,32,4,4,128]{4,3,2,1,0:T(4,128)(2,1)S(1)} fusion(bf16[1,32,4,4,128]{4,3,2,1,0:T(4,128)(2,1)} %param.5, bf16[1,32,4,4,128]{4,3,2,1,0:T(4,128)(2,1)} %param.4), kind=kLoop, calls=%fused_computation | loop fusion | flops 131072 | bytes 524288 | tf_op jit(solution)/shard_map/concatenate | solution.py:569
  1.8 0.5 %shard_map.67 = (bf16[4,128,128]{2,1,0:T(8,128)(2,1)S(1)}, bf16[4,128,128]{2,1,0:T(8,128)(2,1)S(1)}, bf16[4,128,128]{2,1,0:T(8,128)(2,1)S(1)}, bf16[3,128,128]{2...) custom-call(bf16[2,32,4,4,128]{4,3,2,1,0:T(4,128)(2,1)S(1)} %pad_maximum_fusion.raw_ref), custom_call_target="tpu_custom_call" | custom-call | flops 1000000 | bytes 1000000 | tf_op jit(solution)/shard_map/pallas_call | solution.py:563
  2.3 3.0 %collective-permute-start = (bf16[3,128,128]{2,1,0:T(8,128)(2,1)S(1)}, bf16[3,128,128]{2,1,0:T(8,128)(2,1)S(1)}, u32[]{:S(2)}, u32[]{:S(2)}) collective-permute-start(bf16[3,128,128]{2,1,0:T(8,128)(2,1)S(1)} %get-tuple-element.52.refs_0_), channel_id=1, source_target_pairs={{0,4},{1,5},{2,6},{3,7},{4,0},{5,1},{6,2},{7,3},{8,12},{9,13},{10,... | collective-permute-start | bytes 294920 | tf_op jit(solution)/shard_map/ppermute | solution.py:51
  5.3 1.6 %collective-permute-start.1 = (bf16[3,128,128]{2,1,0:T(8,128)(2,1)S(1)}, bf16[3,128,128]{2,1,0:T(8,128)(2,1)S(1)}, u32[]{:S(2)}, u32[]{:S(2)}) collective-permute-start(bf16[3,128,128]{2,1,0:T(8,128)(2,1)S(1)} %get-tuple-element.53.face_0), channel_id=1, source_target_pairs={{0,8},{1,9},{2,10},{3,11},{4,12},{5,13},{6,14},{7,15},{8,0},{9,1},... | collective-permute-start | bytes 294920 | tf_op jit(solution)/shard_map/ppermute | solution.py:51
  6.9 1.5 %collective-permute-start.2 = (bf16[3,128,128]{2,1,0:T(8,128)(2,1)S(1)}, bf16[3,128,128]{2,1,0:T(8,128)(2,1)S(1)}, u32[]{:S(2)}, u32[]{:S(2)}) collective-permute-start(bf16[3,128,128]{2,1,0:T(8,128)(2,1)S(1)} %get-tuple-element.54.face_1), channel_id=1, source_target_pairs={{8,16},{9,17},{10,18},{11,19},{12,20},{13,21},{14,22},{15,23},{16,... | collective-permute-start | bytes 294920 | tf_op jit(solution)/shard_map/ppermute | solution.py:51
  8.4 0.2 shard_map.70
  8.6 1.7 %collective-permute-start.3 = (bf16[160,128]{1,0:T(8,128)(2,1)S(1)}, bf16[160,128]{1,0:T(8,128)(2,1)S(1)}, u32[]{:S(2)}, u32[]{:S(2)}) collective-permute-start(bf16[160,128]{1,0:T(8,128)(2,1)S(1)} %get-tuple-element.65), channel_id=1, source_target_pairs={{0,12},{1,13},{2,14},{3,15},{4,8},{5,9},{6,10},{7,11},{8,4},{9,5},... | collective-permute-start | bytes 122888 | tf_op jit(solution)/shard_map/ppermute | solution.py:51
  10.3 1.5 %collective-permute-start.4 = (bf16[160,128]{1,0:T(8,128)(2,1)S(1)}, bf16[160,128]{1,0:T(8,128)(2,1)S(1)}, u32[]{:S(2)}, u32[]{:S(2)}) collective-permute-start(bf16[160,128]{1,0:T(8,128)(2,1)S(1)} %get-tuple-element.66), channel_id=1, source_target_pairs={{8,20},{9,21},{10,22},{11,23},{12,16},{13,17},{14,18},{15,19},{16,... | collective-permute-start | bytes 122888 | tf_op jit(solution)/shard_map/ppermute | solution.py:51
  11.8 0.9 %pad_maximum_fusion.1.both_ref = bf16[64,864]{1,0:T(8,128)(2,1)S(1)} fusion(bf16[32,864]{1,0:T(8,128)(2,1)} %param.7, bf16[32,864]{1,0:T(8,128)(2,1)} %param.6), kind=kLoop, calls=%fused_computation.2 | loop fusion | flops 221184 | bytes 221184 | tf_op jit(solution)/shard_map/concatenate | solution.py:581
  12.7 1.0 %shard_map.68 = (bf16[2304,256]{1,0:T(8,128)(2,1)S(1)}, bf16[2304,256]{1,0:T(8,128)(2,1)S(1)}, f32[9,32,128]{2,1,0:T(8,128)S(1)}) custom-call(bf16[64,864]{1,0:T(8,128)(2,1)S(1)} %pad_maximum_fusion.1.both_ref), custom_call_target="tpu_custom_call" | custom-call | flops 1000000 | bytes 4000000 | tf_op jit(solution)/shard_map/pallas_call | solution.py:577
  13.7 0.0 collective-permute-done.refs_2_
  13.7 0.0 collective-permute-done.1.refs_0_
  13.7 0.0 collective-permute-done.2.refs_1_
  13.8 0.1 shard_map.69
  13.9 0.0 collective-permute-done.3.refs_6_
  13.9 0.4 %collective-permute-done.4.refs_7_ = bf16[160,128]{1,0:T(8,128)(2,1)S(1)} collective-permute-done((bf16[160,128]{1,0:T(8,128)(2,1)S(1)}, bf16[160,128]{1,0:T(8,128)(2,1)S(1)}, u32[]{:S(2)}, u32[]{:S(2)}) %collective-permute-start.4) | collective-permute-done | bytes 40992 | tf_op jit(solution)/shard_map/ppermute | solution.py:51
  14.3 0.1 shard_map.71
  14.4 0.1 collective-permute-start.5
  14.5 1.6 %collective-permute-start.6 = (bf16[32,256]{1,0:T(8,128)(2,1)S(1)}, bf16[32,256]{1,0:T(8,128)(2,1)S(1)}, u32[]{:S(2)}, u32[]{:S(2)}) collective-permute-start(bf16[32,256]{1,0:T(8,128)(2,1)S(1)} %get-tuple-element.68), channel_id=1, source_target_pairs={{1,2},{2,1},{5,6},{6,5},{9,10},{10,9},{13,14},{14,13},{17,18},{18,... | collective-permute-start | bytes 49160 | tf_op jit(solution)/shard_map/ppermute | solution.py:51
  16.1 2.0 %shard_map.72 = (bf16[3,8,128,256]{3,2,1,0:T(8,128)(2,1)S(1)}, f32[6,128,256]{2,1,0:T(8,128)S(1)}, f32[4,128,256]{2,1,0:T(8,128)S(1)}, bf16[3,6,128,256]{3,2,1,0:T(8,128)(2,1)S(1)}, f32[4,128,256]{2,1,0:T(8,128)S(1)}) custom-call(bf16[4,128,128]{2,1,0:T(8,128)(2,1)S(1)} %get-tuple-element.50.refs_0_, bf16[4,128,128]{2,1,0:T(8,128)(2,1)S(1)} %get-tuple-element.51.refs_1_, ...), custom_call_target="tpu_custom_call" | custom-call | flops 1000000000 | bytes 1000000 | tf_op jit(solution)/shard_map/pallas_call | solution.py:594
  18.1 0.0 collective-permute-done.5.side_0
  18.1 0.2 collective-permute-done.6.side_1
  18.3 0.4 %shard_map.73 = (bf16[4,6,16,256]{3,2,1,0:T(8,128)(2,1)S(1)}, bf16[2,8,16,256]{3,2,1,0:T(8,128)(2,1)S(1)}, f32[16,256]{1,0:T(8,128)S(1)}, f32[16,256]{1,0:T(8,128)S(1)}) custom-call(f32[6,128,256]{2,1,0:T(8,128)S(1)} %get-tuple-element.77.pre_ref, bf16[3,6,128,256]{3,2,1,0:T(8,128)(2,1)S(1)} %get-tuple-element.78.hid_ref, ...), custom_call_target="tpu_custom_call" | custom-call | flops 1000000 | bytes 1000000 | tf_op jit(solution)/shard_map/pallas_call | solution.py:608
  18.7 0.1 shard_map.74.pre_grad_ref
  18.8 0.7 %shard_map.76 = f32[32,896]{1,0:T(8,128)S(1)} custom-call(bf16[3,8,128,256]{3,2,1,0:T(8,128)(2,1)S(1)} %get-tuple-element.76.wide_field_ref.xs_ref, bf16[2,8,16,256]{3,2,1,0:T(8,128)(2,1)S(1)} %get-tuple-element.83.xs_edge, bf16[3,6,128,256]{3,2,1,0:T(8,128)(2,1)S(1)} %get-tuple-element.78.hid_ref, bf16[4,6,16,256]{3,2,1,0:T(8,128)(2,1)S(1)} %get-tuple-element.84.hid_edge, ...), custom_call_target="tpu_custom_call" | custom-call | flops 1000000000 | bytes 1000000 | tf_op jit(solution)/shard_map/pallas_call | solution.py:622
  19.5 0.2 collective-permute-start.7
  19.7 0.6 %shard_map.75.keep_ref = f32[32,896]{1,0:T(8,128)S(1)} custom-call(bf16[3,8,128,256]{3,2,1,0:T(8,128)(2,1)S(1)} %get-tuple-element.76.wide_field_ref.xs_ref, bf16[2,8,16,256]{3,2,1,0:T(8,128)(2,1)S(1)} %get-tuple-element.83.xs_edge, bf16[3,6,128,256]{3,2,1,0:T(8,128)(2,1)S(1)} %get-tuple-element.78.hid_ref, ...), custom_call_target="tpu_custom_call" | custom-call | flops 1000000000 | bytes 1000000 | tf_op jit(solution)/shard_map/pallas_call | solution.py:624
  20.3 0.6 %collective-permute-done.7.taken_ref = f32[32,896]{1,0:T(8,128)S(1)} collective-permute-done((f32[32,896]{1,0:T(8,128)S(1)}, f32[32,896]{1,0:T(8,128)S(1)}, u32[]{:S(2)}, u32[]{:S(2)}) %collective-permute-start.7) | collective-permute-done | bytes 114720 | tf_op jit(solution)/shard_map/ppermute | solution.py:537
  20.9 1.8 %collective-permute-start.10 = (bf16[32,896]{1,0:T(8,128)(2,1)S(1)}, bf16[32,896]{1,0:T(8,128)(2,1)S(1)}, u32[]{:S(2)}, u32[]{:S(2)}) collective-permute-start(bf16[32,896]{1,0:T(8,128)(2,1)S(1)} %shard_map.77.own_ref), channel_id=1, source_target_pairs={{0,24},{1,7},{2,26},{3,5},{4,28},{5,3},{6,30},{7,1},{8,16},{9,15},... | collective-permute-start | bytes 172040 | tf_op jit(solution)/shard_map/ppermute | solution.py:51
  22.8 1.1 %collective-permute-start.9 = (bf16[32,896]{1,0:T(8,128)(2,1)S(1)}, bf16[32,896]{1,0:T(8,128)(2,1)S(1)}, u32[]{:S(2)}, u32[]{:S(2)}) collective-permute-start(bf16[32,896]{1,0:T(8,128)(2,1)S(1)} %shard_map.77.own_ref), channel_id=1, source_target_pairs={{0,16},{1,5},{2,18},{3,7},{4,20},{5,1},{6,22},{7,3},{8,24},{9,13},... | collective-permute-start | bytes 172040 | tf_op jit(solution)/shard_map/ppermute | solution.py:51
  23.8 1.6 %collective-permute-start.8 = (bf16[32,896]{1,0:T(8,128)(2,1)S(1)}, bf16[32,896]{1,0:T(8,128)(2,1)S(1)}, u32[]{:S(2)}, u32[]{:S(2)}) collective-permute-start(bf16[32,896]{1,0:T(8,128)(2,1)S(1)} %shard_map.77.own_ref), channel_id=1, source_target_pairs={{0,8},{1,3},{2,10},{3,1},{4,12},{5,7},{6,14},{7,5},{8,0},{9,11},{1... | collective-permute-start | bytes 172040 | tf_op jit(solution)/shard_map/ppermute | solution.py:51
  25.4 0.9 %shard_map.78 = bf16[4,128,128]{2,1,0:T(8,128)(2,1)S(1)} custom-call(bf16[3,6,128,256]{3,2,1,0:T(8,128)(2,1)S(1)} %get-tuple-element.78.hid_ref, bf16[4,6,16,256]{3,2,1,0:T(8,128)(2,1)S(1)} %get-tuple-element.84.hid_edge, f32[9,32,128]{2,1,0:T(8,128)S(1)} %get-tuple-element.90.second_ref), custom_call_target="tpu_custom_call" | custom-call | flops 500000000 | bytes 1000000 | tf_op jit(solution)/shard_map/pallas_call | solution.py:627
  26.3 0.7 %copy.9 = bf16[4,4,32,128]{3,1,0,2:T(4,128)(2,1)} copy(bf16[4,4,32,128]{3,2,1,0:T(8,128)(2,1)S(1)} %bitcast.6) | data formatting | bytes 262144 | tf_op jit(solution)/shard_map/reshape | solution.py:633
  27.0 0.0 collective-permute-done.10.refs_2_
  27.0 0.9 %collective-permute-done.9.refs_1_ = bf16[32,896]{1,0:T(8,128)(2,1)S(1)} collective-permute-done((bf16[32,896]{1,0:T(8,128)(2,1)S(1)}, bf16[32,896]{1,0:T(8,128)(2,1)S(1)}, u32[]{:S(2)}, u32[]{:S(2)}) %collective-permute-start.9) | collective-permute-done | bytes 57376 | tf_op jit(solution)/shard_map/ppermute | solution.py:51
  27.9 0.6 %collective-permute-done.8.refs_0_ = bf16[32,896]{1,0:T(8,128)(2,1)S(1)} collective-permute-done((bf16[32,896]{1,0:T(8,128)(2,1)S(1)}, bf16[32,896]{1,0:T(8,128)(2,1)S(1)}, u32[]{:S(2)}, u32[]{:S(2)}) %collective-permute-start.8) | collective-permute-done | bytes 57376 | tf_op jit(solution)/shard_map/ppermute | solution.py:51
  28.5 1.7 %collective-permute-start.13 = (bf16[32,896]{1,0:T(8,128)(2,1)S(1)}, bf16[32,896]{1,0:T(8,128)(2,1)S(1)}, u32[]{:S(2)}, u32[]{:S(2)}) collective-permute-start(bf16[32,896]{1,0:T(8,128)(2,1)S(1)} %shard_map.79.own_ref), channel_id=1, source_target_pairs={{0,6},{1,25},{2,4},{3,27},{4,2},{5,29},{6,0},{7,31},{8,14},{9,17},... | collective-permute-start | bytes 172040 | tf_op jit(solution)/shard_map/ppermute | solution.py:51
  30.2 0.9 %collective-permute-start.12 = (bf16[32,896]{1,0:T(8,128)(2,1)S(1)}, bf16[32,896]{1,0:T(8,128)(2,1)S(1)}, u32[]{:S(2)}, u32[]{:S(2)}) collective-permute-start(bf16[32,896]{1,0:T(8,128)(2,1)S(1)} %shard_map.79.own_ref), channel_id=1, source_target_pairs={{0,4},{1,17},{2,6},{3,19},{4,0},{5,21},{6,2},{7,23},{8,12},{9,25},... | collective-permute-start | bytes 172040 | tf_op jit(solution)/shard_map/ppermute | solution.py:51
  31.0 1.0 %collective-permute-start.11 = (bf16[32,896]{1,0:T(8,128)(2,1)S(1)}, bf16[32,896]{1,0:T(8,128)(2,1)S(1)}, u32[]{:S(2)}, u32[]{:S(2)}) collective-permute-start(bf16[32,896]{1,0:T(8,128)(2,1)S(1)} %shard_map.79.own_ref), channel_id=1, source_target_pairs={{0,2},{1,9},{2,0},{3,11},{4,6},{5,13},{6,4},{7,15},{8,10},{9,1},{1... | collective-permute-start | bytes 172040 | tf_op jit(solution)/shard_map/ppermute | solution.py:51
  32.0 1.6 %collective-permute-done.13.refs_2_ = bf16[32,896]{1,0:T(8,128)(2,1)S(1)} collective-permute-done((bf16[32,896]{1,0:T(8,128)(2,1)S(1)}, bf16[32,896]{1,0:T(8,128)(2,1)S(1)}, u32[]{:S(2)}, u32[]{:S(2)}) %collective-permute-start.13) | collective-permute-done | bytes 57376 | tf_op jit(solution)/shard_map/ppermute | solution.py:51
  33.6 0.7 %collective-permute-done.12.refs_1_ = bf16[32,896]{1,0:T(8,128)(2,1)S(1)} collective-permute-done((bf16[32,896]{1,0:T(8,128)(2,1)S(1)}, bf16[32,896]{1,0:T(8,128)(2,1)S(1)}, u32[]{:S(2)}, u32[]{:S(2)}) %collective-permute-start.12) | collective-permute-done | bytes 57376 | tf_op jit(solution)/shard_map/ppermute | solution.py:51
  34.3 0.9 %collective-permute-done.11.refs_0_ = bf16[32,896]{1,0:T(8,128)(2,1)S(1)} collective-permute-done((bf16[32,896]{1,0:T(8,128)(2,1)S(1)}, bf16[32,896]{1,0:T(8,128)(2,1)S(1)}, u32[]{:S(2)}, u32[]{:S(2)}) %collective-permute-start.11) | collective-permute-done | bytes 57376 | tf_op jit(solution)/shard_map/ppermute | solution.py:51
  35.2 0.1 collective-permute-start.14
  35.3 1.3 %collective-permute-done.14.other_ref = f32[32,896]{1,0:T(8,128)S(1)} collective-permute-done((f32[32,896]{1,0:T(8,128)S(1)}, f32[32,896]{1,0:T(8,128)S(1)}, u32[]{:S(2)}, u32[]{:S(2)}) %collective-permute-start.14) | collective-permute-done | bytes 114720 | tf_op jit(solution)/shard_map/ppermute | solution.py:537
  36.6 0.7 %shard_map.81 = (f32[32,864]{1,0:T(8,128)}, f32[32,864]{1,0:T(8,128)}) custom-call(f32[32,896]{1,0:T(8,128)S(1)} %shard_map.80.mine_ref, f32[32,896]{1,0:T(8,128)S(1)} %collective-permute-done.14.other_ref), custom_call_target="tpu_custom_call" | custom-call | flops 1000000 | bytes 1000000 | tf_op jit(solution)/shard_map/pallas_call | solution.py:654
  (3 shorter events, 0.1 us)
Async XLA Ops:
  2.3 11.5 %collective-permute-start = (bf16[3,128,128]{2,1,0:T(8,128)(2,1)S(1)}, bf16[3,128,128]{2,1,0:T(8,128)(2,1)S(1)}, u32[]{:S(2)}, u32[]{:S(2)}) collective-permute-start(bf16[3,128,128]{2,1,0:T(8,128)(2,1)S(1)} %get-tuple-element.52.refs_0_), channel_id=1, source_target_pairs={{0,4},{1,5},{2,6},{3,7},{4,0},{5,1},{6,2},{7,3},{8,12},{9,13},{10,... | collective-permute-start | bytes 294920 | tf_op jit(solution)/shard_map/ppermute | solution.py:51
  5.3 8.5 %collective-permute-start.1 = (bf16[3,128,128]{2,1,0:T(8,128)(2,1)S(1)}, bf16[3,128,128]{2,1,0:T(8,128)(2,1)S(1)}, u32[]{:S(2)}, u32[]{:S(2)}) collective-permute-start(bf16[3,128,128]{2,1,0:T(8,128)(2,1)S(1)} %get-tuple-element.53.face_0), channel_id=1, source_target_pairs={{0,8},{1,9},{2,10},{3,11},{4,12},{5,13},{6,14},{7,15},{8,0},{9,1},... | collective-permute-start | bytes 294920 | tf_op jit(solution)/shard_map/ppermute | solution.py:51
  6.9 6.9 %collective-permute-start.2 = (bf16[3,128,128]{2,1,0:T(8,128)(2,1)S(1)}, bf16[3,128,128]{2,1,0:T(8,128)(2,1)S(1)}, u32[]{:S(2)}, u32[]{:S(2)}) collective-permute-start(bf16[3,128,128]{2,1,0:T(8,128)(2,1)S(1)} %get-tuple-element.54.face_1), channel_id=1, source_target_pairs={{8,16},{9,17},{10,18},{11,19},{12,20},{13,21},{14,22},{15,23},{16,... | collective-permute-start | bytes 294920 | tf_op jit(solution)/shard_map/ppermute | solution.py:51
  8.6 5.3 %collective-permute-start.3 = (bf16[160,128]{1,0:T(8,128)(2,1)S(1)}, bf16[160,128]{1,0:T(8,128)(2,1)S(1)}, u32[]{:S(2)}, u32[]{:S(2)}) collective-permute-start(bf16[160,128]{1,0:T(8,128)(2,1)S(1)} %get-tuple-element.65), channel_id=1, source_target_pairs={{0,12},{1,13},{2,14},{3,15},{4,8},{5,9},{6,10},{7,11},{8,4},{9,5},... | collective-permute-start | bytes 122888 | tf_op jit(solution)/shard_map/ppermute | solution.py:51
  10.3 4.0 %collective-permute-start.4 = (bf16[160,128]{1,0:T(8,128)(2,1)S(1)}, bf16[160,128]{1,0:T(8,128)(2,1)S(1)}, u32[]{:S(2)}, u32[]{:S(2)}) collective-permute-start(bf16[160,128]{1,0:T(8,128)(2,1)S(1)} %get-tuple-element.66), channel_id=1, source_target_pairs={{8,20},{9,21},{10,22},{11,23},{12,16},{13,17},{14,18},{15,19},{16,... | collective-permute-start | bytes 122888 | tf_op jit(solution)/shard_map/ppermute | solution.py:51
  14.4 3.6 %collective-permute-start.5 = (bf16[32,256]{1,0:T(8,128)(2,1)S(1)}, bf16[32,256]{1,0:T(8,128)(2,1)S(1)}, u32[]{:S(2)}, u32[]{:S(2)}) collective-permute-start(bf16[32,256]{1,0:T(8,128)(2,1)S(1)} %get-tuple-element.67), channel_id=1, source_target_pairs={{0,1},{1,0},{2,3},{3,2},{4,5},{5,4},{6,7},{7,6},{8,9},{9,8},{10,11... | collective-permute-start | bytes 49160 | tf_op jit(solution)/shard_map/ppermute | solution.py:51
  14.5 3.8 %collective-permute-start.6 = (bf16[32,256]{1,0:T(8,128)(2,1)S(1)}, bf16[32,256]{1,0:T(8,128)(2,1)S(1)}, u32[]{:S(2)}, u32[]{:S(2)}) collective-permute-start(bf16[32,256]{1,0:T(8,128)(2,1)S(1)} %get-tuple-element.68), channel_id=1, source_target_pairs={{1,2},{2,1},{5,6},{6,5},{9,10},{10,9},{13,14},{14,13},{17,18},{18,... | collective-permute-start | bytes 49160 | tf_op jit(solution)/shard_map/ppermute | solution.py:51
  19.5 1.4 %collective-permute-start.7 = (f32[32,896]{1,0:T(8,128)S(1)}, f32[32,896]{1,0:T(8,128)S(1)}, u32[]{:S(2)}, u32[]{:S(2)}) collective-permute-start(f32[32,896]{1,0:T(8,128)S(1)} %shard_map.76), channel_id=1, source_target_pairs={{0,1},{1,0},{2,3},{3,2},{4,5},{5,4},{6,7},{7,6},{8,9},{9,8},{10,11... | collective-permute-start | bytes 344072 | tf_op jit(solution)/shard_map/ppermute | solution.py:537
  20.9 6.1 %collective-permute-start.10 = (bf16[32,896]{1,0:T(8,128)(2,1)S(1)}, bf16[32,896]{1,0:T(8,128)(2,1)S(1)}, u32[]{:S(2)}, u32[]{:S(2)}) collective-permute-start(bf16[32,896]{1,0:T(8,128)(2,1)S(1)} %shard_map.77.own_ref), channel_id=1, source_target_pairs={{0,24},{1,7},{2,26},{3,5},{4,28},{5,3},{6,30},{7,1},{8,16},{9,15},... | collective-permute-start | bytes 172040 | tf_op jit(solution)/shard_map/ppermute | solution.py:51
  22.8 5.1 %collective-permute-start.9 = (bf16[32,896]{1,0:T(8,128)(2,1)S(1)}, bf16[32,896]{1,0:T(8,128)(2,1)S(1)}, u32[]{:S(2)}, u32[]{:S(2)}) collective-permute-start(bf16[32,896]{1,0:T(8,128)(2,1)S(1)} %shard_map.77.own_ref), channel_id=1, source_target_pairs={{0,16},{1,5},{2,18},{3,7},{4,20},{5,1},{6,22},{7,3},{8,24},{9,13},... | collective-permute-start | bytes 172040 | tf_op jit(solution)/shard_map/ppermute | solution.py:51
  23.8 4.6 %collective-permute-start.8 = (bf16[32,896]{1,0:T(8,128)(2,1)S(1)}, bf16[32,896]{1,0:T(8,128)(2,1)S(1)}, u32[]{:S(2)}, u32[]{:S(2)}) collective-permute-start(bf16[32,896]{1,0:T(8,128)(2,1)S(1)} %shard_map.77.own_ref), channel_id=1, source_target_pairs={{0,8},{1,3},{2,10},{3,1},{4,12},{5,7},{6,14},{7,5},{8,0},{9,11},{1... | collective-permute-start | bytes 172040 | tf_op jit(solution)/shard_map/ppermute | solution.py:51
  28.5 5.1 %collective-permute-start.13 = (bf16[32,896]{1,0:T(8,128)(2,1)S(1)}, bf16[32,896]{1,0:T(8,128)(2,1)S(1)}, u32[]{:S(2)}, u32[]{:S(2)}) collective-permute-start(bf16[32,896]{1,0:T(8,128)(2,1)S(1)} %shard_map.79.own_ref), channel_id=1, source_target_pairs={{0,6},{1,25},{2,4},{3,27},{4,2},{5,29},{6,0},{7,31},{8,14},{9,17},... | collective-permute-start | bytes 172040 | tf_op jit(solution)/shard_map/ppermute | solution.py:51
  30.2 4.2 %collective-permute-start.12 = (bf16[32,896]{1,0:T(8,128)(2,1)S(1)}, bf16[32,896]{1,0:T(8,128)(2,1)S(1)}, u32[]{:S(2)}, u32[]{:S(2)}) collective-permute-start(bf16[32,896]{1,0:T(8,128)(2,1)S(1)} %shard_map.79.own_ref), channel_id=1, source_target_pairs={{0,4},{1,17},{2,6},{3,19},{4,0},{5,21},{6,2},{7,23},{8,12},{9,25},... | collective-permute-start | bytes 172040 | tf_op jit(solution)/shard_map/ppermute | solution.py:51
  31.0 4.2 %collective-permute-start.11 = (bf16[32,896]{1,0:T(8,128)(2,1)S(1)}, bf16[32,896]{1,0:T(8,128)(2,1)S(1)}, u32[]{:S(2)}, u32[]{:S(2)}) collective-permute-start(bf16[32,896]{1,0:T(8,128)(2,1)S(1)} %shard_map.79.own_ref), channel_id=1, source_target_pairs={{0,2},{1,9},{2,0},{3,11},{4,6},{5,13},{6,4},{7,15},{8,10},{9,1},{1... | collective-permute-start | bytes 172040 | tf_op jit(solution)/shard_map/ppermute | solution.py:51
  35.2 1.4 %collective-permute-start.14 = (f32[32,896]{1,0:T(8,128)S(1)}, f32[32,896]{1,0:T(8,128)S(1)}, u32[]{:S(2)}, u32[]{:S(2)}) collective-permute-start(f32[32,896]{1,0:T(8,128)S(1)} %shard_map.80.mine_ref), channel_id=1, source_target_pairs={{0,1},{1,0},{2,3},{3,2},{4,5},{5,4},{6,7},{7,6},{8,9},{9,8},{10,11... | collective-permute-start | bytes 344072 | tf_op jit(solution)/shard_map/ppermute | solution.py:537

commit v7 on v5

--- a/solution.py
+++ b/solution.py
@@ -602,7 +602,8 @@
         scratch=[pltpu.VMEM((3,) + pre_shape, BF16)],
         flops=1_000_000_000,
     )(field, wide_noise, *got, a1, ab)
-    *z_got, xs, pre, back, hidden, slope = lax.optimization_barrier((*z_got, xs, pre, back, hidden, slope))
+    *z_got, xs, pre, back, hidden, slope = lax.optimization_barrier((*z_got[::-1], xs, pre, back, hidden, slope))
+    z_got = z_got[::-1]
 
     hidden_edge, xs_edge, slope_rows, back_rows = call(
         mend,
@@ -643,7 +644,7 @@
         odd = rounds[(k + turn) % len(rounds)]
         flips = [(even[:1], odd[:1])]
         if len(even) == 2:
-            flips += [(even[1:], odd[1:]), (even, odd)]
+            flips = [(even, odd), (even[1:], odd[1:])] + flips
         got = [masked_swap(send, *pair) for pair in flips]
         if k == 0:
             *got, prediction = lax.optimization_barrier((*got, prediction))

time: 37.5 us -> 38.5 us (1.027)
  waiting for transfers between devices: 7.14 us -> 7.89 us
    ppermute x13, waiting for transfers between devices: 5.26 us -> 6.17 us  [permute(): lax.ppermute(x, AXES, [(number(place), number(to)) for place, to in targe...]
where the time goes in v7:
time: 38.5 us; the launch traced here: 38.3 us
  starting transfers between devices  19.4 us (50%)
  waiting for transfers between devices  7.89 us (20%)
  Pallas kernels  7.5 us (19%)
  other arithmetic  2.02 us (5%)
  between operations  0.77 us (2%)
  local copies, waits for them, and re-layouts  0.72 us (2%)
    ppermute x13, starting transfers between devices, permute(): lax.ppermute(x, AXES, [(number(place), number(to)) for place, to in targe...  19 us
    ppermute x13, waiting for transfers between devices, permute(): lax.ppermute(x, AXES, [(number(place), number(to)) for place, to in targe...  6.17 us
    pallas_call x1, Pallas kernels, local(): call(functools.partial(widen, y_sides), [struct((3, n_field, size_z, 256)...  1.98 us
    ppermute x2, waiting for transfers between devices, flip(): return lax.ppermute(x, axis, [(i, i ^ bit) for i in range(size)])  1.73 us
    concatenate x1, other arithmetic, local(): jnp.concatenate([inputs, noise], axis=0)  1.16 us
    pallas_call x1, Pallas kernels, local(): call(spread_weights, [struct((9 * 256, 256), BF16), struct((9 * 256, 256)...  1.05 us
    pallas_call x1, Pallas kernels, local(): call(predict, struct((size_x, lanes, size_z), BF16), scratch=[pltpu.VMEM(...  0.92 us
    concatenate x1, other arithmetic, local(): jnp.concatenate([w_first, w_second], axis=0)  0.86 us
  transfers between devices with their start and end apart: 15, of which 9 were waited for; matrix products, arithmetic and copies ran while one was open for 4% of the time, Pallas kernels for 13%

profile of v7, /device:TPU:0, one launch (start us, length us, event | category | flops | bytes accessed | tf_op | source)
XLA Modules:
  0.0 38.3 jit_solution(2529612259808410319)
XLA Ops:
  0.6 1.2 %pad_maximum_fusion.raw_ref = bf16[2,32,4,4,128]{4,3,2,1,0:T(4,128)(2,1)S(1)} fusion(bf16[1,32,4,4,128]{4,3,2,1,0:T(4,128)(2,1)} %param.5, bf16[1,32,4,4,128]{4,3,2,1,0:T(4,128)(2,1)} %param.4), kind=kLoop, calls=%fused_computation | loop fusion | flops 131072 | bytes 524288 | tf_op jit(solution)/shard_map/concatenate | solution.py:569
  1.8 0.5 %shard_map.67 = (bf16[4,128,128]{2,1,0:T(8,128)(2,1)S(1)}, bf16[4,128,128]{2,1,0:T(8,128)(2,1)S(1)}, bf16[4,128,128]{2,1,0:T(8,128)(2,1)S(1)}, bf16[3,128,128]{2...) custom-call(bf16[2,32,4,4,128]{4,3,2,1,0:T(4,128)(2,1)S(1)} %pad_maximum_fusion.raw_ref), custom_call_target="tpu_custom_call" | custom-call | flops 1000000 | bytes 1000000 | tf_op jit(solution)/shard_map/pallas_call | solution.py:563
  2.3 3.1 %collective-permute-start = (bf16[3,128,128]{2,1,0:T(8,128)(2,1)S(1)}, bf16[3,128,128]{2,1,0:T(8,128)(2,1)S(1)}, u32[]{:S(2)}, u32[]{:S(2)}) collective-permute-start(bf16[3,128,128]{2,1,0:T(8,128)(2,1)S(1)} %get-tuple-element.52.face_0), channel_id=1, source_target_pairs={{0,8},{1,9},{2,10},{3,11},{4,12},{5,13},{6,14},{7,15},{8,0},{9,1},... | collective-permute-start | bytes 294920 | tf_op jit(solution)/shard_map/ppermute | solution.py:51
  5.4 1.5 %collective-permute-start.1 = (bf16[3,128,128]{2,1,0:T(8,128)(2,1)S(1)}, bf16[3,128,128]{2,1,0:T(8,128)(2,1)S(1)}, u32[]{:S(2)}, u32[]{:S(2)}) collective-permute-start(bf16[3,128,128]{2,1,0:T(8,128)(2,1)S(1)} %get-tuple-element.53.face_1), channel_id=1, source_target_pairs={{8,16},{9,17},{10,18},{11,19},{12,20},{13,21},{14,22},{15,23},{16,... | collective-permute-start | bytes 294920 | tf_op jit(solution)/shard_map/ppermute | solution.py:51
  6.9 1.5 %collective-permute-start.2 = (bf16[3,128,128]{2,1,0:T(8,128)(2,1)S(1)}, bf16[3,128,128]{2,1,0:T(8,128)(2,1)S(1)}, u32[]{:S(2)}, u32[]{:S(2)}) collective-permute-start(bf16[3,128,128]{2,1,0:T(8,128)(2,1)S(1)} %get-tuple-element.54.refs_0_), channel_id=1, source_target_pairs={{0,4},{1,5},{2,6},{3,7},{4,0},{5,1},{6,2},{7,3},{8,12},{9,13},{10,... | collective-permute-start | bytes 294920 | tf_op jit(solution)/shard_map/ppermute | solution.py:51
  8.4 0.2 shard_map.70
  8.6 1.7 %collective-permute-start.3 = (bf16[160,128]{1,0:T(8,128)(2,1)S(1)}, bf16[160,128]{1,0:T(8,128)(2,1)S(1)}, u32[]{:S(2)}, u32[]{:S(2)}) collective-permute-start(bf16[160,128]{1,0:T(8,128)(2,1)S(1)} %get-tuple-element.65), channel_id=1, source_target_pairs={{0,12},{1,13},{2,14},{3,15},{4,8},{5,9},{6,10},{7,11},{8,4},{9,5},... | collective-permute-start | bytes 122888 | tf_op jit(solution)/shard_map/ppermute | solution.py:51
  10.3 1.5 %collective-permute-start.4 = (bf16[160,128]{1,0:T(8,128)(2,1)S(1)}, bf16[160,128]{1,0:T(8,128)(2,1)S(1)}, u32[]{:S(2)}, u32[]{:S(2)}) collective-permute-start(bf16[160,128]{1,0:T(8,128)(2,1)S(1)} %get-tuple-element.66), channel_id=1, source_target_pairs={{8,20},{9,21},{10,22},{11,23},{12,16},{13,17},{14,18},{15,19},{16,... | collective-permute-start | bytes 122888 | tf_op jit(solution)/shard_map/ppermute | solution.py:51
  11.8 0.9 %pad_maximum_fusion.1.both_ref = bf16[64,864]{1,0:T(8,128)(2,1)S(1)} fusion(bf16[32,864]{1,0:T(8,128)(2,1)} %param.7, bf16[32,864]{1,0:T(8,128)(2,1)} %param.6), kind=kLoop, calls=%fused_computation.2 | loop fusion | flops 221184 | bytes 221184 | tf_op jit(solution)/shard_map/concatenate | solution.py:581
  12.7 1.0 %shard_map.68 = (bf16[2304,256]{1,0:T(8,128)(2,1)S(1)}, bf16[2304,256]{1,0:T(8,128)(2,1)S(1)}, f32[9,32,128]{2,1,0:T(8,128)S(1)}) custom-call(bf16[64,864]{1,0:T(8,128)(2,1)S(1)} %pad_maximum_fusion.1.both_ref), custom_call_target="tpu_custom_call" | custom-call | flops 1000000 | bytes 4000000 | tf_op jit(solution)/shard_map/pallas_call | solution.py:577
  13.7 0.0 collective-permute-done.refs_0_
  13.7 0.0 collective-permute-done.1.refs_1_
  13.7 0.0 collective-permute-done.2.refs_2_
  13.8 0.1 shard_map.69
  13.9 0.0 collective-permute-done.3.refs_6_
  13.9 0.4 %collective-permute-done.4.refs_7_ = bf16[160,128]{1,0:T(8,128)(2,1)S(1)} collective-permute-done((bf16[160,128]{1,0:T(8,128)(2,1)S(1)}, bf16[160,128]{1,0:T(8,128)(2,1)S(1)}, u32[]{:S(2)}, u32[]{:S(2)}) %collective-permute-start.4) | collective-permute-done | bytes 40992 | tf_op jit(solution)/shard_map/ppermute | solution.py:51
  14.3 0.1 shard_map.71
  14.4 1.6 %collective-permute-start.5 = (bf16[32,256]{1,0:T(8,128)(2,1)S(1)}, bf16[32,256]{1,0:T(8,128)(2,1)S(1)}, u32[]{:S(2)}, u32[]{:S(2)}) collective-permute-start(bf16[32,256]{1,0:T(8,128)(2,1)S(1)} %get-tuple-element.67), channel_id=1, source_target_pairs={{1,2},{2,1},{5,6},{6,5},{9,10},{10,9},{13,14},{14,13},{17,18},{18,... | collective-permute-start | bytes 49160 | tf_op jit(solution)/shard_map/ppermute | solution.py:51
  16.0 0.1 collective-permute-start.6
  16.1 2.0 %shard_map.72 = (bf16[3,8,128,256]{3,2,1,0:T(8,128)(2,1)S(1)}, f32[6,128,256]{2,1,0:T(8,128)S(1)}, f32[4,128,256]{2,1,0:T(8,128)S(1)}, bf16[3,6,128,256]{3,2,1,0:T(8,128)(2,1)S(1)}, f32[4,128,256]{2,1,0:T(8,128)S(1)}) custom-call(bf16[4,128,128]{2,1,0:T(8,128)(2,1)S(1)} %get-tuple-element.50.refs_0_, bf16[4,128,128]{2,1,0:T(8,128)(2,1)S(1)} %get-tuple-element.51.refs_1_, ...), custom_call_target="tpu_custom_call" | custom-call | flops 1000000000 | bytes 1000000 | tf_op jit(solution)/shard_map/pallas_call | solution.py:593
  18.1 0.1 collective-permute-done.5.side_1
  18.2 0.0 collective-permute-done.6.side_0
  18.2 0.4 %shard_map.73 = (bf16[4,6,16,256]{3,2,1,0:T(8,128)(2,1)S(1)}, bf16[2,8,16,256]{3,2,1,0:T(8,128)(2,1)S(1)}, f32[16,256]{1,0:T(8,128)S(1)}, f32[16,256]{1,0:T(8,128)S(1)}) custom-call(f32[6,128,256]{2,1,0:T(8,128)S(1)} %get-tuple-element.77.pre_ref, bf16[3,6,128,256]{3,2,1,0:T(8,128)(2,1)S(1)} %get-tuple-element.78.hid_ref, ...), custom_call_target="tpu_custom_call" | custom-call | flops 1000000 | bytes 1000000 | tf_op jit(solution)/shard_map/pallas_call | solution.py:608
  18.6 0.1 shard_map.74.pre_grad_ref
  18.8 0.7 %shard_map.76 = f32[32,896]{1,0:T(8,128)S(1)} custom-call(bf16[3,8,128,256]{3,2,1,0:T(8,128)(2,1)S(1)} %get-tuple-element.76.wide_field_ref.xs_ref, bf16[2,8,16,256]{3,2,1,0:T(8,128)(2,1)S(1)} %get-tuple-element.83.xs_edge, bf16[3,6,128,256]{3,2,1,0:T(8,128)(2,1)S(1)} %get-tuple-element.78.hid_ref, bf16[4,6,16,256]{3,2,1,0:T(8,128)(2,1)S(1)} %get-tuple-element.84.hid_edge, ...), custom_call_target="tpu_custom_call" | custom-call | flops 1000000000 | bytes 1000000 | tf_op jit(solution)/shard_map/pallas_call | solution.py:622
  19.4 0.3 collective-permute-start.7
  19.8 0.6 %shard_map.75.keep_ref = f32[32,896]{1,0:T(8,128)S(1)} custom-call(bf16[3,8,128,256]{3,2,1,0:T(8,128)(2,1)S(1)} %get-tuple-element.76.wide_field_ref.xs_ref, bf16[2,8,16,256]{3,2,1,0:T(8,128)(2,1)S(1)} %get-tuple-element.83.xs_edge, bf16[3,6,128,256]{3,2,1,0:T(8,128)(2,1)S(1)} %get-tuple-element.78.hid_ref, ...), custom_call_target="tpu_custom_call" | custom-call | flops 1000000000 | bytes 1000000 | tf_op jit(solution)/shard_map/pallas_call | solution.py:624
  20.4 0.4 %collective-permute-done.7.taken_ref = f32[32,896]{1,0:T(8,128)S(1)} collective-permute-done((f32[32,896]{1,0:T(8,128)S(1)}, f32[32,896]{1,0:T(8,128)S(1)}, u32[]{:S(2)}, u32[]{:S(2)}) %collective-permute-start.7) | collective-permute-done | bytes 114720 | tf_op jit(solution)/shard_map/ppermute | solution.py:537
  20.8 1.4 %collective-permute-start.10 = (bf16[32,896]{1,0:T(8,128)(2,1)S(1)}, bf16[32,896]{1,0:T(8,128)(2,1)S(1)}, u32[]{:S(2)}, u32[]{:S(2)}) collective-permute-start(bf16[32,896]{1,0:T(8,128)(2,1)S(1)} %shard_map.77.own_ref), channel_id=1, source_target_pairs={{0,8},{1,3},{2,10},{3,1},{4,12},{5,7},{6,14},{7,5},{8,0},{9,11},{1... | collective-permute-start | bytes 172040 | tf_op jit(solution)/shard_map/ppermute | solution.py:51
  22.3 1.0 %collective-permute-start.9 = (bf16[32,896]{1,0:T(8,128)(2,1)S(1)}, bf16[32,896]{1,0:T(8,128)(2,1)S(1)}, u32[]{:S(2)}, u32[]{:S(2)}) collective-permute-start(bf16[32,896]{1,0:T(8,128)(2,1)S(1)} %shard_map.77.own_ref), channel_id=1, source_target_pairs={{0,16},{1,5},{2,18},{3,7},{4,20},{5,1},{6,22},{7,3},{8,24},{9,13},... | collective-permute-start | bytes 172040 | tf_op jit(solution)/shard_map/ppermute | solution.py:51
  23.3 2.0 %collective-permute-start.8 = (bf16[32,896]{1,0:T(8,128)(2,1)S(1)}, bf16[32,896]{1,0:T(8,128)(2,1)S(1)}, u32[]{:S(2)}, u32[]{:S(2)}) collective-permute-start(bf16[32,896]{1,0:T(8,128)(2,1)S(1)} %shard_map.77.own_ref), channel_id=1, source_target_pairs={{0,24},{1,7},{2,26},{3,5},{4,28},{5,3},{6,30},{7,1},{8,16},{9,15},... | collective-permute-start | bytes 172040 | tf_op jit(solution)/shard_map/ppermute | solution.py:51
  25.3 0.9 %shard_map.78 = bf16[4,128,128]{2,1,0:T(8,128)(2,1)S(1)} custom-call(bf16[3,6,128,256]{3,2,1,0:T(8,128)(2,1)S(1)} %get-tuple-element.78.hid_ref, bf16[4,6,16,256]{3,2,1,0:T(8,128)(2,1)S(1)} %get-tuple-element.84.hid_edge, f32[9,32,128]{2,1,0:T(8,128)S(1)} %get-tuple-element.90.second_ref), custom_call_target="tpu_custom_call" | custom-call | flops 500000000 | bytes 1000000 | tf_op jit(solution)/shard_map/pallas_call | solution.py:627
  26.2 0.7 %copy.9 = bf16[4,4,32,128]{3,1,0,2:T(4,128)(2,1)} copy(bf16[4,4,32,128]{3,2,1,0:T(8,128)(2,1)S(1)} %bitcast.6) | data formatting | bytes 262144 | tf_op jit(solution)/shard_map/reshape | solution.py:633
  26.9 0.0 collective-permute-done.10.refs_2_
  27.0 1.0 %collective-permute-done.9.refs_1_ = bf16[32,896]{1,0:T(8,128)(2,1)S(1)} collective-permute-done((bf16[32,896]{1,0:T(8,128)(2,1)S(1)}, bf16[32,896]{1,0:T(8,128)(2,1)S(1)}, u32[]{:S(2)}, u32[]{:S(2)}) %collective-permute-start.9) | collective-permute-done | bytes 57376 | tf_op jit(solution)/shard_map/ppermute | solution.py:51
  28.0 1.4 %collective-permute-done.8.refs_0_ = bf16[32,896]{1,0:T(8,128)(2,1)S(1)} collective-permute-done((bf16[32,896]{1,0:T(8,128)(2,1)S(1)}, bf16[32,896]{1,0:T(8,128)(2,1)S(1)}, u32[]{:S(2)}, u32[]{:S(2)}) %collective-permute-start.8) | collective-permute-done | bytes 57376 | tf_op jit(solution)/shard_map/ppermute | solution.py:51
  29.4 0.2 collective-permute-start.13
  29.6 1.5 %collective-permute-start.12 = (bf16[32,896]{1,0:T(8,128)(2,1)S(1)}, bf16[32,896]{1,0:T(8,128)(2,1)S(1)}, u32[]{:S(2)}, u32[]{:S(2)}) collective-permute-start(bf16[32,896]{1,0:T(8,128)(2,1)S(1)} %shard_map.79.own_ref), channel_id=1, source_target_pairs={{0,4},{1,17},{2,6},{3,19},{4,0},{5,21},{6,2},{7,23},{8,12},{9,25},... | collective-permute-start | bytes 172040 | tf_op jit(solution)/shard_map/ppermute | solution.py:51
  31.1 1.9 %collective-permute-start.11 = (bf16[32,896]{1,0:T(8,128)(2,1)S(1)}, bf16[32,896]{1,0:T(8,128)(2,1)S(1)}, u32[]{:S(2)}, u32[]{:S(2)}) collective-permute-start(bf16[32,896]{1,0:T(8,128)(2,1)S(1)} %shard_map.79.own_ref), channel_id=1, source_target_pairs={{0,6},{1,25},{2,4},{3,27},{4,2},{5,29},{6,0},{7,31},{8,14},{9,17},... | collective-permute-start | bytes 172040 | tf_op jit(solution)/shard_map/ppermute | solution.py:51
  33.0 0.7 %collective-permute-done.13.refs_2_ = bf16[32,896]{1,0:T(8,128)(2,1)S(1)} collective-permute-done((bf16[32,896]{1,0:T(8,128)(2,1)S(1)}, bf16[32,896]{1,0:T(8,128)(2,1)S(1)}, u32[]{:S(2)}, u32[]{:S(2)}) %collective-permute-start.13) | collective-permute-done | bytes 57376 | tf_op jit(solution)/shard_map/ppermute | solution.py:51
  33.7 0.2 collective-permute-done.12.refs_1_
  33.8 2.4 %collective-permute-done.11.refs_0_ = bf16[32,896]{1,0:T(8,128)(2,1)S(1)} collective-permute-done((bf16[32,896]{1,0:T(8,128)(2,1)S(1)}, bf16[32,896]{1,0:T(8,128)(2,1)S(1)}, u32[]{:S(2)}, u32[]{:S(2)}) %collective-permute-start.11) | collective-permute-done | bytes 57376 | tf_op jit(solution)/shard_map/ppermute | solution.py:51
  36.2 0.1 collective-permute-start.14
  36.3 1.3 %collective-permute-done.14.other_ref = f32[32,896]{1,0:T(8,128)S(1)} collective-permute-done((f32[32,896]{1,0:T(8,128)S(1)}, f32[32,896]{1,0:T(8,128)S(1)}, u32[]{:S(2)}, u32[]{:S(2)}) %collective-permute-start.14) | collective-permute-done | bytes 114720 | tf_op jit(solution)/shard_map/ppermute | solution.py:537
  37.6 0.7 %shard_map.81 = (f32[32,864]{1,0:T(8,128)}, f32[32,864]{1,0:T(8,128)}) custom-call(f32[32,896]{1,0:T(8,128)S(1)} %shard_map.80.mine_ref, f32[32,896]{1,0:T(8,128)S(1)} %collective-permute-done.14.other_ref), custom_call_target="tpu_custom_call" | custom-call | flops 1000000 | bytes 1000000 | tf_op jit(solution)/shard_map/pallas_call | solution.py:654
  (3 shorter events, 0.1 us)
Async XLA Ops:
  2.3 11.5 %collective-permute-start = (bf16[3,128,128]{2,1,0:T(8,128)(2,1)S(1)}, bf16[3,128,128]{2,1,0:T(8,128)(2,1)S(1)}, u32[]{:S(2)}, u32[]{:S(2)}) collective-permute-start(bf16[3,128,128]{2,1,0:T(8,128)(2,1)S(1)} %get-tuple-element.52.face_0), channel_id=1, source_target_pairs={{0,8},{1,9},{2,10},{3,11},{4,12},{5,13},{6,14},{7,15},{8,0},{9,1},... | collective-permute-start | bytes 294920 | tf_op jit(solution)/shard_map/ppermute | solution.py:51
  5.4 8.4 %collective-permute-start.1 = (bf16[3,128,128]{2,1,0:T(8,128)(2,1)S(1)}, bf16[3,128,128]{2,1,0:T(8,128)(2,1)S(1)}, u32[]{:S(2)}, u32[]{:S(2)}) collective-permute-start(bf16[3,128,128]{2,1,0:T(8,128)(2,1)S(1)} %get-tuple-element.53.face_1), channel_id=1, source_target_pairs={{8,16},{9,17},{10,18},{11,19},{12,20},{13,21},{14,22},{15,23},{16,... | collective-permute-start | bytes 294920 | tf_op jit(solution)/shard_map/ppermute | solution.py:51
  6.9 6.9 %collective-permute-start.2 = (bf16[3,128,128]{2,1,0:T(8,128)(2,1)S(1)}, bf16[3,128,128]{2,1,0:T(8,128)(2,1)S(1)}, u32[]{:S(2)}, u32[]{:S(2)}) collective-permute-start(bf16[3,128,128]{2,1,0:T(8,128)(2,1)S(1)} %get-tuple-element.54.refs_0_), channel_id=1, source_target_pairs={{0,4},{1,5},{2,6},{3,7},{4,0},{5,1},{6,2},{7,3},{8,12},{9,13},{10,... | collective-permute-start | bytes 294920 | tf_op jit(solution)/shard_map/ppermute | solution.py:51
  8.6 5.3 %collective-permute-start.3 = (bf16[160,128]{1,0:T(8,128)(2,1)S(1)}, bf16[160,128]{1,0:T(8,128)(2,1)S(1)}, u32[]{:S(2)}, u32[]{:S(2)}) collective-permute-start(bf16[160,128]{1,0:T(8,128)(2,1)S(1)} %get-tuple-element.65), channel_id=1, source_target_pairs={{0,12},{1,13},{2,14},{3,15},{4,8},{5,9},{6,10},{7,11},{8,4},{9,5},... | collective-permute-start | bytes 122888 | tf_op jit(solution)/shard_map/ppermute | solution.py:51
  10.3 4.0 %collective-permute-start.4 = (bf16[160,128]{1,0:T(8,128)(2,1)S(1)}, bf16[160,128]{1,0:T(8,128)(2,1)S(1)}, u32[]{:S(2)}, u32[]{:S(2)}) collective-permute-start(bf16[160,128]{1,0:T(8,128)(2,1)S(1)} %get-tuple-element.66), channel_id=1, source_target_pairs={{8,20},{9,21},{10,22},{11,23},{12,16},{13,17},{14,18},{15,19},{16,... | collective-permute-start | bytes 122888 | tf_op jit(solution)/shard_map/ppermute | solution.py:51
  14.4 3.8 %collective-permute-start.5 = (bf16[32,256]{1,0:T(8,128)(2,1)S(1)}, bf16[32,256]{1,0:T(8,128)(2,1)S(1)}, u32[]{:S(2)}, u32[]{:S(2)}) collective-permute-start(bf16[32,256]{1,0:T(8,128)(2,1)S(1)} %get-tuple-element.67), channel_id=1, source_target_pairs={{1,2},{2,1},{5,6},{6,5},{9,10},{10,9},{13,14},{14,13},{17,18},{18,... | collective-permute-start | bytes 49160 | tf_op jit(solution)/shard_map/ppermute | solution.py:51
  16.0 2.2 %collective-permute-start.6 = (bf16[32,256]{1,0:T(8,128)(2,1)S(1)}, bf16[32,256]{1,0:T(8,128)(2,1)S(1)}, u32[]{:S(2)}, u32[]{:S(2)}) collective-permute-start(bf16[32,256]{1,0:T(8,128)(2,1)S(1)} %get-tuple-element.68), channel_id=1, source_target_pairs={{0,1},{1,0},{2,3},{3,2},{4,5},{5,4},{6,7},{7,6},{8,9},{9,8},{10,11... | collective-permute-start | bytes 49160 | tf_op jit(solution)/shard_map/ppermute | solution.py:51
  19.4 1.4 %collective-permute-start.7 = (f32[32,896]{1,0:T(8,128)S(1)}, f32[32,896]{1,0:T(8,128)S(1)}, u32[]{:S(2)}, u32[]{:S(2)}) collective-permute-start(f32[32,896]{1,0:T(8,128)S(1)} %shard_map.76), channel_id=1, source_target_pairs={{0,1},{1,0},{2,3},{3,2},{4,5},{5,4},{6,7},{7,6},{8,9},{9,8},{10,11... | collective-permute-start | bytes 344072 | tf_op jit(solution)/shard_map/ppermute | solution.py:537
  20.8 6.1 %collective-permute-start.10 = (bf16[32,896]{1,0:T(8,128)(2,1)S(1)}, bf16[32,896]{1,0:T(8,128)(2,1)S(1)}, u32[]{:S(2)}, u32[]{:S(2)}) collective-permute-start(bf16[32,896]{1,0:T(8,128)(2,1)S(1)} %shard_map.77.own_ref), channel_id=1, source_target_pairs={{0,8},{1,3},{2,10},{3,1},{4,12},{5,7},{6,14},{7,5},{8,0},{9,11},{1... | collective-permute-start | bytes 172040 | tf_op jit(solution)/shard_map/ppermute | solution.py:51
  22.3 5.7 %collective-permute-start.9 = (bf16[32,896]{1,0:T(8,128)(2,1)S(1)}, bf16[32,896]{1,0:T(8,128)(2,1)S(1)}, u32[]{:S(2)}, u32[]{:S(2)}) collective-permute-start(bf16[32,896]{1,0:T(8,128)(2,1)S(1)} %shard_map.77.own_ref), channel_id=1, source_target_pairs={{0,16},{1,5},{2,18},{3,7},{4,20},{5,1},{6,22},{7,3},{8,24},{9,13},... | collective-permute-start | bytes 172040 | tf_op jit(solution)/shard_map/ppermute | solution.py:51
  23.3 6.1 %collective-permute-start.8 = (bf16[32,896]{1,0:T(8,128)(2,1)S(1)}, bf16[32,896]{1,0:T(8,128)(2,1)S(1)}, u32[]{:S(2)}, u32[]{:S(2)}) collective-permute-start(bf16[32,896]{1,0:T(8,128)(2,1)S(1)} %shard_map.77.own_ref), channel_id=1, source_target_pairs={{0,24},{1,7},{2,26},{3,5},{4,28},{5,3},{6,30},{7,1},{8,16},{9,15},... | collective-permute-start | bytes 172040 | tf_op jit(solution)/shard_map/ppermute | solution.py:51
  29.4 4.2 %collective-permute-start.13 = (bf16[32,896]{1,0:T(8,128)(2,1)S(1)}, bf16[32,896]{1,0:T(8,128)(2,1)S(1)}, u32[]{:S(2)}, u32[]{:S(2)}) collective-permute-start(bf16[32,896]{1,0:T(8,128)(2,1)S(1)} %shard_map.79.own_ref), channel_id=1, source_target_pairs={{0,2},{1,9},{2,0},{3,11},{4,6},{5,13},{6,4},{7,15},{8,10},{9,1},{1... | collective-permute-start | bytes 172040 | tf_op jit(solution)/shard_map/ppermute | solution.py:51
  29.6 4.2 %collective-permute-start.12 = (bf16[32,896]{1,0:T(8,128)(2,1)S(1)}, bf16[32,896]{1,0:T(8,128)(2,1)S(1)}, u32[]{:S(2)}, u32[]{:S(2)}) collective-permute-start(bf16[32,896]{1,0:T(8,128)(2,1)S(1)} %shard_map.79.own_ref), channel_id=1, source_target_pairs={{0,4},{1,17},{2,6},{3,19},{4,0},{5,21},{6,2},{7,23},{8,12},{9,25},... | collective-permute-start | bytes 172040 | tf_op jit(solution)/shard_map/ppermute | solution.py:51
  31.1 5.1 %collective-permute-start.11 = (bf16[32,896]{1,0:T(8,128)(2,1)S(1)}, bf16[32,896]{1,0:T(8,128)(2,1)S(1)}, u32[]{:S(2)}, u32[]{:S(2)}) collective-permute-start(bf16[32,896]{1,0:T(8,128)(2,1)S(1)} %shard_map.79.own_ref), channel_id=1, source_target_pairs={{0,6},{1,25},{2,4},{3,27},{4,2},{5,29},{6,0},{7,31},{8,14},{9,17},... | collective-permute-start | bytes 172040 | tf_op jit(solution)/shard_map/ppermute | solution.py:51
  36.2 1.4 %collective-permute-start.14 = (f32[32,896]{1,0:T(8,128)S(1)}, f32[32,896]{1,0:T(8,128)S(1)}, u32[]{:S(2)}, u32[]{:S(2)}) collective-permute-start(f32[32,896]{1,0:T(8,128)S(1)} %shard_map.80.mine_ref), channel_id=1, source_target_pairs={{0,1},{1,0},{2,3},{3,2},{4,5},{5,4},{6,7},{7,6},{8,9},{9,8},{10,11... | collective-permute-start | bytes 344072 | tf_op jit(solution)/shard_map/ppermute | solution.py:537

commit v8 on v7

--- a/solution.py
+++ b/solution.py
@@ -13,13 +13,12 @@
 C = 32
 
 
-def call(body, out_shapes, scratch=(), flops=1_000_000, moved=1_000_000, vmem=24, **more):
+def call(body, out_shapes, scratch=(), flops=1_000_000, moved=1_000_000):
     return pl.pallas_call(
         body,
-        **more,
         out_shape=out_shapes,
         scratch_shapes=list(scratch),
-        compiler_params=pltpu.CompilerParams(vmem_limit_bytes=vmem * 1024 * 1024),
+        compiler_params=pltpu.CompilerParams(vmem_limit_bytes=24 * 1024 * 1024),
         cost_estimate=pl.CostEstimate(flops=flops, bytes_accessed=moved, transcendentals=0),
     )
 
@@ -521,7 +520,7 @@
 
 
 def first_sum(keep_ref, taken_ref, send_ref):
-    send_ref[...] = (keep_ref[...] + taken_ref[...]).astype(BF16)
+    send_ref[...] = (keep_ref[...] + taken_ref[...]).astype(send_ref.dtype)
 
 
 def round_sum(own_ref, *refs):
@@ -622,7 +621,6 @@
     give = call(functools.partial(weight_grad, True), half, flops=1_000_000_000)(*parts)
     taken = flip(give, "gz", 1)
     keep = call(functools.partial(weight_grad, False), half, flops=1_000_000_000)(*parts)
-    send = call(first_sum, rounded)(keep, taken)
 
     prediction_rows = call(
         predict,
@@ -640,15 +638,17 @@
             bit *= 2
     rounds = [steps[k : k + 2] for k in range(0, len(steps), 2)]
     turn = len(rounds) // 2 if len(steps) % 2 == 0 else 0
+    carried = [half] * (len(rounds) - 2) + [rounded] * min(len(rounds), 2) + [half]
+    send = call(first_sum, carried[0])(keep, taken)
     for k, even in enumerate(rounds):
         odd = rounds[(k + turn) % len(rounds)]
         flips = [(even[:1], odd[:1])]
         if len(even) == 2:
-            flips = [(even, odd), (even[1:], odd[1:])] + flips
+            flips += [(even[1:], odd[1:]), (even, odd)]
         got = [masked_swap(send, *pair) for pair in flips]
         if k == 0:
             *got, prediction = lax.optimization_barrier((*got, prediction))
-        send = call(round_sum, half if k == len(rounds) - 1 else rounded)(send, *got)
+        send = call(round_sum, carried[k + 1])(send, *got)
     mine = send
     other = flip(mine, "gz", 1)
     fisher_first, fisher_second = call(

time: 38.5 us -> 37.4 us (0.971)
  waiting for transfers between devices: 7.89 us -> 6.84 us
    ppermute x13, waiting for transfers between devices: 6.17 us -> 5.11 us  [permute(): lax.ppermute(x, AXES, [(number(place), number(to)) for place, to in targe...]
where the time goes in v8:
time: 37.4 us; the launch traced here: 37.2 us
  starting transfers between devices  19.4 us (52%)
  Pallas kernels  7.5 us (20%)
  waiting for transfers between devices  6.84 us (18%)
  other arithmetic  2.02 us (5%)
  between operations  0.77 us (2%)
  local copies, waits for them, and re-layouts  0.72 us (2%)
    ppermute x13, starting transfers between devices, permute(): lax.ppermute(x, AXES, [(number(place), number(to)) for place, to in targe...  19 us
    ppermute x13, waiting for transfers between devices, permute(): lax.ppermute(x, AXES, [(number(place), number(to)) for place, to in targe...  5.11 us
    pallas_call x1, Pallas kernels, local(): call(functools.partial(widen, y_sides), [struct((3, n_field, size_z, 256)...  1.98 us
    ppermute x2, waiting for transfers between devices, flip(): return lax.ppermute(x, axis, [(i, i ^ bit) for i in range(size)])  1.73 us
    concatenate x1, other arithmetic, local(): jnp.concatenate([inputs, noise], axis=0)  1.16 us
    pallas_call x1, Pallas kernels, local(): call(spread_weights, [struct((9 * 256, 256), BF16), struct((9 * 256, 256)...  1.05 us
    pallas_call x1, Pallas kernels, local(): call(predict, struct((size_x, lanes, size_z), BF16), scratch=[pltpu.VMEM(...  0.92 us
    concatenate x1, other arithmetic, local(): jnp.concatenate([w_first, w_second], axis=0)  0.86 us
  transfers between devices with their start and end apart: 15, of which 9 were waited for; matrix products, arithmetic and copies ran while one was open for 4% of the time, Pallas kernels for 13%

profile of v8, /device:TPU:0, one launch (start us, length us, event | category | flops | bytes accessed | tf_op | source)
XLA Modules:
  0.0 37.2 jit_solution(17808253906518425099)
XLA Ops:
  0.6 1.2 %pad_maximum_fusion.raw_ref = bf16[2,32,4,4,128]{4,3,2,1,0:T(4,128)(2,1)S(1)} fusion(bf16[1,32,4,4,128]{4,3,2,1,0:T(4,128)(2,1)} %param.5, bf16[1,32,4,4,128]{4,3,2,1,0:T(4,128)(2,1)} %param.4), kind=kLoop, calls=%fused_computation | loop fusion | flops 131072 | bytes 524288 | tf_op jit(solution)/shard_map/concatenate | solution.py:568
  1.8 0.5 %shard_map.67 = (bf16[4,128,128]{2,1,0:T(8,128)(2,1)S(1)}, bf16[4,128,128]{2,1,0:T(8,128)(2,1)S(1)}, bf16[4,128,128]{2,1,0:T(8,128)(2,1)S(1)}, bf16[3,128,128]{2...) custom-call(bf16[2,32,4,4,128]{4,3,2,1,0:T(4,128)(2,1)S(1)} %pad_maximum_fusion.raw_ref), custom_call_target="tpu_custom_call" | custom-call | flops 1000000 | bytes 1000000 | tf_op jit(solution)/shard_map/pallas_call | solution.py:562
  2.3 3.1 %collective-permute-start = (bf16[3,128,128]{2,1,0:T(8,128)(2,1)S(1)}, bf16[3,128,128]{2,1,0:T(8,128)(2,1)S(1)}, u32[]{:S(2)}, u32[]{:S(2)}) collective-permute-start(bf16[3,128,128]{2,1,0:T(8,128)(2,1)S(1)} %get-tuple-element.52.face_0), channel_id=1, source_target_pairs={{0,8},{1,9},{2,10},{3,11},{4,12},{5,13},{6,14},{7,15},{8,0},{9,1},... | collective-permute-start | bytes 294920 | tf_op jit(solution)/shard_map/ppermute | solution.py:50
  5.4 1.5 %collective-permute-start.1 = (bf16[3,128,128]{2,1,0:T(8,128)(2,1)S(1)}, bf16[3,128,128]{2,1,0:T(8,128)(2,1)S(1)}, u32[]{:S(2)}, u32[]{:S(2)}) collective-permute-start(bf16[3,128,128]{2,1,0:T(8,128)(2,1)S(1)} %get-tuple-element.53.face_1), channel_id=1, source_target_pairs={{8,16},{9,17},{10,18},{11,19},{12,20},{13,21},{14,22},{15,23},{16,... | collective-permute-start | bytes 294920 | tf_op jit(solution)/shard_map/ppermute | solution.py:50
  6.9 1.5 %collective-permute-start.2 = (bf16[3,128,128]{2,1,0:T(8,128)(2,1)S(1)}, bf16[3,128,128]{2,1,0:T(8,128)(2,1)S(1)}, u32[]{:S(2)}, u32[]{:S(2)}) collective-permute-start(bf16[3,128,128]{2,1,0:T(8,128)(2,1)S(1)} %get-tuple-element.54.refs_0_), channel_id=1, source_target_pairs={{0,4},{1,5},{2,6},{3,7},{4,0},{5,1},{6,2},{7,3},{8,12},{9,13},{10,... | collective-permute-start | bytes 294920 | tf_op jit(solution)/shard_map/ppermute | solution.py:50
  8.4 0.2 shard_map.70
  8.6 1.7 %collective-permute-start.3 = (bf16[160,128]{1,0:T(8,128)(2,1)S(1)}, bf16[160,128]{1,0:T(8,128)(2,1)S(1)}, u32[]{:S(2)}, u32[]{:S(2)}) collective-permute-start(bf16[160,128]{1,0:T(8,128)(2,1)S(1)} %get-tuple-element.65), channel_id=1, source_target_pairs={{0,12},{1,13},{2,14},{3,15},{4,8},{5,9},{6,10},{7,11},{8,4},{9,5},... | collective-permute-start | bytes 122888 | tf_op jit(solution)/shard_map/ppermute | solution.py:50
  10.3 1.5 %collective-permute-start.4 = (bf16[160,128]{1,0:T(8,128)(2,1)S(1)}, bf16[160,128]{1,0:T(8,128)(2,1)S(1)}, u32[]{:S(2)}, u32[]{:S(2)}) collective-permute-start(bf16[160,128]{1,0:T(8,128)(2,1)S(1)} %get-tuple-element.66), channel_id=1, source_target_pairs={{8,20},{9,21},{10,22},{11,23},{12,16},{13,17},{14,18},{15,19},{16,... | collective-permute-start | bytes 122888 | tf_op jit(solution)/shard_map/ppermute | solution.py:50
  11.8 0.9 %pad_maximum_fusion.1.both_ref = bf16[64,864]{1,0:T(8,128)(2,1)S(1)} fusion(bf16[32,864]{1,0:T(8,128)(2,1)} %param.7, bf16[32,864]{1,0:T(8,128)(2,1)} %param.6), kind=kLoop, calls=%fused_computation.2 | loop fusion | flops 221184 | bytes 221184 | tf_op jit(solution)/shard_map/concatenate | solution.py:580
  12.7 1.0 %shard_map.68 = (bf16[2304,256]{1,0:T(8,128)(2,1)S(1)}, bf16[2304,256]{1,0:T(8,128)(2,1)S(1)}, f32[9,32,128]{2,1,0:T(8,128)S(1)}) custom-call(bf16[64,864]{1,0:T(8,128)(2,1)S(1)} %pad_maximum_fusion.1.both_ref), custom_call_target="tpu_custom_call" | custom-call | flops 1000000 | bytes 4000000 | tf_op jit(solution)/shard_map/pallas_call | solution.py:576
  13.7 0.0 collective-permute-done.refs_0_
  13.7 0.0 collective-permute-done.1.refs_1_
  13.7 0.0 collective-permute-done.2.refs_2_
  13.8 0.1 shard_map.69
  13.9 0.0 collective-permute-done.3.refs_6_
  13.9 0.4 %collective-permute-done.4.refs_7_ = bf16[160,128]{1,0:T(8,128)(2,1)S(1)} collective-permute-done((bf16[160,128]{1,0:T(8,128)(2,1)S(1)}, bf16[160,128]{1,0:T(8,128)(2,1)S(1)}, u32[]{:S(2)}, u32[]{:S(2)}) %collective-permute-start.4) | collective-permute-done | bytes 40992 | tf_op jit(solution)/shard_map/ppermute | solution.py:50
  14.3 0.1 shard_map.71
  14.4 1.6 %collective-permute-start.5 = (bf16[32,256]{1,0:T(8,128)(2,1)S(1)}, bf16[32,256]{1,0:T(8,128)(2,1)S(1)}, u32[]{:S(2)}, u32[]{:S(2)}) collective-permute-start(bf16[32,256]{1,0:T(8,128)(2,1)S(1)} %get-tuple-element.67), channel_id=1, source_target_pairs={{1,2},{2,1},{5,6},{6,5},{9,10},{10,9},{13,14},{14,13},{17,18},{18,... | collective-permute-start | bytes 49160 | tf_op jit(solution)/shard_map/ppermute | solution.py:50
  16.0 0.1 collective-permute-start.6
  16.1 2.0 %shard_map.72 = (bf16[3,8,128,256]{3,2,1,0:T(8,128)(2,1)S(1)}, f32[6,128,256]{2,1,0:T(8,128)S(1)}, f32[4,128,256]{2,1,0:T(8,128)S(1)}, bf16[3,6,128,256]{3,2,1,0:T(8,128)(2,1)S(1)}, f32[4,128,256]{2,1,0:T(8,128)S(1)}) custom-call(bf16[4,128,128]{2,1,0:T(8,128)(2,1)S(1)} %get-tuple-element.50.refs_0_, bf16[4,128,128]{2,1,0:T(8,128)(2,1)S(1)} %get-tuple-element.51.refs_1_, ...), custom_call_target="tpu_custom_call" | custom-call | flops 1000000000 | bytes 1000000 | tf_op jit(solution)/shard_map/pallas_call | solution.py:592
  18.1 0.1 collective-permute-done.5.side_1
  18.2 0.0 collective-permute-done.6.side_0
  18.2 0.4 %shard_map.73 = (bf16[4,6,16,256]{3,2,1,0:T(8,128)(2,1)S(1)}, bf16[2,8,16,256]{3,2,1,0:T(8,128)(2,1)S(1)}, f32[16,256]{1,0:T(8,128)S(1)}, f32[16,256]{1,0:T(8,128)S(1)}) custom-call(f32[6,128,256]{2,1,0:T(8,128)S(1)} %get-tuple-element.77.pre_ref, bf16[3,6,128,256]{3,2,1,0:T(8,128)(2,1)S(1)} %get-tuple-element.78.hid_ref, ...), custom_call_target="tpu_custom_call" | custom-call | flops 1000000 | bytes 1000000 | tf_op jit(solution)/shard_map/pallas_call | solution.py:607
  18.6 0.1 shard_map.74.pre_grad_ref
  18.8 0.7 %shard_map.76 = f32[32,896]{1,0:T(8,128)S(1)} custom-call(bf16[3,8,128,256]{3,2,1,0:T(8,128)(2,1)S(1)} %get-tuple-element.76.wide_field_ref.xs_ref, bf16[2,8,16,256]{3,2,1,0:T(8,128)(2,1)S(1)} %get-tuple-element.83.xs_edge, bf16[3,6,128,256]{3,2,1,0:T(8,128)(2,1)S(1)} %get-tuple-element.78.hid_ref, bf16[4,6,16,256]{3,2,1,0:T(8,128)(2,1)S(1)} %get-tuple-element.84.hid_edge, ...), custom_call_target="tpu_custom_call" | custom-call | flops 1000000000 | bytes 1000000 | tf_op jit(solution)/shard_map/pallas_call | solution.py:621
  19.4 0.3 collective-permute-start.7
  19.8 0.6 %shard_map.75.keep_ref = f32[32,896]{1,0:T(8,128)S(1)} custom-call(bf16[3,8,128,256]{3,2,1,0:T(8,128)(2,1)S(1)} %get-tuple-element.76.wide_field_ref.xs_ref, bf16[2,8,16,256]{3,2,1,0:T(8,128)(2,1)S(1)} %get-tuple-element.83.xs_edge, bf16[3,6,128,256]{3,2,1,0:T(8,128)(2,1)S(1)} %get-tuple-element.78.hid_ref, ...), custom_call_target="tpu_custom_call" | custom-call | flops 1000000000 | bytes 1000000 | tf_op jit(solution)/shard_map/pallas_call | solution.py:623
  20.4 0.4 %collective-permute-done.7.taken_ref = f32[32,896]{1,0:T(8,128)S(1)} collective-permute-done((f32[32,896]{1,0:T(8,128)S(1)}, f32[32,896]{1,0:T(8,128)S(1)}, u32[]{:S(2)}, u32[]{:S(2)}) %collective-permute-start.7) | collective-permute-done | bytes 114720 | tf_op jit(solution)/shard_map/ppermute | solution.py:536
  20.8 1.8 %collective-permute-start.10 = (bf16[32,896]{1,0:T(8,128)(2,1)S(1)}, bf16[32,896]{1,0:T(8,128)(2,1)S(1)}, u32[]{:S(2)}, u32[]{:S(2)}) collective-permute-start(bf16[32,896]{1,0:T(8,128)(2,1)S(1)} %shard_map.77.own_ref), channel_id=1, source_target_pairs={{0,24},{1,7},{2,26},{3,5},{4,28},{5,3},{6,30},{7,1},{8,16},{9,15},... | collective-permute-start | bytes 172040 | tf_op jit(solution)/shard_map/ppermute | solution.py:50
  22.7 1.1 %collective-permute-start.9 = (bf16[32,896]{1,0:T(8,128)(2,1)S(1)}, bf16[32,896]{1,0:T(8,128)(2,1)S(1)}, u32[]{:S(2)}, u32[]{:S(2)}) collective-permute-start(bf16[32,896]{1,0:T(8,128)(2,1)S(1)} %shard_map.77.own_ref), channel_id=1, source_target_pairs={{0,16},{1,5},{2,18},{3,7},{4,20},{5,1},{6,22},{7,3},{8,24},{9,13},... | collective-permute-start | bytes 172040 | tf_op jit(solution)/shard_map/ppermute | solution.py:50
  23.7 1.6 %collective-permute-start.8 = (bf16[32,896]{1,0:T(8,128)(2,1)S(1)}, bf16[32,896]{1,0:T(8,128)(2,1)S(1)}, u32[]{:S(2)}, u32[]{:S(2)}) collective-permute-start(bf16[32,896]{1,0:T(8,128)(2,1)S(1)} %shard_map.77.own_ref), channel_id=1, source_target_pairs={{0,8},{1,3},{2,10},{3,1},{4,12},{5,7},{6,14},{7,5},{8,0},{9,11},{1... | collective-permute-start | bytes 172040 | tf_op jit(solution)/shard_map/ppermute | solution.py:50
  25.3 0.9 %shard_map.78 = bf16[4,128,128]{2,1,0:T(8,128)(2,1)S(1)} custom-call(bf16[3,6,128,256]{3,2,1,0:T(8,128)(2,1)S(1)} %get-tuple-element.78.hid_ref, bf16[4,6,16,256]{3,2,1,0:T(8,128)(2,1)S(1)} %get-tuple-element.84.hid_edge, f32[9,32,128]{2,1,0:T(8,128)S(1)} %get-tuple-element.90.second_ref), custom_call_target="tpu_custom_call" | custom-call | flops 500000000 | bytes 1000000 | tf_op jit(solution)/shard_map/pallas_call | solution.py:625
  26.2 0.7 %copy.9 = bf16[4,4,32,128]{3,1,0,2:T(4,128)(2,1)} copy(bf16[4,4,32,128]{3,2,1,0:T(8,128)(2,1)S(1)} %bitcast.6) | data formatting | bytes 262144 | tf_op jit(solution)/shard_map/reshape | solution.py:631
  27.0 0.0 collective-permute-done.10.refs_2_
  27.0 0.9 %collective-permute-done.9.refs_1_ = bf16[32,896]{1,0:T(8,128)(2,1)S(1)} collective-permute-done((bf16[32,896]{1,0:T(8,128)(2,1)S(1)}, bf16[32,896]{1,0:T(8,128)(2,1)S(1)}, u32[]{:S(2)}, u32[]{:S(2)}) %collective-permute-start.9) | collective-permute-done | bytes 57376 | tf_op jit(solution)/shard_map/ppermute | solution.py:50
  27.8 0.6 %collective-permute-done.8.refs_0_ = bf16[32,896]{1,0:T(8,128)(2,1)S(1)} collective-permute-done((bf16[32,896]{1,0:T(8,128)(2,1)S(1)}, bf16[32,896]{1,0:T(8,128)(2,1)S(1)}, u32[]{:S(2)}, u32[]{:S(2)}) %collective-permute-start.8) | collective-permute-done | bytes 57376 | tf_op jit(solution)/shard_map/ppermute | solution.py:50
  28.4 1.7 %collective-permute-start.13 = (bf16[32,896]{1,0:T(8,128)(2,1)S(1)}, bf16[32,896]{1,0:T(8,128)(2,1)S(1)}, u32[]{:S(2)}, u32[]{:S(2)}) collective-permute-start(bf16[32,896]{1,0:T(8,128)(2,1)S(1)} %shard_map.79.own_ref), channel_id=1, source_target_pairs={{0,6},{1,25},{2,4},{3,27},{4,2},{5,29},{6,0},{7,31},{8,14},{9,17},... | collective-permute-start | bytes 172040 | tf_op jit(solution)/shard_map/ppermute | solution.py:50
  30.1 0.8 %collective-permute-start.12 = (bf16[32,896]{1,0:T(8,128)(2,1)S(1)}, bf16[32,896]{1,0:T(8,128)(2,1)S(1)}, u32[]{:S(2)}, u32[]{:S(2)}) collective-permute-start(bf16[32,896]{1,0:T(8,128)(2,1)S(1)} %shard_map.79.own_ref), channel_id=1, source_target_pairs={{0,4},{1,17},{2,6},{3,19},{4,0},{5,21},{6,2},{7,23},{8,12},{9,25},... | collective-permute-start | bytes 172040 | tf_op jit(solution)/shard_map/ppermute | solution.py:50
  30.9 1.0 %collective-permute-start.11 = (bf16[32,896]{1,0:T(8,128)(2,1)S(1)}, bf16[32,896]{1,0:T(8,128)(2,1)S(1)}, u32[]{:S(2)}, u32[]{:S(2)}) collective-permute-start(bf16[32,896]{1,0:T(8,128)(2,1)S(1)} %shard_map.79.own_ref), channel_id=1, source_target_pairs={{0,2},{1,9},{2,0},{3,11},{4,6},{5,13},{6,4},{7,15},{8,10},{9,1},{1... | collective-permute-start | bytes 172040 | tf_op jit(solution)/shard_map/ppermute | solution.py:50
  32.0 1.6 %collective-permute-done.13.refs_2_ = bf16[32,896]{1,0:T(8,128)(2,1)S(1)} collective-permute-done((bf16[32,896]{1,0:T(8,128)(2,1)S(1)}, bf16[32,896]{1,0:T(8,128)(2,1)S(1)}, u32[]{:S(2)}, u32[]{:S(2)}) %collective-permute-start.13) | collective-permute-done | bytes 57376 | tf_op jit(solution)/shard_map/ppermute | solution.py:50
  33.6 0.7 %collective-permute-done.12.refs_1_ = bf16[32,896]{1,0:T(8,128)(2,1)S(1)} collective-permute-done((bf16[32,896]{1,0:T(8,128)(2,1)S(1)}, bf16[32,896]{1,0:T(8,128)(2,1)S(1)}, u32[]{:S(2)}, u32[]{:S(2)}) %collective-permute-start.12) | collective-permute-done | bytes 57376 | tf_op jit(solution)/shard_map/ppermute | solution.py:50
  34.3 0.8 %collective-permute-done.11.refs_0_ = bf16[32,896]{1,0:T(8,128)(2,1)S(1)} collective-permute-done((bf16[32,896]{1,0:T(8,128)(2,1)S(1)}, bf16[32,896]{1,0:T(8,128)(2,1)S(1)}, u32[]{:S(2)}, u32[]{:S(2)}) %collective-permute-start.11) | collective-permute-done | bytes 57376 | tf_op jit(solution)/shard_map/ppermute | solution.py:50
  35.2 0.1 collective-permute-start.14
  35.2 1.3 %collective-permute-done.14.other_ref = f32[32,896]{1,0:T(8,128)S(1)} collective-permute-done((f32[32,896]{1,0:T(8,128)S(1)}, f32[32,896]{1,0:T(8,128)S(1)}, u32[]{:S(2)}, u32[]{:S(2)}) %collective-permute-start.14) | collective-permute-done | bytes 114720 | tf_op jit(solution)/shard_map/ppermute | solution.py:536
  36.5 0.7 %shard_map.81 = (f32[32,864]{1,0:T(8,128)}, f32[32,864]{1,0:T(8,128)}) custom-call(f32[32,896]{1,0:T(8,128)S(1)} %shard_map.80.mine_ref, f32[32,896]{1,0:T(8,128)S(1)} %collective-permute-done.14.other_ref), custom_call_target="tpu_custom_call" | custom-call | flops 1000000 | bytes 1000000 | tf_op jit(solution)/shard_map/pallas_call | solution.py:654
  (3 shorter events, 0.1 us)
Async XLA Ops:
  2.3 11.5 %collective-permute-start = (bf16[3,128,128]{2,1,0:T(8,128)(2,1)S(1)}, bf16[3,128,128]{2,1,0:T(8,128)(2,1)S(1)}, u32[]{:S(2)}, u32[]{:S(2)}) collective-permute-start(bf16[3,128,128]{2,1,0:T(8,128)(2,1)S(1)} %get-tuple-element.52.face_0), channel_id=1, source_target_pairs={{0,8},{1,9},{2,10},{3,11},{4,12},{5,13},{6,14},{7,15},{8,0},{9,1},... | collective-permute-start | bytes 294920 | tf_op jit(solution)/shard_map/ppermute | solution.py:50
  5.4 8.4 %collective-permute-start.1 = (bf16[3,128,128]{2,1,0:T(8,128)(2,1)S(1)}, bf16[3,128,128]{2,1,0:T(8,128)(2,1)S(1)}, u32[]{:S(2)}, u32[]{:S(2)}) collective-permute-start(bf16[3,128,128]{2,1,0:T(8,128)(2,1)S(1)} %get-tuple-element.53.face_1), channel_id=1, source_target_pairs={{8,16},{9,17},{10,18},{11,19},{12,20},{13,21},{14,22},{15,23},{16,... | collective-permute-start | bytes 294920 | tf_op jit(solution)/shard_map/ppermute | solution.py:50
  6.9 6.9 %collective-permute-start.2 = (bf16[3,128,128]{2,1,0:T(8,128)(2,1)S(1)}, bf16[3,128,128]{2,1,0:T(8,128)(2,1)S(1)}, u32[]{:S(2)}, u32[]{:S(2)}) collective-permute-start(bf16[3,128,128]{2,1,0:T(8,128)(2,1)S(1)} %get-tuple-element.54.refs_0_), channel_id=1, source_target_pairs={{0,4},{1,5},{2,6},{3,7},{4,0},{5,1},{6,2},{7,3},{8,12},{9,13},{10,... | collective-permute-start | bytes 294920 | tf_op jit(solution)/shard_map/ppermute | solution.py:50
  8.6 5.3 %collective-permute-start.3 = (bf16[160,128]{1,0:T(8,128)(2,1)S(1)}, bf16[160,128]{1,0:T(8,128)(2,1)S(1)}, u32[]{:S(2)}, u32[]{:S(2)}) collective-permute-start(bf16[160,128]{1,0:T(8,128)(2,1)S(1)} %get-tuple-element.65), channel_id=1, source_target_pairs={{0,12},{1,13},{2,14},{3,15},{4,8},{5,9},{6,10},{7,11},{8,4},{9,5},... | collective-permute-start | bytes 122888 | tf_op jit(solution)/shard_map/ppermute | solution.py:50
  10.3 4.0 %collective-permute-start.4 = (bf16[160,128]{1,0:T(8,128)(2,1)S(1)}, bf16[160,128]{1,0:T(8,128)(2,1)S(1)}, u32[]{:S(2)}, u32[]{:S(2)}) collective-permute-start(bf16[160,128]{1,0:T(8,128)(2,1)S(1)} %get-tuple-element.66), channel_id=1, source_target_pairs={{8,20},{9,21},{10,22},{11,23},{12,16},{13,17},{14,18},{15,19},{16,... | collective-permute-start | bytes 122888 | tf_op jit(solution)/shard_map/ppermute | solution.py:50
  14.4 3.8 %collective-permute-start.5 = (bf16[32,256]{1,0:T(8,128)(2,1)S(1)}, bf16[32,256]{1,0:T(8,128)(2,1)S(1)}, u32[]{:S(2)}, u32[]{:S(2)}) collective-permute-start(bf16[32,256]{1,0:T(8,128)(2,1)S(1)} %get-tuple-element.67), channel_id=1, source_target_pairs={{1,2},{2,1},{5,6},{6,5},{9,10},{10,9},{13,14},{14,13},{17,18},{18,... | collective-permute-start | bytes 49160 | tf_op jit(solution)/shard_map/ppermute | solution.py:50
  16.0 2.2 %collective-permute-start.6 = (bf16[32,256]{1,0:T(8,128)(2,1)S(1)}, bf16[32,256]{1,0:T(8,128)(2,1)S(1)}, u32[]{:S(2)}, u32[]{:S(2)}) collective-permute-start(bf16[32,256]{1,0:T(8,128)(2,1)S(1)} %get-tuple-element.68), channel_id=1, source_target_pairs={{0,1},{1,0},{2,3},{3,2},{4,5},{5,4},{6,7},{7,6},{8,9},{9,8},{10,11... | collective-permute-start | bytes 49160 | tf_op jit(solution)/shard_map/ppermute | solution.py:50
  19.4 1.4 %collective-permute-start.7 = (f32[32,896]{1,0:T(8,128)S(1)}, f32[32,896]{1,0:T(8,128)S(1)}, u32[]{:S(2)}, u32[]{:S(2)}) collective-permute-start(f32[32,896]{1,0:T(8,128)S(1)} %shard_map.76), channel_id=1, source_target_pairs={{0,1},{1,0},{2,3},{3,2},{4,5},{5,4},{6,7},{7,6},{8,9},{9,8},{10,11... | collective-permute-start | bytes 344072 | tf_op jit(solution)/shard_map/ppermute | solution.py:536
  20.8 6.1 %collective-permute-start.10 = (bf16[32,896]{1,0:T(8,128)(2,1)S(1)}, bf16[32,896]{1,0:T(8,128)(2,1)S(1)}, u32[]{:S(2)}, u32[]{:S(2)}) collective-permute-start(bf16[32,896]{1,0:T(8,128)(2,1)S(1)} %shard_map.77.own_ref), channel_id=1, source_target_pairs={{0,24},{1,7},{2,26},{3,5},{4,28},{5,3},{6,30},{7,1},{8,16},{9,15},... | collective-permute-start | bytes 172040 | tf_op jit(solution)/shard_map/ppermute | solution.py:50
  22.7 5.1 %collective-permute-start.9 = (bf16[32,896]{1,0:T(8,128)(2,1)S(1)}, bf16[32,896]{1,0:T(8,128)(2,1)S(1)}, u32[]{:S(2)}, u32[]{:S(2)}) collective-permute-start(bf16[32,896]{1,0:T(8,128)(2,1)S(1)} %shard_map.77.own_ref), channel_id=1, source_target_pairs={{0,16},{1,5},{2,18},{3,7},{4,20},{5,1},{6,22},{7,3},{8,24},{9,13},... | collective-permute-start | bytes 172040 | tf_op jit(solution)/shard_map/ppermute | solution.py:50
  23.7 4.6 %collective-permute-start.8 = (bf16[32,896]{1,0:T(8,128)(2,1)S(1)}, bf16[32,896]{1,0:T(8,128)(2,1)S(1)}, u32[]{:S(2)}, u32[]{:S(2)}) collective-permute-start(bf16[32,896]{1,0:T(8,128)(2,1)S(1)} %shard_map.77.own_ref), channel_id=1, source_target_pairs={{0,8},{1,3},{2,10},{3,1},{4,12},{5,7},{6,14},{7,5},{8,0},{9,11},{1... | collective-permute-start | bytes 172040 | tf_op jit(solution)/shard_map/ppermute | solution.py:50
  28.4 5.1 %collective-permute-start.13 = (bf16[32,896]{1,0:T(8,128)(2,1)S(1)}, bf16[32,896]{1,0:T(8,128)(2,1)S(1)}, u32[]{:S(2)}, u32[]{:S(2)}) collective-permute-start(bf16[32,896]{1,0:T(8,128)(2,1)S(1)} %shard_map.79.own_ref), channel_id=1, source_target_pairs={{0,6},{1,25},{2,4},{3,27},{4,2},{5,29},{6,0},{7,31},{8,14},{9,17},... | collective-permute-start | bytes 172040 | tf_op jit(solution)/shard_map/ppermute | solution.py:50
  30.1 4.2 %collective-permute-start.12 = (bf16[32,896]{1,0:T(8,128)(2,1)S(1)}, bf16[32,896]{1,0:T(8,128)(2,1)S(1)}, u32[]{:S(2)}, u32[]{:S(2)}) collective-permute-start(bf16[32,896]{1,0:T(8,128)(2,1)S(1)} %shard_map.79.own_ref), channel_id=1, source_target_pairs={{0,4},{1,17},{2,6},{3,19},{4,0},{5,21},{6,2},{7,23},{8,12},{9,25},... | collective-permute-start | bytes 172040 | tf_op jit(solution)/shard_map/ppermute | solution.py:50
  30.9 4.2 %collective-permute-start.11 = (bf16[32,896]{1,0:T(8,128)(2,1)S(1)}, bf16[32,896]{1,0:T(8,128)(2,1)S(1)}, u32[]{:S(2)}, u32[]{:S(2)}) collective-permute-start(bf16[32,896]{1,0:T(8,128)(2,1)S(1)} %shard_map.79.own_ref), channel_id=1, source_target_pairs={{0,2},{1,9},{2,0},{3,11},{4,6},{5,13},{6,4},{7,15},{8,10},{9,1},{1... | collective-permute-start | bytes 172040 | tf_op jit(solution)/shard_map/ppermute | solution.py:50
  35.2 1.4 %collective-permute-start.14 = (f32[32,896]{1,0:T(8,128)S(1)}, f32[32,896]{1,0:T(8,128)S(1)}, u32[]{:S(2)}, u32[]{:S(2)}) collective-permute-start(f32[32,896]{1,0:T(8,128)S(1)} %shard_map.80.mine_ref), channel_id=1, source_target_pairs={{0,1},{1,0},{2,3},{3,2},{4,5},{5,4},{6,7},{7,6},{8,9},{9,8},{10,11... | collective-permute-start | bytes 344072 | tf_op jit(solution)/shard_map/ppermute | solution.py:536

commit v9 on v8

--- a/solution.py
+++ b/solution.py
@@ -63,7 +63,7 @@
         return None
     alone = [place for place in places if place not in target]
     fills = (
-        lambda i, j, k: (i, j, k ^ 2),
+        lambda i, j, k: (i, j, k ^ 1),
         lambda i, j, k: (i, j ^ 1, k),
         lambda i, j, k: (i ^ 1, j, k),
         lambda i, j, k: (i, j, k),

time: 37.4 us -> 37 us (0.989)
  starting transfers between devices: 19.4 us -> 18.2 us
  waiting for transfers between devices: 6.84 us -> 7.56 us
    ppermute x13, starting transfers between devices: 19 us -> 17.8 us  [permute(): lax.ppermute(x, AXES, [(number(place), number(to)) for place, to in targe...]
    ppermute x13, waiting for transfers between devices: 5.11 us -> 5.83 us  [permute(): lax.ppermute(x, AXES, [(number(place), number(to)) for place, to in targe...]
  transfers between devices with their start and end apart: 15 -> 15, of which waited for: 9 -> 8; matrix products, arithmetic and copies ran while one was open for 4% -> 4% of each run, Pallas kernels for 13% -> 13%
where the time goes in v9:
time: 37 us; the launch traced here: 36.8 us
  starting transfers between devices  18.2 us (49%)
  waiting for transfers between devices  7.56 us (20%)
  Pallas kernels  7.5 us (20%)
  other arithmetic  2.02 us (5%)
  between operations  0.78 us (2%)
  local copies, waits for them, and re-layouts  0.72 us (2%)
    ppermute x13, starting transfers between devices, permute(): lax.ppermute(x, AXES, [(number(place), number(to)) for place, to in targe...  17.8 us
    ppermute x13, waiting for transfers between devices, permute(): lax.ppermute(x, AXES, [(number(place), number(to)) for place, to in targe...  5.83 us
    pallas_call x1, Pallas kernels, local(): call(functools.partial(widen, y_sides), [struct((3, n_field, size_z, 256)...  1.98 us
    ppermute x2, waiting for transfers between devices, flip(): return lax.ppermute(x, axis, [(i, i ^ bit) for i in range(size)])  1.73 us
    concatenate x1, other arithmetic, local(): jnp.concatenate([inputs, noise], axis=0)  1.16 us
    pallas_call x1, Pallas kernels, local(): call(spread_weights, [struct((9 * 256, 256), BF16), struct((9 * 256, 256)...  1.05 us
    pallas_call x1, Pallas kernels, local(): call(predict, struct((size_x, lanes, size_z), BF16), scratch=[pltpu.VMEM(...  0.92 us
    concatenate x1, other arithmetic, local(): jnp.concatenate([w_first, w_second], axis=0)  0.86 us
  transfers between devices with their start and end apart: 15, of which 8 were waited for; matrix products, arithmetic and copies ran while one was open for 4% of the time, Pallas kernels for 13%

profile of v9, /device:TPU:0, one launch (start us, length us, event | category | flops | bytes accessed | tf_op | source)
XLA Modules:
  0.0 36.8 jit_solution(2656320183756044429)
XLA Ops:
  0.6 1.2 %pad_maximum_fusion.raw_ref = bf16[2,32,4,4,128]{4,3,2,1,0:T(4,128)(2,1)S(1)} fusion(bf16[1,32,4,4,128]{4,3,2,1,0:T(4,128)(2,1)} %param.5, bf16[1,32,4,4,128]{4,3,2,1,0:T(4,128)(2,1)} %param.4), kind=kLoop, calls=%fused_computation | loop fusion | flops 131072 | bytes 524288 | tf_op jit(solution)/shard_map/concatenate | solution.py:568
  1.8 0.5 %shard_map.67 = (bf16[4,128,128]{2,1,0:T(8,128)(2,1)S(1)}, bf16[4,128,128]{2,1,0:T(8,128)(2,1)S(1)}, bf16[4,128,128]{2,1,0:T(8,128)(2,1)S(1)}, bf16[3,128,128]{2...) custom-call(bf16[2,32,4,4,128]{4,3,2,1,0:T(4,128)(2,1)S(1)} %pad_maximum_fusion.raw_ref), custom_call_target="tpu_custom_call" | custom-call | flops 1000000 | bytes 1000000 | tf_op jit(solution)/shard_map/pallas_call | solution.py:562
  2.3 3.1 %collective-permute-start = (bf16[3,128,128]{2,1,0:T(8,128)(2,1)S(1)}, bf16[3,128,128]{2,1,0:T(8,128)(2,1)S(1)}, u32[]{:S(2)}, u32[]{:S(2)}) collective-permute-start(bf16[3,128,128]{2,1,0:T(8,128)(2,1)S(1)} %get-tuple-element.52.face_0), channel_id=1, source_target_pairs={{0,8},{1,9},{2,10},{3,11},{4,12},{5,13},{6,14},{7,15},{8,0},{9,1},... | collective-permute-start | bytes 294920 | tf_op jit(solution)/shard_map/ppermute | solution.py:50
  5.4 0.0 collective-permute-start.1
  5.4 1.5 %collective-permute-start.2 = (bf16[3,128,128]{2,1,0:T(8,128)(2,1)S(1)}, bf16[3,128,128]{2,1,0:T(8,128)(2,1)S(1)}, u32[]{:S(2)}, u32[]{:S(2)}) collective-permute-start(bf16[3,128,128]{2,1,0:T(8,128)(2,1)S(1)} %get-tuple-element.54.refs_0_), channel_id=1, source_target_pairs={{0,4},{1,5},{2,6},{3,7},{4,0},{5,1},{6,2},{7,3},{8,12},{9,13},{10,... | collective-permute-start | bytes 294920 | tf_op jit(solution)/shard_map/ppermute | solution.py:50
  6.9 0.2 shard_map.70
  7.1 3.2 %collective-permute-start.3 = (bf16[160,128]{1,0:T(8,128)(2,1)S(1)}, bf16[160,128]{1,0:T(8,128)(2,1)S(1)}, u32[]{:S(2)}, u32[]{:S(2)}) collective-permute-start(bf16[160,128]{1,0:T(8,128)(2,1)S(1)} %get-tuple-element.65), channel_id=1, source_target_pairs={{0,12},{1,13},{2,14},{3,15},{4,8},{5,9},{6,10},{7,11},{8,4},{9,5},... | collective-permute-start | bytes 122888 | tf_op jit(solution)/shard_map/ppermute | solution.py:50
  10.3 0.0 collective-permute-start.4
  10.3 0.9 %pad_maximum_fusion.1.both_ref = bf16[64,864]{1,0:T(8,128)(2,1)S(1)} fusion(bf16[32,864]{1,0:T(8,128)(2,1)} %param.7, bf16[32,864]{1,0:T(8,128)(2,1)} %param.6), kind=kLoop, calls=%fused_computation.2 | loop fusion | flops 221184 | bytes 221184 | tf_op jit(solution)/shard_map/concatenate | solution.py:580
  11.1 1.0 %shard_map.68 = (bf16[2304,256]{1,0:T(8,128)(2,1)S(1)}, bf16[2304,256]{1,0:T(8,128)(2,1)S(1)}, f32[9,32,128]{2,1,0:T(8,128)S(1)}) custom-call(bf16[64,864]{1,0:T(8,128)(2,1)S(1)} %pad_maximum_fusion.1.both_ref), custom_call_target="tpu_custom_call" | custom-call | flops 1000000 | bytes 4000000 | tf_op jit(solution)/shard_map/pallas_call | solution.py:576
  12.2 0.0 collective-permute-done.refs_0_
  12.2 0.0 collective-permute-done.1.refs_1_
  12.2 0.0 collective-permute-done.2.refs_2_
  12.2 0.1 shard_map.69
  12.4 0.0 collective-permute-done.3.refs_6_
  12.4 0.0 collective-permute-done.4.refs_7_
  12.4 0.1 shard_map.71
  12.5 1.6 %collective-permute-start.5 = (bf16[32,256]{1,0:T(8,128)(2,1)S(1)}, bf16[32,256]{1,0:T(8,128)(2,1)S(1)}, u32[]{:S(2)}, u32[]{:S(2)}) collective-permute-start(bf16[32,256]{1,0:T(8,128)(2,1)S(1)} %get-tuple-element.67), channel_id=1, source_target_pairs={{1,2},{2,1},{5,6},{6,5},{9,10},{10,9},{13,14},{14,13},{17,18},{18,... | collective-permute-start | bytes 49160 | tf_op jit(solution)/shard_map/ppermute | solution.py:50
  14.1 0.1 collective-permute-start.6
  14.2 2.0 %shard_map.72 = (bf16[3,8,128,256]{3,2,1,0:T(8,128)(2,1)S(1)}, f32[6,128,256]{2,1,0:T(8,128)S(1)}, f32[4,128,256]{2,1,0:T(8,128)S(1)}, bf16[3,6,128,256]{3,2,1,0:T(8,128)(2,1)S(1)}, f32[4,128,256]{2,1,0:T(8,128)S(1)}) custom-call(bf16[4,128,128]{2,1,0:T(8,128)(2,1)S(1)} %get-tuple-element.50.refs_0_, bf16[4,128,128]{2,1,0:T(8,128)(2,1)S(1)} %get-tuple-element.51.refs_1_, ...), custom_call_target="tpu_custom_call" | custom-call | flops 1000000000 | bytes 1000000 | tf_op jit(solution)/shard_map/pallas_call | solution.py:592
  16.2 0.1 collective-permute-done.5.side_1
  16.3 0.0 collective-permute-done.6.side_0
  16.3 0.4 %shard_map.73 = (bf16[4,6,16,256]{3,2,1,0:T(8,128)(2,1)S(1)}, bf16[2,8,16,256]{3,2,1,0:T(8,128)(2,1)S(1)}, f32[16,256]{1,0:T(8,128)S(1)}, f32[16,256]{1,0:T(8,128)S(1)}) custom-call(f32[6,128,256]{2,1,0:T(8,128)S(1)} %get-tuple-element.77.pre_ref, bf16[3,6,128,256]{3,2,1,0:T(8,128)(2,1)S(1)} %get-tuple-element.78.hid_ref, ...), custom_call_target="tpu_custom_call" | custom-call | flops 1000000 | bytes 1000000 | tf_op jit(solution)/shard_map/pallas_call | solution.py:607
  16.7 0.1 shard_map.74.pre_grad_ref
  16.9 0.7 %shard_map.76 = f32[32,896]{1,0:T(8,128)S(1)} custom-call(bf16[3,8,128,256]{3,2,1,0:T(8,128)(2,1)S(1)} %get-tuple-element.76.wide_field_ref.xs_ref, bf16[2,8,16,256]{3,2,1,0:T(8,128)(2,1)S(1)} %get-tuple-element.83.xs_edge, bf16[3,6,128,256]{3,2,1,0:T(8,128)(2,1)S(1)} %get-tuple-element.78.hid_ref, bf16[4,6,16,256]{3,2,1,0:T(8,128)(2,1)S(1)} %get-tuple-element.84.hid_edge, ...), custom_call_target="tpu_custom_call" | custom-call | flops 1000000000 | bytes 1000000 | tf_op jit(solution)/shard_map/pallas_call | solution.py:621
  17.5 0.3 collective-permute-start.7
  17.9 0.6 %shard_map.75.keep_ref = f32[32,896]{1,0:T(8,128)S(1)} custom-call(bf16[3,8,128,256]{3,2,1,0:T(8,128)(2,1)S(1)} %get-tuple-element.76.wide_field_ref.xs_ref, bf16[2,8,16,256]{3,2,1,0:T(8,128)(2,1)S(1)} %get-tuple-element.83.xs_edge, bf16[3,6,128,256]{3,2,1,0:T(8,128)(2,1)S(1)} %get-tuple-element.78.hid_ref, ...), custom_call_target="tpu_custom_call" | custom-call | flops 1000000000 | bytes 1000000 | tf_op jit(solution)/shard_map/pallas_call | solution.py:623
  18.5 0.4 %collective-permute-done.7.taken_ref = f32[32,896]{1,0:T(8,128)S(1)} collective-permute-done((f32[32,896]{1,0:T(8,128)S(1)}, f32[32,896]{1,0:T(8,128)S(1)}, u32[]{:S(2)}, u32[]{:S(2)}) %collective-permute-start.7) | collective-permute-done | bytes 114720 | tf_op jit(solution)/shard_map/ppermute | solution.py:536
  18.9 2.2 %collective-permute-start.10 = (bf16[32,896]{1,0:T(8,128)(2,1)S(1)}, bf16[32,896]{1,0:T(8,128)(2,1)S(1)}, u32[]{:S(2)}, u32[]{:S(2)}) collective-permute-start(bf16[32,896]{1,0:T(8,128)(2,1)S(1)} %shard_map.77.own_ref), channel_id=1, source_target_pairs={{0,24},{1,7},{2,26},{3,5},{4,28},{5,3},{6,30},{7,1},{8,16},{9,15},... | collective-permute-start | bytes 172040 | tf_op jit(solution)/shard_map/ppermute | solution.py:50
  21.2 2.6 %collective-permute-start.9 = (bf16[32,896]{1,0:T(8,128)(2,1)S(1)}, bf16[32,896]{1,0:T(8,128)(2,1)S(1)}, u32[]{:S(2)}, u32[]{:S(2)}) collective-permute-start(bf16[32,896]{1,0:T(8,128)(2,1)S(1)} %shard_map.77.own_ref), channel_id=1, source_target_pairs={{0,16},{1,5},{2,18},{3,7},{4,20},{5,1},{6,22},{7,3},{8,24},{9,13},... | collective-permute-start | bytes 172040 | tf_op jit(solution)/shard_map/ppermute | solution.py:50
  23.7 0.0 collective-permute-start.8
  23.7 0.9 %shard_map.78 = bf16[4,128,128]{2,1,0:T(8,128)(2,1)S(1)} custom-call(bf16[3,6,128,256]{3,2,1,0:T(8,128)(2,1)S(1)} %get-tuple-element.78.hid_ref, bf16[4,6,16,256]{3,2,1,0:T(8,128)(2,1)S(1)} %get-tuple-element.84.hid_edge, f32[9,32,128]{2,1,0:T(8,128)S(1)} %get-tuple-element.90.second_ref), custom_call_target="tpu_custom_call" | custom-call | flops 500000000 | bytes 1000000 | tf_op jit(solution)/shard_map/pallas_call | solution.py:625
  24.7 0.7 %copy.9 = bf16[4,4,32,128]{3,1,0,2:T(4,128)(2,1)} copy(bf16[4,4,32,128]{3,2,1,0:T(8,128)(2,1)S(1)} %bitcast.6) | data formatting | bytes 262144 | tf_op jit(solution)/shard_map/reshape | solution.py:631
  25.4 0.0 collective-permute-done.10.refs_2_
  25.4 1.7 %collective-permute-done.9.refs_1_ = bf16[32,896]{1,0:T(8,128)(2,1)S(1)} collective-permute-done((bf16[32,896]{1,0:T(8,128)(2,1)S(1)}, bf16[32,896]{1,0:T(8,128)(2,1)S(1)}, u32[]{:S(2)}, u32[]{:S(2)}) %collective-permute-start.9) | collective-permute-done | bytes 57376 | tf_op jit(solution)/shard_map/ppermute | solution.py:50
  27.1 0.8 %collective-permute-done.8.refs_0_ = bf16[32,896]{1,0:T(8,128)(2,1)S(1)} collective-permute-done((bf16[32,896]{1,0:T(8,128)(2,1)S(1)}, bf16[32,896]{1,0:T(8,128)(2,1)S(1)}, u32[]{:S(2)}, u32[]{:S(2)}) %collective-permute-start.8) | collective-permute-done | bytes 57376 | tf_op jit(solution)/shard_map/ppermute | solution.py:50
  28.0 1.0 %collective-permute-start.13 = (bf16[32,896]{1,0:T(8,128)(2,1)S(1)}, bf16[32,896]{1,0:T(8,128)(2,1)S(1)}, u32[]{:S(2)}, u32[]{:S(2)}) collective-permute-start(bf16[32,896]{1,0:T(8,128)(2,1)S(1)} %shard_map.79.own_ref), channel_id=1, source_target_pairs={{0,6},{1,25},{2,4},{3,27},{4,2},{5,29},{6,0},{7,31},{8,14},{9,17},... | collective-permute-start | bytes 172040 | tf_op jit(solution)/shard_map/ppermute | solution.py:50
  28.9 1.6 %collective-permute-start.12 = (bf16[32,896]{1,0:T(8,128)(2,1)S(1)}, bf16[32,896]{1,0:T(8,128)(2,1)S(1)}, u32[]{:S(2)}, u32[]{:S(2)}) collective-permute-start(bf16[32,896]{1,0:T(8,128)(2,1)S(1)} %shard_map.79.own_ref), channel_id=1, source_target_pairs={{0,4},{1,17},{2,6},{3,19},{4,0},{5,21},{6,2},{7,23},{8,12},{9,25},... | collective-permute-start | bytes 172040 | tf_op jit(solution)/shard_map/ppermute | solution.py:50
  30.5 1.0 %collective-permute-start.11 = (bf16[32,896]{1,0:T(8,128)(2,1)S(1)}, bf16[32,896]{1,0:T(8,128)(2,1)S(1)}, u32[]{:S(2)}, u32[]{:S(2)}) collective-permute-start(bf16[32,896]{1,0:T(8,128)(2,1)S(1)} %shard_map.79.own_ref), channel_id=1, source_target_pairs={{0,2},{1,9},{2,0},{3,11},{4,6},{5,13},{6,4},{7,15},{8,10},{9,1},{1... | collective-permute-start | bytes 172040 | tf_op jit(solution)/shard_map/ppermute | solution.py:50
  31.5 1.6 %collective-permute-done.13.refs_2_ = bf16[32,896]{1,0:T(8,128)(2,1)S(1)} collective-permute-done((bf16[32,896]{1,0:T(8,128)(2,1)S(1)}, bf16[32,896]{1,0:T(8,128)(2,1)S(1)}, u32[]{:S(2)}, u32[]{:S(2)}) %collective-permute-start.13) | collective-permute-done | bytes 57376 | tf_op jit(solution)/shard_map/ppermute | solution.py:50
  33.1 0.2 collective-permute-done.12.refs_1_
  33.3 1.4 %collective-permute-done.11.refs_0_ = bf16[32,896]{1,0:T(8,128)(2,1)S(1)} collective-permute-done((bf16[32,896]{1,0:T(8,128)(2,1)S(1)}, bf16[32,896]{1,0:T(8,128)(2,1)S(1)}, u32[]{:S(2)}, u32[]{:S(2)}) %collective-permute-start.11) | collective-permute-done | bytes 57376 | tf_op jit(solution)/shard_map/ppermute | solution.py:50
  34.7 0.1 collective-permute-start.14
  34.8 1.3 %collective-permute-done.14.other_ref = f32[32,896]{1,0:T(8,128)S(1)} collective-permute-done((f32[32,896]{1,0:T(8,128)S(1)}, f32[32,896]{1,0:T(8,128)S(1)}, u32[]{:S(2)}, u32[]{:S(2)}) %collective-permute-start.14) | collective-permute-done | bytes 114720 | tf_op jit(solution)/shard_map/ppermute | solution.py:536
  36.1 0.7 %shard_map.81 = (f32[32,864]{1,0:T(8,128)}, f32[32,864]{1,0:T(8,128)}) custom-call(f32[32,896]{1,0:T(8,128)S(1)} %shard_map.80.mine_ref, f32[32,896]{1,0:T(8,128)S(1)} %collective-permute-done.14.other_ref), custom_call_target="tpu_custom_call" | custom-call | flops 1000000 | bytes 1000000 | tf_op jit(solution)/shard_map/pallas_call | solution.py:654
  (3 shorter events, 0.1 us)
Async XLA Ops:
  2.3 9.9 %collective-permute-start = (bf16[3,128,128]{2,1,0:T(8,128)(2,1)S(1)}, bf16[3,128,128]{2,1,0:T(8,128)(2,1)S(1)}, u32[]{:S(2)}, u32[]{:S(2)}) collective-permute-start(bf16[3,128,128]{2,1,0:T(8,128)(2,1)S(1)} %get-tuple-element.52.face_0), channel_id=1, source_target_pairs={{0,8},{1,9},{2,10},{3,11},{4,12},{5,13},{6,14},{7,15},{8,0},{9,1},... | collective-permute-start | bytes 294920 | tf_op jit(solution)/shard_map/ppermute | solution.py:50
  5.4 6.9 %collective-permute-start.1 = (bf16[3,128,128]{2,1,0:T(8,128)(2,1)S(1)}, bf16[3,128,128]{2,1,0:T(8,128)(2,1)S(1)}, u32[]{:S(2)}, u32[]{:S(2)}) collective-permute-start(bf16[3,128,128]{2,1,0:T(8,128)(2,1)S(1)} %get-tuple-element.53.face_1), channel_id=1, source_target_pairs={{8,16},{9,17},{10,18},{11,19},{12,20},{13,21},{14,22},{15,23},{16,... | collective-permute-start | bytes 294920 | tf_op jit(solution)/shard_map/ppermute | solution.py:50
  5.4 6.9 %collective-permute-start.2 = (bf16[3,128,128]{2,1,0:T(8,128)(2,1)S(1)}, bf16[3,128,128]{2,1,0:T(8,128)(2,1)S(1)}, u32[]{:S(2)}, u32[]{:S(2)}) collective-permute-start(bf16[3,128,128]{2,1,0:T(8,128)(2,1)S(1)} %get-tuple-element.54.refs_0_), channel_id=1, source_target_pairs={{0,4},{1,5},{2,6},{3,7},{4,0},{5,1},{6,2},{7,3},{8,12},{9,13},{10,... | collective-permute-start | bytes 294920 | tf_op jit(solution)/shard_map/ppermute | solution.py:50
  7.1 5.3 %collective-permute-start.3 = (bf16[160,128]{1,0:T(8,128)(2,1)S(1)}, bf16[160,128]{1,0:T(8,128)(2,1)S(1)}, u32[]{:S(2)}, u32[]{:S(2)}) collective-permute-start(bf16[160,128]{1,0:T(8,128)(2,1)S(1)} %get-tuple-element.65), channel_id=1, source_target_pairs={{0,12},{1,13},{2,14},{3,15},{4,8},{5,9},{6,10},{7,11},{8,4},{9,5},... | collective-permute-start | bytes 122888 | tf_op jit(solution)/shard_map/ppermute | solution.py:50
  10.3 2.1 %collective-permute-start.4 = (bf16[160,128]{1,0:T(8,128)(2,1)S(1)}, bf16[160,128]{1,0:T(8,128)(2,1)S(1)}, u32[]{:S(2)}, u32[]{:S(2)}) collective-permute-start(bf16[160,128]{1,0:T(8,128)(2,1)S(1)} %get-tuple-element.66), channel_id=1, source_target_pairs={{8,20},{9,21},{10,22},{11,23},{12,16},{13,17},{14,18},{15,19},{16,... | collective-permute-start | bytes 122888 | tf_op jit(solution)/shard_map/ppermute | solution.py:50
  12.5 3.8 %collective-permute-start.5 = (bf16[32,256]{1,0:T(8,128)(2,1)S(1)}, bf16[32,256]{1,0:T(8,128)(2,1)S(1)}, u32[]{:S(2)}, u32[]{:S(2)}) collective-permute-start(bf16[32,256]{1,0:T(8,128)(2,1)S(1)} %get-tuple-element.67), channel_id=1, source_target_pairs={{1,2},{2,1},{5,6},{6,5},{9,10},{10,9},{13,14},{14,13},{17,18},{18,... | collective-permute-start | bytes 49160 | tf_op jit(solution)/shard_map/ppermute | solution.py:50
  14.1 2.2 %collective-permute-start.6 = (bf16[32,256]{1,0:T(8,128)(2,1)S(1)}, bf16[32,256]{1,0:T(8,128)(2,1)S(1)}, u32[]{:S(2)}, u32[]{:S(2)}) collective-permute-start(bf16[32,256]{1,0:T(8,128)(2,1)S(1)} %get-tuple-element.68), channel_id=1, source_target_pairs={{0,1},{1,0},{2,3},{3,2},{4,5},{5,4},{6,7},{7,6},{8,9},{9,8},{10,11... | collective-permute-start | bytes 49160 | tf_op jit(solution)/shard_map/ppermute | solution.py:50
  17.5 1.4 %collective-permute-start.7 = (f32[32,896]{1,0:T(8,128)S(1)}, f32[32,896]{1,0:T(8,128)S(1)}, u32[]{:S(2)}, u32[]{:S(2)}) collective-permute-start(f32[32,896]{1,0:T(8,128)S(1)} %shard_map.76), channel_id=1, source_target_pairs={{0,1},{1,0},{2,3},{3,2},{4,5},{5,4},{6,7},{7,6},{8,9},{9,8},{10,11... | collective-permute-start | bytes 344072 | tf_op jit(solution)/shard_map/ppermute | solution.py:536
  18.9 6.5 %collective-permute-start.10 = (bf16[32,896]{1,0:T(8,128)(2,1)S(1)}, bf16[32,896]{1,0:T(8,128)(2,1)S(1)}, u32[]{:S(2)}, u32[]{:S(2)}) collective-permute-start(bf16[32,896]{1,0:T(8,128)(2,1)S(1)} %shard_map.77.own_ref), channel_id=1, source_target_pairs={{0,24},{1,7},{2,26},{3,5},{4,28},{5,3},{6,30},{7,1},{8,16},{9,15},... | collective-permute-start | bytes 172040 | tf_op jit(solution)/shard_map/ppermute | solution.py:50
  21.2 6.0 %collective-permute-start.9 = (bf16[32,896]{1,0:T(8,128)(2,1)S(1)}, bf16[32,896]{1,0:T(8,128)(2,1)S(1)}, u32[]{:S(2)}, u32[]{:S(2)}) collective-permute-start(bf16[32,896]{1,0:T(8,128)(2,1)S(1)} %shard_map.77.own_ref), channel_id=1, source_target_pairs={{0,16},{1,5},{2,18},{3,7},{4,20},{5,1},{6,22},{7,3},{8,24},{9,13},... | collective-permute-start | bytes 172040 | tf_op jit(solution)/shard_map/ppermute | solution.py:50
  23.7 4.2 %collective-permute-start.8 = (bf16[32,896]{1,0:T(8,128)(2,1)S(1)}, bf16[32,896]{1,0:T(8,128)(2,1)S(1)}, u32[]{:S(2)}, u32[]{:S(2)}) collective-permute-start(bf16[32,896]{1,0:T(8,128)(2,1)S(1)} %shard_map.77.own_ref), channel_id=1, source_target_pairs={{0,8},{1,3},{2,10},{3,1},{4,12},{5,7},{6,14},{7,5},{8,0},{9,11},{1... | collective-permute-start | bytes 172040 | tf_op jit(solution)/shard_map/ppermute | solution.py:50
  28.0 5.1 %collective-permute-start.13 = (bf16[32,896]{1,0:T(8,128)(2,1)S(1)}, bf16[32,896]{1,0:T(8,128)(2,1)S(1)}, u32[]{:S(2)}, u32[]{:S(2)}) collective-permute-start(bf16[32,896]{1,0:T(8,128)(2,1)S(1)} %shard_map.79.own_ref), channel_id=1, source_target_pairs={{0,6},{1,25},{2,4},{3,27},{4,2},{5,29},{6,0},{7,31},{8,14},{9,17},... | collective-permute-start | bytes 172040 | tf_op jit(solution)/shard_map/ppermute | solution.py:50
  28.9 4.3 %collective-permute-start.12 = (bf16[32,896]{1,0:T(8,128)(2,1)S(1)}, bf16[32,896]{1,0:T(8,128)(2,1)S(1)}, u32[]{:S(2)}, u32[]{:S(2)}) collective-permute-start(bf16[32,896]{1,0:T(8,128)(2,1)S(1)} %shard_map.79.own_ref), channel_id=1, source_target_pairs={{0,4},{1,17},{2,6},{3,19},{4,0},{5,21},{6,2},{7,23},{8,12},{9,25},... | collective-permute-start | bytes 172040 | tf_op jit(solution)/shard_map/ppermute | solution.py:50
  30.5 4.2 %collective-permute-start.11 = (bf16[32,896]{1,0:T(8,128)(2,1)S(1)}, bf16[32,896]{1,0:T(8,128)(2,1)S(1)}, u32[]{:S(2)}, u32[]{:S(2)}) collective-permute-start(bf16[32,896]{1,0:T(8,128)(2,1)S(1)} %shard_map.79.own_ref), channel_id=1, source_target_pairs={{0,2},{1,9},{2,0},{3,11},{4,6},{5,13},{6,4},{7,15},{8,10},{9,1},{1... | collective-permute-start | bytes 172040 | tf_op jit(solution)/shard_map/ppermute | solution.py:50
  34.7 1.4 %collective-permute-start.14 = (f32[32,896]{1,0:T(8,128)S(1)}, f32[32,896]{1,0:T(8,128)S(1)}, u32[]{:S(2)}, u32[]{:S(2)}) collective-permute-start(f32[32,896]{1,0:T(8,128)S(1)} %shard_map.80.mine_ref), channel_id=1, source_target_pairs={{0,1},{1,0},{2,3},{3,2},{4,5},{5,4},{6,7},{7,6},{8,9},{9,8},{10,11... | collective-permute-start | bytes 344072 | tf_op jit(solution)/shard_map/ppermute | solution.py:536

commit v10 on v9

--- a/solution.py
+++ b/solution.py
@@ -578,7 +578,8 @@
         [struct((9 * 256, 256), BF16), struct((9 * 256, 256), BF16), struct((9, C, 128), F32)],
         moved=4_000_000,
     )(jnp.concatenate([w_first, w_second], axis=0))
-    *near, a1, ab, second = lax.optimization_barrier((*got[:n_near], a1, ab, second))
+    *near, a1, ab, second = lax.optimization_barrier((got[1], got[0], *got[2:n_near], a1, ab, second))
+    near[:2] = near[1::-1]
     got = [*call(functools.partial(sort_faces, y_sides), [face] * 2 + [y_face] * 2)(*near), *got[n_near:]]
 
     n_field, n_noise = size_x + 4, size_x + 2

time: 37 us -> 37.3 us (level)
  waiting for transfers between devices: 7.56 us -> 9.96 us
  starting transfers between devices: 18.2 us -> 16.1 us
    ppermute x13, waiting for transfers between devices: 5.83 us -> 8 us  [permute(): lax.ppermute(x, AXES, [(number(place), number(to)) for place, to in targe...]
    ppermute x13, starting transfers between devices: 17.8 us -> 16 us  [permute(): lax.ppermute(x, AXES, [(number(place), number(to)) for place, to in targe...]
  transfers between devices with their start and end apart: 15 -> 15, of which waited for: 8 -> 10; matrix products, arithmetic and copies ran while one was open for 4% -> 4% of each run, Pallas kernels for 13% -> 13%
where the time goes in v10:
time: 37.3 us; the launch traced here: 37.1 us
  starting transfers between devices  16.1 us (43%)
  waiting for transfers between devices  9.96 us (27%)
  Pallas kernels  7.51 us (20%)
  other arithmetic  2.02 us (5%)
  between operations  0.78 us (2%)
  local copies, waits for them, and re-layouts  0.72 us (2%)
    ppermute x13, starting transfers between devices, permute(): lax.ppermute(x, AXES, [(number(place), number(to)) for place, to in targe...  16 us
    ppermute x13, waiting for transfers between devices, permute(): lax.ppermute(x, AXES, [(number(place), number(to)) for place, to in targe...  8 us
    pallas_call x1, Pallas kernels, local(): call(functools.partial(widen, y_sides), [struct((3, n_field, size_z, 256)...  1.98 us
    ppermute x2, waiting for transfers between devices, flip(): return lax.ppermute(x, axis, [(i, i ^ bit) for i in range(size)])  1.96 us
    concatenate x1, other arithmetic, local(): jnp.concatenate([inputs, noise], axis=0)  1.16 us
    pallas_call x1, Pallas kernels, local(): call(spread_weights, [struct((9 * 256, 256), BF16), struct((9 * 256, 256)...  1.05 us
    pallas_call x1, Pallas kernels, local(): call(predict, struct((size_x, lanes, size_z), BF16), scratch=[pltpu.VMEM(...  0.92 us
    concatenate x1, other arithmetic, local(): jnp.concatenate([w_first, w_second], axis=0)  0.86 us
  transfers between devices with their start and end apart: 15, of which 10 were waited for; matrix products, arithmetic and copies ran while one was open for 4% of the time, Pallas kernels for 13%

profile of v10, /device:TPU:0, one launch (start us, length us, event | category | flops | bytes accessed | tf_op | source)
XLA Modules:
  0.0 37.1 jit_solution(8357092934797128878)
XLA Ops:
  0.6 1.2 %pad_maximum_fusion.raw_ref = bf16[2,32,4,4,128]{4,3,2,1,0:T(4,128)(2,1)S(1)} fusion(bf16[1,32,4,4,128]{4,3,2,1,0:T(4,128)(2,1)} %param.5, bf16[1,32,4,4,128]{4,3,2,1,0:T(4,128)(2,1)} %param.4), kind=kLoop, calls=%fused_computation | loop fusion | flops 131072 | bytes 524288 | tf_op jit(solution)/shard_map/concatenate | solution.py:568
  1.8 0.5 %shard_map.67 = (bf16[4,128,128]{2,1,0:T(8,128)(2,1)S(1)}, bf16[4,128,128]{2,1,0:T(8,128)(2,1)S(1)}, bf16[4,128,128]{2,1,0:T(8,128)(2,1)S(1)}, bf16[3,128,128]{2...) custom-call(bf16[2,32,4,4,128]{4,3,2,1,0:T(4,128)(2,1)S(1)} %pad_maximum_fusion.raw_ref), custom_call_target="tpu_custom_call" | custom-call | flops 1000000 | bytes 1000000 | tf_op jit(solution)/shard_map/pallas_call | solution.py:562
  2.3 0.5 %collective-permute-start = (bf16[3,128,128]{2,1,0:T(8,128)(2,1)S(1)}, bf16[3,128,128]{2,1,0:T(8,128)(2,1)S(1)}, u32[]{:S(2)}, u32[]{:S(2)}) collective-permute-start(bf16[3,128,128]{2,1,0:T(8,128)(2,1)S(1)} %get-tuple-element.52.face_1), channel_id=1, source_target_pairs={{8,16},{9,17},{10,18},{11,19},{12,20},{13,21},{14,22},{15,23},{16,... | collective-permute-start | bytes 294920 | tf_op jit(solution)/shard_map/ppermute | solution.py:50
  2.8 4.1 %collective-permute-start.1 = (bf16[3,128,128]{2,1,0:T(8,128)(2,1)S(1)}, bf16[3,128,128]{2,1,0:T(8,128)(2,1)S(1)}, u32[]{:S(2)}, u32[]{:S(2)}) collective-permute-start(bf16[3,128,128]{2,1,0:T(8,128)(2,1)S(1)} %get-tuple-element.53.face_0), channel_id=1, source_target_pairs={{0,8},{1,9},{2,10},{3,11},{4,12},{5,13},{6,14},{7,15},{8,0},{9,1},... | collective-permute-start | bytes 294920 | tf_op jit(solution)/shard_map/ppermute | solution.py:50
  6.9 1.5 %collective-permute-start.2 = (bf16[3,128,128]{2,1,0:T(8,128)(2,1)S(1)}, bf16[3,128,128]{2,1,0:T(8,128)(2,1)S(1)}, u32[]{:S(2)}, u32[]{:S(2)}) collective-permute-start(bf16[3,128,128]{2,1,0:T(8,128)(2,1)S(1)} %get-tuple-element.54.refs_0_), channel_id=1, source_target_pairs={{0,4},{1,5},{2,6},{3,7},{4,0},{5,1},{6,2},{7,3},{8,12},{9,13},{10,... | collective-permute-start | bytes 294920 | tf_op jit(solution)/shard_map/ppermute | solution.py:50
  8.4 0.2 shard_map.70
  8.7 0.1 collective-permute-start.3
  8.7 0.1 collective-permute-start.4
  8.8 0.9 %pad_maximum_fusion.1.both_ref = bf16[64,864]{1,0:T(8,128)(2,1)S(1)} fusion(bf16[32,864]{1,0:T(8,128)(2,1)} %param.7, bf16[32,864]{1,0:T(8,128)(2,1)} %param.6), kind=kLoop, calls=%fused_computation.2 | loop fusion | flops 221184 | bytes 221184 | tf_op jit(solution)/shard_map/concatenate | solution.py:580
  9.7 1.0 %shard_map.68 = (bf16[2304,256]{1,0:T(8,128)(2,1)S(1)}, bf16[2304,256]{1,0:T(8,128)(2,1)S(1)}, f32[9,32,128]{2,1,0:T(8,128)S(1)}) custom-call(bf16[64,864]{1,0:T(8,128)(2,1)S(1)} %pad_maximum_fusion.1.both_ref), custom_call_target="tpu_custom_call" | custom-call | flops 1000000 | bytes 4000000 | tf_op jit(solution)/shard_map/pallas_call | solution.py:576
  10.7 0.0 collective-permute-done.refs_1_
  10.8 0.0 collective-permute-done.1.refs_0_
  10.8 1.2 %collective-permute-done.2.refs_2_ = bf16[3,128,128]{2,1,0:T(8,128)(2,1)S(1)} collective-permute-done((bf16[3,128,128]{2,1,0:T(8,128)(2,1)S(1)}, bf16[3,128,128]{2,1,0:T(8,128)(2,1)S(1)}, u32[]{:S(2)}, u32[]{:S(2)}) %collective-permute-start.2) | collective-permute-done | bytes 98336 | tf_op jit(solution)/shard_map/ppermute | solution.py:50
  12.0 0.1 shard_map.69
  12.1 1.5 %collective-permute-done.3.refs_6_ = bf16[160,128]{1,0:T(8,128)(2,1)S(1)} collective-permute-done((bf16[160,128]{1,0:T(8,128)(2,1)S(1)}, bf16[160,128]{1,0:T(8,128)(2,1)S(1)}, u32[]{:S(2)}, u32[]{:S(2)}) %collective-permute-start.3) | collective-permute-done | bytes 40992 | tf_op jit(solution)/shard_map/ppermute | solution.py:50
  13.6 0.0 collective-permute-done.4.refs_7_
  13.6 0.1 shard_map.71
  13.8 0.6 %collective-permute-start.5 = (bf16[32,256]{1,0:T(8,128)(2,1)S(1)}, bf16[32,256]{1,0:T(8,128)(2,1)S(1)}, u32[]{:S(2)}, u32[]{:S(2)}) collective-permute-start(bf16[32,256]{1,0:T(8,128)(2,1)S(1)} %get-tuple-element.67), channel_id=1, source_target_pairs={{1,2},{2,1},{5,6},{6,5},{9,10},{10,9},{13,14},{14,13},{17,18},{18,... | collective-permute-start | bytes 49160 | tf_op jit(solution)/shard_map/ppermute | solution.py:50
  14.4 1.1 %collective-permute-start.6 = (bf16[32,256]{1,0:T(8,128)(2,1)S(1)}, bf16[32,256]{1,0:T(8,128)(2,1)S(1)}, u32[]{:S(2)}, u32[]{:S(2)}) collective-permute-start(bf16[32,256]{1,0:T(8,128)(2,1)S(1)} %get-tuple-element.68), channel_id=1, source_target_pairs={{0,1},{1,0},{2,3},{3,2},{4,5},{5,4},{6,7},{7,6},{8,9},{9,8},{10,11... | collective-permute-start | bytes 49160 | tf_op jit(solution)/shard_map/ppermute | solution.py:50
  15.5 2.0 %shard_map.72 = (bf16[3,8,128,256]{3,2,1,0:T(8,128)(2,1)S(1)}, f32[6,128,256]{2,1,0:T(8,128)S(1)}, f32[4,128,256]{2,1,0:T(8,128)S(1)}, bf16[3,6,128,256]{3,2,1,0:T(8,128)(2,1)S(1)}, f32[4,128,256]{2,1,0:T(8,128)S(1)}) custom-call(bf16[4,128,128]{2,1,0:T(8,128)(2,1)S(1)} %get-tuple-element.50.refs_0_, bf16[4,128,128]{2,1,0:T(8,128)(2,1)S(1)} %get-tuple-element.51.refs_1_, ...), custom_call_target="tpu_custom_call" | custom-call | flops 1000000000 | bytes 1000000 | tf_op jit(solution)/shard_map/pallas_call | solution.py:593
  17.5 0.1 collective-permute-done.5.side_1
  17.6 0.0 collective-permute-done.6.side_0
  17.6 0.4 %shard_map.73 = (bf16[4,6,16,256]{3,2,1,0:T(8,128)(2,1)S(1)}, bf16[2,8,16,256]{3,2,1,0:T(8,128)(2,1)S(1)}, f32[16,256]{1,0:T(8,128)S(1)}, f32[16,256]{1,0:T(8,128)S(1)}) custom-call(f32[6,128,256]{2,1,0:T(8,128)S(1)} %get-tuple-element.77.pre_ref, bf16[3,6,128,256]{3,2,1,0:T(8,128)(2,1)S(1)} %get-tuple-element.78.hid_ref, ...), custom_call_target="tpu_custom_call" | custom-call | flops 1000000 | bytes 1000000 | tf_op jit(solution)/shard_map/pallas_call | solution.py:608
  18.0 0.1 shard_map.74.pre_grad_ref
  18.1 0.7 %shard_map.76 = f32[32,896]{1,0:T(8,128)S(1)} custom-call(bf16[3,8,128,256]{3,2,1,0:T(8,128)(2,1)S(1)} %get-tuple-element.76.wide_field_ref.xs_ref, bf16[2,8,16,256]{3,2,1,0:T(8,128)(2,1)S(1)} %get-tuple-element.83.xs_edge, bf16[3,6,128,256]{3,2,1,0:T(8,128)(2,1)S(1)} %get-tuple-element.78.hid_ref, bf16[4,6,16,256]{3,2,1,0:T(8,128)(2,1)S(1)} %get-tuple-element.84.hid_edge, ...), custom_call_target="tpu_custom_call" | custom-call | flops 1000000000 | bytes 1000000 | tf_op jit(solution)/shard_map/pallas_call | solution.py:622
  18.8 0.1 collective-permute-start.7
  18.9 0.7 %shard_map.75.keep_ref = f32[32,896]{1,0:T(8,128)S(1)} custom-call(bf16[3,8,128,256]{3,2,1,0:T(8,128)(2,1)S(1)} %get-tuple-element.76.wide_field_ref.xs_ref, bf16[2,8,16,256]{3,2,1,0:T(8,128)(2,1)S(1)} %get-tuple-element.83.xs_edge, bf16[3,6,128,256]{3,2,1,0:T(8,128)(2,1)S(1)} %get-tuple-element.78.hid_ref, ...), custom_call_target="tpu_custom_call" | custom-call | flops 1000000000 | bytes 1000000 | tf_op jit(solution)/shard_map/pallas_call | solution.py:624
  19.5 0.6 %collective-permute-done.7.taken_ref = f32[32,896]{1,0:T(8,128)S(1)} collective-permute-done((f32[32,896]{1,0:T(8,128)S(1)}, f32[32,896]{1,0:T(8,128)S(1)}, u32[]{:S(2)}, u32[]{:S(2)}) %collective-permute-start.7) | collective-permute-done | bytes 114720 | tf_op jit(solution)/shard_map/ppermute | solution.py:536
  20.2 1.4 %collective-permute-start.10 = (bf16[32,896]{1,0:T(8,128)(2,1)S(1)}, bf16[32,896]{1,0:T(8,128)(2,1)S(1)}, u32[]{:S(2)}, u32[]{:S(2)}) collective-permute-start(bf16[32,896]{1,0:T(8,128)(2,1)S(1)} %shard_map.77.own_ref), channel_id=1, source_target_pairs={{0,24},{1,7},{2,26},{3,5},{4,28},{5,3},{6,30},{7,1},{8,16},{9,15},... | collective-permute-start | bytes 172040 | tf_op jit(solution)/shard_map/ppermute | solution.py:50
  21.6 2.1 %collective-permute-start.9 = (bf16[32,896]{1,0:T(8,128)(2,1)S(1)}, bf16[32,896]{1,0:T(8,128)(2,1)S(1)}, u32[]{:S(2)}, u32[]{:S(2)}) collective-permute-start(bf16[32,896]{1,0:T(8,128)(2,1)S(1)} %shard_map.77.own_ref), channel_id=1, source_target_pairs={{0,16},{1,5},{2,18},{3,7},{4,20},{5,1},{6,22},{7,3},{8,24},{9,13},... | collective-permute-start | bytes 172040 | tf_op jit(solution)/shard_map/ppermute | solution.py:50
  23.7 0.9 %collective-permute-start.8 = (bf16[32,896]{1,0:T(8,128)(2,1)S(1)}, bf16[32,896]{1,0:T(8,128)(2,1)S(1)}, u32[]{:S(2)}, u32[]{:S(2)}) collective-permute-start(bf16[32,896]{1,0:T(8,128)(2,1)S(1)} %shard_map.77.own_ref), channel_id=1, source_target_pairs={{0,8},{1,3},{2,10},{3,1},{4,12},{5,7},{6,14},{7,5},{8,0},{9,11},{1... | collective-permute-start | bytes 172040 | tf_op jit(solution)/shard_map/ppermute | solution.py:50
  24.7 0.9 %shard_map.78 = bf16[4,128,128]{2,1,0:T(8,128)(2,1)S(1)} custom-call(bf16[3,6,128,256]{3,2,1,0:T(8,128)(2,1)S(1)} %get-tuple-element.78.hid_ref, bf16[4,6,16,256]{3,2,1,0:T(8,128)(2,1)S(1)} %get-tuple-element.84.hid_edge, f32[9,32,128]{2,1,0:T(8,128)S(1)} %get-tuple-element.90.second_ref), custom_call_target="tpu_custom_call" | custom-call | flops 500000000 | bytes 1000000 | tf_op jit(solution)/shard_map/pallas_call | solution.py:626
  25.6 0.7 %copy.9 = bf16[4,4,32,128]{3,1,0,2:T(4,128)(2,1)} copy(bf16[4,4,32,128]{3,2,1,0:T(8,128)(2,1)S(1)} %bitcast.6) | data formatting | bytes 262144 | tf_op jit(solution)/shard_map/reshape | solution.py:632
  26.3 0.0 collective-permute-done.10.refs_2_
  26.4 1.4 %collective-permute-done.9.refs_1_ = bf16[32,896]{1,0:T(8,128)(2,1)S(1)} collective-permute-done((bf16[32,896]{1,0:T(8,128)(2,1)S(1)}, bf16[32,896]{1,0:T(8,128)(2,1)S(1)}, u32[]{:S(2)}, u32[]{:S(2)}) %collective-permute-start.9) | collective-permute-done | bytes 57376 | tf_op jit(solution)/shard_map/ppermute | solution.py:50
  27.8 0.6 %collective-permute-done.8.refs_0_ = bf16[32,896]{1,0:T(8,128)(2,1)S(1)} collective-permute-done((bf16[32,896]{1,0:T(8,128)(2,1)S(1)}, bf16[32,896]{1,0:T(8,128)(2,1)S(1)}, u32[]{:S(2)}, u32[]{:S(2)}) %collective-permute-start.8) | collective-permute-done | bytes 57376 | tf_op jit(solution)/shard_map/ppermute | solution.py:50
  28.4 1.5 %collective-permute-start.13 = (bf16[32,896]{1,0:T(8,128)(2,1)S(1)}, bf16[32,896]{1,0:T(8,128)(2,1)S(1)}, u32[]{:S(2)}, u32[]{:S(2)}) collective-permute-start(bf16[32,896]{1,0:T(8,128)(2,1)S(1)} %shard_map.79.own_ref), channel_id=1, source_target_pairs={{0,6},{1,25},{2,4},{3,27},{4,2},{5,29},{6,0},{7,31},{8,14},{9,17},... | collective-permute-start | bytes 172040 | tf_op jit(solution)/shard_map/ppermute | solution.py:50
  29.9 1.0 %collective-permute-start.12 = (bf16[32,896]{1,0:T(8,128)(2,1)S(1)}, bf16[32,896]{1,0:T(8,128)(2,1)S(1)}, u32[]{:S(2)}, u32[]{:S(2)}) collective-permute-start(bf16[32,896]{1,0:T(8,128)(2,1)S(1)} %shard_map.79.own_ref), channel_id=1, source_target_pairs={{0,4},{1,17},{2,6},{3,19},{4,0},{5,21},{6,2},{7,23},{8,12},{9,25},... | collective-permute-start | bytes 172040 | tf_op jit(solution)/shard_map/ppermute | solution.py:50
  30.8 1.1 %collective-permute-start.11 = (bf16[32,896]{1,0:T(8,128)(2,1)S(1)}, bf16[32,896]{1,0:T(8,128)(2,1)S(1)}, u32[]{:S(2)}, u32[]{:S(2)}) collective-permute-start(bf16[32,896]{1,0:T(8,128)(2,1)S(1)} %shard_map.79.own_ref), channel_id=1, source_target_pairs={{0,2},{1,9},{2,0},{3,11},{4,6},{5,13},{6,4},{7,15},{8,10},{9,1},{1... | collective-permute-start | bytes 172040 | tf_op jit(solution)/shard_map/ppermute | solution.py:50
  31.9 1.6 %collective-permute-done.13.refs_2_ = bf16[32,896]{1,0:T(8,128)(2,1)S(1)} collective-permute-done((bf16[32,896]{1,0:T(8,128)(2,1)S(1)}, bf16[32,896]{1,0:T(8,128)(2,1)S(1)}, u32[]{:S(2)}, u32[]{:S(2)}) %collective-permute-start.13) | collective-permute-done | bytes 57376 | tf_op jit(solution)/shard_map/ppermute | solution.py:50
  33.5 0.5 %collective-permute-done.12.refs_1_ = bf16[32,896]{1,0:T(8,128)(2,1)S(1)} collective-permute-done((bf16[32,896]{1,0:T(8,128)(2,1)S(1)}, bf16[32,896]{1,0:T(8,128)(2,1)S(1)}, u32[]{:S(2)}, u32[]{:S(2)}) %collective-permute-start.12) | collective-permute-done | bytes 57376 | tf_op jit(solution)/shard_map/ppermute | solution.py:50
  34.1 1.0 %collective-permute-done.11.refs_0_ = bf16[32,896]{1,0:T(8,128)(2,1)S(1)} collective-permute-done((bf16[32,896]{1,0:T(8,128)(2,1)S(1)}, bf16[32,896]{1,0:T(8,128)(2,1)S(1)}, u32[]{:S(2)}, u32[]{:S(2)}) %collective-permute-start.11) | collective-permute-done | bytes 57376 | tf_op jit(solution)/shard_map/ppermute | solution.py:50
  35.1 0.1 collective-permute-start.14
  35.1 1.3 %collective-permute-done.14.other_ref = f32[32,896]{1,0:T(8,128)S(1)} collective-permute-done((f32[32,896]{1,0:T(8,128)S(1)}, f32[32,896]{1,0:T(8,128)S(1)}, u32[]{:S(2)}, u32[]{:S(2)}) %collective-permute-start.14) | collective-permute-done | bytes 114720 | tf_op jit(solution)/shard_map/ppermute | solution.py:536
  36.4 0.7 %shard_map.81 = (f32[32,864]{1,0:T(8,128)}, f32[32,864]{1,0:T(8,128)}) custom-call(f32[32,896]{1,0:T(8,128)S(1)} %shard_map.80.mine_ref, f32[32,896]{1,0:T(8,128)S(1)} %collective-permute-done.14.other_ref), custom_call_target="tpu_custom_call" | custom-call | flops 1000000 | bytes 1000000 | tf_op jit(solution)/shard_map/pallas_call | solution.py:655
  (3 shorter events, 0.1 us)
Async XLA Ops:
  2.3 8.5 %collective-permute-start = (bf16[3,128,128]{2,1,0:T(8,128)(2,1)S(1)}, bf16[3,128,128]{2,1,0:T(8,128)(2,1)S(1)}, u32[]{:S(2)}, u32[]{:S(2)}) collective-permute-start(bf16[3,128,128]{2,1,0:T(8,128)(2,1)S(1)} %get-tuple-element.52.face_1), channel_id=1, source_target_pairs={{8,16},{9,17},{10,18},{11,19},{12,20},{13,21},{14,22},{15,23},{16,... | collective-permute-start | bytes 294920 | tf_op jit(solution)/shard_map/ppermute | solution.py:50
  2.8 8.0 %collective-permute-start.1 = (bf16[3,128,128]{2,1,0:T(8,128)(2,1)S(1)}, bf16[3,128,128]{2,1,0:T(8,128)(2,1)S(1)}, u32[]{:S(2)}, u32[]{:S(2)}) collective-permute-start(bf16[3,128,128]{2,1,0:T(8,128)(2,1)S(1)} %get-tuple-element.53.face_0), channel_id=1, source_target_pairs={{0,8},{1,9},{2,10},{3,11},{4,12},{5,13},{6,14},{7,15},{8,0},{9,1},... | collective-permute-start | bytes 294920 | tf_op jit(solution)/shard_map/ppermute | solution.py:50
  6.9 5.1 %collective-permute-start.2 = (bf16[3,128,128]{2,1,0:T(8,128)(2,1)S(1)}, bf16[3,128,128]{2,1,0:T(8,128)(2,1)S(1)}, u32[]{:S(2)}, u32[]{:S(2)}) collective-permute-start(bf16[3,128,128]{2,1,0:T(8,128)(2,1)S(1)} %get-tuple-element.54.refs_0_), channel_id=1, source_target_pairs={{0,4},{1,5},{2,6},{3,7},{4,0},{5,1},{6,2},{7,3},{8,12},{9,13},{10,... | collective-permute-start | bytes 294920 | tf_op jit(solution)/shard_map/ppermute | solution.py:50
  8.7 5.0 %collective-permute-start.3 = (bf16[160,128]{1,0:T(8,128)(2,1)S(1)}, bf16[160,128]{1,0:T(8,128)(2,1)S(1)}, u32[]{:S(2)}, u32[]{:S(2)}) collective-permute-start(bf16[160,128]{1,0:T(8,128)(2,1)S(1)} %get-tuple-element.65), channel_id=1, source_target_pairs={{0,12},{1,13},{2,14},{3,15},{4,8},{5,9},{6,10},{7,11},{8,4},{9,5},... | collective-permute-start | bytes 122888 | tf_op jit(solution)/shard_map/ppermute | solution.py:50
  8.7 4.9 %collective-permute-start.4 = (bf16[160,128]{1,0:T(8,128)(2,1)S(1)}, bf16[160,128]{1,0:T(8,128)(2,1)S(1)}, u32[]{:S(2)}, u32[]{:S(2)}) collective-permute-start(bf16[160,128]{1,0:T(8,128)(2,1)S(1)} %get-tuple-element.66), channel_id=1, source_target_pairs={{8,20},{9,21},{10,22},{11,23},{12,16},{13,17},{14,18},{15,19},{16,... | collective-permute-start | bytes 122888 | tf_op jit(solution)/shard_map/ppermute | solution.py:50
  13.8 3.8 %collective-permute-start.5 = (bf16[32,256]{1,0:T(8,128)(2,1)S(1)}, bf16[32,256]{1,0:T(8,128)(2,1)S(1)}, u32[]{:S(2)}, u32[]{:S(2)}) collective-permute-start(bf16[32,256]{1,0:T(8,128)(2,1)S(1)} %get-tuple-element.67), channel_id=1, source_target_pairs={{1,2},{2,1},{5,6},{6,5},{9,10},{10,9},{13,14},{14,13},{17,18},{18,... | collective-permute-start | bytes 49160 | tf_op jit(solution)/shard_map/ppermute | solution.py:50
  14.4 3.2 %collective-permute-start.6 = (bf16[32,256]{1,0:T(8,128)(2,1)S(1)}, bf16[32,256]{1,0:T(8,128)(2,1)S(1)}, u32[]{:S(2)}, u32[]{:S(2)}) collective-permute-start(bf16[32,256]{1,0:T(8,128)(2,1)S(1)} %get-tuple-element.68), channel_id=1, source_target_pairs={{0,1},{1,0},{2,3},{3,2},{4,5},{5,4},{6,7},{7,6},{8,9},{9,8},{10,11... | collective-permute-start | bytes 49160 | tf_op jit(solution)/shard_map/ppermute | solution.py:50
  18.8 1.4 %collective-permute-start.7 = (f32[32,896]{1,0:T(8,128)S(1)}, f32[32,896]{1,0:T(8,128)S(1)}, u32[]{:S(2)}, u32[]{:S(2)}) collective-permute-start(f32[32,896]{1,0:T(8,128)S(1)} %shard_map.76), channel_id=1, source_target_pairs={{0,1},{1,0},{2,3},{3,2},{4,5},{5,4},{6,7},{7,6},{8,9},{9,8},{10,11... | collective-permute-start | bytes 344072 | tf_op jit(solution)/shard_map/ppermute | solution.py:536
  20.2 6.1 %collective-permute-start.10 = (bf16[32,896]{1,0:T(8,128)(2,1)S(1)}, bf16[32,896]{1,0:T(8,128)(2,1)S(1)}, u32[]{:S(2)}, u32[]{:S(2)}) collective-permute-start(bf16[32,896]{1,0:T(8,128)(2,1)S(1)} %shard_map.77.own_ref), channel_id=1, source_target_pairs={{0,24},{1,7},{2,26},{3,5},{4,28},{5,3},{6,30},{7,1},{8,16},{9,15},... | collective-permute-start | bytes 172040 | tf_op jit(solution)/shard_map/ppermute | solution.py:50
  21.6 6.1 %collective-permute-start.9 = (bf16[32,896]{1,0:T(8,128)(2,1)S(1)}, bf16[32,896]{1,0:T(8,128)(2,1)S(1)}, u32[]{:S(2)}, u32[]{:S(2)}) collective-permute-start(bf16[32,896]{1,0:T(8,128)(2,1)S(1)} %shard_map.77.own_ref), channel_id=1, source_target_pairs={{0,16},{1,5},{2,18},{3,7},{4,20},{5,1},{6,22},{7,3},{8,24},{9,13},... | collective-permute-start | bytes 172040 | tf_op jit(solution)/shard_map/ppermute | solution.py:50
  23.7 4.6 %collective-permute-start.8 = (bf16[32,896]{1,0:T(8,128)(2,1)S(1)}, bf16[32,896]{1,0:T(8,128)(2,1)S(1)}, u32[]{:S(2)}, u32[]{:S(2)}) collective-permute-start(bf16[32,896]{1,0:T(8,128)(2,1)S(1)} %shard_map.77.own_ref), channel_id=1, source_target_pairs={{0,8},{1,3},{2,10},{3,1},{4,12},{5,7},{6,14},{7,5},{8,0},{9,11},{1... | collective-permute-start | bytes 172040 | tf_op jit(solution)/shard_map/ppermute | solution.py:50
  28.4 5.1 %collective-permute-start.13 = (bf16[32,896]{1,0:T(8,128)(2,1)S(1)}, bf16[32,896]{1,0:T(8,128)(2,1)S(1)}, u32[]{:S(2)}, u32[]{:S(2)}) collective-permute-start(bf16[32,896]{1,0:T(8,128)(2,1)S(1)} %shard_map.79.own_ref), channel_id=1, source_target_pairs={{0,6},{1,25},{2,4},{3,27},{4,2},{5,29},{6,0},{7,31},{8,14},{9,17},... | collective-permute-start | bytes 172040 | tf_op jit(solution)/shard_map/ppermute | solution.py:50
  29.9 4.2 %collective-permute-start.12 = (bf16[32,896]{1,0:T(8,128)(2,1)S(1)}, bf16[32,896]{1,0:T(8,128)(2,1)S(1)}, u32[]{:S(2)}, u32[]{:S(2)}) collective-permute-start(bf16[32,896]{1,0:T(8,128)(2,1)S(1)} %shard_map.79.own_ref), channel_id=1, source_target_pairs={{0,4},{1,17},{2,6},{3,19},{4,0},{5,21},{6,2},{7,23},{8,12},{9,25},... | collective-permute-start | bytes 172040 | tf_op jit(solution)/shard_map/ppermute | solution.py:50
  30.8 4.2 %collective-permute-start.11 = (bf16[32,896]{1,0:T(8,128)(2,1)S(1)}, bf16[32,896]{1,0:T(8,128)(2,1)S(1)}, u32[]{:S(2)}, u32[]{:S(2)}) collective-permute-start(bf16[32,896]{1,0:T(8,128)(2,1)S(1)} %shard_map.79.own_ref), channel_id=1, source_target_pairs={{0,2},{1,9},{2,0},{3,11},{4,6},{5,13},{6,4},{7,15},{8,10},{9,1},{1... | collective-permute-start | bytes 172040 | tf_op jit(solution)/shard_map/ppermute | solution.py:50
  35.1 1.4 %collective-permute-start.14 = (f32[32,896]{1,0:T(8,128)S(1)}, f32[32,896]{1,0:T(8,128)S(1)}, u32[]{:S(2)}, u32[]{:S(2)}) collective-permute-start(f32[32,896]{1,0:T(8,128)S(1)} %shard_map.80.mine_ref), channel_id=1, source_target_pairs={{0,1},{1,0},{2,3},{3,2},{4,5},{5,4},{6,7},{7,6},{8,9},{9,8},{10,11... | collective-permute-start | bytes 344072 | tf_op jit(solution)/shard_map/ppermute | solution.py:536

commit v11 on v9

--- a/solution.py
+++ b/solution.py
@@ -88,7 +88,7 @@
     lanes = raw_ref.shape[1] * raw_ref.shape[3]
     for x in range(size_x):
         for a, ref in enumerate((field_ref, wide_noise_ref)):
-            rows = jnp.transpose(raw_ref[a, :, x].astype(F32), (1, 0, 2)).reshape(lanes, size_z).astype(BF16)
+            rows = jnp.transpose(raw_ref[a, :, x], (1, 0, 2)).reshape(lanes, size_z)
             if a:
                 noise_rows_ref[x] = rows
             ref[x] = rows.T

time: 37 us -> 37 us (level)
  no operation moved by 1% of the time
where the time goes in v11:
time: 37 us; the launch traced here: 36.8 us
  starting transfers between devices  18.2 us (49%)
  waiting for transfers between devices  7.55 us (20%)
  Pallas kernels  7.52 us (20%)
  other arithmetic  2.02 us (5%)
  between operations  0.78 us (2%)
  local copies, waits for them, and re-layouts  0.72 us (2%)
    ppermute x13, starting transfers between devices, permute(): lax.ppermute(x, AXES, [(number(place), number(to)) for place, to in targe...  17.8 us
    ppermute x13, waiting for transfers between devices, permute(): lax.ppermute(x, AXES, [(number(place), number(to)) for place, to in targe...  5.83 us
    pallas_call x1, Pallas kernels, local(): call(functools.partial(widen, y_sides), [struct((3, n_field, size_z, 256)...  1.98 us
    ppermute x2, waiting for transfers between devices, flip(): return lax.ppermute(x, axis, [(i, i ^ bit) for i in range(size)])  1.73 us
    concatenate x1, other arithmetic, local(): jnp.concatenate([inputs, noise], axis=0)  1.16 us
    pallas_call x1, Pallas kernels, local(): call(spread_weights, [struct((9 * 256, 256), BF16), struct((9 * 256, 256)...  1.05 us
    pallas_call x1, Pallas kernels, local(): call(predict, struct((size_x, lanes, size_z), BF16), scratch=[pltpu.VMEM(...  0.92 us
    concatenate x1, other arithmetic, local(): jnp.concatenate([w_first, w_second], axis=0)  0.86 us
  transfers between devices with their start and end apart: 15, of which 8 were waited for; matrix products, arithmetic and copies ran while one was open for 4% of the time, Pallas kernels for 13%

profile of v11, /device:TPU:0, one launch (start us, length us, event | category | flops | bytes accessed | tf_op | source)
XLA Modules:
  0.0 36.8 jit_solution(14518575951535012754)
XLA Ops:
  0.6 1.2 %pad_maximum_fusion.raw_ref = bf16[2,32,4,4,128]{4,3,2,1,0:T(4,128)(2,1)S(1)} fusion(bf16[1,32,4,4,128]{4,3,2,1,0:T(4,128)(2,1)} %param.5, bf16[1,32,4,4,128]{4,3,2,1,0:T(4,128)(2,1)} %param.4), kind=kLoop, calls=%fused_computation | loop fusion | flops 131072 | bytes 524288 | tf_op jit(solution)/shard_map/concatenate | solution.py:568
  1.8 0.5 %shard_map.67 = (bf16[4,128,128]{2,1,0:T(8,128)(2,1)S(1)}, bf16[4,128,128]{2,1,0:T(8,128)(2,1)S(1)}, bf16[4,128,128]{2,1,0:T(8,128)(2,1)S(1)}, bf16[3,128,128]{2...) custom-call(bf16[2,32,4,4,128]{4,3,2,1,0:T(4,128)(2,1)S(1)} %pad_maximum_fusion.raw_ref), custom_call_target="tpu_custom_call" | custom-call | flops 1000000 | bytes 1000000 | tf_op jit(solution)/shard_map/pallas_call | solution.py:562
  2.3 3.1 %collective-permute-start = (bf16[3,128,128]{2,1,0:T(8,128)(2,1)S(1)}, bf16[3,128,128]{2,1,0:T(8,128)(2,1)S(1)}, u32[]{:S(2)}, u32[]{:S(2)}) collective-permute-start(bf16[3,128,128]{2,1,0:T(8,128)(2,1)S(1)} %get-tuple-element.52.face_0), channel_id=1, source_target_pairs={{0,8},{1,9},{2,10},{3,11},{4,12},{5,13},{6,14},{7,15},{8,0},{9,1},... | collective-permute-start | bytes 294920 | tf_op jit(solution)/shard_map/ppermute | solution.py:50
  5.4 0.0 collective-permute-start.1
  5.4 1.5 %collective-permute-start.2 = (bf16[3,128,128]{2,1,0:T(8,128)(2,1)S(1)}, bf16[3,128,128]{2,1,0:T(8,128)(2,1)S(1)}, u32[]{:S(2)}, u32[]{:S(2)}) collective-permute-start(bf16[3,128,128]{2,1,0:T(8,128)(2,1)S(1)} %get-tuple-element.54.refs_0_), channel_id=1, source_target_pairs={{0,4},{1,5},{2,6},{3,7},{4,0},{5,1},{6,2},{7,3},{8,12},{9,13},{10,... | collective-permute-start | bytes 294920 | tf_op jit(solution)/shard_map/ppermute | solution.py:50
  6.9 0.2 shard_map.70
  7.1 3.2 %collective-permute-start.3 = (bf16[160,128]{1,0:T(8,128)(2,1)S(1)}, bf16[160,128]{1,0:T(8,128)(2,1)S(1)}, u32[]{:S(2)}, u32[]{:S(2)}) collective-permute-start(bf16[160,128]{1,0:T(8,128)(2,1)S(1)} %get-tuple-element.65), channel_id=1, source_target_pairs={{0,12},{1,13},{2,14},{3,15},{4,8},{5,9},{6,10},{7,11},{8,4},{9,5},... | collective-permute-start | bytes 122888 | tf_op jit(solution)/shard_map/ppermute | solution.py:50
  10.3 0.0 collective-permute-start.4
  10.3 0.9 %pad_maximum_fusion.1.both_ref = bf16[64,864]{1,0:T(8,128)(2,1)S(1)} fusion(bf16[32,864]{1,0:T(8,128)(2,1)} %param.7, bf16[32,864]{1,0:T(8,128)(2,1)} %param.6), kind=kLoop, calls=%fused_computation.2 | loop fusion | flops 221184 | bytes 221184 | tf_op jit(solution)/shard_map/concatenate | solution.py:580
  11.2 1.0 %shard_map.68 = (bf16[2304,256]{1,0:T(8,128)(2,1)S(1)}, bf16[2304,256]{1,0:T(8,128)(2,1)S(1)}, f32[9,32,128]{2,1,0:T(8,128)S(1)}) custom-call(bf16[64,864]{1,0:T(8,128)(2,1)S(1)} %pad_maximum_fusion.1.both_ref), custom_call_target="tpu_custom_call" | custom-call | flops 1000000 | bytes 4000000 | tf_op jit(solution)/shard_map/pallas_call | solution.py:576
  12.2 0.0 collective-permute-done.refs_0_
  12.2 0.0 collective-permute-done.1.refs_1_
  12.2 0.0 collective-permute-done.2.refs_2_
  12.2 0.1 shard_map.69
  12.4 0.0 collective-permute-done.3.refs_6_
  12.4 0.0 collective-permute-done.4.refs_7_
  12.4 0.1 shard_map.71
  12.5 1.6 %collective-permute-start.5 = (bf16[32,256]{1,0:T(8,128)(2,1)S(1)}, bf16[32,256]{1,0:T(8,128)(2,1)S(1)}, u32[]{:S(2)}, u32[]{:S(2)}) collective-permute-start(bf16[32,256]{1,0:T(8,128)(2,1)S(1)} %get-tuple-element.67), channel_id=1, source_target_pairs={{1,2},{2,1},{5,6},{6,5},{9,10},{10,9},{13,14},{14,13},{17,18},{18,... | collective-permute-start | bytes 49160 | tf_op jit(solution)/shard_map/ppermute | solution.py:50
  14.1 0.1 collective-permute-start.6
  14.2 2.0 %shard_map.72 = (bf16[3,8,128,256]{3,2,1,0:T(8,128)(2,1)S(1)}, f32[6,128,256]{2,1,0:T(8,128)S(1)}, f32[4,128,256]{2,1,0:T(8,128)S(1)}, bf16[3,6,128,256]{3,2,1,0:T(8,128)(2,1)S(1)}, f32[4,128,256]{2,1,0:T(8,128)S(1)}) custom-call(bf16[4,128,128]{2,1,0:T(8,128)(2,1)S(1)} %get-tuple-element.50.refs_0_, bf16[4,128,128]{2,1,0:T(8,128)(2,1)S(1)} %get-tuple-element.51.refs_1_, ...), custom_call_target="tpu_custom_call" | custom-call | flops 1000000000 | bytes 1000000 | tf_op jit(solution)/shard_map/pallas_call | solution.py:592
  16.2 0.1 collective-permute-done.5.side_1
  16.3 0.0 collective-permute-done.6.side_0
  16.3 0.4 %shard_map.73 = (bf16[4,6,16,256]{3,2,1,0:T(8,128)(2,1)S(1)}, bf16[2,8,16,256]{3,2,1,0:T(8,128)(2,1)S(1)}, f32[16,256]{1,0:T(8,128)S(1)}, f32[16,256]{1,0:T(8,128)S(1)}) custom-call(f32[6,128,256]{2,1,0:T(8,128)S(1)} %get-tuple-element.77.pre_ref, bf16[3,6,128,256]{3,2,1,0:T(8,128)(2,1)S(1)} %get-tuple-element.78.hid_ref, ...), custom_call_target="tpu_custom_call" | custom-call | flops 1000000 | bytes 1000000 | tf_op jit(solution)/shard_map/pallas_call | solution.py:607
  16.8 0.1 shard_map.74.pre_grad_ref
  16.9 0.7 %shard_map.76 = f32[32,896]{1,0:T(8,128)S(1)} custom-call(bf16[3,8,128,256]{3,2,1,0:T(8,128)(2,1)S(1)} %get-tuple-element.76.wide_field_ref.xs_ref, bf16[2,8,16,256]{3,2,1,0:T(8,128)(2,1)S(1)} %get-tuple-element.83.xs_edge, bf16[3,6,128,256]{3,2,1,0:T(8,128)(2,1)S(1)} %get-tuple-element.78.hid_ref, bf16[4,6,16,256]{3,2,1,0:T(8,128)(2,1)S(1)} %get-tuple-element.84.hid_edge, ...), custom_call_target="tpu_custom_call" | custom-call | flops 1000000000 | bytes 1000000 | tf_op jit(solution)/shard_map/pallas_call | solution.py:621
  17.5 0.3 collective-permute-start.7
  17.9 0.6 %shard_map.75.keep_ref = f32[32,896]{1,0:T(8,128)S(1)} custom-call(bf16[3,8,128,256]{3,2,1,0:T(8,128)(2,1)S(1)} %get-tuple-element.76.wide_field_ref.xs_ref, bf16[2,8,16,256]{3,2,1,0:T(8,128)(2,1)S(1)} %get-tuple-element.83.xs_edge, bf16[3,6,128,256]{3,2,1,0:T(8,128)(2,1)S(1)} %get-tuple-element.78.hid_ref, ...), custom_call_target="tpu_custom_call" | custom-call | flops 1000000000 | bytes 1000000 | tf_op jit(solution)/shard_map/pallas_call | solution.py:623
  18.5 0.4 %collective-permute-done.7.taken_ref = f32[32,896]{1,0:T(8,128)S(1)} collective-permute-done((f32[32,896]{1,0:T(8,128)S(1)}, f32[32,896]{1,0:T(8,128)S(1)}, u32[]{:S(2)}, u32[]{:S(2)}) %collective-permute-start.7) | collective-permute-done | bytes 114720 | tf_op jit(solution)/shard_map/ppermute | solution.py:536
  18.9 2.2 %collective-permute-start.10 = (bf16[32,896]{1,0:T(8,128)(2,1)S(1)}, bf16[32,896]{1,0:T(8,128)(2,1)S(1)}, u32[]{:S(2)}, u32[]{:S(2)}) collective-permute-start(bf16[32,896]{1,0:T(8,128)(2,1)S(1)} %shard_map.77.own_ref), channel_id=1, source_target_pairs={{0,24},{1,7},{2,26},{3,5},{4,28},{5,3},{6,30},{7,1},{8,16},{9,15},... | collective-permute-start | bytes 172040 | tf_op jit(solution)/shard_map/ppermute | solution.py:50
  21.2 2.6 %collective-permute-start.9 = (bf16[32,896]{1,0:T(8,128)(2,1)S(1)}, bf16[32,896]{1,0:T(8,128)(2,1)S(1)}, u32[]{:S(2)}, u32[]{:S(2)}) collective-permute-start(bf16[32,896]{1,0:T(8,128)(2,1)S(1)} %shard_map.77.own_ref), channel_id=1, source_target_pairs={{0,16},{1,5},{2,18},{3,7},{4,20},{5,1},{6,22},{7,3},{8,24},{9,13},... | collective-permute-start | bytes 172040 | tf_op jit(solution)/shard_map/ppermute | solution.py:50
  23.8 0.0 collective-permute-start.8
  23.8 0.9 %shard_map.78 = bf16[4,128,128]{2,1,0:T(8,128)(2,1)S(1)} custom-call(bf16[3,6,128,256]{3,2,1,0:T(8,128)(2,1)S(1)} %get-tuple-element.78.hid_ref, bf16[4,6,16,256]{3,2,1,0:T(8,128)(2,1)S(1)} %get-tuple-element.84.hid_edge, f32[9,32,128]{2,1,0:T(8,128)S(1)} %get-tuple-element.90.second_ref), custom_call_target="tpu_custom_call" | custom-call | flops 500000000 | bytes 1000000 | tf_op jit(solution)/shard_map/pallas_call | solution.py:625
  24.7 0.7 %copy.9 = bf16[4,4,32,128]{3,1,0,2:T(4,128)(2,1)} copy(bf16[4,4,32,128]{3,2,1,0:T(8,128)(2,1)S(1)} %bitcast.6) | data formatting | bytes 262144 | tf_op jit(solution)/shard_map/reshape | solution.py:631
  25.4 0.0 collective-permute-done.10.refs_2_
  25.4 1.7 %collective-permute-done.9.refs_1_ = bf16[32,896]{1,0:T(8,128)(2,1)S(1)} collective-permute-done((bf16[32,896]{1,0:T(8,128)(2,1)S(1)}, bf16[32,896]{1,0:T(8,128)(2,1)S(1)}, u32[]{:S(2)}, u32[]{:S(2)}) %collective-permute-start.9) | collective-permute-done | bytes 57376 | tf_op jit(solution)/shard_map/ppermute | solution.py:50
  27.1 0.8 %collective-permute-done.8.refs_0_ = bf16[32,896]{1,0:T(8,128)(2,1)S(1)} collective-permute-done((bf16[32,896]{1,0:T(8,128)(2,1)S(1)}, bf16[32,896]{1,0:T(8,128)(2,1)S(1)}, u32[]{:S(2)}, u32[]{:S(2)}) %collective-permute-start.8) | collective-permute-done | bytes 57376 | tf_op jit(solution)/shard_map/ppermute | solution.py:50
  28.0 1.0 %collective-permute-start.13 = (bf16[32,896]{1,0:T(8,128)(2,1)S(1)}, bf16[32,896]{1,0:T(8,128)(2,1)S(1)}, u32[]{:S(2)}, u32[]{:S(2)}) collective-permute-start(bf16[32,896]{1,0:T(8,128)(2,1)S(1)} %shard_map.79.own_ref), channel_id=1, source_target_pairs={{0,6},{1,25},{2,4},{3,27},{4,2},{5,29},{6,0},{7,31},{8,14},{9,17},... | collective-permute-start | bytes 172040 | tf_op jit(solution)/shard_map/ppermute | solution.py:50
  28.9 1.6 %collective-permute-start.12 = (bf16[32,896]{1,0:T(8,128)(2,1)S(1)}, bf16[32,896]{1,0:T(8,128)(2,1)S(1)}, u32[]{:S(2)}, u32[]{:S(2)}) collective-permute-start(bf16[32,896]{1,0:T(8,128)(2,1)S(1)} %shard_map.79.own_ref), channel_id=1, source_target_pairs={{0,4},{1,17},{2,6},{3,19},{4,0},{5,21},{6,2},{7,23},{8,12},{9,25},... | collective-permute-start | bytes 172040 | tf_op jit(solution)/shard_map/ppermute | solution.py:50
  30.5 1.0 %collective-permute-start.11 = (bf16[32,896]{1,0:T(8,128)(2,1)S(1)}, bf16[32,896]{1,0:T(8,128)(2,1)S(1)}, u32[]{:S(2)}, u32[]{:S(2)}) collective-permute-start(bf16[32,896]{1,0:T(8,128)(2,1)S(1)} %shard_map.79.own_ref), channel_id=1, source_target_pairs={{0,2},{1,9},{2,0},{3,11},{4,6},{5,13},{6,4},{7,15},{8,10},{9,1},{1... | collective-permute-start | bytes 172040 | tf_op jit(solution)/shard_map/ppermute | solution.py:50
  31.5 1.6 %collective-permute-done.13.refs_2_ = bf16[32,896]{1,0:T(8,128)(2,1)S(1)} collective-permute-done((bf16[32,896]{1,0:T(8,128)(2,1)S(1)}, bf16[32,896]{1,0:T(8,128)(2,1)S(1)}, u32[]{:S(2)}, u32[]{:S(2)}) %collective-permute-start.13) | collective-permute-done | bytes 57376 | tf_op jit(solution)/shard_map/ppermute | solution.py:50
  33.1 0.2 collective-permute-done.12.refs_1_
  33.3 1.4 %collective-permute-done.11.refs_0_ = bf16[32,896]{1,0:T(8,128)(2,1)S(1)} collective-permute-done((bf16[32,896]{1,0:T(8,128)(2,1)S(1)}, bf16[32,896]{1,0:T(8,128)(2,1)S(1)}, u32[]{:S(2)}, u32[]{:S(2)}) %collective-permute-start.11) | collective-permute-done | bytes 57376 | tf_op jit(solution)/shard_map/ppermute | solution.py:50
  34.7 0.1 collective-permute-start.14
  34.8 1.3 %collective-permute-done.14.other_ref = f32[32,896]{1,0:T(8,128)S(1)} collective-permute-done((f32[32,896]{1,0:T(8,128)S(1)}, f32[32,896]{1,0:T(8,128)S(1)}, u32[]{:S(2)}, u32[]{:S(2)}) %collective-permute-start.14) | collective-permute-done | bytes 114720 | tf_op jit(solution)/shard_map/ppermute | solution.py:536
  36.1 0.7 %shard_map.81 = (f32[32,864]{1,0:T(8,128)}, f32[32,864]{1,0:T(8,128)}) custom-call(f32[32,896]{1,0:T(8,128)S(1)} %shard_map.80.mine_ref, f32[32,896]{1,0:T(8,128)S(1)} %collective-permute-done.14.other_ref), custom_call_target="tpu_custom_call" | custom-call | flops 1000000 | bytes 1000000 | tf_op jit(solution)/shard_map/pallas_call | solution.py:654
  (3 shorter events, 0.1 us)
Async XLA Ops:
  2.3 9.9 %collective-permute-start = (bf16[3,128,128]{2,1,0:T(8,128)(2,1)S(1)}, bf16[3,128,128]{2,1,0:T(8,128)(2,1)S(1)}, u32[]{:S(2)}, u32[]{:S(2)}) collective-permute-start(bf16[3,128,128]{2,1,0:T(8,128)(2,1)S(1)} %get-tuple-element.52.face_0), channel_id=1, source_target_pairs={{0,8},{1,9},{2,10},{3,11},{4,12},{5,13},{6,14},{7,15},{8,0},{9,1},... | collective-permute-start | bytes 294920 | tf_op jit(solution)/shard_map/ppermute | solution.py:50
  5.4 6.9 %collective-permute-start.1 = (bf16[3,128,128]{2,1,0:T(8,128)(2,1)S(1)}, bf16[3,128,128]{2,1,0:T(8,128)(2,1)S(1)}, u32[]{:S(2)}, u32[]{:S(2)}) collective-permute-start(bf16[3,128,128]{2,1,0:T(8,128)(2,1)S(1)} %get-tuple-element.53.face_1), channel_id=1, source_target_pairs={{8,16},{9,17},{10,18},{11,19},{12,20},{13,21},{14,22},{15,23},{16,... | collective-permute-start | bytes 294920 | tf_op jit(solution)/shard_map/ppermute | solution.py:50
  5.4 6.9 %collective-permute-start.2 = (bf16[3,128,128]{2,1,0:T(8,128)(2,1)S(1)}, bf16[3,128,128]{2,1,0:T(8,128)(2,1)S(1)}, u32[]{:S(2)}, u32[]{:S(2)}) collective-permute-start(bf16[3,128,128]{2,1,0:T(8,128)(2,1)S(1)} %get-tuple-element.54.refs_0_), channel_id=1, source_target_pairs={{0,4},{1,5},{2,6},{3,7},{4,0},{5,1},{6,2},{7,3},{8,12},{9,13},{10,... | collective-permute-start | bytes 294920 | tf_op jit(solution)/shard_map/ppermute | solution.py:50
  7.1 5.3 %collective-permute-start.3 = (bf16[160,128]{1,0:T(8,128)(2,1)S(1)}, bf16[160,128]{1,0:T(8,128)(2,1)S(1)}, u32[]{:S(2)}, u32[]{:S(2)}) collective-permute-start(bf16[160,128]{1,0:T(8,128)(2,1)S(1)} %get-tuple-element.65), channel_id=1, source_target_pairs={{0,12},{1,13},{2,14},{3,15},{4,8},{5,9},{6,10},{7,11},{8,4},{9,5},... | collective-permute-start | bytes 122888 | tf_op jit(solution)/shard_map/ppermute | solution.py:50
  10.3 2.1 %collective-permute-start.4 = (bf16[160,128]{1,0:T(8,128)(2,1)S(1)}, bf16[160,128]{1,0:T(8,128)(2,1)S(1)}, u32[]{:S(2)}, u32[]{:S(2)}) collective-permute-start(bf16[160,128]{1,0:T(8,128)(2,1)S(1)} %get-tuple-element.66), channel_id=1, source_target_pairs={{8,20},{9,21},{10,22},{11,23},{12,16},{13,17},{14,18},{15,19},{16,... | collective-permute-start | bytes 122888 | tf_op jit(solution)/shard_map/ppermute | solution.py:50
  12.5 3.8 %collective-permute-start.5 = (bf16[32,256]{1,0:T(8,128)(2,1)S(1)}, bf16[32,256]{1,0:T(8,128)(2,1)S(1)}, u32[]{:S(2)}, u32[]{:S(2)}) collective-permute-start(bf16[32,256]{1,0:T(8,128)(2,1)S(1)} %get-tuple-element.67), channel_id=1, source_target_pairs={{1,2},{2,1},{5,6},{6,5},{9,10},{10,9},{13,14},{14,13},{17,18},{18,... | collective-permute-start | bytes 49160 | tf_op jit(solution)/shard_map/ppermute | solution.py:50
  14.1 2.2 %collective-permute-start.6 = (bf16[32,256]{1,0:T(8,128)(2,1)S(1)}, bf16[32,256]{1,0:T(8,128)(2,1)S(1)}, u32[]{:S(2)}, u32[]{:S(2)}) collective-permute-start(bf16[32,256]{1,0:T(8,128)(2,1)S(1)} %get-tuple-element.68), channel_id=1, source_target_pairs={{0,1},{1,0},{2,3},{3,2},{4,5},{5,4},{6,7},{7,6},{8,9},{9,8},{10,11... | collective-permute-start | bytes 49160 | tf_op jit(solution)/shard_map/ppermute | solution.py:50
  17.5 1.4 %collective-permute-start.7 = (f32[32,896]{1,0:T(8,128)S(1)}, f32[32,896]{1,0:T(8,128)S(1)}, u32[]{:S(2)}, u32[]{:S(2)}) collective-permute-start(f32[32,896]{1,0:T(8,128)S(1)} %shard_map.76), channel_id=1, source_target_pairs={{0,1},{1,0},{2,3},{3,2},{4,5},{5,4},{6,7},{7,6},{8,9},{9,8},{10,11... | collective-permute-start | bytes 344072 | tf_op jit(solution)/shard_map/ppermute | solution.py:536
  18.9 6.5 %collective-permute-start.10 = (bf16[32,896]{1,0:T(8,128)(2,1)S(1)}, bf16[32,896]{1,0:T(8,128)(2,1)S(1)}, u32[]{:S(2)}, u32[]{:S(2)}) collective-permute-start(bf16[32,896]{1,0:T(8,128)(2,1)S(1)} %shard_map.77.own_ref), channel_id=1, source_target_pairs={{0,24},{1,7},{2,26},{3,5},{4,28},{5,3},{6,30},{7,1},{8,16},{9,15},... | collective-permute-start | bytes 172040 | tf_op jit(solution)/shard_map/ppermute | solution.py:50
  21.2 6.0 %collective-permute-start.9 = (bf16[32,896]{1,0:T(8,128)(2,1)S(1)}, bf16[32,896]{1,0:T(8,128)(2,1)S(1)}, u32[]{:S(2)}, u32[]{:S(2)}) collective-permute-start(bf16[32,896]{1,0:T(8,128)(2,1)S(1)} %shard_map.77.own_ref), channel_id=1, source_target_pairs={{0,16},{1,5},{2,18},{3,7},{4,20},{5,1},{6,22},{7,3},{8,24},{9,13},... | collective-permute-start | bytes 172040 | tf_op jit(solution)/shard_map/ppermute | solution.py:50
  23.8 4.2 %collective-permute-start.8 = (bf16[32,896]{1,0:T(8,128)(2,1)S(1)}, bf16[32,896]{1,0:T(8,128)(2,1)S(1)}, u32[]{:S(2)}, u32[]{:S(2)}) collective-permute-start(bf16[32,896]{1,0:T(8,128)(2,1)S(1)} %shard_map.77.own_ref), channel_id=1, source_target_pairs={{0,8},{1,3},{2,10},{3,1},{4,12},{5,7},{6,14},{7,5},{8,0},{9,11},{1... | collective-permute-start | bytes 172040 | tf_op jit(solution)/shard_map/ppermute | solution.py:50
  28.0 5.1 %collective-permute-start.13 = (bf16[32,896]{1,0:T(8,128)(2,1)S(1)}, bf16[32,896]{1,0:T(8,128)(2,1)S(1)}, u32[]{:S(2)}, u32[]{:S(2)}) collective-permute-start(bf16[32,896]{1,0:T(8,128)(2,1)S(1)} %shard_map.79.own_ref), channel_id=1, source_target_pairs={{0,6},{1,25},{2,4},{3,27},{4,2},{5,29},{6,0},{7,31},{8,14},{9,17},... | collective-permute-start | bytes 172040 | tf_op jit(solution)/shard_map/ppermute | solution.py:50
  28.9 4.3 %collective-permute-start.12 = (bf16[32,896]{1,0:T(8,128)(2,1)S(1)}, bf16[32,896]{1,0:T(8,128)(2,1)S(1)}, u32[]{:S(2)}, u32[]{:S(2)}) collective-permute-start(bf16[32,896]{1,0:T(8,128)(2,1)S(1)} %shard_map.79.own_ref), channel_id=1, source_target_pairs={{0,4},{1,17},{2,6},{3,19},{4,0},{5,21},{6,2},{7,23},{8,12},{9,25},... | collective-permute-start | bytes 172040 | tf_op jit(solution)/shard_map/ppermute | solution.py:50
  30.5 4.2 %collective-permute-start.11 = (bf16[32,896]{1,0:T(8,128)(2,1)S(1)}, bf16[32,896]{1,0:T(8,128)(2,1)S(1)}, u32[]{:S(2)}, u32[]{:S(2)}) collective-permute-start(bf16[32,896]{1,0:T(8,128)(2,1)S(1)} %shard_map.79.own_ref), channel_id=1, source_target_pairs={{0,2},{1,9},{2,0},{3,11},{4,6},{5,13},{6,4},{7,15},{8,10},{9,1},{1... | collective-permute-start | bytes 172040 | tf_op jit(solution)/shard_map/ppermute | solution.py:50
  34.7 1.4 %collective-permute-start.14 = (f32[32,896]{1,0:T(8,128)S(1)}, f32[32,896]{1,0:T(8,128)S(1)}, u32[]{:S(2)}, u32[]{:S(2)}) collective-permute-start(f32[32,896]{1,0:T(8,128)S(1)} %shard_map.80.mine_ref), channel_id=1, source_target_pairs={{0,1},{1,0},{2,3},{3,2},{4,5},{5,4},{6,7},{7,6},{8,9},{9,8},{10,11... | collective-permute-start | bytes 344072 | tf_op jit(solution)/shard_map/ppermute | solution.py:536
